TPU v7x, 256 devices: a whole 4x4x8 slice. The times are simulated.
256 devices in a mesh: ctx: 128 (over y_lo, z, x, core), tp: 2 (over y_hi).
Axes of the slice: x: 4, y: 4 (y_hi: 2, y_lo: 2; y = y_hi * 2 + y_lo), z: 8, core: 2. Of those that a mesh axis runs over, the one named last changes fastest.
Arguments:
- audio_feats: bfloat16 [2, 65536, 512], P('tp', 'ctx'), may hold values from -6 to 6
- res_conv: bfloat16 [2, 3, 512, 256], P('tp'), may hold values from -0.15625 to 0.15625
- res_out: bfloat16 [2, 256, 512], P('tp'), may hold values from -0.375 to 0.375
- down_conv: bfloat16 [2, 4, 512, 512], P('tp'), may hold values from -0.125 to 0.125
- stream_embed: bfloat16 [2, 512, 4096], P('tp'), may hold values from -0.25 to 0.25
- turn_lengths: int32 [2, 32], replicated, may hold values from 1 to 4096, 32768 in all within a row
- speaker_table: float32 [2, 4096], replicated, may hold values from -6 to 6
- norm_gain: float32 [4096], replicated, may hold values from 0.25 to 1.75
- qkv_weight: bfloat16 [3, 4096, 2048], P(None, 'ctx', 'tp')
Outputs:
- embedded: bfloat16 [32768, 4096], P('ctx', 'tp')
- attended: bfloat16 [32768, 2048], P('ctx', 'tp')
Inputs may be any that keep to these rules, and one draw needn't show every extreme that they name: `turn_lengths`: each row holds the 32 turn lengths of one stream; they sum to 32768 and the longest is exactly 4096.
All inputs are finite; a program needn't handle non-finite values.
Results may differ from a plain program's by a relative error of at most 0.0085.
Values may be sent and summed in bfloat16 or wider, within the bound.
No kernel may reach another device: no remote copies, remote signals or barrier semaphores. Data moves between devices by JAX's collectives and lax.ppermute only.
A program may use at most 128 MiB of HBM per device.

v0:
```python
import jax
import jax.numpy as jnp
from jax import lax
from jax.sharding import PartitionSpec as P

HD = 128
LAGS = 7


def from_behind(shard, axis, by):
    count = lax.axis_size(axis)
    pairs = [(i, i + by) for i in range(count) if 0 <= i + by < count]
    return lax.ppermute(shard, axis, pairs)


def elu_act(values):
    return jax.nn.elu(values.astype(jnp.float32))


def residual_unit(extended, conv_taps, conv_back):
    steps = extended.shape[0] - 6
    channels = extended.shape[1]
    inputs = elu_act(extended).astype(jnp.bfloat16)
    stacked = jnp.concatenate(
        [inputs[0:steps], inputs[3 : 3 + steps], inputs[6 : 6 + steps]], axis=1
    )
    inner = jnp.dot(
        stacked,
        conv_taps.reshape(3 * channels, conv_taps.shape[2]),
        preferred_element_type=jnp.float32,
    )
    hidden = elu_act(inner).astype(jnp.bfloat16)
    return (
        extended[6:].astype(jnp.float32)
        + jnp.dot(hidden, conv_back, preferred_element_type=jnp.float32)
    ).astype(jnp.bfloat16)


def on_device(
    audio_feats,
    res_conv,
    res_out,
    down_conv,
    stream_embed,
    turn_lengths,
    speaker_table,
    norm_gain,
    qkv_weight,
):
    audio = audio_feats[0]
    steps = audio.shape[0]
    channels = audio.shape[1]
    frames = steps // 2
    rim = from_behind(audio[steps - 6 :], "ctx", 1)
    resid = residual_unit(jnp.concatenate([rim, audio], axis=0), res_conv[0], res_out[0])
    prior = from_behind(resid[steps - 2 :], "ctx", 1)
    activ = elu_act(jnp.concatenate([prior, resid], axis=0)).astype(jnp.bfloat16)
    first = activ[:steps].reshape(frames, 2 * channels)
    second = activ[2 : steps + 2].reshape(frames, 2 * channels)
    stacked = jnp.concatenate([first, second], axis=1)
    latent = jnp.dot(
        stacked, down_conv[0].reshape(4 * channels, channels), preferred_element_type=jnp.float32
    ).astype(jnp.bfloat16)
    term = jnp.dot(latent, stream_embed[0], preferred_element_type=jnp.float32)
    block_id = lax.axis_index("ctx")
    positions = block_id * frames + jnp.arange(frames, dtype=jnp.int32)
    bounds = jnp.cumsum(turn_lengths, axis=1)
    turn = jnp.sum((bounds[:, :, None] <= positions[None, None, :]).astype(jnp.int32), axis=1)
    active = (turn % 2 == 1).astype(jnp.float32)
    width = speaker_table.shape[1]
    half = width // lax.axis_size("tp")
    offset = lax.axis_index("tp") * half
    summed = lax.psum(term, "tp")
    x_full = (
        summed
        + active[0][:, None] * speaker_table[0][None, :]
        + active[1][:, None] * speaker_table[1][None, :]
    )
    embedded = lax.dynamic_slice_in_dim(x_full, offset, half, 1).astype(jnp.bfloat16)
    meansq = jnp.mean(x_full * x_full, axis=1)
    normed = (x_full * lax.rsqrt(meansq + 1e-05)[:, None] * norm_gain[None, :]).astype(jnp.bfloat16)
    columns = qkv_weight.shape[2]
    projected = jnp.einsum(
        "fd,idc->ifc",
        normed,
        lax.all_gather(qkv_weight, "ctx", axis=1, tiled=True),
        preferred_element_type=jnp.float32,
    ).astype(jnp.bfloat16)
    query = projected[0]
    keyval = projected[1:3]
    blocks = [keyval]
    current = keyval
    for lag in range(LAGS):
        current = from_behind(current, "ctx", 1)
        blocks.insert(0, current)
    window = jnp.concatenate(blocks, axis=1)
    heads = columns // HD
    span = window.shape[1]
    qblock = query.reshape(frames, heads, HD)
    kblock = window[0].reshape(span, heads, HD)
    vblock = window[1].reshape(span, heads, HD)
    scores = jnp.einsum("qhd,khd->hqk", qblock, kblock, preferred_element_type=jnp.float32) * (
        1.0 / HD**0.5
    )
    rows = jnp.arange(frames, dtype=jnp.int32)[:, None]
    cols = jnp.arange(span, dtype=jnp.int32)[None, :]
    diff = LAGS * frames + rows - cols
    keypos = (block_id - LAGS) * frames + cols
    allowed = (diff >= 0) & (diff < LAGS * frames) & (keypos >= 0)
    scores = jnp.where(allowed[None], scores, -1e30)
    top = jnp.max(scores, axis=-1, keepdims=True)
    expo = jnp.exp(scores - top)
    weights = (expo / jnp.sum(expo, axis=-1, keepdims=True)).astype(jnp.bfloat16)
    attended = jnp.einsum("hqk,khd->qhd", weights, vblock, preferred_element_type=jnp.float32)
    attended = attended.astype(jnp.bfloat16).reshape(frames, columns)
    return (embedded, attended)


def solution(mesh):
    placed = (
        P("tp", "ctx", None),
        P("tp", None, None, None),
        P("tp", None, None),
        P("tp", None, None, None),
        P("tp", None, None),
        P(),
        P(),
        P(),
        P(None, "ctx", "tp"),
    )
    return jax.shard_map(
        on_device,
        mesh=mesh,
        in_specs=placed,
        out_specs=(P("ctx", "tp"), P("ctx", "tp")),
        check_vma=False,
    )
```

profile of v0, /device:TPU:8, one launch (start us, length us, event | category | flops | bytes accessed | tf_op | source)
XLA Modules:
  0.0 585.6 jit_solution(10835247749384572320)
XLA Ops:
  8.0 0.0 copy-start
  8.0 0.0 copy-start.8
  8.0 0.0 copy-start.12
  8.0 0.0 all-reduce.2.cloned.1.call-start
  8.1 0.9 slice_bitcast_fusion.2
  8.9 1.9 collective-permute-start
  10.9 8.7 %collective-permute-done = bf16[6,512]{1,0:T(8,128)(2,1)S(1)} collective-permute-done((bf16[6,512]{1,0:T(8,128)(2,1)S(1)}, bf16[6,512]{1,0:T(8,128)(2,1)S(1)}, u32[]{:S(2)}, u32[]{:S(2)}) %collective-permute-start) | collective-permute-done | bytes 6176 | tf_op jit(solution)/shard_map/ppermute | solution.py:13
  19.5 1.6 fusion.34
  21.1 1.3 fusion.62
  22.4 2.7 fusion.31
  25.1 1.9 collective-permute-start.1
  27.0 7.2 %collective-permute-done.1 = bf16[2,512]{1,0:T(2,128)(2,1)S(1)} collective-permute-done((bf16[2,512]{1,0:T(2,128)(2,1)S(1)}, bf16[2,512]{1,0:T(2,128)(2,1)S(1)}, u32[]{:S(2)}, u32[]{:S(2)}) %collective-permute-start.1) | collective-permute-done | bytes 2080 | tf_op jit(solution)/shard_map/ppermute | solution.py:13
  34.2 0.5 fusion.36
  34.7 0.9 fusion.61
  35.6 0.2 reshape.80
  35.8 1.2 reshape.81
  37.1 6.0 %fusion.6 = f32[256,4096]{1,0:T(8,128)} fusion(bf16[1,512,4096]{2,1,0:T(8,128)(2,1)} %param.13, bf16[2048,512]{1,0:T(8,128)(2,1)S(1)} %bitcast.41, bf16[256,1024]{1,0:T(8,128)(2,1)S(1)} %reshape.81, bf16[256,1024]{1,0:T(8,128)(2,1)S(1)} %reshape.80), kind=kOutput, calls=%fused_computation.10 | convolution fusion | flops 1612840960 | bytes 11534336 | tf_op jit(solution)/shard_map/dot_general | solution.py:64
  43.1 0.0 all-reduce.2.cloned.1.call-update
  43.1 0.0 all-gather.2.cloned.1.call-start
  43.2 0.5 all-gather.2.cloned.1.call-update
  43.7 0.1 copy-done.11
  43.8 0.2 reduce_window_sum.11
  44.0 0.1 convert_reduce_fusion
  44.1 120.2 %all-reduce.2.cloned.1.call-done = f32[256,4096]{1,0:T(8,128)} async-done(((f32[256,4096]{1,0:T(8,128)}), f32[256,4096]{1,0:T(8,128)}) %all-reduce.2.cloned.1.call-update) | async-done | bytes 4194320 | tf_op jit(solution)/shard_map/psum | solution.py:73
  164.4 5.1 multiply_reduce_fusion
  169.5 191.7 %all-gather.2.cloned.1.call-done = bf16[3,4096,1024]{2,1,0:T(8,128)(2,1)} async-done(((bf16[3,32,1024]{2,1,0:T(8,128)(2,1)}), bf16[3,4096,1024]{2,1,0:T(8,128)(2,1)}) %all-gather.2.cloned.1.call-update) | async-done | bytes 25165840 | tf_op jit(solution)/shard_map/all_gather | solution.py:86
  361.1 12.8 %fusion.28 = bf16[3,256,1024]{2,1,0:T(8,128)(2,1)S(1)} fusion(bf16[3,4096,1024]{2,1,0:T(8,128)(2,1)} %all-gather.2.cloned.1.call-done, f32[256,4096]{1,0:T(8,128)} %get-tuple-element.7, f32[4096]{0:T(1024)S(1)} %copy-done.13, f32[256]{0:T(256)S(1)} %add_rsqrt_fusion), kind=kOutput, calls=%fused_computation.40 | convolution fusion | flops 6446383104 | bytes 30950400 | tf_op jit(solution)/shard_map/fd,idc->ifc/dot_general | solution.py:83
  374.0 0.1 slice.72
  374.0 1.9 collective-permute-start.2
  376.0 18.4 %collective-permute-done.2 = bf16[2,256,1024]{2,1,0:T(8,128)(2,1)S(1)} collective-permute-done((bf16[2,256,1024]{2,1,0:T(8,128)(2,1)S(1)}, bf16[2,256,1024]{2,1,0:T(8,128)(2,1)S(1)}, u32[]{:S(2)}, u32[]{:S(2)}) %collective-permute-start.2) | collective-permute-done | bytes 1048608 | tf_op jit(solution)/shard_map/ppermute | solution.py:13
  394.4 1.9 collective-permute-start.3
  396.3 18.4 %collective-permute-done.3 = bf16[2,256,1024]{2,1,0:T(8,128)(2,1)S(1)} collective-permute-done((bf16[2,256,1024]{2,1,0:T(8,128)(2,1)S(1)}, bf16[2,256,1024]{2,1,0:T(8,128)(2,1)S(1)}, u32[]{:S(2)}, u32[]{:S(2)}) %collective-permute-start.3) | collective-permute-done | bytes 1048608 | tf_op jit(solution)/shard_map/ppermute | solution.py:13
  414.7 1.0 copy-done.2
  415.7 1.9 collective-permute-start.4
  417.6 18.4 %collective-permute-done.4 = bf16[2,256,1024]{2,1,0:T(8,128)(2,1)S(1)} collective-permute-done((bf16[2,256,1024]{2,1,0:T(8,128)(2,1)S(1)}, bf16[2,256,1024]{2,1,0:T(8,128)(2,1)S(1)}, u32[]{:S(2)}, u32[]{:S(2)}) %collective-permute-start.4) | collective-permute-done | bytes 1048608 | tf_op jit(solution)/shard_map/ppermute | solution.py:13
  436.0 1.0 copy-done.4
  437.0 1.9 collective-permute-start.5
  438.9 18.4 %collective-permute-done.5 = bf16[2,256,1024]{2,1,0:T(8,128)(2,1)S(1)} collective-permute-done((bf16[2,256,1024]{2,1,0:T(8,128)(2,1)S(1)}, bf16[2,256,1024]{2,1,0:T(8,128)(2,1)S(1)}, u32[]{:S(2)}, u32[]{:S(2)}) %collective-permute-start.5) | collective-permute-done | bytes 1048608 | tf_op jit(solution)/shard_map/ppermute | solution.py:13
  457.3 1.0 copy-done.6
  458.3 1.9 collective-permute-start.6
  460.2 18.5 %collective-permute-done.6 = bf16[2,256,1024]{2,1,0:T(8,128)(2,1)} collective-permute-done((bf16[2,256,1024]{2,1,0:T(8,128)(2,1)S(1)}, bf16[2,256,1024]{2,1,0:T(8,128)(2,1)}, u32[]{:S(2)}, u32[]{:S(2)}) %collective-permute-start.6) | collective-permute-done | bytes 1048608 | tf_op jit(solution)/shard_map/ppermute | solution.py:13
  478.7 1.9 collective-permute-start.7
  480.7 18.7 %collective-permute-done.7 = bf16[2,256,1024]{2,1,0:T(8,128)(2,1)} collective-permute-done((bf16[2,256,1024]{2,1,0:T(8,128)(2,1)}, bf16[2,256,1024]{2,1,0:T(8,128)(2,1)}, u32[]{:S(2)}, u32[]{:S(2)}) %collective-permute-start.7) | collective-permute-done | bytes 1048608 | tf_op jit(solution)/shard_map/ppermute | solution.py:13
  499.4 1.9 collective-permute-start.8
  501.3 1.4 fusion.18
  502.7 2.7 dynamic-slice_convert_fusion
  505.5 0.1 copy.20
  505.6 0.0 copy-start.5
  505.6 14.3 %collective-permute-done.8 = bf16[2,256,1024]{2,1,0:T(8,128)(2,1)S(1)} collective-permute-done((bf16[2,256,1024]{2,1,0:T(8,128)(2,1)}, bf16[2,256,1024]{2,1,0:T(8,128)(2,1)S(1)}, u32[]{:S(2)}, u32[]{:S(2)}) %collective-permute-start.8) | collective-permute-done | bytes 1048608 | tf_op jit(solution)/shard_map/ppermute | solution.py:13
  519.9 0.1 constant_dynamic-update-slice_fusion.7
  520.0 1.4 constant_dynamic-update-slice_fusion.6
  521.4 1.3 constant_dynamic-update-slice_fusion.5
  522.7 0.1 constant_dynamic-update-slice_fusion.4
  522.8 0.1 constant_dynamic-update-slice_fusion.3
  522.9 0.1 constant_dynamic-update-slice_fusion.2
  523.0 0.1 constant_dynamic-update-slice_fusion.1
  523.0 0.1 constant_dynamic-update-slice_fusion
  523.1 3.0 slice_bitcast_fusion
  526.1 3.0 copy.21
  529.2 6.5 %copy.19 = bf16[1,2048,1024]{1,2,0:T(8,128)(2,1)} copy(bf16[1,2048,1024]{2,1,0:T(8,128)(2,1)} %get-tuple-element.9) | data formatting | bytes 8388608 | tf_op jit(solution)/shard_map/reshape;squeeze | solution.py:101
  535.7 10.4 %fusion.8 = f32[8,256,2048]{2,1,0:T(8,128)} fusion(bf16[2048,8,128]{2,1,0:T(8,128)(2,1)} %bitcast.42, bf16[256,8,128]{2,1,0:T(8,128)(2,1)S(1)} %bitcast.44), kind=kOutput, calls=%fused_computation.12 | convolution fusion | flops 1073741824 | bytes 21495808 | tf_op jit(solution)/shard_map/qhd,khd->hqk/dot_general | solution.py:102
  546.1 20.9 %fusion.65 = (f32[8,256]{1,0:T(8,128)S(1)}, f32[8,256,2048]{2,1,0:T(8,128)}) fusion(f32[8,256,2048]{2,1,0:T(8,128)} %fusion.8, pred[256,2048]{1,0:T(8,128)(4,1)S(1)} %copy-done.9), kind=kOutput, calls=%fused_computation.86 | output fusion | flops 25167872 | bytes 34086912 | tf_op jit(solution)/shard_map/sub | solution.py:112
  567.0 10.2 %fusion.32 = bf16[8,128,256]{2,1,0:T(8,128)(2,1)S(1)} fusion(bf16[2048,8,128]{0,2,1:T(8,128)(2,1)} %bitcast.43, f32[8,256,2048]{2,1,0:T(8,128)} %get-tuple-element.20, f32[8,256]{1,0:T(8,128)S(1)} %get-tuple-element.19), kind=kOutput, calls=%fused_computation.43 | convolution fusion | flops 1082392576 | bytes 21504000 | tf_op jit(solution)/shard_map/hqk,khd->qhd/dot_general | solution.py:114
  577.1 1.0 copy.18
  (29 shorter events, 0.1 us)
Async XLA Ops:
  8.0 29.0 %copy-start = (bf16[1,4,512,512]{3,2,1,0:T(8,128)(2,1)S(1)}, bf16[1,4,512,512]{3,2,1,0:T(8,128)(2,1)}, u32[]{:S(2)}) copy-start(bf16[1,4,512,512]{3,2,1,0:T(8,128)(2,1)} %param.12) | copy-start | bytes 6291460
  8.0 14.4 %copy-start.8 = (bf16[1,512,512]{2,1,0:T(8,128)(2,1)S(1)}, bf16[1,512,512]{2,1,0:T(8,128)(2,1)}, u32[]{:S(2)}) copy-start(bf16[1,512,512]{2,1,0:T(8,128)(2,1)} %param.9) | copy-start | bytes 1572868
  8.0 14.4 %copy-start.12 = (bf16[1,256,512]{2,1,0:T(8,128)(2,1)S(1)}, bf16[1,256,512]{2,1,0:T(8,128)(2,1)}, u32[]{:S(2)}) copy-start(bf16[1,256,512]{2,1,0:T(8,128)(2,1)} %param.11) | copy-start | bytes 786436
  8.0 156.3 %all-reduce.2.cloned.1.call-start = ((), (), s32[]{:S(2)}) async-start(), calls=%async_computation | async-start | bytes 8388608 | tf_op jit(solution)/shard_map/psum | solution.py:73
  8.9 10.6 %collective-permute-start = (bf16[6,512]{1,0:T(8,128)(2,1)S(1)}, bf16[6,512]{1,0:T(8,128)(2,1)S(1)}, u32[]{:S(2)}, u32[]{:S(2)}) collective-permute-start(bf16[6,512]{1,0:T(8,128)(2,1)S(1)} %slice_bitcast_fusion.2), channel_id=1, source_target_pairs={{0,2},{2,4},{4,6},{6,8},{8,10},{10,12},{12,14},{14,16},{16,18},{18... | collective-permute-start | bytes 18440 | tf_op jit(solution)/shard_map/ppermute | solution.py:13
  25.1 9.1 %collective-permute-start.1 = (bf16[2,512]{1,0:T(2,128)(2,1)S(1)}, bf16[2,512]{1,0:T(2,128)(2,1)S(1)}, u32[]{:S(2)}, u32[]{:S(2)}) collective-permute-start(bf16[2,512]{1,0:T(2,128)(2,1)S(1)} %slice.67), channel_id=1, source_target_pairs={{0,2},{2,4},{4,6},{6,8},{8,10},{10,12},{12,14},{14,16},{16,18},{18... | collective-permute-start | bytes 6152 | tf_op jit(solution)/shard_map/ppermute | solution.py:13
  43.1 0.7 copy-start.11
  43.1 1.0 copy-start.10
  43.1 318.0 %all-gather.2.cloned.1.call-start = ((), (), s32[]{:S(2)}) async-start(), calls=%async_computation.1 | async-start | bytes 25362432 | tf_op jit(solution)/shard_map/all_gather | solution.py:86
  164.4 196.8 %copy-start.13 = (f32[4096]{0:T(1024)S(1)}, f32[4096]{0:T(1024)}, u32[]{:S(2)}) copy-start(f32[4096]{0:T(1024)} %param.16) | copy-start | bytes 49156
  374.0 20.3 %collective-permute-start.2 = (bf16[2,256,1024]{2,1,0:T(8,128)(2,1)S(1)}, bf16[2,256,1024]{2,1,0:T(8,128)(2,1)S(1)}, u32[]{:S(2)}, u32[]{:S(2)}) collective-permute-start(bf16[2,256,1024]{2,1,0:T(8,128)(2,1)S(1)} %slice.72), channel_id=1, source_target_pairs={{0,2},{2,4},{4,6},{6,8},{8,10},{10,12},{12,14},{14,16},{16,18},{18... | collective-permute-start | bytes 3145736 | tf_op jit(solution)/shard_map/ppermute | solution.py:13
  394.4 20.3 %collective-permute-start.3 = (bf16[2,256,1024]{2,1,0:T(8,128)(2,1)S(1)}, bf16[2,256,1024]{2,1,0:T(8,128)(2,1)S(1)}, u32[]{:S(2)}, u32[]{:S(2)}) collective-permute-start(bf16[2,256,1024]{2,1,0:T(8,128)(2,1)S(1)} %collective-permute-done.2), channel_id=1, source_target_pairs={{0,2},{2,4},{4,6},{6,8},{8,10},{10,12},{12,14},{14,16},{16,18},{18... | collective-permute-start | bytes 3145736 | tf_op jit(solution)/shard_map/ppermute | solution.py:13
  414.7 1.0 copy-start.2
  415.7 20.3 %collective-permute-start.4 = (bf16[2,256,1024]{2,1,0:T(8,128)(2,1)S(1)}, bf16[2,256,1024]{2,1,0:T(8,128)(2,1)S(1)}, u32[]{:S(2)}, u32[]{:S(2)}) collective-permute-start(bf16[2,256,1024]{2,1,0:T(8,128)(2,1)S(1)} %collective-permute-done.3), channel_id=1, source_target_pairs={{0,2},{2,4},{4,6},{6,8},{8,10},{10,12},{12,14},{14,16},{16,18},{18... | collective-permute-start | bytes 3145736 | tf_op jit(solution)/shard_map/ppermute | solution.py:13
  436.0 1.0 copy-start.4
  437.0 20.3 %collective-permute-start.5 = (bf16[2,256,1024]{2,1,0:T(8,128)(2,1)S(1)}, bf16[2,256,1024]{2,1,0:T(8,128)(2,1)S(1)}, u32[]{:S(2)}, u32[]{:S(2)}) collective-permute-start(bf16[2,256,1024]{2,1,0:T(8,128)(2,1)S(1)} %collective-permute-done.4), channel_id=1, source_target_pairs={{0,2},{2,4},{4,6},{6,8},{8,10},{10,12},{12,14},{14,16},{16,18},{18... | collective-permute-start | bytes 3145736 | tf_op jit(solution)/shard_map/ppermute | solution.py:13
  457.3 1.0 copy-start.6
  458.3 20.4 %collective-permute-start.6 = (bf16[2,256,1024]{2,1,0:T(8,128)(2,1)S(1)}, bf16[2,256,1024]{2,1,0:T(8,128)(2,1)}, u32[]{:S(2)}, u32[]{:S(2)}) collective-permute-start(bf16[2,256,1024]{2,1,0:T(8,128)(2,1)S(1)} %collective-permute-done.5), channel_id=1, source_target_pairs={{0,2},{2,4},{4,6},{6,8},{8,10},{10,12},{12,14},{14,16},{16,18},{18... | collective-permute-start | bytes 3145736 | tf_op jit(solution)/shard_map/ppermute | solution.py:13
  478.7 20.6 %collective-permute-start.7 = (bf16[2,256,1024]{2,1,0:T(8,128)(2,1)}, bf16[2,256,1024]{2,1,0:T(8,128)(2,1)}, u32[]{:S(2)}, u32[]{:S(2)}) collective-permute-start(bf16[2,256,1024]{2,1,0:T(8,128)(2,1)} %collective-permute-done.6), channel_id=1, source_target_pairs={{0,2},{2,4},{4,6},{6,8},{8,10},{10,12},{12,14},{14,16},{16,18},{18... | collective-permute-start | bytes 3145736 | tf_op jit(solution)/shard_map/ppermute | solution.py:13
  499.4 20.5 %collective-permute-start.8 = (bf16[2,256,1024]{2,1,0:T(8,128)(2,1)}, bf16[2,256,1024]{2,1,0:T(8,128)(2,1)S(1)}, u32[]{:S(2)}, u32[]{:S(2)}) collective-permute-start(bf16[2,256,1024]{2,1,0:T(8,128)(2,1)} %collective-permute-done.7), channel_id=1, source_target_pairs={{0,2},{2,4},{4,6},{6,8},{8,10},{10,12},{12,14},{14,16},{16,18},{18... | collective-permute-start | bytes 3145736 | tf_op jit(solution)/shard_map/ppermute | solution.py:13
  505.4 17.3 %copy-start.7 = (bf16[2,256,1024]{2,1,0:T(8,128)(2,1)S(1)}, bf16[2,256,1024]{2,1,0:T(8,128)(2,1)}, u32[]{:S(2)}) copy-start(bf16[2,256,1024]{2,1,0:T(8,128)(2,1)} %copy-done.6) | copy-start | bytes 3145732
  505.6 17.2 %copy-start.5 = (bf16[2,256,1024]{2,1,0:T(8,128)(2,1)S(1)}, bf16[2,256,1024]{2,1,0:T(8,128)(2,1)}, u32[]{:S(2)}) copy-start(bf16[2,256,1024]{2,1,0:T(8,128)(2,1)} %copy-done.4) | copy-start | bytes 3145732
  520.0 2.9 copy-start.3
  535.7 10.4 %copy-start.9 = (pred[256,2048]{1,0:T(8,128)(4,1)S(1)}, pred[256,2048]{1,0:T(8,128)(4,1)}, u32[]{:S(2)}) copy-start(pred[256,2048]{1,0:T(8,128)(4,1)} %fusion.18) | copy-start | bytes 1572868
  567.0 11.2 %copy-start.1 = (bf16[1,4,512,512]{3,2,1,0:T(8,128)(2,1)S(1)}, bf16[1,4,512,512]{3,2,1,0:T(8,128)(2,1)}, u32[]{:S(2)}) copy-start(bf16[1,4,512,512]{3,2,1,0:T(8,128)(2,1)} %param.12) | copy-start | bytes 6291460
Sparse Core Ops, SparseCore 0:
  43.2 121.0 all-reduce.1
Sparse Core Ops, SparseCore 1:
  45.6 315.4 all-gather.1
where the time goes:
time: 587 us; the launch traced here: 586 us
  waiting for transfers between devices  454 us (77%)
  matrix products  42.1 us (7%)
  other arithmetic  29.8 us (5%)
  local copies, waits for them, and re-layouts  27.2 us (5%)
  starting transfers between devices  17.3 us (3%)
  between operations  15.8 us (3%)
    all_gather x1, waiting for transfers between devices, on_device(): lax.all_gather(qkv_weight, 'ctx', axis=1, tiled=True)  192 us
    ppermute x9, waiting for transfers between devices, from_behind(): return lax.ppermute(shard, axis, pairs)  141 us
    psum x1, waiting for transfers between devices, on_device(): summed = lax.psum(term, 'tp')  120 us
    sub x1, other arithmetic, on_device(): expo = jnp.exp(scores - top)  20.9 us
    ppermute x9, starting transfers between devices, from_behind(): return lax.ppermute(shard, axis, pairs)  17.2 us
    unnamed x40, local copies, waits for them, and re-layouts  13.3 us
    dot_general x1, matrix products, on_device(): jnp.einsum('fd,idc->ifc', normed, lax.all_gather(qkv_weight, 'ctx', axis=...  12.8 us
  transfers between devices with their start and end apart: 11, of which 11 were waited for; matrix products, arithmetic and copies ran while one was open for 2% of the time, Pallas kernels for 0%

commit v1 on v0

v1 whole, which is shorter than its diff:
```python
import functools

import jax
import jax.numpy as jnp
from jax import lax
from jax.experimental import pallas as pl
from jax.experimental.pallas import tpu as pltpu
from jax.sharding import Mesh, PartitionSpec as P

HD = 128
BLOCK = 256
LAGS = 7
D = 4096
CH = 512
CTX = ("yl", "z", "x", "c")
ROW = ("x", "c")
SWAP = [(0, 1), (1, 0)]
BF = jnp.bfloat16
F32 = jnp.float32


def elu(v):
    return jnp.where(v > 0, v, jnp.exp(jnp.minimum(v, 0.0)) - 1.0)


def dot(a, b):
    return jnp.dot(a, b, preferred_element_type=F32)


def encoder(ext, conv_taps, conv_back, conv_down):
    wide = ext.astype(F32)
    u = elu(wide).astype(BF)
    rows = ext.shape[0] - 6
    inner = (
        dot(u[0:rows], conv_taps[0]) + dot(u[3 : 3 + rows], conv_taps[1]) + dot(u[6 : 6 + rows], conv_taps[2])
    )
    hidden = elu(inner).astype(BF)
    resid = (wide[6:] + dot(hidden, conv_back)).astype(BF)
    act = elu(resid.astype(F32)).astype(BF)
    pairs = act.reshape(rows // 2, 2 * CH)
    taps = conv_down.reshape(2, 2 * CH, CH)
    return (dot(pairs[:-1], taps[0]) + dot(pairs[1:], taps[1])).astype(BF)


def attention_kernel(first_ref, q_ref, k_ref, v_ref, o_ref):
    block = pl.program_id(0)
    start = pl.multiple_of((block + 1) * BLOCK, BLOCK)
    span = (LAGS + 1) * BLOCK
    q = q_ref[...]
    k = k_ref[pl.ds(start, span), :]
    s = lax.dot_general(q, k, (((1,), (1,)), ((), ())), preferred_element_type=F32)
    rows = lax.broadcasted_iota(jnp.int32, (BLOCK, span), 0)
    cols = lax.broadcasted_iota(jnp.int32, (BLOCK, span), 1)
    diff = LAGS * BLOCK + rows - cols
    least = jnp.where(first_ref[0] == 1, (LAGS - block) * BLOCK, 0)
    allowed = (diff >= 0) & (diff < LAGS * BLOCK) & (cols >= least)
    s = jnp.where(allowed, s, -1e30)
    top = jnp.max(s, axis=-1, keepdims=True)
    p = jnp.exp(s - top)
    total = jnp.sum(p, axis=-1, keepdims=True)
    o = dot(p.astype(BF), v_ref[pl.ds(start, span), :])
    o_ref[...] = (o / total).astype(BF)


def attention(first, q, k, v):
    rows = q.shape[0]
    return pl.pallas_call(
        attention_kernel,
        grid=(rows // BLOCK,),
        in_specs=[
            pl.BlockSpec(memory_space=pltpu.SMEM),
            pl.BlockSpec((BLOCK, HD), lambda i: (i, 0)),
            pl.BlockSpec(k.shape, lambda i: (0, 0)),
            pl.BlockSpec(v.shape, lambda i: (0, 0)),
        ],
        out_specs=pl.BlockSpec((BLOCK, HD), lambda i: (i, 0)),
        out_shape=jax.ShapeDtypeStruct(q.shape, BF),
        compiler_params=pltpu.CompilerParams(vmem_limit_bytes=40 * 1024 * 1024),
        cost_estimate=pl.CostEstimate(flops=4 * rows * 2048 * HD, bytes_accessed=4 * rows * HD * 2, transcendentals=rows * 2048),
    )(first, q, k, v)


def head_weights(stream_embed, speaker_table, norm_gain, qkv_weight):
    yl = lax.axis_index("yl")
    z = lax.axis_index("z")
    w = lax.all_to_all(qkv_weight, ROW, 2, 1, tiled=True)
    w = lax.all_gather(w, "yl", axis=0)
    w = w.transpose(0, 2, 1, 3).reshape(512, 3 * HD)

    def of_z(a):
        a = a.reshape(a.shape[:-1] + (2, 8, 256))
        a = lax.dynamic_index_in_dim(a, z, a.ndim - 2, keepdims=False)
        return a.reshape(a.shape[:-2] + (512,))

    gain = of_z(norm_gain)
    mine = of_z(lax.dynamic_slice_in_dim(stream_embed, yl * 256, 256, 0))
    rest = lax.ppermute(mine, "tp", SWAP)
    embed = (jnp.concatenate([mine, rest], axis=0).astype(F32) * gain).astype(BF)
    table = of_z(speaker_table) * gain
    high = table.astype(BF)
    low = (table - high.astype(F32)).astype(BF)
    part = dot(embed, w).astype(BF).reshape(8, 64, 3 * HD)
    line = dot(high, w) + dot(low, w)
    top = line.astype(BF)
    rem = (line - top.astype(F32)).astype(BF)
    tail = jnp.concatenate([top, rem, jnp.zeros((12, 3 * HD), BF)], axis=0)
    packed = jnp.concatenate([part, jnp.broadcast_to(tail[None], (8, 16, 3 * HD))], axis=1)
    packed = lax.all_to_all(packed, "z", 0, 0, tiled=True)
    total = jnp.sum(packed.astype(F32), axis=0)
    lines = total[64:66] + total[66:68]
    m = lax.all_gather(total[:64].astype(BF), "z", axis=0, tiled=True)
    m = lax.all_gather(m, "yl", axis=0)
    m = m.reshape(2, 2, 256, 3 * HD).transpose(1, 0, 2, 3).reshape(2 * CH, 3 * HD)
    return m, lines


def on_device(
    audio_feats,
    res_conv,
    res_out,
    down_conv,
    stream_embed,
    turn_lengths,
    speaker_table,
    norm_gain,
    qkv_weight,
):
    tp = lax.axis_index("tp")
    row = lax.axis_index("yl") * 8 + lax.axis_index("z")
    audio = audio_feats[0]
    halo = lax.ppermute(audio[-8:], CTX, [(i, i + 1) for i in range(127)])
    latent = encoder(jnp.concatenate([halo, audio], axis=0), res_conv[0], res_out[0], down_conv[0])
    other = lax.ppermute(latent, "tp", SWAP)
    y = jnp.concatenate([latent, other], axis=1)
    behind = [(i, i + 1) for i in range(15)]
    prev = lax.ppermute(y, ("yl", "z"), behind)
    both = jnp.stack([prev, y])
    every = lax.all_gather(both, ROW, axis=1)
    every = every.reshape(16 * BLOCK, 2 * CH)

    m, lines = head_weights(stream_embed[0], speaker_table, norm_gain, qkv_weight)

    bounds = jnp.cumsum(turn_lengths, axis=1)
    frames = (row - 1) * 8 * BLOCK + jnp.arange(16 * BLOCK, dtype=jnp.int32)
    turn = jnp.sum((bounds[:, None, :] <= frames[None, :, None]).astype(jnp.int32), axis=2)
    active = (turn % 2 == 1).astype(F32)
    here = 8 * BLOCK + (lax.axis_index("x") * 2 + lax.axis_index("c")) * BLOCK
    active_here = lax.dynamic_slice_in_dim(active, here, BLOCK, 1)

    embed = stream_embed[0].reshape(CH, 2, D // 2)
    own = dot(latent, lax.dynamic_index_in_dim(embed, tp, 1, keepdims=False))
    give = dot(latent, lax.dynamic_index_in_dim(embed, 1 - tp, 1, keepdims=False)).astype(BF)
    got = lax.ppermute(give, "tp", SWAP)
    table = lax.dynamic_slice_in_dim(speaker_table, tp * (D // 2), D // 2, 1)
    x = own + got.astype(F32) + active_here[0][:, None] * table[0] + active_here[1][:, None] * table[1]
    embedded = x.astype(BF)
    square = jnp.sum(x * x, axis=1)
    square = square + lax.ppermute(square, "tp", SWAP)
    scale = lax.rsqrt(square * (1.0 / D) + 1e-05)
    scale_prev = lax.ppermute(scale, ("yl", "z"), behind)
    scales = lax.all_gather(jnp.stack([scale_prev, scale]), ROW, axis=1).reshape(16 * BLOCK, 1)

    def project(rows, weight, line, act, factor):
        extra = act[0][:, None] * line[0] + act[1][:, None] * line[1]
        return ((dot(rows, weight) + extra) * factor).astype(BF)

    q = project(every[8 * BLOCK :], m[:, :HD], lines[:, :HD], active[:, 8 * BLOCK :], scales[8 * BLOCK :] * HD**-0.5)
    kv = project(every, m[:, HD:], lines[:, HD:], active, scales)
    first = (row == 0).astype(jnp.int32).reshape(1)
    out = attention(first, q, kv[:, :HD], kv[:, HD:])
    attended = lax.all_to_all(out, ROW, 0, 1, tiled=True)
    return embedded, attended


def solution(mesh):
    fine = Mesh(mesh.devices.reshape(2, 8, 4, 2, 2), CTX + ("tp",))
    placed = (
        P("tp", CTX, None),
        P("tp", None, None, None),
        P("tp", None, None),
        P("tp", None, None, None),
        P("tp", None, None),
        P(),
        P(),
        P(),
        P(None, CTX, "tp"),
    )
    return jax.shard_map(
        on_device,
        mesh=fine,
        in_specs=placed,
        out_specs=(P(CTX, "tp"), P(CTX, "tp")),
        check_vma=False,
    )
```

time: 587 us -> 219 us (0.37)
  waiting for transfers between devices: 454 us -> 32.9 us
  blocking collectives: 0 us -> 86.5 us
  other arithmetic: 29.8 us -> 4.21 us
  matrix products: 42.1 us -> 20.8 us
  starting transfers between devices: 17.3 us -> 27.5 us
  Pallas kernels: 0 us -> 9.13 us
  local copies, waits for them, and re-layouts: 27.2 us -> 20.8 us
    all_gather x1, waiting for transfers between devices: 192 us -> 0.02 us  [on_device(): every = lax.all_gather(both, ROW, axis=1)]
    psum x1 -> x0, waiting for transfers between devices: 120 us -> none  [on_device(): summed = lax.psum(term, 'tp')]
    ppermute x9 -> x7, waiting for transfers between devices: 141 us -> 32.8 us  [the longest x1 11.3 us: on_device(): prev = lax.ppermute(y, ('yl', 'z'), behind)]
    all_gather x0 -> x4, blocking collectives: none -> 73 us  [the longest x1 27.8 us: head_weights(): w = lax.all_gather(w, 'yl', axis=0)]
    dot_general x5 -> x12, matrix products: 42.1 us -> 20.8 us  [dot(): return jnp.dot(a, b, preferred_element_type=F32)]
    sub x1 -> x0, other arithmetic: 20.9 us -> none  [on_device(): expo = jnp.exp(scores - top)]
    all_to_all x0 -> x1, blocking collectives: none -> 13.5 us  [on_device(): attended = lax.all_to_all(out, ROW, 0, 1, tiled=True)]
    all_to_all x0 -> x2, starting transfers between devices: none -> 12.4 us  [the longest x1 6.29 us: head_weights(): packed = lax.all_to_all(packed, 'z', 0, 0, tiled=True)]
  transfers between devices with their start and end apart: 11 -> 10, of which waited for: 11 -> 4; matrix products, arithmetic and copies ran while one was open for 2% -> 11% of each run, Pallas kernels for 0% -> 0%
where the time goes in v1:
time: 219 us; the launch traced here: 216 us
  blocking collectives  86.5 us (39%)
  waiting for transfers between devices  32.9 us (15%)
  starting transfers between devices  27.5 us (13%)
  local copies, waits for them, and re-layouts  20.8 us (9%)
  matrix products  20.8 us (9%)
  between operations  14.4 us (7%)
  Pallas kernels  9.13 us (4%)
  other arithmetic  4.21 us (2%)
    all_gather x1, blocking collectives, head_weights(): w = lax.all_gather(w, 'yl', axis=0)  27.8 us
    all_gather x1, blocking collectives, head_weights(): m = lax.all_gather(total[:64].astype(BF), 'z', axis=0, tiled=True)  25 us
    dot_general x12, matrix products, dot(): return jnp.dot(a, b, preferred_element_type=F32)  20.8 us
    all_to_all x1, blocking collectives, on_device(): attended = lax.all_to_all(out, ROW, 0, 1, tiled=True)  13.5 us
    all_gather x1, blocking collectives, on_device(): lax.all_gather(jnp.stack([scale_prev, scale]), ROW, axis=1)  11.6 us
    ppermute x1, waiting for transfers between devices, on_device(): prev = lax.ppermute(y, ('yl', 'z'), behind)  11.3 us
    unnamed x26, local copies, waits for them, and re-layouts  9.47 us
    ppermute x1, waiting for transfers between devices, on_device(): scale_prev = lax.ppermute(scale, ('yl', 'z'), behind)  9.25 us
  transfers between devices with their start and end apart: 10, of which 4 were waited for; matrix products, arithmetic and copies ran while one was open for 11% of the time, Pallas kernels for 0%

profile of v1, /device:TPU:8, one launch (start us, length us, event | category | flops | bytes accessed | tf_op | source)
XLA Modules:
  0.0 216.3 jit_solution(10474469034441864125)
XLA Ops:
  7.2 0.0 copy-start
  7.2 0.0 all-gather.5.cloned.1.call-start
  7.2 0.7 slice_bitcast_fusion.8
  8.0 2.0 collective-permute-start
  10.0 1.7 fusion.59
  11.7 7.0 %collective-permute-done = bf16[8,512]{1,0:T(8,128)(2,1)S(1)} collective-permute-done((bf16[8,512]{1,0:T(8,128)(2,1)S(1)}, bf16[8,512]{1,0:T(8,128)(2,1)S(1)}, u32[]{:S(2)}, u32[]{:S(2)}) %collective-permute-start) | collective-permute-done | bytes 8224 | tf_op jit(solution)/shard_map/ppermute | solution.py:131
  18.7 0.3 fusion.16
  19.0 0.3 fusion.22
  19.3 1.1 convolution_add_fusion.2
  20.4 1.1 maximum_convert_fusion
  21.5 3.0 %fusion.17 = bf16[514,512]{1,0:T(8,128)(2,1)} fusion(f32[520,512]{1,0:T(8,128)} %maximum_convert_fusion, f32[514,256]{1,0:T(8,128)} %convolution_add_fusion.2, bf16[520,512]{1,0:T(8,128)(2,1)S(1)} %fusion.16, bf16[1,256,512]{2,1,0:T(8,128)(2,1)S(1)} %copy-done, bf16[1,3,512,256]{3,2,1,0:T(8,128)(2,1)} %param.10), kind=kOutput, calls=%fused_computation.29 | convolution fusion | flops 272378880 | bytes 3180544 | tf_op jit(solution)/shard_map/dot_general | solution.py:27
  24.6 2.2 %fusion.60 = (bf16[512,512]{1,0:T(8,128)(2,1)}, bf16[512,512]{1,0:T(8,128)(2,1)S(1)}) fusion(bf16[514,512]{1,0:T(8,128)(2,1)} %fusion.17), kind=kLoop, calls=%fused_computation.98 | loop fusion | bytes 2097152 | tf_op jit(solution)/shard_map/slice | solution.py:42
  26.7 1.0 slice.137
  27.7 1.2 slice.140
  28.9 1.5 fusion.64
  30.4 0.4 fusion.13
  30.9 2.7 %collective-permute-start.2 = (bf16[256,512]{1,0:T(8,128)(2,1)S(1)}, bf16[256,512]{1,0:T(8,128)(2,1)S(1)}, u32[]{:S(2)}, u32[]{:S(2)}) collective-permute-start(bf16[256,512]{1,0:T(8,128)(2,1)S(1)} %fusion.13), channel_id=1, source_target_pairs={{0,1},{1,0},{2,3},{3,2},{4,5},{5,4},{6,7},{7,6},{8,9},{9,8},{10,11... | collective-permute-start | bytes 786440 | tf_op jit(solution)/shard_map/ppermute | solution.py:133
  33.5 5.3 %collective-permute-done.2 = bf16[256,512]{1,0:T(8,128)(2,1)S(1)} collective-permute-done((bf16[256,512]{1,0:T(8,128)(2,1)S(1)}, bf16[256,512]{1,0:T(8,128)(2,1)S(1)}, u32[]{:S(2)}, u32[]{:S(2)}) %collective-permute-start.2) | collective-permute-done | bytes 262176 | tf_op jit(solution)/shard_map/ppermute | solution.py:133
  38.8 0.1 pad_maximum_fusion.1
  39.0 1.9 collective-permute-start.3
  40.9 11.3 %collective-permute-done.3 = bf16[256,1024]{1,0:T(8,128)(2,1)S(1)} collective-permute-done((bf16[256,1024]{1,0:T(8,128)(2,1)S(1)}, bf16[256,1024]{1,0:T(8,128)(2,1)S(1)}, u32[]{:S(2)}, u32[]{:S(2)}) %collective-permute-start.3) | collective-permute-done | bytes 524320 | tf_op jit(solution)/shard_map/ppermute | solution.py:136
  52.2 1.1 pad_maximum_fusion
  53.3 0.0 all-gather.5.cloned.1.call-update
  53.3 0.7 copy.39
  54.0 1.4 reshape.127
  55.4 6.1 %all-to-all-start = ((bf16[8,2,6144]{2,1,0:T(2,128)(2,1)}), bf16[8,2,6144]{2,1,0:T(2,128)(2,1)S(1)}, u32[]{:S(2)}, u32[]{:S(2)}) async-start(bf16[8,2,6144]{2,1,0:T(2,128)(2,1)} %reshape.127), calls=%async_computation | async-start | bytes 393216 | tf_op jit(solution)/shard_map/all_to_all | solution.py:86
  61.5 6.6 %copy.35 = bf16[1,512,4096]{1,2,0:T(8,128)(2,1)} copy(bf16[1,512,4096]{2,1,0:T(8,128)(2,1)} %param.13) | data formatting | bytes 8388608 | tf_op args[4]
  68.1 1.9 constant_dynamic-slice_fusion.4
  70.1 2.9 %collective-permute-start.4 = (bf16[256,512]{0,1:T(8,128)(2,1)S(1)}, bf16[256,512]{0,1:T(8,128)(2,1)S(1)}, u32[]{:S(2)}, u32[]{:S(2)}) collective-permute-start(bf16[256,512]{0,1:T(8,128)(2,1)S(1)} %bitcast.143), channel_id=1, source_target_pairs={{0,1},{1,0},{2,3},{3,2},{4,5},{5,4},{6,7},{7,6},{8,9},{9,8},{10,11... | collective-permute-start | bytes 786440 | tf_op jit(solution)/shard_map/ppermute | solution.py:97
  73.1 0.2 reduce_window_sum.11
  73.3 0.2 convert_reduce_fusion
  73.6 0.1 constant_dynamic-slice_fusion.5
  73.7 0.1 compare_convert_fusion
  73.8 2.3 %convolution_convert_fusion = bf16[256,2048]{1,0:T(8,128)(2,1)S(1)} fusion(bf16[256,512]{1,0:T(8,128)(2,1)S(1)} %fusion.13, bf16[512,2,2048]{0,2,1:T(8,128)(2,1)} %bitcast.123, s32[]{:T(128)S(6)} %select_n.47), kind=kOutput, calls=%fused_computation.7 | convolution fusion | flops 537395200 | bytes 3407876 | tf_op jit(solution)/shard_map/dot_general | solution.py:27
  76.1 0.8 collective-permute-start.1
  76.9 0.1 constant_dynamic-slice_fusion
  77.0 0.1 pad.6.clone
  77.1 0.7 reshape.128
  77.8 0.6 copy.47
  78.3 27.8 %all_gather.30 = bf16[2,3,256,128]{3,2,1,0:T(8,128)(2,1)S(1)} all-gather(bf16[1,3,256,128]{3,2,1,0:T(8,128)(2,1)S(1)} %bitcast.140), channel_id=1, replica_groups=mesh['yl'=2,'z'=8,'x'=4,'c'=2,'tp'=2] {'yl'}, dimensions={0}, use_global_device_ids=true | all-gather | bytes 589824 | tf_op jit(solution)/shard_map/all_gather | solution.py:87
  106.1 0.6 copy.42
  106.7 0.1 copy.51
  106.7 0.2 fusion.65
  106.9 0.2 subtract_convert_fusion.1
  107.2 0.1 maximum_maximum_fusion
  107.3 0.6 convolution_convert_fusion.1
  108.0 3.8 %multiply_reduce_fusion = (f32[256]{0:T(256)S(1)}, bf16[256,2048]{1,0:T(8,128)(2,1)}) fusion(f32[2048]{0:T(1024)S(1)} %bitcast.157, f32[256]{0:T(256)S(1)} %bitcast.162, f32[2048]{0:T(1024)S(1)} %bitcast.156, f32[256]{0:T(256)S(1)} %bitcast.161, bf16[256,2048]{1,0:T(8,128)(2,1)} %collective-permute-done.1, bf16[256,512]{1,0:T(8,128)(2,1)S(1)} %fusion.13, ...), kind=kOutput, calls=%fused_computation.14 | convolution fusion | flops 541589248 | bytes 4475908 | tf_op jit(solution)/shard_map/dot_general | solution.py:27
  111.7 0.8 collective-permute-start.5
  112.6 0.8 pad_maximum_fusion.2
  113.4 6.3 %all-to-all-start.1 = ((bf16[8,80,384]{2,1,0:T(8,128)(2,1)}), bf16[8,80,384]{2,1,0:T(8,128)(2,1)S(1)}, u32[]{:S(2)}, u32[]{:S(2)}) async-start(bf16[8,80,384]{2,1,0:T(8,128)(2,1)} %pad_maximum_fusion.2), calls=%async_computation.1 | async-start | bytes 983040 | tf_op jit(solution)/shard_map/all_to_all | solution.py:108
  119.7 3.9 %collective-permute-start.6 = (f32[256]{0:T(256)S(1)}, f32[256]{0:T(256)S(1)}, u32[]{:S(2)}, u32[]{:S(2)}) collective-permute-start(f32[256]{0:T(256)S(1)} %add_rsqrt_fusion), channel_id=1, source_target_pairs={{0,16},{16,32},{32,48},{48,64},{64,80},{80,96},{96,112},{112,128},... | collective-permute-start | bytes 3080 | tf_op jit(solution)/shard_map/ppermute | solution.py:160
  123.7 9.3 %collective-permute-done.6 = f32[256]{0:T(256)S(1)} collective-permute-done((f32[256]{0:T(256)S(1)}, f32[256]{0:T(256)S(1)}, u32[]{:S(2)}, u32[]{:S(2)}) %collective-permute-start.6) | collective-permute-done | bytes 1056 | tf_op jit(solution)/shard_map/ppermute | solution.py:160
  132.9 11.6 %all-gather.2 = f32[2,2048]{1,0:T(2,128)S(1)} all-gather(f32[2,256]{1,0:T(2,128)S(1)} %pad_maximum_fusion.3), channel_id=4, replica_groups=mesh['yl'=2,'z'=8,'x'=4,'c'=2,'tp'=2] {'x','c'}, dimensions={1}, use_global_device_ids=true | all-gather | bytes 18432 | tf_op jit(solution)/shard_map/all_gather | solution.py:161
  144.6 0.1 convert_reduce_fusion.1
  144.7 25.0 %all_gather.31 = bf16[512,384]{1,0:T(8,128)(2,1)S(1)} all-gather(bf16[64,384]{1,0:T(8,128)(2,1)S(1)} %slice.238), channel_id=1, replica_groups=mesh['yl'=2,'z'=8,'x'=4,'c'=2,'tp'=2] {'z'}, dimensions={0}, use_global_device_ids=true | all-gather | bytes 442368 | tf_op jit(solution)/shard_map/all_gather | solution.py:111
  169.7 8.6 %all-gather.1 = bf16[1024,384]{1,0:T(8,128)(2,1)S(1)} all-gather(bf16[512,384]{1,0:T(8,128)(2,1)S(1)} %all_gather.31), channel_id=3, replica_groups=mesh['yl'=2,'z'=8,'x'=4,'c'=2,'tp'=2] {'yl'}, dimensions={0}, use_global_device_ids=true | all-gather | bytes 1179648 | tf_op jit(solution)/shard_map/all_gather | solution.py:112
  178.4 0.1 copy.44
  178.5 0.0 all-gather.5.cloned.1.call-done
  178.5 5.8 %fusion.1 = bf16[4096,256]{1,0:T(8,128)(2,1)S(1)} fusion(bf16[4096,1024]{1,0:T(8,128)(2,1)} %bitcast.166, f32[4096]{0:T(1024)S(1)} %bitcast.148, f32[256]{0:T(256)S(1)} %bitcast.165, f32[4096]{0:T(1024)S(1)} %bitcast.150, f32[256]{0:T(256)S(1)} %bitcast.164, f32[4096]{0:T(1024)S(1)} %bitcast.149, bf16[1024,384]{1,0:T(8,128)(2,1)S(1)} %bitcast.138), kind=kOutput, calls=%fused_computation.2 | convolution fusion | flops 2153775104 | bytes 11061248 | tf_op jit(solution)/shard_map/dot_general | solution.py:27
  184.3 0.1 fusion.58
  184.4 1.5 fusion.5.q_ref
  185.9 9.1 %shard_map.104 = bf16[2048,128]{1,0:T(8,128)(2,1)S(1)} custom-call(s32[1]{0:T(128)} %bitcast.15.first_ref, bf16[2048,128]{1,0:T(8,128)(2,1)S(1)} %fusion.5.q_ref, bf16[4096,128]{1,0:T(8,128)(2,1)S(1)} %get-tuple-element.5.k_ref, bf16[4096,128]{1,0:T(8,128)(2,1)S(1)} %get-tuple-element.4.v_ref), custom_call_target="tpu_custom_call" | custom-call | flops 2147483648 | bytes 2097152 | tf_op jit(solution)/shard_map/pallas_call | solution.py:67
  195.0 13.5 %all_to_all.39 = bf16[8,256,128]{2,1,0:T(8,128)(2,1)S(1)} all-to-all(bf16[8,256,128]{2,1,0:T(8,128)(2,1)S(1)} %bitcast.122), channel_id=1, replica_groups=mesh['yl'=2,'z'=8,'x'=4,'c'=2,'tp'=2] {'x','c'}, dimensions={0} | all-to-all | bytes 1048576 | tf_op jit(solution)/shard_map/all_to_all | solution.py:171
  208.6 0.9 copy_bitcast_fusion
  (42 shorter events, 0.2 us)
Async XLA Ops:
  7.2 14.4 %copy-start = (bf16[1,256,512]{2,1,0:T(8,128)(2,1)S(1)}, bf16[1,256,512]{2,1,0:T(8,128)(2,1)}, u32[]{:S(2)}) copy-start(bf16[1,256,512]{2,1,0:T(8,128)(2,1)} %param.11) | copy-start | bytes 786436
  7.2 171.3 %all-gather.5.cloned.1.call-start = ((), (), s32[]{:S(2)}) async-start(), calls=%async_computation.3 | async-start | bytes 9437184 | tf_op jit(solution)/shard_map/all_gather | solution.py:138
  8.0 10.7 %copy-start.1 = (bf16[1,512,512]{2,1,0:T(8,128)(2,1)S(1)}, bf16[1,512,512]{2,1,0:T(8,128)(2,1)}, u32[]{:S(2)}) copy-start(bf16[1,512,512]{2,1,0:T(8,128)(2,1)} %param.9) | copy-start | bytes 1572868
  8.0 11.0 %copy-start.3 = (bf16[1,3,512,256]{3,2,1,0:T(8,128)(2,1)S(1)}, bf16[1,3,512,256]{3,2,1,0:T(8,128)(2,1)}, u32[]{:S(2)}) copy-start(bf16[1,3,512,256]{3,2,1,0:T(8,128)(2,1)} %param.10) | copy-start | bytes 2359300
  8.0 10.7 %collective-permute-start = (bf16[8,512]{1,0:T(8,128)(2,1)S(1)}, bf16[8,512]{1,0:T(8,128)(2,1)S(1)}, u32[]{:S(2)}, u32[]{:S(2)}) collective-permute-start(bf16[8,512]{1,0:T(8,128)(2,1)S(1)} %slice_bitcast_fusion.8), channel_id=1, source_target_pairs={{0,2},{2,4},{4,6},{6,8},{8,10},{10,12},{12,14},{14,16},{16,18},{18... | collective-permute-start | bytes 24584 | tf_op jit(solution)/shard_map/ppermute | solution.py:131
  30.9 22.5 %copy-start.2 = (bf16[3,32,1024]{2,1,0:T(8,128)(2,1)S(1)}, bf16[3,32,1024]{2,1,0:T(8,128)(2,1)}, u32[]{:S(2)}) copy-start(bf16[3,32,1024]{2,1,0:T(8,128)(2,1)} %param.17) | copy-start | bytes 589828
  30.9 8.0 %collective-permute-start.2 = (bf16[256,512]{1,0:T(8,128)(2,1)S(1)}, bf16[256,512]{1,0:T(8,128)(2,1)S(1)}, u32[]{:S(2)}, u32[]{:S(2)}) collective-permute-start(bf16[256,512]{1,0:T(8,128)(2,1)S(1)} %fusion.13), channel_id=1, source_target_pairs={{0,1},{1,0},{2,3},{3,2},{4,5},{5,4},{6,7},{7,6},{8,9},{9,8},{10,11... | collective-permute-start | bytes 786440 | tf_op jit(solution)/shard_map/ppermute | solution.py:133
  39.0 13.2 %collective-permute-start.3 = (bf16[256,1024]{1,0:T(8,128)(2,1)S(1)}, bf16[256,1024]{1,0:T(8,128)(2,1)S(1)}, u32[]{:S(2)}, u32[]{:S(2)}) collective-permute-start(bf16[256,1024]{1,0:T(8,128)(2,1)S(1)} %get-tuple-element.12), channel_id=1, source_target_pairs={{0,16},{16,32},{32,48},{48,64},{64,80},{80,96},{96,112},{112,128},... | collective-permute-start | bytes 1572872 | tf_op jit(solution)/shard_map/ppermute | solution.py:136
  55.4 21.6 %all-to-all-start = ((bf16[8,2,6144]{2,1,0:T(2,128)(2,1)}), bf16[8,2,6144]{2,1,0:T(2,128)(2,1)S(1)}, u32[]{:S(2)}, u32[]{:S(2)}) async-start(bf16[8,2,6144]{2,1,0:T(2,128)(2,1)} %reshape.127), calls=%async_computation | async-start | bytes 393216 | tf_op jit(solution)/shard_map/all_to_all | solution.py:86
  68.1 4.9 %copy-start.5 = (f32[4096]{0:T(1024)S(1)}, f32[4096]{0:T(1024)}, u32[]{:S(2)}) copy-start(f32[4096]{0:T(1024)} %param.16) | copy-start | bytes 49156
  68.1 5.0 %copy-start.4 = (f32[2,4096]{1,0:T(2,128)S(1)}, f32[2,4096]{1,0:T(2,128)}, u32[]{:S(2)}) copy-start(f32[2,4096]{1,0:T(2,128)} %param.15) | copy-start | bytes 98308
  68.1 5.0 %copy-start.6 = (s32[2,32]{1,0:T(2,128)S(1)}, s32[2,32]{1,0:T(2,128)}, u32[]{:S(2)}) copy-start(s32[2,32]{1,0:T(2,128)} %param.14) | copy-start | bytes 772
  70.1 37.2 %collective-permute-start.4 = (bf16[256,512]{0,1:T(8,128)(2,1)S(1)}, bf16[256,512]{0,1:T(8,128)(2,1)S(1)}, u32[]{:S(2)}, u32[]{:S(2)}) collective-permute-start(bf16[256,512]{0,1:T(8,128)(2,1)S(1)} %bitcast.143), channel_id=1, source_target_pairs={{0,1},{1,0},{2,3},{3,2},{4,5},{5,4},{6,7},{7,6},{8,9},{9,8},{10,11... | collective-permute-start | bytes 786440 | tf_op jit(solution)/shard_map/ppermute | solution.py:97
  76.1 31.8 %collective-permute-start.1 = (bf16[256,2048]{1,0:T(8,128)(2,1)S(1)}, bf16[256,2048]{1,0:T(8,128)(2,1)}, u32[]{:S(2)}, u32[]{:S(2)}) collective-permute-start(bf16[256,2048]{1,0:T(8,128)(2,1)S(1)} %convolution_convert_fusion), channel_id=1, source_target_pairs={{0,1},{1,0},{2,3},{3,2},{4,5},{5,4},{6,7},{7,6},{8,9},{9,8},{10,11... | collective-permute-start | bytes 3145736 | tf_op jit(solution)/shard_map/ppermute | solution.py:153
  111.7 8.0 %collective-permute-start.5 = (f32[256]{0:T(256)S(1)}, f32[256]{0:T(256)S(1)}, u32[]{:S(2)}, u32[]{:S(2)}) collective-permute-start(f32[256]{0:T(256)S(1)} %get-tuple-element.6), channel_id=1, source_target_pairs={{0,1},{1,0},{2,3},{3,2},{4,5},{5,4},{6,7},{7,6},{8,9},{9,8},{10,11... | collective-permute-start | bytes 3080 | tf_op jit(solution)/shard_map/ppermute | solution.py:158
  113.4 31.2 %all-to-all-start.1 = ((bf16[8,80,384]{2,1,0:T(8,128)(2,1)}), bf16[8,80,384]{2,1,0:T(8,128)(2,1)S(1)}, u32[]{:S(2)}, u32[]{:S(2)}) async-start(bf16[8,80,384]{2,1,0:T(8,128)(2,1)} %pad_maximum_fusion.2), calls=%async_computation.1 | async-start | bytes 983040 | tf_op jit(solution)/shard_map/all_to_all | solution.py:108
  119.7 13.2 %collective-permute-start.6 = (f32[256]{0:T(256)S(1)}, f32[256]{0:T(256)S(1)}, u32[]{:S(2)}, u32[]{:S(2)}) collective-permute-start(f32[256]{0:T(256)S(1)} %add_rsqrt_fusion), channel_id=1, source_target_pairs={{0,16},{16,32},{32,48},{48,64},{64,80},{80,96},{96,112},{112,128},... | collective-permute-start | bytes 3080 | tf_op jit(solution)/shard_map/ppermute | solution.py:160
  178.5 5.9 %copy-start.7 = (bf16[2,2048,1024]{2,1,0:T(8,128)(2,1)S(1)}, bf16[2,2048,1024]{2,1,0:T(8,128)(2,1)}, u32[]{:S(2)}) copy-start(bf16[2,2048,1024]{2,1,0:T(8,128)(2,1)} %all-gather.5.cloned.1.call-done) | copy-start | bytes 25165828
Sparse Core Ops, SparseCore 0:
  53.4 54.1 all-gather.4

commit v2 on v1

v2 whole, which is shorter than its diff:
```python
import functools

import jax
import jax.numpy as jnp
from jax import lax
from jax.experimental import pallas as pl
from jax.experimental.pallas import tpu as pltpu
from jax.sharding import Mesh, PartitionSpec as P

HD = 128
BLOCK = 256
D = 4096
CH = 512
CTX = ("yl", "z", "x", "c")
SWAP = [(0, 1), (1, 0)]
BF = jnp.bfloat16
F32 = jnp.float32
VMEM_LIMIT = 48 * 1024 * 1024
LOG2E = 1.4426950408889634


def elu(v):
    return jnp.where(v > 0, v, jnp.exp(jnp.minimum(v, 0.0)) - 1.0)


def dot(a, b):
    return jnp.dot(a, b, preferred_element_type=F32)


def in_vmem(n):
    return [pl.BlockSpec(memory_space=pltpu.VMEM)] * n


def params():
    return pltpu.CompilerParams(vmem_limit_bytes=VMEM_LIMIT)


def encoder_kernel(halo_ref, audio_ref, taps_ref, back_ref, down_ref, out_ref, u_ref, e_ref):
    u_ref[0:8, :] = jnp.zeros((8, CH), F32)
    u_ref[8:16, :] = elu(halo_ref[...].astype(F32))
    u_ref[16:, :] = elu(audio_ref[...].astype(F32))
    rows = audio_ref.shape[0] + 8
    inner = dot(u_ref[2 : 2 + rows, :].astype(BF), taps_ref[0])
    inner += dot(u_ref[5 : 5 + rows, :].astype(BF), taps_ref[1])
    inner += dot(u_ref[8 : 8 + rows, :].astype(BF), taps_ref[2])
    hidden = elu(inner).astype(BF)
    branch = dot(hidden, back_ref[...])
    first = (halo_ref[...].astype(F32) + branch[0:8]).astype(BF)
    first = elu(first.astype(F32)).astype(BF).astype(F32)
    rest = (audio_ref[...].astype(F32) + branch[8:]).astype(BF)
    rest = elu(rest.astype(F32)).astype(BF).astype(F32)
    for j in range(CH // 128):
        e_ref[j, 0:8, :] = first[:, j * 128 : (j + 1) * 128]
        e_ref[j, 8:, :] = rest[:, j * 128 : (j + 1) * 128]
    acc = jnp.zeros((BLOCK, CH), F32)
    for k in range(4):
        e = [e_ref[j, pl.ds(6 + k, BLOCK, stride=2), :].astype(BF) for j in range(CH // 128)]
        acc += dot(jnp.concatenate(e, axis=1), down_ref[k])
    out_ref[...] = acc.astype(BF)


def encoder(halo, audio, taps, back, down):
    return pl.pallas_call(
        encoder_kernel,
        in_specs=in_vmem(5),
        out_specs=pl.BlockSpec(memory_space=pltpu.VMEM),
        out_shape=jax.ShapeDtypeStruct((BLOCK, CH), BF),
        scratch_shapes=[pltpu.VMEM((528, CH), F32), pltpu.VMEM((CH // 128, 520, 128), F32)],
        compiler_params=params(),
        cost_estimate=pl.CostEstimate(flops=1100000000, bytes_accessed=4 << 20, transcendentals=600000),
    )(halo, audio, taps, back, down)


def partial_kernel(w_ref, mine_ref, rest_ref, gain_ref, table_ref, out_ref):
    part = None
    line = None
    for y in range(2):
        w = jnp.concatenate(
            [
                jnp.concatenate([w_ref[c, y, x, j] for x in range(4) for c in range(2)], axis=0)
                for j in range(3)
            ],
            axis=1,
        )
        gain = gain_ref[y]
        embed = jnp.concatenate([mine_ref[y], rest_ref[y]], axis=0).astype(F32) * gain
        table = table_ref[y] * gain
        high = table.astype(BF)
        low = (table - high.astype(F32)).astype(BF)
        a = dot(embed.astype(BF), w)
        b = dot(high, w) + dot(low, w)
        part = a if part is None else part + a
        line = b if line is None else line + b
    top = line.astype(BF).astype(F32)
    rem = line - top
    rows = [v[s : s + 1, k * 128 : (k + 1) * 128] for v in (top, rem) for s in range(2) for k in range(6)]
    tail = jnp.concatenate(rows + [jnp.zeros((8, 128), F32)], axis=0).astype(BF)
    for i in range(8):
        out_ref[i, :, 0:768] = part[i * 32 : (i + 1) * 32].astype(BF)
        out_ref[i, :, 768:896] = tail


def head_weights(stream_embed, speaker_table, norm_gain, qkv_weight):
    yl = lax.axis_index("yl")
    z = lax.axis_index("z")
    c = lax.axis_index("c")
    w = qkv_weight.reshape(3, 32, 4, 256).transpose(2, 0, 1, 3)
    w = lax.all_to_all(w, "x", 0, 0, tiled=True)
    w = jnp.stack([w, lax.ppermute(w, "yl", SWAP)])
    w = lax.all_gather(w, "c", axis=0)

    def of_z(a):
        a = a.reshape(a.shape[0], 2, 8, 256)
        return jnp.stack(
            [lax.dynamic_slice(a, (0, y, z, 0), (a.shape[0], 1, 1, 256)).reshape(a.shape[0], 256) for y in (yl, 1 - yl)]
        )

    mine = of_z(lax.dynamic_slice_in_dim(stream_embed, (yl * 2 + c) * 128, 128, 0))
    rest = lax.ppermute(mine, "tp", SWAP)
    packed = pl.pallas_call(
        partial_kernel,
        in_specs=in_vmem(5),
        out_specs=pl.BlockSpec(memory_space=pltpu.VMEM),
        out_shape=jax.ShapeDtypeStruct((8, 32, 896), BF),
        compiler_params=params(),
        cost_estimate=pl.CostEstimate(flops=210000000, bytes_accessed=2 << 20, transcendentals=0),
    )(w, mine, rest, of_z(norm_gain[None]), of_z(jnp.pad(speaker_table, ((0, 6), (0, 0)))))
    packed = lax.all_to_all(packed, "z", 0, 0, tiled=True)
    total = jnp.sum(packed.astype(F32), axis=0)
    lines = (total[0:12, 768:] + total[12:24, 768:]).reshape(2, 768)
    m = total[:, :768].astype(BF)
    m = lax.all_to_all(jnp.broadcast_to(m[None], (8, 32, 768)), "z", 0, 0, tiled=True).reshape(256, 768)
    m = jnp.stack([m, lax.ppermute(m, "yl", SWAP)])
    return lax.all_gather(m, "c", axis=0), lines


def ring(a):
    left = lax.ppermute(a, "x", [(i, (i + 1) % 4) for i in range(4)])
    right = lax.ppermute(a, "x", [(i, (i + 3) % 4) for i in range(4)])
    return left, right


def second_hop(a, b):
    left = lax.ppermute(a, "x", [(i, (i + 1) % 4) for i in range(4)])
    right = lax.ppermute(b, "x", [(i, (i + 3) % 4) for i in range(4)])
    return left, right


def gather_latents(latent, other):
    behind = [(i, i + 1) for i in range(15)]
    a = latent
    al, ar = ring(a)
    prev_a = lax.ppermute(a, ("yl", "z"), behind)
    b = jnp.stack([other, prev_a])
    bl, br = ring(b)
    c = lax.ppermute(other, ("yl", "z"), behind)
    al2, ar2 = second_hop(al[:128], ar[128:])
    cl, cr = ring(c)
    bl2, br2 = second_hop(bl[0], br[1])
    cl2, cr2 = second_hop(cl[:128], cr[128:])
    return (a, al, ar, al2, ar2, b, bl, br, bl2, br2, c, cl, cr, cl2, cr2)


def project_kernel(with_q, place_ref, *refs):
    (a, al, ar, al2, ar2, b, bl, br, bl2, br2, c, cl, cr, cl2, cr2, m_ref, line_ref, side_ref) = refs[:18]
    outs = refs[18:]
    x = place_ref[0]
    yl = place_ref[1]

    def weight(j, s):
        pieces = []
        for y in range(2):
            at = jnp.where(yl == y, 0, 1)
            for cc in range(2):
                pieces.append(m_ref[cc, at, s * 128 : (s + 1) * 128, j * 256 : (j + 1) * 256])
        return jnp.concatenate(pieces, axis=0)

    far_a = jnp.concatenate([al2[...], ar2[...]], axis=0)
    far_c = jnp.concatenate([cl2[...], cr2[...]], axis=0)
    own = [(a[...], b[0]), (ar[...], br[0]), (far_a, bl2[...]), (al[...], bl[0])]
    prev = [(b[1], c[...]), (br[1], cr[...]), (br2[...], far_c), (bl[1], cl[...])]
    jobs = [(0, outs[1], False), (1, outs[0], True)] if with_q else [(2, outs[0], True)]
    for j, out, both in jobs:
        w0, w1 = weight(j, 0), weight(j, 1)
        line = line_ref[:, j * 256 : (j + 1) * 256]
        factor = HD**-0.5 * LOG2E if j == 0 else 1.0
        for r, blocks in ((1, own), (0, prev)) if both else ((1, own),):
            for dx in range(4):
                p, q = blocks[dx]
                at = lax.rem(x + dx, 4)
                side = side_ref[4 * r + at]
                acc = dot(p, w0) + dot(q, w1)
                acc = acc + side[:, 0:1] * line[0:1] + side[:, 1:2] * line[1:2]
                acc = acc * (side[:, 2:3] * factor)
                out[4 * r + at if both else at] = acc.astype(BF)


def project(with_q, place, pieces, m, lines, side):
    shapes = [jax.ShapeDtypeStruct((8, BLOCK, 256), BF)]
    if with_q:
        shapes.append(jax.ShapeDtypeStruct((4, BLOCK, 256), BF))
    return pl.pallas_call(
        functools.partial(project_kernel, with_q),
        in_specs=[pl.BlockSpec(memory_space=pltpu.SMEM)] + in_vmem(18),
        out_specs=in_vmem(len(shapes)),
        out_shape=shapes,
        compiler_params=params(),
        cost_estimate=pl.CostEstimate(flops=1600000000, bytes_accessed=6 << 20, transcendentals=0),
    )(place, *pieces, m, lines, side)


def attention_kernel(place_ref, q_ref, km_ref, kt_ref, vm_ref, vt_ref, o_ref):
    at = lax.rem(place_ref[0] + place_ref[3 + pl.program_id(0)], 4)
    core = place_ref[1]
    first = place_ref[2]
    rows = lax.broadcasted_iota(jnp.int32, (BLOCK, 1024), 0)
    cols = lax.broadcasted_iota(jnp.int32, (BLOCK, 1024), 1)
    least_m = jnp.where(first == 1, (3 - at) * BLOCK, 0)
    least_t = jnp.where(first == 1, (4 - at - core) * BLOCK, 0)
    bias_m = jnp.where((cols - 768 <= rows) & (cols >= least_m), 0.0, -1e30)
    bias_t = jnp.where((cols > rows) & (cols >= least_t), 0.0, -1e30)
    contract = (((1,), (1,)), ((), ()))
    for h in range(2):
        lanes = slice(h * HD, (h + 1) * HD)
        q = q_ref[at, :, lanes]
        km = km_ref[pl.ds(at + 1, 4), :, lanes].reshape(1024, HD)
        kt = kt_ref[pl.ds(at + core, 4), :, lanes].reshape(1024, HD)
        sm = lax.dot_general(q, km, contract, preferred_element_type=F32) + bias_m
        st = lax.dot_general(q, kt, contract, preferred_element_type=F32) + bias_t
        top = jnp.maximum(jnp.max(sm, axis=1, keepdims=True), jnp.max(st, axis=1, keepdims=True))
        pm = jnp.exp2(sm - top)
        pt = jnp.exp2(st - top)
        total = jnp.sum(pm, axis=1, keepdims=True) + jnp.sum(pt, axis=1, keepdims=True)
        vm = vm_ref[pl.ds(at + 1, 4), :, lanes].reshape(1024, HD)
        vt = vt_ref[pl.ds(at + core, 4), :, lanes].reshape(1024, HD)
        o = dot(pm.astype(BF), vm) + dot(pt.astype(BF), vt)
        o_ref[0, :, lanes] = (o / total).astype(BF)


def attention(place, offsets, q, km, kt, vm, vt):
    n = len(offsets)
    return pl.pallas_call(
        attention_kernel,
        grid=(n,),
        in_specs=[pl.BlockSpec(memory_space=pltpu.SMEM)] + in_vmem(5),
        out_specs=pl.BlockSpec((1, BLOCK, 256), lambda i: (i, 0, 0)),
        out_shape=jax.ShapeDtypeStruct((n, BLOCK, 256), BF),
        compiler_params=params(),
        cost_estimate=pl.CostEstimate(
            flops=n * 8 * BLOCK * 2048 * HD, bytes_accessed=5 << 20, transcendentals=n * 2 * BLOCK * 2048
        ),
    )(jnp.concatenate([place, jnp.array(offsets, jnp.int32)]), q, km, kt, vm, vt)


def collect_kernel(place_ref, a_ref, b_ref, c_ref, d_ref, o_ref):
    for dx, ref in enumerate((a_ref, b_ref, c_ref, d_ref)):
        at = lax.rem(place_ref[0] + 4 - dx, 4)
        o_ref[:, pl.ds(pl.multiple_of(at * 256, 256), 256)] = ref[0]


def collect(place, parts):
    return pl.pallas_call(
        collect_kernel,
        in_specs=[pl.BlockSpec(memory_space=pltpu.SMEM)] + in_vmem(4),
        out_specs=pl.BlockSpec(memory_space=pltpu.VMEM),
        out_shape=jax.ShapeDtypeStruct((BLOCK, 1024), BF),
        compiler_params=params(),
    )(place, *parts)


def on_device(
    audio_feats,
    res_conv,
    res_out,
    down_conv,
    stream_embed,
    turn_lengths,
    speaker_table,
    norm_gain,
    qkv_weight,
):
    tp = lax.axis_index("tp")
    x_at = lax.axis_index("x")
    core = lax.axis_index("c")
    row = lax.axis_index("yl") * 8 + lax.axis_index("z")
    audio = audio_feats[0]
    halo = lax.ppermute(audio[-8:], CTX, [(i, i + 1) for i in range(127)])
    latent = encoder(halo, audio, res_conv[0], res_out[0], down_conv[0])
    other = lax.ppermute(latent, "tp", SWAP)
    pieces = gather_latents(latent, other)

    m, lines = head_weights(stream_embed[0], speaker_table, norm_gain, qkv_weight)

    bounds = jnp.cumsum(turn_lengths, axis=1)
    start = ((row - 1 + jnp.arange(2)[:, None]) * 8 + 2 * jnp.arange(4)[None, :] + core) * BLOCK
    frames = (start[:, :, None] + jnp.arange(BLOCK)).reshape(8 * BLOCK)
    turn = jnp.sum((bounds[:, None, :] <= frames[None, :, None]).astype(jnp.int32), axis=2)
    active = (turn % 2 == 1).astype(F32)
    active_here = lax.dynamic_slice_in_dim(active, (4 + x_at) * BLOCK, BLOCK, 1)

    embed = stream_embed[0].reshape(CH, 2, D // 2)
    own = dot(latent, lax.dynamic_index_in_dim(embed, tp, 1, keepdims=False))
    give = dot(latent, lax.dynamic_index_in_dim(embed, 1 - tp, 1, keepdims=False)).astype(BF)
    got = lax.ppermute(give, "tp", SWAP)
    table = lax.dynamic_slice_in_dim(speaker_table, tp * (D // 2), D // 2, 1)
    x = own + got.astype(F32) + active_here[0][:, None] * table[0] + active_here[1][:, None] * table[1]
    embedded = x.astype(BF)
    square = jnp.sum(x * x, axis=1)
    square = square + lax.ppermute(square, "tp", SWAP)
    scale = lax.rsqrt(square * (1.0 / D) + 1e-05)
    scale_prev = lax.ppermute(scale, ("yl", "z"), [(i, i + 1) for i in range(15)])
    scales = jnp.broadcast_to(jnp.stack([scale_prev, scale])[None], (4, 2, BLOCK))
    scales = lax.all_to_all(scales, "x", 0, 0, tiled=True).transpose(1, 0, 2).reshape(8 * BLOCK)
    side = jnp.stack([active[0], active[1], scales] + [jnp.zeros_like(scales)] * 5, axis=1).reshape(8, BLOCK, 8)

    place = jnp.stack([x_at, lax.axis_index("yl")]).astype(jnp.int32)
    km, q = project(True, place, pieces, m, lines, side)
    kt = lax.ppermute(km, "c", SWAP)
    (vm,) = project(False, place, pieces, m, lines, side)
    vt = lax.ppermute(vm, "c", SWAP)

    place = jnp.stack([x_at, core, (row == 0).astype(jnp.int32)]).astype(jnp.int32)
    parts = [None] * 4
    for dx in (2, 1, 3, 0):
        part = attention(place, (dx,), q, km, kt, vm, vt)
        parts[dx] = lax.ppermute(part, "x", [(i, (i + dx) % 4) for i in range(4)]) if dx else part
    return embedded, collect(place, parts)


def solution(mesh):
    fine = Mesh(mesh.devices.reshape(2, 8, 4, 2, 2), CTX + ("tp",))
    placed = (
        P("tp", CTX, None),
        P("tp", None, None, None),
        P("tp", None, None),
        P("tp", None, None, None),
        P("tp", None, None),
        P(),
        P(),
        P(),
        P(None, CTX, "tp"),
    )
    return jax.shard_map(
        on_device,
        mesh=fine,
        in_specs=placed,
        out_specs=(P(CTX, "tp"), P(CTX, "tp")),
        check_vma=False,
    )
```

time: 219 us -> 244 us (1.11)
  blocking collectives: 86.5 us -> 2.5 us
  waiting for transfers between devices: 32.9 us -> 78.8 us
  starting transfers between devices: 27.5 us -> 63.6 us
  local copies, waits for them, and re-layouts: 20.8 us -> 46.1 us
  Pallas kernels: 9.13 us -> 25.3 us
  matrix products: 20.8 us -> 7.31 us
    all_gather x4 -> x1, blocking collectives: 73 us -> 2.5 us  [head_weights(): w = lax.all_gather(w, 'c', axis=0)]
    ppermute x2 -> x22, starting transfers between devices: 5.84 us -> 33.1 us  [the longest x3 6.24 us: second_hop(): right = lax.ppermute(b, 'x', [(i, (i + 3) % 4) for i in range(4)])]
    pallas_call x1 -> x9, Pallas kernels: 9.13 us -> 25.3 us  [the longest x4 12.8 us: attention(): pl.pallas_call(attention_kernel, grid=(n,), in_specs=[pl.BlockSpec(memory...]
    all_to_all x1 -> x0, blocking collectives: 13.5 us -> none  [on_device(): attended = lax.all_to_all(out, ROW, 0, 1, tiled=True)]
    ppermute x2 -> x22, waiting for transfers between devices: 20.5 us -> 34 us  [the longest x1 12.8 us: head_weights(): m = jnp.stack([m, lax.ppermute(m, 'yl', SWAP)])]
    dot_general x12 -> x2, matrix products: 20.8 us -> 7.31 us  [dot(): return jnp.dot(a, b, preferred_element_type=F32)]
    ppermute x1, waiting for transfers between devices: 5.28 us -> 18.8 us  [on_device(): other = lax.ppermute(latent, 'tp', SWAP)]
    unnamed x26 -> x74, local copies, waits for them, and re-layouts: 9.47 us -> 22.8 us
  transfers between devices with their start and end apart: 10 -> 32, of which waited for: 4 -> 12; matrix products, arithmetic and copies ran while one was open for 11% -> 16% of each run, Pallas kernels for 0% -> 7%
where the time goes in v2:
time: 244 us; the launch traced here: 242 us
  waiting for transfers between devices  78.8 us (32%)
  starting transfers between devices  63.6 us (26%)
  local copies, waits for them, and re-layouts  46.1 us (19%)
  Pallas kernels  25.3 us (10%)
  between operations  14.5 us (6%)
  matrix products  7.31 us (3%)
  other arithmetic  3.85 us (2%)
  blocking collectives  2.5 us (1%)
    unnamed x74, local copies, waits for them, and re-layouts  22.8 us
    ppermute x1, waiting for transfers between devices, on_device(): other = lax.ppermute(latent, 'tp', SWAP)  18.8 us
    another operation x6, local copies, waits for them, and re-layouts, on_device(): jnp.stack([active[0], active[1], scales] + [jnp.zeros_like(scales)] * 5,...  13.2 us
    ppermute x1, waiting for transfers between devices, head_weights(): m = jnp.stack([m, lax.ppermute(m, 'yl', SWAP)])  12.8 us
    pallas_call x4, Pallas kernels, attention(): pl.pallas_call(attention_kernel, grid=(n,), in_specs=[pl.BlockSpec(memory...  12.8 us
    all_to_all x1, waiting for transfers between devices, head_weights(): packed = lax.all_to_all(packed, 'z', 0, 0, tiled=True)  12.2 us
    all_to_all x1, starting transfers between devices, head_weights(): packed = lax.all_to_all(packed, 'z', 0, 0, tiled=True)  8.15 us
    dot_general x2, matrix products, dot(): return jnp.dot(a, b, preferred_element_type=F32)  7.31 us
  transfers between devices with their start and end apart: 32, of which 12 were waited for; matrix products, arithmetic and copies ran while one was open for 16% of the time, Pallas kernels for 7%

profile of v2, /device:TPU:8, one launch (start us, length us, event | category | flops | bytes accessed | tf_op | source)
XLA Modules:
  0.0 242.1 jit_solution(6743004429378396146)
XLA Ops:
  7.9 1.9 collective-permute-start
  9.8 6.5 %copy.71 = bf16[1,512,4096]{1,2,0:T(8,128)(2,1)} copy(bf16[1,512,4096]{2,1,0:T(8,128)(2,1)} %param.17) | data formatting | bytes 8388608 | tf_op args[4]
  16.3 1.3 constant_dynamic-slice_fusion.5
  17.9 2.4 collective-permute-start.18
  21.1 4.3 %all-to-all-start = ((bf16[4,3,32,256]{3,2,1,0:T(8,128)(2,1)}), bf16[4,3,32,256]{3,2,1,0:T(8,128)(2,1)S(1)}, u32[]{:S(2)}, u32[]{:S(2)}) async-start(bf16[4,3,32,256]{3,2,1,0:T(8,128)(2,1)} %copy.74), calls=%async_computation | async-start | bytes 393216 | tf_op jit(solution)/shard_map/all_to_all | solution.py:108
  25.5 7.2 %all-to-all-done = bf16[4,3,32,256]{3,2,1,0:T(8,128)(2,1)S(1)} async-done(((bf16[4,3,32,256]{3,2,1,0:T(8,128)(2,1)}), bf16[4,3,32,256]{3,2,1,0:T(8,128)(2,1)S(1)}, u32[]{:S(2)}, u32[]{:S(2)}) %all-to-all-start) | async-done | bytes 196640 | tf_op jit(solution)/shard_map/all_to_all | solution.py:108
  32.6 1.3 collective-permute-start.17
  34.0 5.6 %collective-permute-done.17 = bf16[4,3,32,256]{3,2,1,0:T(8,128)(2,1)S(1)} collective-permute-done((bf16[4,3,32,256]{3,2,1,0:T(8,128)(2,1)S(1)}, bf16[4,3,32,256]{3,2,1,0:T(8,128)(2,1)S(1)}, u32[]{:S(2)}, u32[]{:S(2)}) %collective-permute-start.17) | collective-permute-done | bytes 196640 | tf_op jit(solution)/shard_map/ppermute | solution.py:109
  39.6 2.5 %all-gather = bf16[4,4,3,32,256]{4,3,2,1,0:T(8,128)(2,1)S(1)} all-gather(bf16[2,4,3,32,256]{4,3,2,1,0:T(8,128)(2,1)S(1)} %pad_maximum_fusion.2), channel_id=2, replica_groups=mesh['yl'=2,'z'=8,'x'=4,'c'=2,'tp'=2] {'c'}, dimensions={0}, use_global_device_ids=true | all-gather | bytes 1179648 | tf_op jit(solution)/shard_map/all_gather | solution.py:110
  42.1 1.3 shard_map.141
  43.5 8.1 %all-to-all-start.1 = ((bf16[8,32,896]{2,1,0:T(8,128)(2,1)}), bf16[8,32,896]{2,1,0:T(8,128)(2,1)}, u32[]{:S(2)}, u32[]{:S(2)}) async-start(bf16[8,32,896]{2,1,0:T(8,128)(2,1)} %shard_map.141), calls=%async_computation.1 | async-start | bytes 917504 | tf_op jit(solution)/shard_map/all_to_all | solution.py:128
  52.2 1.1 copy-done.29
  53.4 2.5 %shard_map.140.refs_0_ = bf16[256,512]{1,0:T(8,128)(2,1)S(1)} custom-call(bf16[8,512]{1,0:T(8,128)(2,1)S(1)} %collective-permute-done.halo_ref, bf16[512,512]{1,0:T(8,128)(2,1)S(1)} %bitcast.60, bf16[3,512,256]{2,1,0:T(8,128)(2,1)S(1)} %bitcast.62, bf16[256,512]{1,0:T(8,128)(2,1)S(1)} %bitcast.63, bf16[4,512,512]{2,1,0:T(8,128)(2,1)S(1)} %bitcast.61), custom_call_target="tpu_custom_call" | custom-call | flops 1100000000 | bytes 4194304 | tf_op jit(solution)/shard_map/pallas_call | solution.py:63
  55.9 12.2 %all-to-all-done.1 = bf16[8,32,896]{2,1,0:T(8,128)(2,1)} async-done(((bf16[8,32,896]{2,1,0:T(8,128)(2,1)}), bf16[8,32,896]{2,1,0:T(8,128)(2,1)}, u32[]{:S(2)}, u32[]{:S(2)}) %all-to-all-start.1) | async-done | bytes 458784 | tf_op jit(solution)/shard_map/all_to_all | solution.py:128
  68.1 1.1 convert_reduce_fusion
  70.6 3.5 %all-to-all-start.2 = ((bf16[8,32,768]{2,1,0:T(8,128)(2,1)}), bf16[8,32,768]{2,1,0:T(8,128)(2,1)S(1)}, u32[]{:S(2)}, u32[]{:S(2)}) async-start(bf16[8,32,768]{2,1,0:T(8,128)(2,1)} %broadcast_in_dim.4), calls=%async_computation.2 | async-start | bytes 786432 | tf_op jit(solution)/shard_map/all_to_all | solution.py:132
  74.1 3.3 %convolution_convert_fusion = bf16[256,2048]{1,0:T(8,128)(2,1)} fusion(bf16[256,512]{1,0:T(8,128)(2,1)S(1)} %shard_map.140.refs_0_, bf16[512,2,2048]{0,2,1:T(8,128)(2,1)} %bitcast.64, s32[]{:T(128)S(6)} %select_n.42), kind=kOutput, calls=%fused_computation.3 | convolution fusion | flops 537395200 | bytes 3407876 | tf_op jit(solution)/shard_map/dot_general | solution.py:27
  77.5 1.2 collective-permute-start.1
  78.7 2.4 collective-permute-start.6
  81.1 3.8 %collective-permute-start.7 = (bf16[256,512]{1,0:T(8,128)(2,1)S(1)}, bf16[256,512]{1,0:T(8,128)(2,1)S(1)}, u32[]{:S(2)}, u32[]{:S(2)}) collective-permute-start(bf16[256,512]{1,0:T(8,128)(2,1)S(1)} %shard_map.140.refs_0_), channel_id=1, source_target_pairs={{0,16},{16,32},{32,48},{48,64},{64,80},{80,96},{96,112},{112,128},... | collective-permute-start | bytes 786440 | tf_op jit(solution)/shard_map/ppermute | solution.py:153
  84.9 4.5 %all-to-all-done.2 = bf16[8,32,768]{2,1,0:T(8,128)(2,1)S(1)} async-done(((bf16[8,32,768]{2,1,0:T(8,128)(2,1)}), bf16[8,32,768]{2,1,0:T(8,128)(2,1)S(1)}, u32[]{:S(2)}, u32[]{:S(2)}) %all-to-all-start.2) | async-done | bytes 393248 | tf_op jit(solution)/shard_map/all_to_all | solution.py:132
  89.3 1.4 collective-permute-start.19
  92.1 18.8 %collective-permute-done.6 = bf16[256,512]{1,0:T(8,128)(2,1)S(1)} collective-permute-done((bf16[256,512]{1,0:T(8,128)(2,1)S(1)}, bf16[256,512]{1,0:T(8,128)(2,1)S(1)}, u32[]{:S(2)}, u32[]{:S(2)}) %collective-permute-start.6) | collective-permute-done | bytes 262176 | tf_op jit(solution)/shard_map/ppermute | solution.py:289
  110.8 3.8 %collective-permute-start.12 = (bf16[256,512]{1,0:T(8,128)(2,1)S(1)}, bf16[256,512]{1,0:T(8,128)(2,1)S(1)}, u32[]{:S(2)}, u32[]{:S(2)}) collective-permute-start(bf16[256,512]{1,0:T(8,128)(2,1)S(1)} %collective-permute-done.6), channel_id=1, source_target_pairs={{0,16},{16,32},{32,48},{48,64},{64,80},{80,96},{96,112},{112,128},... | collective-permute-start | bytes 786440 | tf_op jit(solution)/shard_map/ppermute | solution.py:156
  115.3 12.8 %collective-permute-done.19 = bf16[256,768]{1,0:T(8,128)(2,1)S(1)} collective-permute-done((bf16[256,768]{1,0:T(8,128)(2,1)S(1)}, bf16[256,768]{1,0:T(8,128)(2,1)S(1)}, u32[]{:S(2)}, u32[]{:S(2)}) %collective-permute-start.19) | collective-permute-done | bytes 393248 | tf_op jit(solution)/shard_map/ppermute | solution.py:133
  128.1 1.0 pad_maximum_fusion
  129.2 1.2 collective-permute-start.3
  131.2 1.9 collective-permute-start.4
  134.0 4.0 %multiply_reduce_fusion = (f32[256]{0:T(256)S(1)}, bf16[256,2048]{1,0:T(8,128)(2,1)}) fusion(f32[2048]{0:T(1024)S(1)} %bitcast.82, f32[256]{0:T(256)S(1)} %bitcast.85, f32[2048]{0:T(1024)S(1)} %bitcast.81, f32[256]{0:T(256)S(1)} %bitcast.84, bf16[256,2048]{1,0:T(8,128)(2,1)} %collective-permute-done.1, bf16[256,512]{1,0:T(8,128)(2,1)S(1)} %shard_map.140.refs_0_, ...), kind=kOutput, calls=%fused_computation.6 | convolution fusion | flops 541589248 | bytes 4475908 | tf_op jit(solution)/shard_map/dot_general | solution.py:27
  138.0 2.1 collective-permute-start.20
  140.9 2.2 collective-permute-done.20
  143.1 2.4 collective-permute-start.14
  145.4 4.3 %collective-permute-done.9.refs_7_ = bf16[2,256,512]{2,1,0:T(8,128)(2,1)S(1)} collective-permute-done((bf16[2,256,512]{2,1,0:T(8,128)(2,1)S(1)}, bf16[2,256,512]{2,1,0:T(8,128)(2,1)S(1)}, u32[]{:S(2)}, u32[]{:S(2)}) %collective-permute-start.9) | collective-permute-done | bytes 524320 | tf_op jit(solution)/shard_map/ppermute | solution.py:139
  149.7 1.9 collective-permute-start.21
  152.4 4.9 %collective-permute-done.21 = f32[256]{0:T(256)S(1)} collective-permute-done((f32[256]{0:T(256)S(1)}, f32[256]{0:T(256)S(1)}, u32[]{:S(2)}, u32[]{:S(2)}) %collective-permute-start.21) | collective-permute-done | bytes 1056 | tf_op jit(solution)/shard_map/ppermute | solution.py:311
  158.5 4.5 %all-to-all-start.3 = ((f32[4,2,256]{2,1,0:T(2,128)}), f32[4,2,256]{2,1,0:T(2,128)}, u32[]{:S(2)}, u32[]{:S(2)}) async-start(f32[4,2,256]{2,1,0:T(2,128)} %broadcast_in_dim.5), calls=%async_computation.3 | async-start | bytes 16384 | tf_op jit(solution)/shard_map/all_to_all | solution.py:313
  163.0 3.2 %collective-permute-start.11 = (bf16[256,512]{1,0:T(8,128)(2,1)}, bf16[256,512]{1,0:T(8,128)(2,1)}, u32[]{:S(2)}, u32[]{:S(2)}) collective-permute-start(bf16[256,512]{1,0:T(8,128)(2,1)} %slice_bitcast_fusion), channel_id=1, source_target_pairs={{0,12},{4,0},{8,4},{12,8},{1,13},{5,1},{9,5},{13,9},{2,14},{6,2},{... | collective-permute-start | bytes 786440 | tf_op jit(solution)/shard_map/ppermute | solution.py:145
  166.3 2.6 %stack.103 = f32[8,256,1]{2,1,0:T(8,128)} reshape(f32[2048]{0:T(1024)} %get-tuple-element.7) | data formatting | bytes 16384 | tf_op jit(solution)/shard_map/stack | solution.py:314
  168.9 1.8 stack.104
  172.9 1.2 collective-permute-start.15
  175.5 1.9 stack.105
  177.4 1.2 stack.100
  178.5 1.0 stack_broadcast_in_dim.3
  179.6 4.7 %stack.101.refs_17_ = f32[8,256,8]{2,1,0:T(8,128)} concatenate(f32[8,256,1]{2,1,0:T(8,128)} %stack.103, f32[8,256,1]{2,1,0:T(8,128)} %stack.104, f32[8,256,1]{2,1,0:T(8,128)} %stack.105, f32[8,256,1]{2,1,0:T(8,128)} %stack_broadcast_in_dim.3, f32[8,256,4]{2,1,0:T(8,128)} %stack.100), dimensions={2} | concatenate | bytes 131072 | tf_op jit(solution)/shard_map/stack | solution.py:314
  184.3 2.1 collective-permute-start.16
  187.9 1.6 collective-permute-done.16.refs_14_
  192.9 0.9 copy-done.20
  193.8 0.9 copy-done.22
  196.6 3.3 %shard_map.143.vm_ref = bf16[8,256,256]{2,1,0:T(8,128)(2,1)S(1)} custom-call(s32[2]{0:T(128)S(1)} %pad_add_fusion.3.place_ref, bf16[256,512]{1,0:T(8,128)(2,1)S(1)} %shard_map.140.refs_0_, bf16[256,512]{1,0:T(8,128)(2,1)S(1)} %collective-permute-done.2.refs_1_, bf16[256,512]{1,0:T(8,128)(2,1)S(1)} %collective-permute-done.3.refs_2_, ...), custom_call_target="tpu_custom_call" | custom-call | flops 1600000000 | bytes 6291456 | tf_op jit(solution)/shard_map/pallas_call | solution.py:202
  200.3 1.0 copy-done.4
  201.3 1.0 copy-done.6
  202.3 1.0 copy-done.8
  203.4 0.9 copy-done.10
  204.3 0.9 copy-done.12
  205.3 4.0 %shard_map.142 = (bf16[8,256,256]{2,1,0:T(8,128)(2,1)S(1)}, bf16[4,256,256]{2,1,0:T(8,128)(2,1)S(1)}) custom-call(s32[2]{0:T(128)S(1)} %pad_add_fusion.3.place_ref, bf16[256,512]{1,0:T(8,128)(2,1)S(1)} %shard_map.140.refs_0_, bf16[256,512]{1,0:T(8,128)(2,1)S(1)} %copy-done.10, bf16[256,512]{1,0:T(8,128)(2,1)S(1)} %copy-done.12, ...), custom_call_target="tpu_custom_call" | custom-call | flops 1600000000 | bytes 6291456 | tf_op jit(solution)/shard_map/pallas_call | solution.py:202
  210.7 2.3 collective-permute-done.22.kt_ref
  212.9 1.0 copy-done.1
  214.0 3.2 %shard_map.147 = bf16[1,256,256]{2,1,0:T(8,128)(2,1)S(1)} custom-call(s32[4]{0:T(128)S(1)} %get-tuple-element.8.place_ref, bf16[4,256,256]{2,1,0:T(8,128)(2,1)S(1)} %copy-done.1, bf16[8,256,256]{2,1,0:T(8,128)(2,1)S(1)} %get-tuple-element.5.km_ref, bf16[8,256,256]{2,1,0:T(8,128)(2,1)} %collective-permute-done.22.kt_ref, ...), custom_call_target="tpu_custom_call" | custom-call | flops 536870912 | bytes 5242880 | tf_op jit(solution)/shard_map/pallas_call | solution.py:242
  217.2 3.4 %collective-permute-start.26 = (bf16[1,256,256]{2,1,0:T(8,128)(2,1)S(1)}, bf16[1,256,256]{2,1,0:T(8,128)(2,1)S(1)}, u32[]{:S(2)}, u32[]{:S(2)}) collective-permute-start(bf16[1,256,256]{2,1,0:T(8,128)(2,1)S(1)} %shard_map.147), channel_id=1, source_target_pairs={{0,12},{4,0},{8,4},{12,8},{1,13},{5,1},{9,5},{13,9},{2,14},{6,2},{... | collective-permute-start | bytes 393224 | tf_op jit(solution)/shard_map/ppermute | solution.py:326
  220.5 3.2 %shard_map.146 = bf16[1,256,256]{2,1,0:T(8,128)(2,1)S(1)} custom-call(s32[4]{0:T(128)S(1)} %get-tuple-element.22.place_ref, bf16[4,256,256]{2,1,0:T(8,128)(2,1)S(1)} %copy-done.1, bf16[8,256,256]{2,1,0:T(8,128)(2,1)S(1)} %get-tuple-element.5.km_ref, bf16[8,256,256]{2,1,0:T(8,128)(2,1)} %collective-permute-done.22.kt_ref, ...), custom_call_target="tpu_custom_call" | custom-call | flops 536870912 | bytes 5242880 | tf_op jit(solution)/shard_map/pallas_call | solution.py:242
  223.8 3.2 %shard_map.145 = bf16[1,256,256]{2,1,0:T(8,128)(2,1)S(1)} custom-call(s32[4]{0:T(128)S(1)} %get-tuple-element.23.place_ref, bf16[4,256,256]{2,1,0:T(8,128)(2,1)S(1)} %copy-done.1, bf16[8,256,256]{2,1,0:T(8,128)(2,1)S(1)} %get-tuple-element.5.km_ref, bf16[8,256,256]{2,1,0:T(8,128)(2,1)} %collective-permute-done.22.kt_ref, ...), custom_call_target="tpu_custom_call" | custom-call | flops 536870912 | bytes 5242880 | tf_op jit(solution)/shard_map/pallas_call | solution.py:242
  228.1 3.2 %shard_map.144.a_ref = bf16[1,256,256]{2,1,0:T(8,128)(2,1)S(1)} custom-call(s32[4]{0:T(128)S(1)} %get-tuple-element.24.place_ref, bf16[4,256,256]{2,1,0:T(8,128)(2,1)S(1)} %copy-done.2, bf16[8,256,256]{2,1,0:T(8,128)(2,1)S(1)} %get-tuple-element.5.km_ref, bf16[8,256,256]{2,1,0:T(8,128)(2,1)} %collective-permute-done.22.kt_ref, ...), custom_call_target="tpu_custom_call" | custom-call | flops 536870912 | bytes 5242880 | tf_op jit(solution)/shard_map/pallas_call | solution.py:242
  231.3 2.6 %collective-permute-done.24.b_ref = bf16[1,256,256]{2,1,0:T(8,128)(2,1)S(1)} collective-permute-done((bf16[1,256,256]{2,1,0:T(8,128)(2,1)S(1)}, bf16[1,256,256]{2,1,0:T(8,128)(2,1)S(1)}, u32[]{:S(2)}, u32[]{:S(2)}) %collective-permute-start.24) | collective-permute-done | bytes 131104 | tf_op jit(solution)/shard_map/ppermute | solution.py:326
  233.8 1.4 shard_map.148
  (139 shorter events, 23.5 us)
Async XLA Ops:
  7.9 44.3 %collective-permute-start = (bf16[8,512]{1,0:T(8,128)(2,1)S(1)}, bf16[8,512]{1,0:T(8,128)(2,1)S(1)}, u32[]{:S(2)}, u32[]{:S(2)}) collective-permute-start(bf16[8,512]{1,0:T(8,128)(2,1)S(1)} %slice_bitcast_fusion.2), channel_id=1, source_target_pairs={{0,2},{2,4},{4,6},{6,8},{8,10},{10,12},{12,14},{14,16},{16,18},{18... | collective-permute-start | bytes 24584 | tf_op jit(solution)/shard_map/ppermute | solution.py:287
  16.3 4.0 %copy-start.32 = (bf16[3,32,1024]{2,1,0:T(8,128)(2,1)S(1)}, bf16[3,32,1024]{2,1,0:T(8,128)(2,1)}, u32[]{:S(2)}) copy-start(bf16[3,32,1024]{2,1,0:T(8,128)(2,1)} %param.21) | copy-start | bytes 589828
  16.3 9.1 %copy-start.34 = (f32[4096]{0:T(1024)S(1)}, f32[4096]{0:T(1024)}, u32[]{:S(2)}) copy-start(f32[4096]{0:T(1024)} %param.20) | copy-start | bytes 49156
  16.3 9.2 %copy-start.33 = (f32[2,4096]{1,0:T(2,128)S(1)}, f32[2,4096]{1,0:T(2,128)}, u32[]{:S(2)}) copy-start(f32[2,4096]{1,0:T(2,128)} %param.19) | copy-start | bytes 98308
  17.9 24.2 %collective-permute-start.18 = (bf16[2,128,256]{2,1,0:T(8,128)(2,1)S(1)}, bf16[2,128,256]{2,1,0:T(8,128)(2,1)S(1)}, u32[]{:S(2)}, u32[]{:S(2)}) collective-permute-start(bf16[2,128,256]{2,1,0:T(8,128)(2,1)S(1)} %pad_maximum_fusion.3.mine_ref), channel_id=1, source_target_pairs={{0,1},{1,0},{2,3},{3,2},{4,5},{5,4},{6,7},{7,6},{8,9},{9,8},{10,11... | collective-permute-start | bytes 393224 | tf_op jit(solution)/shard_map/ppermute | solution.py:119
  21.1 11.5 %all-to-all-start = ((bf16[4,3,32,256]{3,2,1,0:T(8,128)(2,1)}), bf16[4,3,32,256]{3,2,1,0:T(8,128)(2,1)S(1)}, u32[]{:S(2)}, u32[]{:S(2)}) async-start(bf16[4,3,32,256]{3,2,1,0:T(8,128)(2,1)} %copy.74), calls=%async_computation | async-start | bytes 393216 | tf_op jit(solution)/shard_map/all_to_all | solution.py:108
  32.6 6.9 %collective-permute-start.17 = (bf16[4,3,32,256]{3,2,1,0:T(8,128)(2,1)S(1)}, bf16[4,3,32,256]{3,2,1,0:T(8,128)(2,1)S(1)}, u32[]{:S(2)}, u32[]{:S(2)}) collective-permute-start(bf16[4,3,32,256]{3,2,1,0:T(8,128)(2,1)S(1)} %all-to-all-done), channel_id=1, source_target_pairs={{0,128},{128,0},{1,129},{129,1},{2,130},{130,2},{3,131},{131,3},{4... | collective-permute-start | bytes 589832 | tf_op jit(solution)/shard_map/ppermute | solution.py:109
  39.6 12.2 %copy-start.35 = (s32[2,32]{1,0:T(2,128)S(1)}, s32[2,32]{1,0:T(2,128)}, u32[]{:S(2)}) copy-start(s32[2,32]{1,0:T(2,128)} %param.18) | copy-start | bytes 772
  39.6 12.6 %copy-start.27 = (bf16[1,512,512]{2,1,0:T(8,128)(2,1)S(1)}, bf16[1,512,512]{2,1,0:T(8,128)(2,1)}, u32[]{:S(2)}) copy-start(bf16[1,512,512]{2,1,0:T(8,128)(2,1)} %param.13) | copy-start | bytes 1572868
  39.6 12.6 %copy-start.28 = (bf16[1,4,512,512]{3,2,1,0:T(8,128)(2,1)S(1)}, bf16[1,4,512,512]{3,2,1,0:T(8,128)(2,1)}, u32[]{:S(2)}) copy-start(bf16[1,4,512,512]{3,2,1,0:T(8,128)(2,1)} %param.16) | copy-start | bytes 6291460
  39.6 12.6 %copy-start.30 = (bf16[1,256,512]{2,1,0:T(8,128)(2,1)S(1)}, bf16[1,256,512]{2,1,0:T(8,128)(2,1)}, u32[]{:S(2)}) copy-start(bf16[1,256,512]{2,1,0:T(8,128)(2,1)} %param.15) | copy-start | bytes 786436
  43.5 24.6 %all-to-all-start.1 = ((bf16[8,32,896]{2,1,0:T(8,128)(2,1)}), bf16[8,32,896]{2,1,0:T(8,128)(2,1)}, u32[]{:S(2)}, u32[]{:S(2)}) async-start(bf16[8,32,896]{2,1,0:T(8,128)(2,1)} %shard_map.141), calls=%async_computation.1 | async-start | bytes 917504 | tf_op jit(solution)/shard_map/all_to_all | solution.py:128
  52.2 1.1 copy-start.29
  70.6 18.7 %all-to-all-start.2 = ((bf16[8,32,768]{2,1,0:T(8,128)(2,1)}), bf16[8,32,768]{2,1,0:T(8,128)(2,1)S(1)}, u32[]{:S(2)}, u32[]{:S(2)}) async-start(bf16[8,32,768]{2,1,0:T(8,128)(2,1)} %broadcast_in_dim.4), calls=%async_computation.2 | async-start | bytes 786432 | tf_op jit(solution)/shard_map/all_to_all | solution.py:132
  74.1 116.8 %all-gather.4.cloned.1.call-start = ((), (), s32[]{:S(2)}) async-start(), calls=%async_computation.4 | async-start | bytes 2359296 | tf_op jit(solution)/shard_map/all_gather | solution.py:134
  77.5 55.7 %collective-permute-start.1 = (bf16[256,2048]{1,0:T(8,128)(2,1)}, bf16[256,2048]{1,0:T(8,128)(2,1)}, u32[]{:S(2)}, u32[]{:S(2)}) collective-permute-start(bf16[256,2048]{1,0:T(8,128)(2,1)} %convolution_convert_fusion), channel_id=1, source_target_pairs={{0,1},{1,0},{2,3},{3,2},{4,5},{5,4},{6,7},{7,6},{8,9},{9,8},{10,11... | collective-permute-start | bytes 3145736 | tf_op jit(solution)/shard_map/ppermute | solution.py:304
  78.7 32.1 %collective-permute-start.6 = (bf16[256,512]{1,0:T(8,128)(2,1)S(1)}, bf16[256,512]{1,0:T(8,128)(2,1)S(1)}, u32[]{:S(2)}, u32[]{:S(2)}) collective-permute-start(bf16[256,512]{1,0:T(8,128)(2,1)S(1)} %shard_map.140.refs_0_), channel_id=1, source_target_pairs={{0,1},{1,0},{2,3},{3,2},{4,5},{5,4},{6,7},{7,6},{8,9},{9,8},{10,11... | collective-permute-start | bytes 786440 | tf_op jit(solution)/shard_map/ppermute | solution.py:289
  81.1 33.5 %collective-permute-start.7 = (bf16[256,512]{1,0:T(8,128)(2,1)S(1)}, bf16[256,512]{1,0:T(8,128)(2,1)S(1)}, u32[]{:S(2)}, u32[]{:S(2)}) collective-permute-start(bf16[256,512]{1,0:T(8,128)(2,1)S(1)} %shard_map.140.refs_0_), channel_id=1, source_target_pairs={{0,16},{16,32},{32,48},{48,64},{64,80},{80,96},{96,112},{112,128},... | collective-permute-start | bytes 786440 | tf_op jit(solution)/shard_map/ppermute | solution.py:153
  89.3 38.8 %collective-permute-start.19 = (bf16[256,768]{1,0:T(8,128)(2,1)S(1)}, bf16[256,768]{1,0:T(8,128)(2,1)S(1)}, u32[]{:S(2)}, u32[]{:S(2)}) collective-permute-start(bf16[256,768]{1,0:T(8,128)(2,1)S(1)} %bitcast.68), channel_id=1, source_target_pairs={{0,128},{128,0},{1,129},{129,1},{2,130},{130,2},{3,131},{131,3},{4... | collective-permute-start | bytes 1179656 | tf_op jit(solution)/shard_map/ppermute | solution.py:133
  91.4 39.0 %collective-permute-start.2 = (bf16[256,512]{1,0:T(8,128)(2,1)S(1)}, bf16[256,512]{1,0:T(8,128)(2,1)S(1)}, u32[]{:S(2)}, u32[]{:S(2)}) collective-permute-start(bf16[256,512]{1,0:T(8,128)(2,1)S(1)} %shard_map.140.refs_0_), channel_id=1, source_target_pairs={{0,4},{4,8},{8,12},{12,0},{1,5},{5,9},{9,13},{13,1},{2,6},{6,10},{... | collective-permute-start | bytes 786440 | tf_op jit(solution)/shard_map/ppermute | solution.py:138
  110.8 20.4 %collective-permute-start.12 = (bf16[256,512]{1,0:T(8,128)(2,1)S(1)}, bf16[256,512]{1,0:T(8,128)(2,1)S(1)}, u32[]{:S(2)}, u32[]{:S(2)}) collective-permute-start(bf16[256,512]{1,0:T(8,128)(2,1)S(1)} %collective-permute-done.6), channel_id=1, source_target_pairs={{0,16},{16,32},{32,48},{48,64},{64,80},{80,96},{96,112},{112,128},... | collective-permute-start | bytes 786440 | tf_op jit(solution)/shard_map/ppermute | solution.py:156
  114.7 76.2 %copy-start.3 = (bf16[2,256,512]{2,1,0:T(8,128)(2,1)}, bf16[2,256,512]{2,1,0:T(8,128)(2,1)S(1)}, u32[]{:S(2)}) copy-start(bf16[2,256,512]{2,1,0:T(8,128)(2,1)S(1)} %pad_maximum_fusion.1.refs_5_) | copy-start | bytes 1572868
  114.7 23.3 %collective-permute-start.8 = (bf16[2,256,512]{2,1,0:T(8,128)(2,1)S(1)}, bf16[2,256,512]{2,1,0:T(8,128)(2,1)S(1)}, u32[]{:S(2)}, u32[]{:S(2)}) collective-permute-start(bf16[2,256,512]{2,1,0:T(8,128)(2,1)S(1)} %pad_maximum_fusion.1.refs_5_), channel_id=1, source_target_pairs={{0,4},{4,8},{8,12},{12,0},{1,5},{5,9},{9,13},{13,1},{2,6},{6,10},{... | collective-permute-start | bytes 1572872 | tf_op jit(solution)/shard_map/ppermute | solution.py:138
  129.2 33.8 %collective-permute-start.3 = (bf16[256,512]{1,0:T(8,128)(2,1)S(1)}, bf16[256,512]{1,0:T(8,128)(2,1)S(1)}, u32[]{:S(2)}, u32[]{:S(2)}) collective-permute-start(bf16[256,512]{1,0:T(8,128)(2,1)S(1)} %shard_map.140.refs_0_), channel_id=1, source_target_pairs={{0,12},{4,0},{8,4},{12,8},{1,13},{5,1},{9,5},{13,9},{2,14},{6,2},{... | collective-permute-start | bytes 786440 | tf_op jit(solution)/shard_map/ppermute | solution.py:139
  130.4 60.5 %copy-start.9 = (bf16[256,512]{1,0:T(8,128)(2,1)}, bf16[256,512]{1,0:T(8,128)(2,1)S(1)}, u32[]{:S(2)}) copy-start(bf16[256,512]{1,0:T(8,128)(2,1)S(1)} %collective-permute-done.2.refs_1_) | copy-start | bytes 786436
  130.4 19.3 %collective-permute-start.9 = (bf16[2,256,512]{2,1,0:T(8,128)(2,1)S(1)}, bf16[2,256,512]{2,1,0:T(8,128)(2,1)S(1)}, u32[]{:S(2)}, u32[]{:S(2)}) collective-permute-start(bf16[2,256,512]{2,1,0:T(8,128)(2,1)S(1)} %pad_maximum_fusion.1.refs_5_), channel_id=1, source_target_pairs={{0,12},{4,0},{8,4},{12,8},{1,13},{5,1},{9,5},{13,9},{2,14},{6,2},{... | collective-permute-start | bytes 1572872 | tf_op jit(solution)/shard_map/ppermute | solution.py:139
  131.2 11.9 %copy-start.19 = (bf16[256,512]{1,0:T(8,128)(2,1)}, bf16[256,512]{1,0:T(8,128)(2,1)S(1)}, u32[]{:S(2)}) copy-start(bf16[256,512]{1,0:T(8,128)(2,1)S(1)} %collective-permute-done.12.refs_10_) | copy-start | bytes 786436
  131.2 53.1 %collective-permute-start.4 = (bf16[128,512]{1,0:T(8,128)(2,1)}, bf16[128,512]{1,0:T(8,128)(2,1)S(1)}, u32[]{:S(2)}, u32[]{:S(2)}) collective-permute-start(bf16[128,512]{1,0:T(8,128)(2,1)} %slice.69), channel_id=1, source_target_pairs={{0,4},{4,8},{8,12},{12,0},{1,5},{5,9},{9,13},{13,1},{2,6},{6,10},{... | collective-permute-start | bytes 393224 | tf_op jit(solution)/shard_map/ppermute | solution.py:144
  133.1 38.3 %collective-permute-start.13 = (bf16[256,512]{1,0:T(8,128)(2,1)S(1)}, bf16[256,512]{1,0:T(8,128)(2,1)S(1)}, u32[]{:S(2)}, u32[]{:S(2)}) collective-permute-start(bf16[256,512]{1,0:T(8,128)(2,1)S(1)} %collective-permute-done.12.refs_10_), channel_id=1, source_target_pairs={{0,4},{4,8},{8,12},{12,0},{1,5},{5,9},{9,13},{13,1},{2,6},{6,10},{... | collective-permute-start | bytes 786440 | tf_op jit(solution)/shard_map/ppermute | solution.py:138
  138.0 52.9 %copy-start.5 = (bf16[2,256,512]{2,1,0:T(8,128)(2,1)}, bf16[2,256,512]{2,1,0:T(8,128)(2,1)S(1)}, u32[]{:S(2)}) copy-start(bf16[2,256,512]{2,1,0:T(8,128)(2,1)S(1)} %collective-permute-done.8.refs_6_) | copy-start | bytes 1572868
  138.0 5.1 %collective-permute-start.20 = (f32[256]{0:T(256)S(1)}, f32[256]{0:T(256)S(1)}, u32[]{:S(2)}, u32[]{:S(2)}) collective-permute-start(f32[256]{0:T(256)S(1)} %get-tuple-element.10), channel_id=1, source_target_pairs={{0,1},{1,0},{2,3},{3,2},{4,5},{5,4},{6,7},{7,6},{8,9},{9,8},{10,11... | collective-permute-start | bytes 3080 | tf_op jit(solution)/shard_map/ppermute | solution.py:309
  143.1 29.9 %collective-permute-start.14 = (bf16[256,512]{1,0:T(8,128)(2,1)S(1)}, bf16[256,512]{1,0:T(8,128)(2,1)S(1)}, u32[]{:S(2)}, u32[]{:S(2)}) collective-permute-start(bf16[256,512]{1,0:T(8,128)(2,1)S(1)} %collective-permute-done.12.refs_10_), channel_id=1, source_target_pairs={{0,12},{4,0},{8,4},{12,8},{1,13},{5,1},{9,5},{13,9},{2,14},{6,2},{... | collective-permute-start | bytes 786440 | tf_op jit(solution)/shard_map/ppermute | solution.py:139
  149.7 41.2 %copy-start.7 = (bf16[2,256,512]{2,1,0:T(8,128)(2,1)}, bf16[2,256,512]{2,1,0:T(8,128)(2,1)S(1)}, u32[]{:S(2)}) copy-start(bf16[2,256,512]{2,1,0:T(8,128)(2,1)S(1)} %collective-permute-done.9.refs_7_) | copy-start | bytes 1572868
  149.7 7.6 %collective-permute-start.21 = (f32[256]{0:T(256)S(1)}, f32[256]{0:T(256)S(1)}, u32[]{:S(2)}, u32[]{:S(2)}) collective-permute-start(f32[256]{0:T(256)S(1)} %add_rsqrt_fusion), channel_id=1, source_target_pairs={{0,16},{16,32},{32,48},{48,64},{64,80},{80,96},{96,112},{112,128},... | collective-permute-start | bytes 3080 | tf_op jit(solution)/shard_map/ppermute | solution.py:311
  157.3 32.9 %collective-permute-start.10 = (bf16[256,512]{1,0:T(8,128)(2,1)}, bf16[256,512]{1,0:T(8,128)(2,1)S(1)}, u32[]{:S(2)}, u32[]{:S(2)}) collective-permute-start(bf16[256,512]{1,0:T(8,128)(2,1)} %slice_bitcast_fusion.1), channel_id=1, source_target_pairs={{0,4},{4,8},{8,12},{12,0},{1,5},{5,9},{9,13},{13,1},{2,6},{6,10},{... | collective-permute-start | bytes 786440 | tf_op jit(solution)/shard_map/ppermute | solution.py:144
  158.5 16.3 %all-to-all-start.3 = ((f32[4,2,256]{2,1,0:T(2,128)}), f32[4,2,256]{2,1,0:T(2,128)}, u32[]{:S(2)}, u32[]{:S(2)}) async-start(f32[4,2,256]{2,1,0:T(2,128)} %broadcast_in_dim.5), calls=%async_computation.3 | async-start | bytes 16384 | tf_op jit(solution)/shard_map/all_to_all | solution.py:313
  163.0 27.9 %copy-start.11 = (bf16[256,512]{1,0:T(8,128)(2,1)}, bf16[256,512]{1,0:T(8,128)(2,1)S(1)}, u32[]{:S(2)}) copy-start(bf16[256,512]{1,0:T(8,128)(2,1)S(1)} %collective-permute-done.3.refs_2_) | copy-start | bytes 786436
  163.0 27.9 %collective-permute-start.11 = (bf16[256,512]{1,0:T(8,128)(2,1)}, bf16[256,512]{1,0:T(8,128)(2,1)}, u32[]{:S(2)}, u32[]{:S(2)}) collective-permute-start(bf16[256,512]{1,0:T(8,128)(2,1)} %slice_bitcast_fusion), channel_id=1, source_target_pairs={{0,12},{4,0},{8,4},{12,8},{1,13},{5,1},{9,5},{13,9},{2,14},{6,2},{... | collective-permute-start | bytes 786440 | tf_op jit(solution)/shard_map/ppermute | solution.py:145
  171.4 12.8 %copy-start.13 = (bf16[256,512]{1,0:T(8,128)(2,1)}, bf16[256,512]{1,0:T(8,128)(2,1)S(1)}, u32[]{:S(2)}) copy-start(bf16[256,512]{1,0:T(8,128)(2,1)S(1)} %collective-permute-done.13.refs_11_) | copy-start | bytes 786436
  171.4 15.8 %collective-permute-start.5 = (bf16[128,512]{1,0:T(8,128)(2,1)}, bf16[128,512]{1,0:T(8,128)(2,1)}, u32[]{:S(2)}, u32[]{:S(2)}) collective-permute-start(bf16[128,512]{1,0:T(8,128)(2,1)} %slice.70), channel_id=1, source_target_pairs={{0,12},{4,0},{8,4},{12,8},{1,13},{5,1},{9,5},{13,9},{2,14},{6,2},{... | collective-permute-start | bytes 393224 | tf_op jit(solution)/shard_map/ppermute | solution.py:145
  172.9 11.3 %copy-start.16 = (bf16[256,512]{1,0:T(8,128)(2,1)}, bf16[256,512]{1,0:T(8,128)(2,1)S(1)}, u32[]{:S(2)}) copy-start(bf16[256,512]{1,0:T(8,128)(2,1)S(1)} %collective-permute-done.14.refs_12_) | copy-start | bytes 786436
  172.9 14.3 %collective-permute-start.15 = (bf16[128,512]{1,0:T(8,128)(2,1)}, bf16[128,512]{1,0:T(8,128)(2,1)S(1)}, u32[]{:S(2)}, u32[]{:S(2)}) collective-permute-start(bf16[128,512]{1,0:T(8,128)(2,1)} %slice.73), channel_id=1, source_target_pairs={{0,4},{4,8},{8,12},{12,0},{1,5},{5,9},{9,13},{13,1},{2,6},{6,10},{... | collective-permute-start | bytes 393224 | tf_op jit(solution)/shard_map/ppermute | solution.py:144
  184.3 5.3 %collective-permute-start.16 = (bf16[128,512]{1,0:T(8,128)(2,1)}, bf16[128,512]{1,0:T(8,128)(2,1)S(1)}, u32[]{:S(2)}, u32[]{:S(2)}) collective-permute-start(bf16[128,512]{1,0:T(8,128)(2,1)} %slice.74), channel_id=1, source_target_pairs={{0,12},{4,0},{8,4},{12,8},{1,13},{5,1},{9,5},{13,9},{2,14},{6,2},{... | collective-permute-start | bytes 393224 | tf_op jit(solution)/shard_map/ppermute | solution.py:145
  190.9 1.0 copy-start.14
  191.9 0.9 copy-start.17
  192.8 0.9 copy-start.20
  193.8 0.9 copy-start.22
  194.7 0.9 copy-start.24
  195.7 0.9 copy-start.26
  196.6 3.7 %copy-start.15 = (bf16[256,512]{1,0:T(8,128)(2,1)S(1)}, bf16[256,512]{1,0:T(8,128)(2,1)}, u32[]{:S(2)}) copy-start(bf16[256,512]{1,0:T(8,128)(2,1)} %copy-done.13) | copy-start | bytes 786436
  196.6 3.7 %copy-start.18 = (bf16[256,512]{1,0:T(8,128)(2,1)S(1)}, bf16[256,512]{1,0:T(8,128)(2,1)}, u32[]{:S(2)}) copy-start(bf16[256,512]{1,0:T(8,128)(2,1)} %copy-done.16) | copy-start | bytes 786436
  199.9 10.8 %collective-permute-start.23 = (bf16[8,256,256]{2,1,0:T(8,128)(2,1)S(1)}, bf16[8,256,256]{2,1,0:T(8,128)(2,1)S(1)}, u32[]{:S(2)}, u32[]{:S(2)}) collective-permute-start(bf16[8,256,256]{2,1,0:T(8,128)(2,1)S(1)} %shard_map.143.vm_ref), channel_id=1, source_target_pairs={{0,2},{2,0},{1,3},{3,1},{4,6},{6,4},{5,7},{7,5},{8,10},{10,8},{9,1... | collective-permute-start | bytes 3145736 | tf_op jit(solution)/shard_map/ppermute | solution.py:320
  200.2 1.0 copy-start.4
  201.3 1.0 copy-start.6
  202.3 1.0 copy-start.8
  203.4 0.9 copy-start.10
  204.3 0.9 copy-start.12
  209.2 0.8 copy-start
  210.0 2.9 %collective-permute-start.22 = (bf16[8,256,256]{2,1,0:T(8,128)(2,1)S(1)}, bf16[8,256,256]{2,1,0:T(8,128)(2,1)}, u32[]{:S(2)}, u32[]{:S(2)}) collective-permute-start(bf16[8,256,256]{2,1,0:T(8,128)(2,1)S(1)} %get-tuple-element.5.km_ref), channel_id=1, source_target_pairs={{0,2},{2,0},{1,3},{3,1},{4,6},{6,4},{5,7},{7,5},{8,10},{10,8},{9,1... | collective-permute-start | bytes 3145736 | tf_op jit(solution)/shard_map/ppermute | solution.py:318
  212.9 1.0 copy-start.1
  217.2 14.1 %collective-permute-start.26 = (bf16[1,256,256]{2,1,0:T(8,128)(2,1)S(1)}, bf16[1,256,256]{2,1,0:T(8,128)(2,1)S(1)}, u32[]{:S(2)}, u32[]{:S(2)}) collective-permute-start(bf16[1,256,256]{2,1,0:T(8,128)(2,1)S(1)} %shard_map.147), channel_id=1, source_target_pairs={{0,12},{4,0},{8,4},{12,8},{1,13},{5,1},{9,5},{13,9},{2,14},{6,2},{... | collective-permute-start | bytes 393224 | tf_op jit(solution)/shard_map/ppermute | solution.py:326
  223.7 7.5 %collective-permute-start.25 = (bf16[1,256,256]{2,1,0:T(8,128)(2,1)S(1)}, bf16[1,256,256]{2,1,0:T(8,128)(2,1)S(1)}, u32[]{:S(2)}, u32[]{:S(2)}) collective-permute-start(bf16[1,256,256]{2,1,0:T(8,128)(2,1)S(1)} %shard_map.146), channel_id=1, source_target_pairs={{0,8},{4,12},{8,0},{12,4},{1,9},{5,13},{9,1},{13,5},{2,10},{6,14},... | collective-permute-start | bytes 393224 | tf_op jit(solution)/shard_map/ppermute | solution.py:326
  223.8 4.3 %copy-start.2 = (bf16[4,256,256]{2,1,0:T(8,128)(2,1)S(1)}, bf16[4,256,256]{2,1,0:T(8,128)(2,1)}, u32[]{:S(2)}) copy-start(bf16[4,256,256]{2,1,0:T(8,128)(2,1)} %copy-done) | copy-start | bytes 1572868
  227.1 6.8 %collective-permute-start.24 = (bf16[1,256,256]{2,1,0:T(8,128)(2,1)S(1)}, bf16[1,256,256]{2,1,0:T(8,128)(2,1)S(1)}, u32[]{:S(2)}, u32[]{:S(2)}) collective-permute-start(bf16[1,256,256]{2,1,0:T(8,128)(2,1)S(1)} %shard_map.145), channel_id=1, source_target_pairs={{0,4},{4,8},{8,12},{12,0},{1,5},{5,9},{9,13},{13,1},{2,6},{6,10},{... | collective-permute-start | bytes 393224 | tf_op jit(solution)/shard_map/ppermute | solution.py:326
  (4 other events, 2.7 us)
Sparse Core Ops, SparseCore 0:
  129.3 9.2 all-gather.3

commit v3 on v2

v3 whole, which is shorter than its diff:
```python
import functools

import jax
import jax.numpy as jnp
from jax import lax
from jax.experimental import pallas as pl
from jax.experimental.pallas import tpu as pltpu
from jax.sharding import Mesh, PartitionSpec as P

HD = 128
BLOCK = 256
D = 4096
CH = 512
CTX = ("yl", "z", "x", "c")
SWAP = [(0, 1), (1, 0)]
BF = jnp.bfloat16
F32 = jnp.float32
LOG2E = 1.4426950408889634


def elu(v):
    return jnp.where(v > 0, v, jnp.exp(jnp.minimum(v, 0.0)) - 1.0)


def dot(a, b):
    return jnp.dot(a, b, preferred_element_type=F32)


def in_vmem(n):
    return [pl.BlockSpec(memory_space=pltpu.VMEM)] * n


def params(mib):
    return pltpu.CompilerParams(vmem_limit_bytes=mib * 1024 * 1024)


def encoder_kernel(halo_ref, audio_ref, taps_ref, back_ref, down_ref, out_ref, u_ref, e_ref):
    u_ref[0:8, :] = jnp.zeros((8, CH), F32)
    u_ref[8:16, :] = elu(halo_ref[...].astype(F32))
    u_ref[16:, :] = elu(audio_ref[...].astype(F32))
    rows = audio_ref.shape[0] + 8
    inner = dot(u_ref[2 : 2 + rows, :].astype(BF), taps_ref[0])
    inner += dot(u_ref[5 : 5 + rows, :].astype(BF), taps_ref[1])
    inner += dot(u_ref[8 : 8 + rows, :].astype(BF), taps_ref[2])
    hidden = elu(inner).astype(BF)
    branch = dot(hidden, back_ref[...])
    first = (halo_ref[...].astype(F32) + branch[0:8]).astype(BF)
    first = elu(first.astype(F32)).astype(BF).astype(F32)
    rest = (audio_ref[...].astype(F32) + branch[8:]).astype(BF)
    rest = elu(rest.astype(F32)).astype(BF).astype(F32)
    for j in range(CH // 128):
        e_ref[j, 0:8, :] = first[:, j * 128 : (j + 1) * 128]
        e_ref[j, 8:, :] = rest[:, j * 128 : (j + 1) * 128]
    acc = jnp.zeros((BLOCK, CH), F32)
    for k in range(4):
        e = [e_ref[j, pl.ds(6 + k, BLOCK, stride=2), :].astype(BF) for j in range(CH // 128)]
        acc += dot(jnp.concatenate(e, axis=1), down_ref[k])
    out_ref[...] = acc.astype(BF)


def encoder(halo, audio, taps, back, down):
    return pl.pallas_call(
        encoder_kernel,
        in_specs=in_vmem(5),
        out_specs=pl.BlockSpec(memory_space=pltpu.VMEM),
        out_shape=jax.ShapeDtypeStruct((BLOCK, CH), BF),
        scratch_shapes=[pltpu.VMEM((528, CH), F32), pltpu.VMEM((CH // 128, 520, 128), F32)],
        compiler_params=params(20),
        cost_estimate=pl.CostEstimate(flops=1100000000, bytes_accessed=4 << 20, transcendentals=600000),
    )(halo, audio, taps, back, down)


def swap(a, axis):
    return lax.ppermute(a, axis, SWAP)


def shift(a, by):
    return lax.ppermute(a, "x", [(i, (i + by) % 4) for i in range(4)])


def split_kernel(at_ref, w_ref, near_ref, far_ref, *outs):
    x = at_ref[3]
    for dx in range(4):
        lanes = pl.ds(pl.multiple_of(lax.rem(x + dx, 4) * 256, 256), 256)
        outs[dx][...] = w_ref[:, :, lanes]
    outs[4][0] = near_ref[...]
    outs[4][1] = far_ref[...]


def split(at, w, embed):
    whole = lambda shape: pl.BlockSpec(shape, lambda i, at: (0,) * len(shape))
    return pl.pallas_call(
        split_kernel,
        grid_spec=pltpu.PrefetchScalarGridSpec(
            num_scalar_prefetch=1,
            grid=(1,),
            in_specs=[
                whole((3, 32, 1024)),
                pl.BlockSpec((128, 256), lambda i, at: (at[2], at[0])),
                pl.BlockSpec((128, 256), lambda i, at: (at[2], at[1])),
            ],
            out_specs=[whole((3, 32, 256))] * 4 + [whole((2, 128, 256))],
        ),
        out_shape=[jax.ShapeDtypeStruct((3, 32, 256), BF)] * 4 + [jax.ShapeDtypeStruct((2, 128, 256), BF)],
    )(at, w, embed, embed)


def partial_kernel(at_ref, w00, w01, w10, w11, mine_ref, rest_ref, g0, g1, t0, t1, out_ref, w_ref):
    x, core = at_ref[3], at_ref[4]
    for y, pair in enumerate(((w00, w01), (w10, w11))):
        for c, ref in enumerate(pair):
            for dx in range(4):
                row = lax.rem(x + 4 - dx, 4) * 64 + (core ^ c) * 32
                for j in range(3):
                    w_ref[y, pl.ds(pl.multiple_of(row, 32), 32), j * 256 : (j + 1) * 256] = ref[dx, j]
    part = None
    line = None
    for y, (gain_ref, table_ref) in enumerate(((g0, t0), (g1, t1))):
        w = w_ref[y]
        gain = gain_ref[...]
        embed = jnp.concatenate([mine_ref[y], rest_ref[y]], axis=0).astype(F32) * gain
        table = jnp.concatenate([table_ref[...], jnp.zeros((6, 256), F32)], axis=0) * gain
        high = table.astype(BF)
        low = (table - high.astype(F32)).astype(BF)
        a = dot(embed.astype(BF), w)
        b = dot(high, w) + dot(low, w)
        part = a if part is None else part + a
        line = b if line is None else line + b
    top = line.astype(BF).astype(F32)
    rem = line - top
    rows = [v[s : s + 1, k * 128 : (k + 1) * 128] for v in (top, rem) for s in range(2) for k in range(6)]
    tail = jnp.concatenate(rows + [jnp.zeros((8, 128), F32)], axis=0).astype(BF)
    for i in range(8):
        out_ref[i, :, 0:768] = part[i * 32 : (i + 1) * 32].astype(BF)
        out_ref[i, :, 768:896] = tail


def partial_weights(at, ws, mine, rest, gain, table):
    whole = lambda shape: pl.BlockSpec(shape, lambda i, at: (0,) * len(shape))
    here = lambda rows, k: pl.BlockSpec((rows, 256), lambda i, at: (0, at[k]))
    return pl.pallas_call(
        partial_kernel,
        grid_spec=pltpu.PrefetchScalarGridSpec(
            num_scalar_prefetch=1,
            grid=(1,),
            in_specs=[whole((4, 3, 32, 256))] * 4
            + [whole((2, 128, 256))] * 2
            + [here(1, 0), here(1, 1), here(2, 0), here(2, 1)],
            out_specs=whole((8, 32, 896)),
            scratch_shapes=[pltpu.VMEM((2, 256, 768), BF)],
        ),
        out_shape=jax.ShapeDtypeStruct((8, 32, 896), BF),
        compiler_params=params(16),
        cost_estimate=pl.CostEstimate(flops=210000000, bytes_accessed=2 << 20, transcendentals=0),
    )(at, *ws, mine, rest, gain, gain, table, table)


def sum_kernel(p_ref, m_ref, line_ref):
    total = jnp.sum(p_ref[...].astype(F32), axis=0)
    m = total[:, :768].astype(BF)
    for i in range(8):
        m_ref[i] = m
    both = total[0:12, 768:] + total[12:24, 768:]
    line_ref[...] = jnp.zeros((8, 768), F32)
    for s in range(2):
        for k in range(6):
            line_ref[s : s + 1, k * 128 : (k + 1) * 128] = both[s * 6 + k : s * 6 + k + 1]


def sum_weights(packed):
    return pl.pallas_call(
        sum_kernel,
        in_specs=in_vmem(1),
        out_specs=in_vmem(2),
        out_shape=[jax.ShapeDtypeStruct((8, 32, 768), BF), jax.ShapeDtypeStruct((8, 768), F32)],
        compiler_params=params(8),
    )(packed)


def give_kernel(at_ref, latent_ref, embed_ref, *refs):
    refs[-1][...] = dot(latent_ref[...], embed_ref[...]).astype(BF)


def give_term(at, latent, embed, after):
    return pl.pallas_call(
        give_kernel,
        grid_spec=pltpu.PrefetchScalarGridSpec(
            num_scalar_prefetch=1,
            grid=(2,),
            in_specs=[
                pl.BlockSpec((BLOCK, CH), lambda i, at: (0, 0)),
                pl.BlockSpec((CH, 1024), lambda i, at: (0, (1 - at[5]) * 2 + i)),
            ]
            + [pl.BlockSpec(memory_space=pl.ANY)] * len(after),
            out_specs=pl.BlockSpec((BLOCK, 1024), lambda i, at: (0, i)),
        ),
        out_shape=jax.ShapeDtypeStruct((BLOCK, D // 2), BF),
        compiler_params=params(16),
        cost_estimate=pl.CostEstimate(flops=540000000, bytes_accessed=3 << 20, transcendentals=0),
    )(at, latent, embed, *after)


def embed_kernel(at_ref, latent_ref, embed_ref, got_ref, active_ref, table_ref, out_ref, square_ref):
    act = active_ref[:, pl.ds(at_ref[3] + 4, 1), :].reshape(2, BLOCK)
    cols = jnp.concatenate([act, jnp.zeros((6, BLOCK), F32)], axis=0).T
    x = dot(latent_ref[...], embed_ref[...]) + got_ref[...].astype(F32)
    x = x + cols[:, 0:1] * table_ref[0:1] + cols[:, 1:2] * table_ref[1:2]
    out_ref[...] = x.astype(BF)
    square = jnp.sum(x * x, axis=1, keepdims=True)
    square = jnp.broadcast_to(square, (BLOCK, 128)).T[0:8]

    @pl.when(pl.program_id(0) == 0)
    def _():
        square_ref[...] = square

    @pl.when(pl.program_id(0) != 0)
    def _():
        square_ref[...] += square


def embed_rows(at, latent, embed, got, active, table):
    mine = lambda rows: pl.BlockSpec((rows, 1024), lambda i, at: (0, at[5] * 2 + i))
    tile = pl.BlockSpec((BLOCK, 1024), lambda i, at: (0, i))
    return pl.pallas_call(
        embed_kernel,
        grid_spec=pltpu.PrefetchScalarGridSpec(
            num_scalar_prefetch=1,
            grid=(2,),
            in_specs=[
                pl.BlockSpec((BLOCK, CH), lambda i, at: (0, 0)),
                mine(CH),
                tile,
                pl.BlockSpec((2, 8, BLOCK), lambda i, at: (0, 0, 0)),
                mine(2),
            ],
            out_specs=[tile, pl.BlockSpec((8, BLOCK), lambda i, at: (0, 0))],
        ),
        out_shape=[jax.ShapeDtypeStruct((BLOCK, D // 2), BF), jax.ShapeDtypeStruct((8, BLOCK), F32)],
        compiler_params=params(20),
        cost_estimate=pl.CostEstimate(flops=540000000, bytes_accessed=5 << 20, transcendentals=0),
    )(at, latent, embed, got, active, table)


def project_kernel(with_q, at_ref, *refs):
    (a, al, ar, af, b, bl, br, bf, m00, m01, m10, m11, line_ref, active_ref, s0, s1, s2, s3) = refs[:18]
    outs, m_ref = refs[18:-1], refs[-1]
    x, core, yl = at_ref[3], at_ref[4], at_ref[6]
    lanes = slice(0, 512) if with_q else slice(512, 768)
    for y, pair in enumerate(((m00, m01), (m10, m11))):
        for c, ref in enumerate(pair):
            row = ((yl ^ y) * 2 + (core ^ c)) * 128
            for s in range(2):
                m_ref[pl.ds(pl.multiple_of(s * 512 + row, 128), 128), :] = ref[s * 128 : (s + 1) * 128, lanes]
    own = (a, ar, af, al)
    prev = (b, br, bf, bl)
    scales = (s0, s1, s2, s3)
    jobs = [(0, outs[1], 0), (1, outs[0], 1)] if with_q else [(2, outs[0], 1)]
    for r, blocks in ((1, own), (0, prev)):
        for dx in range(4):
            at = lax.rem(x + dx, 4)
            m = 4 * r + at
            act = active_ref[:, pl.ds(m, 1), :].reshape(2, BLOCK)
            side = jnp.concatenate([act, scales[dx][r : r + 1, :], jnp.zeros((5, BLOCK), F32)], axis=0).T
            rows = blocks[dx]
            for j, out, both in jobs:
                if not both and r == 0:
                    continue
                at_j = j * 256 - lanes.start
                line = line_ref[:, j * 256 : (j + 1) * 256]
                acc = dot(rows[0], m_ref[0:512, at_j : at_j + 256]) + dot(rows[1], m_ref[512:1024, at_j : at_j + 256])
                acc = acc + side[:, 0:1] * line[0:1] + side[:, 1:2] * line[1:2]
                acc = acc * (side[:, 2:3] * (HD**-0.5 * LOG2E if j == 0 else 1.0))
                out[m if both else at] = acc.astype(BF)


def project(with_q, at, pieces, ms, lines, active, scales):
    shapes = [jax.ShapeDtypeStruct((8, BLOCK, 256), BF)]
    if with_q:
        shapes.append(jax.ShapeDtypeStruct((4, BLOCK, 256), BF))
    return pl.pallas_call(
        functools.partial(project_kernel, with_q),
        in_specs=[pl.BlockSpec(memory_space=pltpu.SMEM)] + in_vmem(18),
        out_specs=in_vmem(len(shapes)),
        out_shape=shapes,
        scratch_shapes=[pltpu.VMEM((1024, 512 if with_q else 256), BF)],
        compiler_params=params(20),
        cost_estimate=pl.CostEstimate(flops=1600000000, bytes_accessed=6 << 20, transcendentals=0),
    )(at, *pieces, *ms, lines, active, *scales)


def attention_kernel(place_ref, q_ref, km_ref, kt_ref, vm_ref, vt_ref, o_ref):
    at = lax.rem(place_ref[0] + place_ref[3 + pl.program_id(0)], 4)
    core = place_ref[1]
    first = place_ref[2]
    rows = lax.broadcasted_iota(jnp.int32, (BLOCK, 1024), 0)
    cols = lax.broadcasted_iota(jnp.int32, (BLOCK, 1024), 1)
    least_m = jnp.where(first == 1, (3 - at) * BLOCK, 0)
    least_t = jnp.where(first == 1, (4 - at - core) * BLOCK, 0)
    bias_m = jnp.where((cols - 768 <= rows) & (cols >= least_m), 0.0, -1e30)
    bias_t = jnp.where((cols > rows) & (cols >= least_t), 0.0, -1e30)
    contract = (((1,), (1,)), ((), ()))
    for h in range(2):
        lanes = slice(h * HD, (h + 1) * HD)
        q = q_ref[at, :, lanes]
        km = km_ref[pl.ds(at + 1, 4), :, lanes].reshape(1024, HD)
        kt = kt_ref[pl.ds(at + core, 4), :, lanes].reshape(1024, HD)
        sm = lax.dot_general(q, km, contract, preferred_element_type=F32) + bias_m
        st = lax.dot_general(q, kt, contract, preferred_element_type=F32) + bias_t
        top = jnp.maximum(jnp.max(sm, axis=1, keepdims=True), jnp.max(st, axis=1, keepdims=True))
        pm = jnp.exp2(sm - top)
        pt = jnp.exp2(st - top)
        total = jnp.sum(pm, axis=1, keepdims=True) + jnp.sum(pt, axis=1, keepdims=True)
        vm = vm_ref[pl.ds(at + 1, 4), :, lanes].reshape(1024, HD)
        vt = vt_ref[pl.ds(at + core, 4), :, lanes].reshape(1024, HD)
        o = dot(pm.astype(BF), vm) + dot(pt.astype(BF), vt)
        o_ref[0, :, lanes] = (o / total).astype(BF)


def attention(place, offsets, q, km, kt, vm, vt):
    n = len(offsets)
    return pl.pallas_call(
        attention_kernel,
        grid=(n,),
        in_specs=[pl.BlockSpec(memory_space=pltpu.SMEM)] + in_vmem(5),
        out_specs=pl.BlockSpec((1, BLOCK, 256), lambda i: (i, 0, 0)),
        out_shape=jax.ShapeDtypeStruct((n, BLOCK, 256), BF),
        compiler_params=params(20),
        cost_estimate=pl.CostEstimate(
            flops=n * 8 * BLOCK * 2048 * HD, bytes_accessed=5 << 20, transcendentals=n * 2 * BLOCK * 2048
        ),
    )(jnp.concatenate([place, jnp.array(offsets, jnp.int32)]), q, km, kt, vm, vt)


def collect_kernel(place_ref, a_ref, b_ref, c_ref, d_ref, o_ref):
    for dx, ref in enumerate((a_ref, b_ref, c_ref, d_ref)):
        at = lax.rem(place_ref[0] + 4 - dx, 4)
        o_ref[:, pl.ds(pl.multiple_of(at * 256, 256), 256)] = ref[0]


def collect(place, parts):
    return pl.pallas_call(
        collect_kernel,
        in_specs=[pl.BlockSpec(memory_space=pltpu.SMEM)] + in_vmem(4),
        out_specs=pl.BlockSpec(memory_space=pltpu.VMEM),
        out_shape=jax.ShapeDtypeStruct((BLOCK, 1024), BF),
        compiler_params=params(20),
    )(place, *parts)


def on_device(
    audio_feats,
    res_conv,
    res_out,
    down_conv,
    stream_embed,
    turn_lengths,
    speaker_table,
    norm_gain,
    qkv_weight,
):
    tp = lax.axis_index("tp")
    x_at = lax.axis_index("x")
    core = lax.axis_index("c")
    yl = lax.axis_index("yl")
    z = lax.axis_index("z")
    row = yl * 8 + z
    at = jnp.stack([yl * 8 + z, (1 - yl) * 8 + z, yl * 2 + core, x_at, core, tp, yl]).astype(jnp.int32)
    behind = [(i, i + 1) for i in range(15)]

    audio = audio_feats[0]
    halo = lax.ppermute(audio[-8:], CTX, [(i, i + 1) for i in range(127)])
    embed = stream_embed[0]
    *chunks, mine = split(at, qkv_weight, embed)
    w00 = jnp.stack([chunks[0]] + [shift(chunks[dx], dx) for dx in (1, 2, 3)])
    rest = swap(mine, "tp")
    w10 = swap(w00, "yl")
    w01 = swap(w00, "c")
    w11 = swap(w10, "c")

    latent = encoder(halo, audio, res_conv[0], res_out[0], down_conv[0])
    other = swap(latent, "tp")
    prev = lax.ppermute(latent, ("yl", "z"), behind)
    a = jnp.stack([latent, other])
    al, ar = shift(a, 1), shift(a, 3)
    b = jnp.stack([prev, lax.ppermute(other, ("yl", "z"), behind)])
    bl, br = shift(b, 1), shift(b, 3)
    pieces = (a, al, ar, shift(al, 1), b, bl, br, shift(br, 3))

    packed = partial_weights(at, (w00, w01, w10, w11), mine, rest, norm_gain[None], speaker_table)
    packed = lax.all_to_all(packed, "z", 0, 0, tiled=True)
    m, lines = sum_weights(packed)
    m00 = lax.all_to_all(m, "z", 0, 0, tiled=True).reshape(256, 768)
    m10 = swap(m00, "yl")
    m01 = swap(m00, "c")
    m11 = swap(m10, "c")

    bounds = jnp.cumsum(turn_lengths, axis=1)
    start = ((row - 1 + jnp.arange(2)[:, None]) * 8 + 2 * jnp.arange(4)[None, :] + core) * BLOCK
    frames = start.reshape(8, 1) + jnp.arange(BLOCK)
    turn = jnp.sum((bounds[:, :, None, None] <= frames[None, None]).astype(jnp.int32), axis=1)
    active = (turn % 2 == 1).astype(F32)

    got = swap(give_term(at, latent, embed, (other, w11)), "tp")
    embedded, square = embed_rows(at, latent, embed, got, active, speaker_table)
    square = square + swap(square, "tp")
    scale = lax.rsqrt(square[0:1] * (1.0 / D) + 1e-05)
    scale = jnp.concatenate([lax.ppermute(scale, ("yl", "z"), behind), scale])
    scales = [scale] + [shift(scale, 4 - dx) for dx in (1, 2, 3)]

    ms = (m00, m01, m10, m11)
    km, q = project(True, at, pieces, ms, lines, active, scales)
    kt = swap(km, "c")
    (vm,) = project(False, at, pieces, ms, lines, active, scales)
    vt = swap(vm, "c")

    place = jnp.stack([x_at, core, (row == 0).astype(jnp.int32)]).astype(jnp.int32)
    parts = [None] * 4
    for dx in (2, 1, 3, 0):
        part = attention(place, (dx,), q, km, kt, vm, vt)
        parts[dx] = shift(part, dx) if dx else part
    return embedded, collect(place, parts)


def solution(mesh):
    fine = Mesh(mesh.devices.reshape(2, 8, 4, 2, 2), CTX + ("tp",))
    placed = (
        P("tp", CTX, None),
        P("tp", None, None, None),
        P("tp", None, None),
        P("tp", None, None, None),
        P("tp", None, None),
        P(),
        P(),
        P(),
        P(None, CTX, "tp"),
    )
    return jax.shard_map(
        on_device,
        mesh=fine,
        in_specs=placed,
        out_specs=(P(CTX, "tp"), P(CTX, "tp")),
        check_vma=False,
    )
```

time: 244 us -> 175 us (0.72)
  the two profiles are of different devices: /device:TPU:8 before, /device:TPU:1 now
where the time goes in v3:
time: 175 us; the launch traced here: 174 us
  starting transfers between devices  78.6 us (45%)
  waiting for transfers between devices  44.7 us (26%)
  Pallas kernels  33.6 us (19%)
  local copies, waits for them, and re-layouts  13.3 us (8%)
  other arithmetic  2.71 us (2%)
    ppermute x12, starting transfers between devices, swap(): return lax.ppermute(a, axis, SWAP)  30 us
    ppermute x15, starting transfers between devices, shift(): return lax.ppermute(a, 'x', [(i, (i + by) % 4) for i in range(4)])  27.9 us
    ppermute x12, waiting for transfers between devices, swap(): return lax.ppermute(a, axis, SWAP)  24.7 us
    ppermute x15, waiting for transfers between devices, shift(): return lax.ppermute(a, 'x', [(i, (i + by) % 4) for i in range(4)])  18.5 us
    pallas_call x4, Pallas kernels, attention(): pl.pallas_call(attention_kernel, grid=(n,), in_specs=[pl.BlockSpec(memory...  12.7 us
    unnamed x46, local copies, waits for them, and re-layouts  12.6 us
    all_to_all x1, starting transfers between devices, on_device(): packed = lax.all_to_all(packed, 'z', 0, 0, tiled=True)  8.08 us
    pallas_call x2, Pallas kernels, project(): pl.pallas_call(functools.partial(project_kernel, with_q), in_specs=[pl.Bl...  6.2 us
  transfers between devices with their start and end apart: 33, of which 12 were waited for; matrix products, arithmetic and copies ran while one was open for 1% of the time, Pallas kernels for 12%

profile of v3, /device:TPU:1, one launch (start us, length us, event | category | flops | bytes accessed | tf_op | source)
XLA Modules:
  0.0 173.9 jit_solution(783721909529699647)
XLA Ops:
  1.3 2.5 %shard_map.141 = (bf16[3,32,256]{2,1,0:T(8,128)(2,1)}, bf16[3,32,256]{2,1,0:T(8,128)(2,1)}, bf16[3,32,256]{2,1,0:T(8,128)(2,1)}, bf16[3,32,256]{2,1,0:T(8,128)(2,1)}, bf16[2,128,256]{2,1,0:T(8,128)(2,1)}) custom-call(s32[7]{0:T(128)} %stack.75.at_ref, bf16[3,32,1024]{2,1,0:T(8,128)(2,1)} %w_ref.1, bf16[512,4096]{1,0:T(8,128)(2,1)} %bitcast.25, ...), custom_call_target="tpu_custom_call" | custom-call | tf_op jit(solution)/shard_map/pallas_call | solution.py:92
  3.8 2.0 %collective-permute-start.2 = (bf16[3,32,256]{2,1,0:T(8,128)(2,1)}, bf16[3,32,256]{2,1,0:T(8,128)(2,1)S(1)}, u32[]{:S(2)}, u32[]{:S(2)}) collective-permute-start(bf16[3,32,256]{2,1,0:T(8,128)(2,1)} %get-tuple-element.14), channel_id=1, source_target_pairs={{0,4},{4,8},{8,12},{12,0},{1,5},{5,9},{9,13},{13,1},{2,6},{6,10},{... | collective-permute-start | bytes 147464 | tf_op jit(solution)/shard_map/ppermute | solution.py:78
  5.8 2.5 %collective-permute-start.3 = (bf16[3,32,256]{2,1,0:T(8,128)(2,1)}, bf16[3,32,256]{2,1,0:T(8,128)(2,1)S(1)}, u32[]{:S(2)}, u32[]{:S(2)}) collective-permute-start(bf16[3,32,256]{2,1,0:T(8,128)(2,1)} %get-tuple-element.15), channel_id=1, source_target_pairs={{0,8},{4,12},{8,0},{12,4},{1,9},{5,13},{9,1},{13,5},{2,10},{6,14},... | collective-permute-start | bytes 147464 | tf_op jit(solution)/shard_map/ppermute | solution.py:78
  8.3 1.2 collective-permute-start.4
  9.4 1.1 collective-permute-done.3
  10.5 1.2 collective-permute-done.4
  11.7 0.8 pad_maximum_fusion.2.w00
  12.5 1.5 collective-permute-start.5
  14.0 2.3 %collective-permute-start.16 = (bf16[4,3,32,256]{3,2,1,0:T(8,128)(2,1)S(1)}, bf16[4,3,32,256]{3,2,1,0:T(8,128)(2,1)S(1)}, u32[]{:S(2)}, u32[]{:S(2)}) collective-permute-start(bf16[4,3,32,256]{3,2,1,0:T(8,128)(2,1)S(1)} %pad_maximum_fusion.2.w00), channel_id=1, source_target_pairs={{0,2},{2,0},{1,3},{3,1},{4,6},{6,4},{5,7},{7,5},{8,10},{10,8},{9,1... | collective-permute-start | bytes 589832 | tf_op jit(solution)/shard_map/ppermute | solution.py:74
  16.3 0.9 collective-permute-done.5.w10
  17.2 3.3 %collective-permute-start.6 = (bf16[4,3,32,256]{3,2,1,0:T(8,128)(2,1)S(1)}, bf16[4,3,32,256]{3,2,1,0:T(8,128)(2,1)S(1)}, u32[]{:S(2)}, u32[]{:S(2)}) collective-permute-start(bf16[4,3,32,256]{3,2,1,0:T(8,128)(2,1)S(1)} %collective-permute-done.5.w10), channel_id=1, source_target_pairs={{0,2},{2,0},{1,3},{3,1},{4,6},{6,4},{5,7},{7,5},{8,10},{10,8},{9,1... | collective-permute-start | bytes 589832 | tf_op jit(solution)/shard_map/ppermute | solution.py:74
  20.5 2.8 %collective-permute-start.17 = (bf16[2,128,256]{2,1,0:T(8,128)(2,1)}, bf16[2,128,256]{2,1,0:T(8,128)(2,1)S(1)}, u32[]{:S(2)}, u32[]{:S(2)}) collective-permute-start(bf16[2,128,256]{2,1,0:T(8,128)(2,1)} %get-tuple-element.18.mine_ref), channel_id=1, source_target_pairs={{0,1},{1,0},{2,3},{3,2},{4,5},{5,4},{6,7},{7,6},{8,9},{9,8},{10,11... | collective-permute-start | bytes 393224 | tf_op jit(solution)/shard_map/ppermute | solution.py:74
  23.3 4.0 %collective-permute-done.17.rest_ref = bf16[2,128,256]{2,1,0:T(8,128)(2,1)S(1)} collective-permute-done((bf16[2,128,256]{2,1,0:T(8,128)(2,1)}, bf16[2,128,256]{2,1,0:T(8,128)(2,1)S(1)}, u32[]{:S(2)}, u32[]{:S(2)}) %collective-permute-start.17) | collective-permute-done | bytes 131104 | tf_op jit(solution)/shard_map/ppermute | solution.py:74
  27.4 0.9 copy-done.12
  28.3 1.9 %shard_map.144 = bf16[8,32,896]{2,1,0:T(8,128)(2,1)} custom-call(s32[7]{0:T(128)S(1)} %copy-done.17, bf16[4,3,32,256]{3,2,1,0:T(8,128)(2,1)S(1)} %pad_maximum_fusion.2.w00, bf16[4,3,32,256]{3,2,1,0:T(8,128)(2,1)S(1)} %collective-permute-done.16.w01, bf16[4,3,32,256]{3,2,1,0:T(8,128)(2,1)S(1)} %collective-permute-done.5.w10, ...), custom_call_target="tpu_custom_call" | custom-call | flops 210000000 | bytes 2097152 | tf_op jit(solution)/shard_map/pallas_call | solution.py:141
  30.2 8.1 %all-to-all-start = ((bf16[8,32,896]{2,1,0:T(8,128)(2,1)}), bf16[8,32,896]{2,1,0:T(8,128)(2,1)S(1)}, u32[]{:S(2)}, u32[]{:S(2)}) async-start(bf16[8,32,896]{2,1,0:T(8,128)(2,1)} %shard_map.144), calls=%async_computation | async-start | bytes 917504 | tf_op jit(solution)/shard_map/all_to_all | solution.py:390
  38.3 3.0 %collective-permute-start = (bf16[8,512]{1,0:T(8,128)(2,1)S(1)}, bf16[8,512]{1,0:T(8,128)(2,1)S(1)}, u32[]{:S(2)}, u32[]{:S(2)}) collective-permute-start(bf16[8,512]{1,0:T(8,128)(2,1)S(1)} %slice_bitcast_fusion), channel_id=1, source_target_pairs={{0,2},{2,4},{4,6},{6,8},{8,10},{10,12},{12,14},{14,16},{16,18},{18... | collective-permute-start | bytes 24584 | tf_op jit(solution)/shard_map/ppermute | solution.py:371
  41.3 0.8 collective-permute-done.halo_ref
  42.1 1.6 copy-done.19
  43.7 2.5 %shard_map.140.latent_ref = bf16[256,512]{1,0:T(8,128)(2,1)S(1)} custom-call(bf16[8,512]{1,0:T(8,128)(2,1)S(1)} %collective-permute-done.halo_ref, bf16[512,512]{1,0:T(8,128)(2,1)S(1)} %bitcast.37, bf16[3,512,256]{2,1,0:T(8,128)(2,1)S(1)} %bitcast.39, bf16[256,512]{1,0:T(8,128)(2,1)S(1)} %bitcast.40, bf16[4,512,512]{2,1,0:T(8,128)(2,1)S(1)} %bitcast.38), custom_call_target="tpu_custom_call" | custom-call | flops 1100000000 | bytes 4194304 | tf_op jit(solution)/shard_map/pallas_call | solution.py:62
  46.2 3.0 %collective-permute-start.1 = (bf16[256,512]{1,0:T(8,128)(2,1)S(1)}, bf16[256,512]{1,0:T(8,128)(2,1)S(1)}, u32[]{:S(2)}, u32[]{:S(2)}) collective-permute-start(bf16[256,512]{1,0:T(8,128)(2,1)S(1)} %shard_map.140.latent_ref), channel_id=1, source_target_pairs={{0,1},{1,0},{2,3},{3,2},{4,5},{5,4},{6,7},{7,6},{8,9},{9,8},{10,11... | collective-permute-start | bytes 786440 | tf_op jit(solution)/shard_map/ppermute | solution.py:74
  49.2 6.9 %collective-permute-done.1.refs_0_ = bf16[256,512]{1,0:T(8,128)(2,1)S(1)} collective-permute-done((bf16[256,512]{1,0:T(8,128)(2,1)S(1)}, bf16[256,512]{1,0:T(8,128)(2,1)S(1)}, u32[]{:S(2)}, u32[]{:S(2)}) %collective-permute-start.1) | collective-permute-done | bytes 262176 | tf_op jit(solution)/shard_map/ppermute | solution.py:74
  56.1 2.2 %copy-done = bf16[1,512,4096]{2,1,0:T(8,128)(2,1)S(1)} copy-done((bf16[1,512,4096]{2,1,0:T(8,128)(2,1)S(1)}, bf16[1,512,4096]{2,1,0:T(8,128)(2,1)}, u32[]{:S(2)}) %copy-start) | copy-done | bytes 4194328
  58.3 2.4 %shard_map.142 = bf16[256,2048]{1,0:T(8,128)(2,1)} custom-call(s32[7]{0:T(128)S(1)} %copy-done.17, bf16[256,512]{1,0:T(8,128)(2,1)S(1)} %shard_map.140.latent_ref, bf16[512,4096]{1,0:T(8,128)(2,1)S(1)} %bitcast.27, bf16[256,512]{1,0:T(8,128)(2,1)S(1)} %collective-permute-done.1.refs_0_, bf16[4,3,32,256]{3,2,1,0:T(8,128)(2,1)S(1)} %collective-permute-done.6.refs_1_.w11), custom_call_target="tpu_custom_call" | custom-call | flops 540000000 | bytes 3145728 | tf_op jit(solution)/shard_map/pallas_call | solution.py:185
  60.7 2.8 %collective-permute-start.7 = (bf16[256,2048]{1,0:T(8,128)(2,1)}, bf16[256,2048]{1,0:T(8,128)(2,1)S(1)}, u32[]{:S(2)}, u32[]{:S(2)}) collective-permute-start(bf16[256,2048]{1,0:T(8,128)(2,1)} %shard_map.142), channel_id=1, source_target_pairs={{0,1},{1,0},{2,3},{3,2},{4,5},{5,4},{6,7},{7,6},{8,9},{9,8},{10,11... | collective-permute-start | bytes 3145736 | tf_op jit(solution)/shard_map/ppermute | solution.py:74
  63.5 2.0 %collective-permute-start.11 = (bf16[256,512]{1,0:T(8,128)(2,1)S(1)}, bf16[256,512]{1,0:T(8,128)(2,1)}, u32[]{:S(2)}, u32[]{:S(2)}) collective-permute-start(bf16[256,512]{1,0:T(8,128)(2,1)S(1)} %shard_map.140.latent_ref), channel_id=1, source_target_pairs={{0,16},{16,32},{32,48},{48,64},{64,80},{80,96},{96,112},{112,128},... | collective-permute-start | bytes 786440 | tf_op jit(solution)/shard_map/ppermute | solution.py:382
  65.5 2.5 %collective-permute-start.12 = (bf16[256,512]{1,0:T(8,128)(2,1)S(1)}, bf16[256,512]{1,0:T(8,128)(2,1)}, u32[]{:S(2)}, u32[]{:S(2)}) collective-permute-start(bf16[256,512]{1,0:T(8,128)(2,1)S(1)} %collective-permute-done.1.refs_0_), channel_id=1, source_target_pairs={{0,16},{16,32},{32,48},{48,64},{64,80},{80,96},{96,112},{112,128},... | collective-permute-start | bytes 786440 | tf_op jit(solution)/shard_map/ppermute | solution.py:385
  68.0 0.8 shard_map.145
  68.8 3.9 %all-to-all-start.1 = ((bf16[8,32,768]{2,1,0:T(8,128)(2,1)}), bf16[8,32,768]{2,1,0:T(8,128)(2,1)S(1)}, u32[]{:S(2)}, u32[]{:S(2)}) async-start(bf16[8,32,768]{2,1,0:T(8,128)(2,1)} %get-tuple-element.19), calls=%async_computation.1 | async-start | bytes 786432 | tf_op jit(solution)/shard_map/all_to_all | solution.py:392
  73.1 1.8 %collective-permute-start.8 = (bf16[2,256,512]{2,1,0:T(8,128)(2,1)S(1)}, bf16[2,256,512]{2,1,0:T(8,128)(2,1)S(1)}, u32[]{:S(2)}, u32[]{:S(2)}) collective-permute-start(bf16[2,256,512]{2,1,0:T(8,128)(2,1)S(1)} %pad_maximum_fusion.refs_0_), channel_id=1, source_target_pairs={{0,4},{4,8},{8,12},{12,0},{1,5},{5,9},{9,13},{13,1},{2,6},{6,10},{... | collective-permute-start | bytes 1572872 | tf_op jit(solution)/shard_map/ppermute | solution.py:78
  75.0 1.1 pad_maximum_fusion.1.refs_4_
  76.1 8.9 %collective-permute-start.14 = (bf16[2,256,512]{2,1,0:T(8,128)(2,1)S(1)}, bf16[2,256,512]{2,1,0:T(8,128)(2,1)}, u32[]{:S(2)}, u32[]{:S(2)}) collective-permute-start(bf16[2,256,512]{2,1,0:T(8,128)(2,1)S(1)} %pad_maximum_fusion.1.refs_4_), channel_id=1, source_target_pairs={{0,12},{4,0},{8,4},{12,8},{1,13},{5,1},{9,5},{13,9},{2,14},{6,2},{... | collective-permute-start | bytes 1572872 | tf_op jit(solution)/shard_map/ppermute | solution.py:78
  85.3 2.4 %collective-permute-start.19 = (bf16[256,768]{1,0:T(8,128)(2,1)S(1)}, bf16[256,768]{1,0:T(8,128)(2,1)S(1)}, u32[]{:S(2)}, u32[]{:S(2)}) collective-permute-start(bf16[256,768]{1,0:T(8,128)(2,1)S(1)} %bitcast.30), channel_id=1, source_target_pairs={{0,128},{128,0},{1,129},{129,1},{2,130},{130,2},{3,131},{131,3},{4... | collective-permute-start | bytes 1179656 | tf_op jit(solution)/shard_map/ppermute | solution.py:74
  87.6 10.4 %collective-permute-done.7.got_ref = bf16[256,2048]{1,0:T(8,128)(2,1)S(1)} collective-permute-done((bf16[256,2048]{1,0:T(8,128)(2,1)}, bf16[256,2048]{1,0:T(8,128)(2,1)S(1)}, u32[]{:S(2)}, u32[]{:S(2)}) %collective-permute-start.7) | collective-permute-done | bytes 1048608 | tf_op jit(solution)/shard_map/ppermute | solution.py:74
  98.0 2.2 %copy-done.1 = bf16[1,512,4096]{2,1,0:T(8,128)(2,1)S(1)} copy-done((bf16[1,512,4096]{2,1,0:T(8,128)(2,1)S(1)}, bf16[1,512,4096]{2,1,0:T(8,128)(2,1)}, u32[]{:S(2)}) %copy-start.1) | copy-done | bytes 4194328
  100.2 0.8 copy-done.11
  100.9 3.0 %shard_map.143 = (bf16[256,2048]{1,0:T(8,128)(2,1)}, f32[8,256]{1,0:T(8,128)S(1)}) custom-call(s32[7]{0:T(128)S(1)} %copy-done.17, bf16[256,512]{1,0:T(8,128)(2,1)S(1)} %shard_map.140.latent_ref, bf16[512,4096]{1,0:T(8,128)(2,1)S(1)} %bitcast.28, bf16[256,2048]{1,0:T(8,128)(2,1)S(1)} %collective-permute-done.7.got_ref, ...), custom_call_target="tpu_custom_call" | custom-call | flops 540000000 | bytes 5242880 | tf_op jit(solution)/shard_map/pallas_call | solution.py:224
  104.0 2.8 %collective-permute-start.21 = (f32[8,256]{1,0:T(8,128)S(1)}, f32[8,256]{1,0:T(8,128)S(1)}, u32[]{:S(2)}, u32[]{:S(2)}) collective-permute-start(f32[8,256]{1,0:T(8,128)S(1)} %get-tuple-element.21), channel_id=1, source_target_pairs={{0,1},{1,0},{2,3},{3,2},{4,5},{5,4},{6,7},{7,6},{8,9},{9,8},{10,11... | collective-permute-start | bytes 24584 | tf_op jit(solution)/shard_map/ppermute | solution.py:74
  106.8 2.3 %collective-permute-start.10 = (bf16[2,256,512]{2,1,0:T(8,128)(2,1)S(1)}, bf16[2,256,512]{2,1,0:T(8,128)(2,1)S(1)}, u32[]{:S(2)}, u32[]{:S(2)}) collective-permute-start(bf16[2,256,512]{2,1,0:T(8,128)(2,1)S(1)} %collective-permute-done.8.refs_1_), channel_id=1, source_target_pairs={{0,4},{4,8},{8,12},{12,0},{1,5},{5,9},{9,13},{13,1},{2,6},{6,10},{... | collective-permute-start | bytes 1572872 | tf_op jit(solution)/shard_map/ppermute | solution.py:78
  109.1 3.9 %collective-permute-start.15 = (bf16[2,256,512]{2,1,0:T(8,128)(2,1)}, bf16[2,256,512]{2,1,0:T(8,128)(2,1)S(1)}, u32[]{:S(2)}, u32[]{:S(2)}) collective-permute-start(bf16[2,256,512]{2,1,0:T(8,128)(2,1)} %collective-permute-done.14.refs_6_), channel_id=1, source_target_pairs={{0,12},{4,0},{8,4},{12,8},{1,13},{5,1},{9,5},{13,9},{2,14},{6,2},{... | collective-permute-start | bytes 1572872 | tf_op jit(solution)/shard_map/ppermute | solution.py:78
  113.0 1.3 collective-permute-start.22
  114.3 0.7 collective-permute-done.22
  115.0 4.7 %collective-permute-start.18 = (bf16[256,768]{1,0:T(8,128)(2,1)S(1)}, bf16[256,768]{1,0:T(8,128)(2,1)S(1)}, u32[]{:S(2)}, u32[]{:S(2)}) collective-permute-start(bf16[256,768]{1,0:T(8,128)(2,1)S(1)} %bitcast.31), channel_id=1, source_target_pairs={{0,2},{2,0},{1,3},{3,1},{4,6},{6,4},{5,7},{7,5},{8,10},{10,8},{9,1... | collective-permute-start | bytes 1179656 | tf_op jit(solution)/shard_map/ppermute | solution.py:74
  119.7 2.2 %collective-permute-done.13.refs_5_ = bf16[2,256,512]{2,1,0:T(8,128)(2,1)S(1)} collective-permute-done((bf16[2,256,512]{2,1,0:T(8,128)(2,1)S(1)}, bf16[2,256,512]{2,1,0:T(8,128)(2,1)S(1)}, u32[]{:S(2)}, u32[]{:S(2)}) %collective-permute-start.13) | collective-permute-done | bytes 524320 | tf_op jit(solution)/shard_map/ppermute | solution.py:78
  122.0 11.2 %collective-permute-done.10.refs_3_ = bf16[2,256,512]{2,1,0:T(8,128)(2,1)S(1)} collective-permute-done((bf16[2,256,512]{2,1,0:T(8,128)(2,1)S(1)}, bf16[2,256,512]{2,1,0:T(8,128)(2,1)S(1)}, u32[]{:S(2)}, u32[]{:S(2)}) %collective-permute-start.10) | collective-permute-done | bytes 524320 | tf_op jit(solution)/shard_map/ppermute | solution.py:78
  133.4 1.1 collective-permute-start.23
  134.4 2.7 %collective-permute-done.24.refs_16_ = f32[2,256]{1,0:T(2,128)S(1)} collective-permute-done((f32[2,256]{1,0:T(2,128)S(1)}, f32[2,256]{1,0:T(2,128)S(1)}, u32[]{:S(2)}, u32[]{:S(2)}) %collective-permute-start.24) | collective-permute-done | bytes 2080 | tf_op jit(solution)/shard_map/ppermute | solution.py:78
  137.2 3.4 %shard_map.146 = (bf16[8,256,256]{2,1,0:T(8,128)(2,1)S(1)}, bf16[4,256,256]{2,1,0:T(8,128)(2,1)S(1)}) custom-call(s32[7]{0:T(128)S(1)} %copy-done.17, bf16[2,256,512]{2,1,0:T(8,128)(2,1)S(1)} %pad_maximum_fusion.refs_0_, bf16[2,256,512]{2,1,0:T(8,128)(2,1)S(1)} %collective-permute-done.8.refs_1_, bf16[2,256,512]{2,1,0:T(8,128)(2,1)} %collective-permute-done.9.refs_2_, ...), custom_call_target="tpu_custom_call" | custom-call | flops 1600000000 | bytes 6291456 | tf_op jit(solution)/shard_map/pallas_call | solution.py:280
  140.6 0.8 copy-done.2
  141.4 4.0 %collective-permute-start.26 = (bf16[8,256,256]{2,1,0:T(8,128)(2,1)S(1)}, bf16[8,256,256]{2,1,0:T(8,128)(2,1)S(1)}, u32[]{:S(2)}, u32[]{:S(2)}) collective-permute-start(bf16[8,256,256]{2,1,0:T(8,128)(2,1)S(1)} %get-tuple-element.23.km_ref), channel_id=1, source_target_pairs={{0,2},{2,0},{1,3},{3,1},{4,6},{6,4},{5,7},{7,5},{8,10},{10,8},{9,1... | collective-permute-start | bytes 3145736 | tf_op jit(solution)/shard_map/ppermute | solution.py:74
  145.4 1.0 copy-done.5
  146.5 1.0 copy-done.7
  147.5 1.0 copy-done.9
  148.6 2.8 %shard_map.147.vm_ref = bf16[8,256,256]{2,1,0:T(8,128)(2,1)S(1)} custom-call(s32[7]{0:T(128)S(1)} %copy-done.17, bf16[2,256,512]{2,1,0:T(8,128)(2,1)S(1)} %copy-done.5, bf16[2,256,512]{2,1,0:T(8,128)(2,1)S(1)} %copy-done.9, bf16[2,256,512]{2,1,0:T(8,128)(2,1)} %collective-permute-done.9.refs_2_, bf16[2,256,512]{2,1,0:T(8,128)(2,1)S(1)} %collective-permute-done.10.refs_3_, ...), custom_call_target="tpu_custom_call" | custom-call | flops 1600000000 | bytes 6291456 | tf_op jit(solution)/shard_map/pallas_call | solution.py:280
  151.9 2.6 %collective-permute-done.27.vt_ref = bf16[8,256,256]{2,1,0:T(8,128)(2,1)} collective-permute-done((bf16[8,256,256]{2,1,0:T(8,128)(2,1)S(1)}, bf16[8,256,256]{2,1,0:T(8,128)(2,1)}, u32[]{:S(2)}, u32[]{:S(2)}) %collective-permute-start.27) | collective-permute-done | bytes 1048608 | tf_op jit(solution)/shard_map/ppermute | solution.py:74
  154.5 1.0 copy-done.3
  155.5 3.2 %shard_map.149 = bf16[1,256,256]{2,1,0:T(8,128)(2,1)S(1)} custom-call(s32[4]{0:T(128)S(1)} %get-tuple-element.27.place_ref, bf16[4,256,256]{2,1,0:T(8,128)(2,1)S(1)} %copy-done.3, bf16[8,256,256]{2,1,0:T(8,128)(2,1)S(1)} %get-tuple-element.23.km_ref, bf16[8,256,256]{2,1,0:T(8,128)(2,1)S(1)} %collective-permute-done.26.kt_ref, ...), custom_call_target="tpu_custom_call" | custom-call | flops 536870912 | bytes 5242880 | tf_op jit(solution)/shard_map/pallas_call | solution.py:321
  158.7 0.9 collective-permute-start.28
  159.6 3.2 %shard_map.150 = bf16[1,256,256]{2,1,0:T(8,128)(2,1)S(1)} custom-call(s32[4]{0:T(128)S(1)} %get-tuple-element.26.place_ref, bf16[4,256,256]{2,1,0:T(8,128)(2,1)S(1)} %copy-done.3, bf16[8,256,256]{2,1,0:T(8,128)(2,1)S(1)} %get-tuple-element.23.km_ref, bf16[8,256,256]{2,1,0:T(8,128)(2,1)S(1)} %collective-permute-done.26.kt_ref, ...), custom_call_target="tpu_custom_call" | custom-call | flops 536870912 | bytes 5242880 | tf_op jit(solution)/shard_map/pallas_call | solution.py:321
  162.8 1.9 %collective-permute-start.29 = (bf16[1,256,256]{2,1,0:T(8,128)(2,1)S(1)}, bf16[1,256,256]{2,1,0:T(8,128)(2,1)S(1)}, u32[]{:S(2)}, u32[]{:S(2)}) collective-permute-start(bf16[1,256,256]{2,1,0:T(8,128)(2,1)S(1)} %shard_map.150), channel_id=1, source_target_pairs={{0,8},{4,12},{8,0},{12,4},{1,9},{5,13},{9,1},{13,5},{2,10},{6,14},... | collective-permute-start | bytes 393224 | tf_op jit(solution)/shard_map/ppermute | solution.py:78
  164.7 3.2 %shard_map.151 = bf16[1,256,256]{2,1,0:T(8,128)(2,1)S(1)} custom-call(s32[4]{0:T(128)S(1)} %get-tuple-element.24.place_ref, bf16[4,256,256]{2,1,0:T(8,128)(2,1)S(1)} %copy-done.3, bf16[8,256,256]{2,1,0:T(8,128)(2,1)S(1)} %get-tuple-element.23.km_ref, bf16[8,256,256]{2,1,0:T(8,128)(2,1)S(1)} %collective-permute-done.26.kt_ref, ...), custom_call_target="tpu_custom_call" | custom-call | flops 536870912 | bytes 5242880 | tf_op jit(solution)/shard_map/pallas_call | solution.py:321
  167.9 1.2 collective-permute-start.30
  169.2 3.2 %shard_map.148.a_ref = bf16[1,256,256]{2,1,0:T(8,128)(2,1)S(1)} custom-call(s32[4]{0:T(128)S(1)} %get-tuple-element.28.place_ref, bf16[4,256,256]{2,1,0:T(8,128)(2,1)S(1)} %copy-done.3, bf16[8,256,256]{2,1,0:T(8,128)(2,1)S(1)} %get-tuple-element.23.km_ref, bf16[8,256,256]{2,1,0:T(8,128)(2,1)S(1)} %collective-permute-done.26.kt_ref, ...), custom_call_target="tpu_custom_call" | custom-call | flops 536870912 | bytes 5242880 | tf_op jit(solution)/shard_map/pallas_call | solution.py:321
  172.4 1.4 shard_map.152
  (79 shorter events, 2.1 us)
Async XLA Ops:
  1.2 26.1 %copy-start.10 = (f32[2,4096]{1,0:T(2,128)S(1)}, f32[2,4096]{1,0:T(2,128)}, u32[]{:S(2)}) copy-start(f32[2,4096]{1,0:T(2,128)} %t1.1) | copy-start | bytes 98308
  1.2 26.1 %copy-start.13 = (f32[4096]{0:T(1024)S(1)}, f32[4096]{0:T(1024)}, u32[]{:S(2)}) copy-start(f32[4096]{0:T(1024)} %param.20) | copy-start | bytes 49156
  1.2 26.1 %copy-start.17 = (s32[7]{0:T(128)S(1)}, s32[7]{0:T(128)}, u32[]{:S(2)}) copy-start(s32[7]{0:T(128)} %stack.75.at_ref) | copy-start | bytes 88
  1.2 37.1 %copy-start.18 = (bf16[1,512,512]{2,1,0:T(8,128)(2,1)S(1)}, bf16[1,512,512]{2,1,0:T(8,128)(2,1)}, u32[]{:S(2)}) copy-start(bf16[1,512,512]{2,1,0:T(8,128)(2,1)} %param.13) | copy-start | bytes 1572868
  1.2 40.8 %copy-start.20 = (bf16[1,3,512,256]{3,2,1,0:T(8,128)(2,1)S(1)}, bf16[1,3,512,256]{3,2,1,0:T(8,128)(2,1)}, u32[]{:S(2)}) copy-start(bf16[1,3,512,256]{3,2,1,0:T(8,128)(2,1)} %param.14) | copy-start | bytes 2359300
  1.2 40.8 %copy-start.21 = (bf16[1,256,512]{2,1,0:T(8,128)(2,1)S(1)}, bf16[1,256,512]{2,1,0:T(8,128)(2,1)}, u32[]{:S(2)}) copy-start(bf16[1,256,512]{2,1,0:T(8,128)(2,1)} %param.15) | copy-start | bytes 786436
  3.8 5.6 %collective-permute-start.2 = (bf16[3,32,256]{2,1,0:T(8,128)(2,1)}, bf16[3,32,256]{2,1,0:T(8,128)(2,1)S(1)}, u32[]{:S(2)}, u32[]{:S(2)}) collective-permute-start(bf16[3,32,256]{2,1,0:T(8,128)(2,1)} %get-tuple-element.14), channel_id=1, source_target_pairs={{0,4},{4,8},{8,12},{12,0},{1,5},{5,9},{9,13},{13,1},{2,6},{6,10},{... | collective-permute-start | bytes 147464 | tf_op jit(solution)/shard_map/ppermute | solution.py:78
  5.8 4.7 %collective-permute-start.3 = (bf16[3,32,256]{2,1,0:T(8,128)(2,1)}, bf16[3,32,256]{2,1,0:T(8,128)(2,1)S(1)}, u32[]{:S(2)}, u32[]{:S(2)}) collective-permute-start(bf16[3,32,256]{2,1,0:T(8,128)(2,1)} %get-tuple-element.15), channel_id=1, source_target_pairs={{0,8},{4,12},{8,0},{12,4},{1,9},{5,13},{9,1},{13,5},{2,10},{6,14},... | collective-permute-start | bytes 147464 | tf_op jit(solution)/shard_map/ppermute | solution.py:78
  8.3 3.4 %collective-permute-start.4 = (bf16[3,32,256]{2,1,0:T(8,128)(2,1)}, bf16[3,32,256]{2,1,0:T(8,128)(2,1)S(1)}, u32[]{:S(2)}, u32[]{:S(2)}) collective-permute-start(bf16[3,32,256]{2,1,0:T(8,128)(2,1)} %get-tuple-element.16), channel_id=1, source_target_pairs={{0,12},{4,0},{8,4},{12,8},{1,13},{5,1},{9,5},{13,9},{2,14},{6,2},{... | collective-permute-start | bytes 147464 | tf_op jit(solution)/shard_map/ppermute | solution.py:78
  12.5 4.6 %collective-permute-start.5 = (bf16[4,3,32,256]{3,2,1,0:T(8,128)(2,1)S(1)}, bf16[4,3,32,256]{3,2,1,0:T(8,128)(2,1)S(1)}, u32[]{:S(2)}, u32[]{:S(2)}) collective-permute-start(bf16[4,3,32,256]{3,2,1,0:T(8,128)(2,1)S(1)} %pad_maximum_fusion.2.w00), channel_id=1, source_target_pairs={{0,128},{128,0},{1,129},{129,1},{2,130},{130,2},{3,131},{131,3},{4... | collective-permute-start | bytes 589832 | tf_op jit(solution)/shard_map/ppermute | solution.py:74
  14.0 13.4 %collective-permute-start.16 = (bf16[4,3,32,256]{3,2,1,0:T(8,128)(2,1)S(1)}, bf16[4,3,32,256]{3,2,1,0:T(8,128)(2,1)S(1)}, u32[]{:S(2)}, u32[]{:S(2)}) collective-permute-start(bf16[4,3,32,256]{3,2,1,0:T(8,128)(2,1)S(1)} %pad_maximum_fusion.2.w00), channel_id=1, source_target_pairs={{0,2},{2,0},{1,3},{3,1},{4,6},{6,4},{5,7},{7,5},{8,10},{10,8},{9,1... | collective-permute-start | bytes 589832 | tf_op jit(solution)/shard_map/ppermute | solution.py:74
  17.2 10.2 %collective-permute-start.6 = (bf16[4,3,32,256]{3,2,1,0:T(8,128)(2,1)S(1)}, bf16[4,3,32,256]{3,2,1,0:T(8,128)(2,1)S(1)}, u32[]{:S(2)}, u32[]{:S(2)}) collective-permute-start(bf16[4,3,32,256]{3,2,1,0:T(8,128)(2,1)S(1)} %collective-permute-done.5.w10), channel_id=1, source_target_pairs={{0,2},{2,0},{1,3},{3,1},{4,6},{6,4},{5,7},{7,5},{8,10},{10,8},{9,1... | collective-permute-start | bytes 589832 | tf_op jit(solution)/shard_map/ppermute | solution.py:74
  20.5 6.8 %collective-permute-start.17 = (bf16[2,128,256]{2,1,0:T(8,128)(2,1)}, bf16[2,128,256]{2,1,0:T(8,128)(2,1)S(1)}, u32[]{:S(2)}, u32[]{:S(2)}) collective-permute-start(bf16[2,128,256]{2,1,0:T(8,128)(2,1)} %get-tuple-element.18.mine_ref), channel_id=1, source_target_pairs={{0,1},{1,0},{2,3},{3,2},{4,5},{5,4},{6,7},{7,6},{8,9},{9,8},{10,11... | collective-permute-start | bytes 393224 | tf_op jit(solution)/shard_map/ppermute | solution.py:74
  27.4 0.9 copy-start.12
  30.2 37.8 %all-to-all-start = ((bf16[8,32,896]{2,1,0:T(8,128)(2,1)}), bf16[8,32,896]{2,1,0:T(8,128)(2,1)S(1)}, u32[]{:S(2)}, u32[]{:S(2)}) async-start(bf16[8,32,896]{2,1,0:T(8,128)(2,1)} %shard_map.144), calls=%async_computation | async-start | bytes 917504 | tf_op jit(solution)/shard_map/all_to_all | solution.py:390
  38.3 3.8 %collective-permute-start = (bf16[8,512]{1,0:T(8,128)(2,1)S(1)}, bf16[8,512]{1,0:T(8,128)(2,1)S(1)}, u32[]{:S(2)}, u32[]{:S(2)}) collective-permute-start(bf16[8,512]{1,0:T(8,128)(2,1)S(1)} %slice_bitcast_fusion), channel_id=1, source_target_pairs={{0,2},{2,4},{4,6},{6,8},{8,10},{10,12},{12,14},{14,16},{16,18},{18... | collective-permute-start | bytes 24584 | tf_op jit(solution)/shard_map/ppermute | solution.py:371
  42.1 1.6 copy-start.19
  46.2 26.6 %copy-start.22 = (s32[2,32]{1,0:T(2,128)S(1)}, s32[2,32]{1,0:T(2,128)}, u32[]{:S(2)}) copy-start(s32[2,32]{1,0:T(2,128)} %param.18) | copy-start | bytes 772
  46.2 9.9 %collective-permute-start.1 = (bf16[256,512]{1,0:T(8,128)(2,1)S(1)}, bf16[256,512]{1,0:T(8,128)(2,1)S(1)}, u32[]{:S(2)}, u32[]{:S(2)}) collective-permute-start(bf16[256,512]{1,0:T(8,128)(2,1)S(1)} %shard_map.140.latent_ref), channel_id=1, source_target_pairs={{0,1},{1,0},{2,3},{3,2},{4,5},{5,4},{6,7},{7,6},{8,9},{9,8},{10,11... | collective-permute-start | bytes 786440 | tf_op jit(solution)/shard_map/ppermute | solution.py:74
  56.1 2.2 %copy-start = (bf16[1,512,4096]{2,1,0:T(8,128)(2,1)S(1)}, bf16[1,512,4096]{2,1,0:T(8,128)(2,1)}, u32[]{:S(2)}) copy-start(bf16[1,512,4096]{2,1,0:T(8,128)(2,1)} %param.17) | copy-start | bytes 12582916
  60.7 37.3 %collective-permute-start.7 = (bf16[256,2048]{1,0:T(8,128)(2,1)}, bf16[256,2048]{1,0:T(8,128)(2,1)S(1)}, u32[]{:S(2)}, u32[]{:S(2)}) collective-permute-start(bf16[256,2048]{1,0:T(8,128)(2,1)} %shard_map.142), channel_id=1, source_target_pairs={{0,1},{1,0},{2,3},{3,2},{4,5},{5,4},{6,7},{7,6},{8,9},{9,8},{10,11... | collective-permute-start | bytes 3145736 | tf_op jit(solution)/shard_map/ppermute | solution.py:74
  63.5 11.4 %collective-permute-start.11 = (bf16[256,512]{1,0:T(8,128)(2,1)S(1)}, bf16[256,512]{1,0:T(8,128)(2,1)}, u32[]{:S(2)}, u32[]{:S(2)}) collective-permute-start(bf16[256,512]{1,0:T(8,128)(2,1)S(1)} %shard_map.140.latent_ref), channel_id=1, source_target_pairs={{0,16},{16,32},{32,48},{48,64},{64,80},{80,96},{96,112},{112,128},... | collective-permute-start | bytes 786440 | tf_op jit(solution)/shard_map/ppermute | solution.py:382
  65.5 9.4 %collective-permute-start.12 = (bf16[256,512]{1,0:T(8,128)(2,1)S(1)}, bf16[256,512]{1,0:T(8,128)(2,1)}, u32[]{:S(2)}, u32[]{:S(2)}) collective-permute-start(bf16[256,512]{1,0:T(8,128)(2,1)S(1)} %collective-permute-done.1.refs_0_), channel_id=1, source_target_pairs={{0,16},{16,32},{32,48},{48,64},{64,80},{80,96},{96,112},{112,128},... | collective-permute-start | bytes 786440 | tf_op jit(solution)/shard_map/ppermute | solution.py:385
  68.8 4.2 %copy-start.14 = (f32[8,768]{1,0:T(8,128)}, f32[8,768]{1,0:T(8,128)S(1)}, u32[]{:S(2)}) copy-start(f32[8,768]{1,0:T(8,128)S(1)} %get-tuple-element.20.refs_12_) | copy-start | bytes 73732
  68.8 16.4 %all-to-all-start.1 = ((bf16[8,32,768]{2,1,0:T(8,128)(2,1)}), bf16[8,32,768]{2,1,0:T(8,128)(2,1)S(1)}, u32[]{:S(2)}, u32[]{:S(2)}) async-start(bf16[8,32,768]{2,1,0:T(8,128)(2,1)} %get-tuple-element.19), calls=%async_computation.1 | async-start | bytes 786432 | tf_op jit(solution)/shard_map/all_to_all | solution.py:392
  73.1 67.5 %copy-start.4 = (bf16[2,256,512]{2,1,0:T(8,128)(2,1)}, bf16[2,256,512]{2,1,0:T(8,128)(2,1)S(1)}, u32[]{:S(2)}) copy-start(bf16[2,256,512]{2,1,0:T(8,128)(2,1)S(1)} %pad_maximum_fusion.refs_0_) | copy-start | bytes 1572868
  73.1 33.7 %collective-permute-start.8 = (bf16[2,256,512]{2,1,0:T(8,128)(2,1)S(1)}, bf16[2,256,512]{2,1,0:T(8,128)(2,1)S(1)}, u32[]{:S(2)}, u32[]{:S(2)}) collective-permute-start(bf16[2,256,512]{2,1,0:T(8,128)(2,1)S(1)} %pad_maximum_fusion.refs_0_), channel_id=1, source_target_pairs={{0,4},{4,8},{8,12},{12,0},{1,5},{5,9},{9,13},{13,1},{2,6},{6,10},{... | collective-permute-start | bytes 1572872 | tf_op jit(solution)/shard_map/ppermute | solution.py:78
  74.9 62.2 %copy-start.15 = (f32[8,768]{1,0:T(8,128)S(1)}, f32[8,768]{1,0:T(8,128)}, u32[]{:S(2)}) copy-start(f32[8,768]{1,0:T(8,128)} %copy-done.14) | copy-start | bytes 73732
  76.0 64.5 %copy-start.6 = (bf16[2,256,512]{2,1,0:T(8,128)(2,1)}, bf16[2,256,512]{2,1,0:T(8,128)(2,1)S(1)}, u32[]{:S(2)}) copy-start(bf16[2,256,512]{2,1,0:T(8,128)(2,1)S(1)} %pad_maximum_fusion.1.refs_4_) | copy-start | bytes 1572868
  76.1 30.7 %collective-permute-start.14 = (bf16[2,256,512]{2,1,0:T(8,128)(2,1)S(1)}, bf16[2,256,512]{2,1,0:T(8,128)(2,1)}, u32[]{:S(2)}, u32[]{:S(2)}) collective-permute-start(bf16[2,256,512]{2,1,0:T(8,128)(2,1)S(1)} %pad_maximum_fusion.1.refs_4_), channel_id=1, source_target_pairs={{0,12},{4,0},{8,4},{12,8},{1,13},{5,1},{9,5},{13,9},{2,14},{6,2},{... | collective-permute-start | bytes 1572872 | tf_op jit(solution)/shard_map/ppermute | solution.py:78
  85.1 27.9 %collective-permute-start.9 = (bf16[2,256,512]{2,1,0:T(8,128)(2,1)S(1)}, bf16[2,256,512]{2,1,0:T(8,128)(2,1)}, u32[]{:S(2)}, u32[]{:S(2)}) collective-permute-start(bf16[2,256,512]{2,1,0:T(8,128)(2,1)S(1)} %pad_maximum_fusion.refs_0_), channel_id=1, source_target_pairs={{0,12},{4,0},{8,4},{12,8},{1,13},{5,1},{9,5},{13,9},{2,14},{6,2},{... | collective-permute-start | bytes 1572872 | tf_op jit(solution)/shard_map/ppermute | solution.py:78
  85.3 34.5 %collective-permute-start.19 = (bf16[256,768]{1,0:T(8,128)(2,1)S(1)}, bf16[256,768]{1,0:T(8,128)(2,1)S(1)}, u32[]{:S(2)}, u32[]{:S(2)}) collective-permute-start(bf16[256,768]{1,0:T(8,128)(2,1)S(1)} %bitcast.30), channel_id=1, source_target_pairs={{0,128},{128,0},{1,129},{129,1},{2,130},{130,2},{3,131},{131,3},{4... | collective-permute-start | bytes 1179656 | tf_op jit(solution)/shard_map/ppermute | solution.py:74
  98.0 2.2 %copy-start.1 = (bf16[1,512,4096]{2,1,0:T(8,128)(2,1)S(1)}, bf16[1,512,4096]{2,1,0:T(8,128)(2,1)}, u32[]{:S(2)}) copy-start(bf16[1,512,4096]{2,1,0:T(8,128)(2,1)} %param.17) | copy-start | bytes 12582916
  100.2 0.8 copy-start.11
  104.0 41.5 %copy-start.16 = (f32[8,768]{1,0:T(8,128)S(1)}, f32[8,768]{1,0:T(8,128)}, u32[]{:S(2)}) copy-start(f32[8,768]{1,0:T(8,128)} %copy-done.14) | copy-start | bytes 73732
  104.0 5.1 %collective-permute-start.21 = (f32[8,256]{1,0:T(8,128)S(1)}, f32[8,256]{1,0:T(8,128)S(1)}, u32[]{:S(2)}, u32[]{:S(2)}) collective-permute-start(f32[8,256]{1,0:T(8,128)S(1)} %get-tuple-element.21), channel_id=1, source_target_pairs={{0,1},{1,0},{2,3},{3,2},{4,5},{5,4},{6,7},{7,6},{8,9},{9,8},{10,11... | collective-permute-start | bytes 24584 | tf_op jit(solution)/shard_map/ppermute | solution.py:74
  106.8 33.8 %copy-start.8 = (bf16[2,256,512]{2,1,0:T(8,128)(2,1)}, bf16[2,256,512]{2,1,0:T(8,128)(2,1)S(1)}, u32[]{:S(2)}) copy-start(bf16[2,256,512]{2,1,0:T(8,128)(2,1)S(1)} %collective-permute-done.8.refs_1_) | copy-start | bytes 1572868
  106.8 15.2 %collective-permute-start.13 = (bf16[2,256,512]{2,1,0:T(8,128)(2,1)S(1)}, bf16[2,256,512]{2,1,0:T(8,128)(2,1)S(1)}, u32[]{:S(2)}, u32[]{:S(2)}) collective-permute-start(bf16[2,256,512]{2,1,0:T(8,128)(2,1)S(1)} %pad_maximum_fusion.1.refs_4_), channel_id=1, source_target_pairs={{0,4},{4,8},{8,12},{12,0},{1,5},{5,9},{9,13},{13,1},{2,6},{6,10},{... | collective-permute-start | bytes 1572872 | tf_op jit(solution)/shard_map/ppermute | solution.py:78
  106.8 26.4 %collective-permute-start.10 = (bf16[2,256,512]{2,1,0:T(8,128)(2,1)S(1)}, bf16[2,256,512]{2,1,0:T(8,128)(2,1)S(1)}, u32[]{:S(2)}, u32[]{:S(2)}) collective-permute-start(bf16[2,256,512]{2,1,0:T(8,128)(2,1)S(1)} %collective-permute-done.8.refs_1_), channel_id=1, source_target_pairs={{0,4},{4,8},{8,12},{12,0},{1,5},{5,9},{9,13},{13,1},{2,6},{6,10},{... | collective-permute-start | bytes 1572872 | tf_op jit(solution)/shard_map/ppermute | solution.py:78
  109.1 28.1 %collective-permute-start.15 = (bf16[2,256,512]{2,1,0:T(8,128)(2,1)}, bf16[2,256,512]{2,1,0:T(8,128)(2,1)S(1)}, u32[]{:S(2)}, u32[]{:S(2)}) collective-permute-start(bf16[2,256,512]{2,1,0:T(8,128)(2,1)} %collective-permute-done.14.refs_6_), channel_id=1, source_target_pairs={{0,12},{4,0},{8,4},{12,8},{1,13},{5,1},{9,5},{13,9},{2,14},{6,2},{... | collective-permute-start | bytes 1572872 | tf_op jit(solution)/shard_map/ppermute | solution.py:78
  113.0 2.0 %collective-permute-start.22 = (f32[1,256]{1,0:T(1,128)S(1)}, f32[1,256]{1,0:T(1,128)S(1)}, u32[]{:S(2)}, u32[]{:S(2)}) collective-permute-start(f32[1,256]{1,0:T(1,128)S(1)} %add_rsqrt_fusion), channel_id=1, source_target_pairs={{0,16},{16,32},{32,48},{48,64},{64,80},{80,96},{96,112},{112,128},... | collective-permute-start | bytes 3080 | tf_op jit(solution)/shard_map/ppermute | solution.py:407
  115.0 22.1 %collective-permute-start.18 = (bf16[256,768]{1,0:T(8,128)(2,1)S(1)}, bf16[256,768]{1,0:T(8,128)(2,1)S(1)}, u32[]{:S(2)}, u32[]{:S(2)}) collective-permute-start(bf16[256,768]{1,0:T(8,128)(2,1)S(1)} %bitcast.31), channel_id=1, source_target_pairs={{0,2},{2,0},{1,3},{3,1},{4,6},{6,4},{5,7},{7,5},{8,10},{10,8},{9,1... | collective-permute-start | bytes 1179656 | tf_op jit(solution)/shard_map/ppermute | solution.py:74
  119.7 17.4 %collective-permute-start.20 = (bf16[256,768]{1,0:T(8,128)(2,1)S(1)}, bf16[256,768]{1,0:T(8,128)(2,1)S(1)}, u32[]{:S(2)}, u32[]{:S(2)}) collective-permute-start(bf16[256,768]{1,0:T(8,128)(2,1)S(1)} %collective-permute-done.19.refs_10_), channel_id=1, source_target_pairs={{0,2},{2,0},{1,3},{3,1},{4,6},{6,4},{5,7},{7,5},{8,10},{10,8},{9,1... | collective-permute-start | bytes 1179656 | tf_op jit(solution)/shard_map/ppermute | solution.py:74
  122.0 11.4 %collective-permute-start.25 = (f32[2,256]{1,0:T(2,128)S(1)}, f32[2,256]{1,0:T(2,128)S(1)}, u32[]{:S(2)}, u32[]{:S(2)}) collective-permute-start(f32[2,256]{1,0:T(2,128)S(1)} %pad_maximum_fusion.3.refs_14_), channel_id=1, source_target_pairs={{0,4},{4,8},{8,12},{12,0},{1,5},{5,9},{9,13},{13,1},{2,6},{6,10},{... | collective-permute-start | bytes 6152 | tf_op jit(solution)/shard_map/ppermute | solution.py:78
  133.2 3.9 %collective-permute-start.24 = (f32[2,256]{1,0:T(2,128)S(1)}, f32[2,256]{1,0:T(2,128)S(1)}, u32[]{:S(2)}, u32[]{:S(2)}) collective-permute-start(f32[2,256]{1,0:T(2,128)S(1)} %pad_maximum_fusion.3.refs_14_), channel_id=1, source_target_pairs={{0,8},{4,12},{8,0},{12,4},{1,9},{5,13},{9,1},{13,5},{2,10},{6,14},... | collective-permute-start | bytes 6152 | tf_op jit(solution)/shard_map/ppermute | solution.py:78
  133.4 3.8 %collective-permute-start.23 = (f32[2,256]{1,0:T(2,128)S(1)}, f32[2,256]{1,0:T(2,128)S(1)}, u32[]{:S(2)}, u32[]{:S(2)}) collective-permute-start(f32[2,256]{1,0:T(2,128)S(1)} %pad_maximum_fusion.3.refs_14_), channel_id=1, source_target_pairs={{0,12},{4,0},{8,4},{12,8},{1,13},{5,1},{9,5},{13,9},{2,14},{6,2},{... | collective-permute-start | bytes 6152 | tf_op jit(solution)/shard_map/ppermute | solution.py:78
  140.6 0.8 copy-start.2
  141.4 10.5 %collective-permute-start.26 = (bf16[8,256,256]{2,1,0:T(8,128)(2,1)S(1)}, bf16[8,256,256]{2,1,0:T(8,128)(2,1)S(1)}, u32[]{:S(2)}, u32[]{:S(2)}) collective-permute-start(bf16[8,256,256]{2,1,0:T(8,128)(2,1)S(1)} %get-tuple-element.23.km_ref), channel_id=1, source_target_pairs={{0,2},{2,0},{1,3},{3,1},{4,6},{6,4},{5,7},{7,5},{8,10},{10,8},{9,1... | collective-permute-start | bytes 3145736 | tf_op jit(solution)/shard_map/ppermute | solution.py:74
  145.4 1.0 copy-start.5
  146.5 1.0 copy-start.7
  147.5 1.0 copy-start.9
  151.4 3.1 %collective-permute-start.27 = (bf16[8,256,256]{2,1,0:T(8,128)(2,1)S(1)}, bf16[8,256,256]{2,1,0:T(8,128)(2,1)}, u32[]{:S(2)}, u32[]{:S(2)}) collective-permute-start(bf16[8,256,256]{2,1,0:T(8,128)(2,1)S(1)} %shard_map.147.vm_ref), channel_id=1, source_target_pairs={{0,2},{2,0},{1,3},{3,1},{4,6},{6,4},{5,7},{7,5},{8,10},{10,8},{9,1... | collective-permute-start | bytes 3145736 | tf_op jit(solution)/shard_map/ppermute | solution.py:74
  154.5 1.0 copy-start.3
  158.7 13.7 %collective-permute-start.28 = (bf16[1,256,256]{2,1,0:T(8,128)(2,1)S(1)}, bf16[1,256,256]{2,1,0:T(8,128)(2,1)S(1)}, u32[]{:S(2)}, u32[]{:S(2)}) collective-permute-start(bf16[1,256,256]{2,1,0:T(8,128)(2,1)S(1)} %shard_map.149), channel_id=1, source_target_pairs={{0,4},{4,8},{8,12},{12,0},{1,5},{5,9},{9,13},{13,1},{2,6},{6,10},{... | collective-permute-start | bytes 393224 | tf_op jit(solution)/shard_map/ppermute | solution.py:78
  162.8 9.6 %collective-permute-start.29 = (bf16[1,256,256]{2,1,0:T(8,128)(2,1)S(1)}, bf16[1,256,256]{2,1,0:T(8,128)(2,1)S(1)}, u32[]{:S(2)}, u32[]{:S(2)}) collective-permute-start(bf16[1,256,256]{2,1,0:T(8,128)(2,1)S(1)} %shard_map.150), channel_id=1, source_target_pairs={{0,8},{4,12},{8,0},{12,4},{1,9},{5,13},{9,1},{13,5},{2,10},{6,14},... | collective-permute-start | bytes 393224 | tf_op jit(solution)/shard_map/ppermute | solution.py:78
  167.9 4.5 %collective-permute-start.30 = (bf16[1,256,256]{2,1,0:T(8,128)(2,1)S(1)}, bf16[1,256,256]{2,1,0:T(8,128)(2,1)S(1)}, u32[]{:S(2)}, u32[]{:S(2)}) collective-permute-start(bf16[1,256,256]{2,1,0:T(8,128)(2,1)S(1)} %shard_map.151), channel_id=1, source_target_pairs={{0,12},{4,0},{8,4},{12,8},{1,13},{5,1},{9,5},{13,9},{2,14},{6,2},{... | collective-permute-start | bytes 393224 | tf_op jit(solution)/shard_map/ppermute | solution.py:78

commit v4 on v3

--- a/solution.py
+++ b/solution.py
@@ -105,7 +105,27 @@
     )(at, w, embed, embed)
 
 
-def partial_kernel(at_ref, w00, w01, w10, w11, mine_ref, rest_ref, g0, g1, t0, t1, out_ref, w_ref):
+def unused(after):
+    return [pl.BlockSpec(memory_space=pl.ANY)] * len(after)
+
+
+def stack_kernel(n, *refs):
+    for i in range(n):
+        refs[-1][i] = refs[i][...]
+
+
+def stack(parts, after=()):
+    return pl.pallas_call(
+        functools.partial(stack_kernel, len(parts)),
+        in_specs=in_vmem(len(parts)) + unused(after),
+        out_specs=pl.BlockSpec(memory_space=pltpu.VMEM),
+        out_shape=jax.ShapeDtypeStruct((len(parts),) + parts[0].shape, parts[0].dtype),
+        compiler_params=params(4),
+    )(*parts, *after)
+
+
+def partial_kernel(at_ref, w00, w01, w10, w11, mine_ref, rest_ref, g0, g1, t0, t1, *refs):
+    out_ref, w_ref = refs[-2:]
     x, core = at_ref[3], at_ref[4]
     for y, pair in enumerate(((w00, w01), (w10, w11))):
         for c, ref in enumerate(pair):
@@ -135,7 +155,7 @@
         out_ref[i, :, 768:896] = tail
 
 
-def partial_weights(at, ws, mine, rest, gain, table):
+def partial_weights(at, ws, mine, rest, gain, table, after):
     whole = lambda shape: pl.BlockSpec(shape, lambda i, at: (0,) * len(shape))
     here = lambda rows, k: pl.BlockSpec((rows, 256), lambda i, at: (0, at[k]))
     return pl.pallas_call(
@@ -145,17 +165,19 @@
             grid=(1,),
             in_specs=[whole((4, 3, 32, 256))] * 4
             + [whole((2, 128, 256))] * 2
-            + [here(1, 0), here(1, 1), here(2, 0), here(2, 1)],
+            + [here(1, 0), here(1, 1), here(2, 0), here(2, 1)]
+            + unused(after),
             out_specs=whole((8, 32, 896)),
             scratch_shapes=[pltpu.VMEM((2, 256, 768), BF)],
         ),
         out_shape=jax.ShapeDtypeStruct((8, 32, 896), BF),
         compiler_params=params(16),
         cost_estimate=pl.CostEstimate(flops=210000000, bytes_accessed=2 << 20, transcendentals=0),
-    )(at, *ws, mine, rest, gain, gain, table, table)
-
-
-def sum_kernel(p_ref, m_ref, line_ref):
+    )(at, *ws, mine, rest, gain, gain, table, table, *after)
+
+
+def sum_kernel(p_ref, *refs):
+    m_ref, line_ref = refs[-2:]
     total = jnp.sum(p_ref[...].astype(F32), axis=0)
     m = total[:, :768].astype(BF)
     for i in range(8):
@@ -167,14 +189,14 @@
             line_ref[s : s + 1, k * 128 : (k + 1) * 128] = both[s * 6 + k : s * 6 + k + 1]
 
 
-def sum_weights(packed):
+def sum_weights(packed, after):
     return pl.pallas_call(
         sum_kernel,
-        in_specs=in_vmem(1),
+        in_specs=in_vmem(1) + unused(after),
         out_specs=in_vmem(2),
         out_shape=[jax.ShapeDtypeStruct((8, 32, 768), BF), jax.ShapeDtypeStruct((8, 768), F32)],
         compiler_params=params(8),
-    )(packed)
+    )(packed, *after)
 
 
 def give_kernel(at_ref, latent_ref, embed_ref, *refs):
@@ -191,7 +213,7 @@
                 pl.BlockSpec((BLOCK, CH), lambda i, at: (0, 0)),
                 pl.BlockSpec((CH, 1024), lambda i, at: (0, (1 - at[5]) * 2 + i)),
             ]
-            + [pl.BlockSpec(memory_space=pl.ANY)] * len(after),
+            + unused(after),
             out_specs=pl.BlockSpec((BLOCK, 1024), lambda i, at: (0, i)),
         ),
         out_shape=jax.ShapeDtypeStruct((BLOCK, D // 2), BF),
@@ -241,94 +263,91 @@
     )(at, latent, embed, got, active, table)
 
 
-def project_kernel(with_q, at_ref, *refs):
-    (a, al, ar, af, b, bl, br, bf, m00, m01, m10, m11, line_ref, active_ref, s0, s1, s2, s3) = refs[:18]
-    outs, m_ref = refs[18:-1], refs[-1]
-    x, core, yl = at_ref[3], at_ref[4], at_ref[6]
-    lanes = slice(0, 512) if with_q else slice(512, 768)
+def project_rows(row, blocks, m_ref, line_ref, active_ref, scales, at_ref, kv_ref, q_ref):
+    x = at_ref[3]
+    cols = slice(0, 768) if q_ref is not None else slice(256, 768)
+    w0, w1 = m_ref[0:512, cols], m_ref[512:1024, cols]
+    line = line_ref[:, cols]
+    for dx in range(4):
+        at = lax.rem(x + dx, 4)
+        act = active_ref[:, pl.ds(4 * row + at, 1), :].reshape(2, BLOCK)
+        side = jnp.concatenate([act, scales[dx][row : row + 1, :], jnp.zeros((5, BLOCK), F32)], axis=0).T
+        acc = dot(blocks[dx][0], w0) + dot(blocks[dx][1], w1)
+        acc = (acc + side[:, 0:1] * line[0:1] + side[:, 1:2] * line[1:2]) * side[:, 2:3]
+        kv_ref[at] = acc[:, -512:].astype(BF)
+        if q_ref is not None:
+            q_ref[at] = (acc[:, :256] * (HD**-0.5 * LOG2E)).astype(BF)
+
+
+def project_own_kernel(at_ref, a, al, ar, af, m00, m01, m10, m11, line_ref, active_ref, s0, s1, s2, s3, kv_ref, q_ref, m_ref):
+    core, yl = at_ref[4], at_ref[6]
     for y, pair in enumerate(((m00, m01), (m10, m11))):
         for c, ref in enumerate(pair):
             row = ((yl ^ y) * 2 + (core ^ c)) * 128
             for s in range(2):
-                m_ref[pl.ds(pl.multiple_of(s * 512 + row, 128), 128), :] = ref[s * 128 : (s + 1) * 128, lanes]
-    own = (a, ar, af, al)
-    prev = (b, br, bf, bl)
-    scales = (s0, s1, s2, s3)
-    jobs = [(0, outs[1], 0), (1, outs[0], 1)] if with_q else [(2, outs[0], 1)]
-    for r, blocks in ((1, own), (0, prev)):
-        for dx in range(4):
-            at = lax.rem(x + dx, 4)
-            m = 4 * r + at
-            act = active_ref[:, pl.ds(m, 1), :].reshape(2, BLOCK)
-            side = jnp.concatenate([act, scales[dx][r : r + 1, :], jnp.zeros((5, BLOCK), F32)], axis=0).T
-            rows = blocks[dx]
-            for j, out, both in jobs:
-                if not both and r == 0:
-                    continue
-                at_j = j * 256 - lanes.start
-                line = line_ref[:, j * 256 : (j + 1) * 256]
-                acc = dot(rows[0], m_ref[0:512, at_j : at_j + 256]) + dot(rows[1], m_ref[512:1024, at_j : at_j + 256])
-                acc = acc + side[:, 0:1] * line[0:1] + side[:, 1:2] * line[1:2]
-                acc = acc * (side[:, 2:3] * (HD**-0.5 * LOG2E if j == 0 else 1.0))
-                out[m if both else at] = acc.astype(BF)
-
-
-def project(with_q, at, pieces, ms, lines, active, scales):
-    shapes = [jax.ShapeDtypeStruct((8, BLOCK, 256), BF)]
-    if with_q:
-        shapes.append(jax.ShapeDtypeStruct((4, BLOCK, 256), BF))
-    return pl.pallas_call(
-        functools.partial(project_kernel, with_q),
-        in_specs=[pl.BlockSpec(memory_space=pltpu.SMEM)] + in_vmem(18),
-        out_specs=in_vmem(len(shapes)),
-        out_shape=shapes,
-        scratch_shapes=[pltpu.VMEM((1024, 512 if with_q else 256), BF)],
-        compiler_params=params(20),
+                m_ref[pl.ds(pl.multiple_of(s * 512 + row, 128), 128), :] = ref[s * 128 : (s + 1) * 128, :]
+    project_rows(1, (a, ar, af, al), m_ref, line_ref, active_ref, (s0, s1, s2, s3), at_ref, kv_ref, q_ref)
+
+
+def project_prev_kernel(at_ref, b, bl, br, bf, m_ref, line_ref, active_ref, s0, s1, s2, s3, kv_ref):
+    project_rows(0, (b, br, bf, bl), m_ref, line_ref, active_ref, (s0, s1, s2, s3), at_ref, kv_ref, None)
+
+
+def project(kernel, outs, *args):
+    return pl.pallas_call(
+        kernel,
+        in_specs=[pl.BlockSpec(memory_space=pltpu.SMEM)] + in_vmem(len(args) - 1),
+        out_specs=in_vmem(len(outs)),
+        out_shape=[jax.ShapeDtypeStruct(o, BF) for o in outs],
+        compiler_params=params(16),
         cost_estimate=pl.CostEstimate(flops=1600000000, bytes_accessed=6 << 20, transcendentals=0),
-    )(at, *pieces, *ms, lines, active, *scales)
-
-
-def attention_kernel(place_ref, q_ref, km_ref, kt_ref, vm_ref, vt_ref, o_ref):
-    at = lax.rem(place_ref[0] + place_ref[3 + pl.program_id(0)], 4)
+    )(*args)
+
+
+def attention_kernel(place_ref, q_ref, om_ref, ot_ref, pm_ref, pt_ref, o_ref):
+    at = lax.rem(place_ref[0] + place_ref[3], 4)
     core = place_ref[1]
     first = place_ref[2]
-    rows = lax.broadcasted_iota(jnp.int32, (BLOCK, 1024), 0)
-    cols = lax.broadcasted_iota(jnp.int32, (BLOCK, 1024), 1)
-    least_m = jnp.where(first == 1, (3 - at) * BLOCK, 0)
-    least_t = jnp.where(first == 1, (4 - at - core) * BLOCK, 0)
-    bias_m = jnp.where((cols - 768 <= rows) & (cols >= least_m), 0.0, -1e30)
-    bias_t = jnp.where((cols > rows) & (cols >= least_t), 0.0, -1e30)
+    rows = lax.broadcasted_iota(jnp.int32, (BLOCK, BLOCK), 0)
+    cols = lax.broadcasted_iota(jnp.int32, (BLOCK, BLOCK), 1)
+    blocks = []
+    for own_ref, prev_ref, begin in ((om_ref, pm_ref, at + 1), (ot_ref, pt_ref, at + core)):
+        for j in range(4):
+            m = begin + j
+            i = lax.rem(m, 4)
+            blocks.append((jnp.where(m >= 4, own_ref[i], prev_ref[i]), jnp.where((m < 4) & (first == 1), 1e30, 0.0)))
     contract = (((1,), (1,)), ((), ()))
     for h in range(2):
-        lanes = slice(h * HD, (h + 1) * HD)
-        q = q_ref[at, :, lanes]
-        km = km_ref[pl.ds(at + 1, 4), :, lanes].reshape(1024, HD)
-        kt = kt_ref[pl.ds(at + core, 4), :, lanes].reshape(1024, HD)
-        sm = lax.dot_general(q, km, contract, preferred_element_type=F32) + bias_m
-        st = lax.dot_general(q, kt, contract, preferred_element_type=F32) + bias_t
-        top = jnp.maximum(jnp.max(sm, axis=1, keepdims=True), jnp.max(st, axis=1, keepdims=True))
-        pm = jnp.exp2(sm - top)
-        pt = jnp.exp2(st - top)
-        total = jnp.sum(pm, axis=1, keepdims=True) + jnp.sum(pt, axis=1, keepdims=True)
-        vm = vm_ref[pl.ds(at + 1, 4), :, lanes].reshape(1024, HD)
-        vt = vt_ref[pl.ds(at + core, 4), :, lanes].reshape(1024, HD)
-        o = dot(pm.astype(BF), vm) + dot(pt.astype(BF), vt)
-        o_ref[0, :, lanes] = (o / total).astype(BF)
-
-
-def attention(place, offsets, q, km, kt, vm, vt):
-    n = len(offsets)
+        q = q_ref[at, :, h * HD : (h + 1) * HD]
+        scores = []
+        top = None
+        for n, (kv, penalty) in enumerate(blocks):
+            s = lax.dot_general(q, kv[:, h * HD : (h + 1) * HD], contract, preferred_element_type=F32)
+            if n == 3:
+                s = jnp.where(cols <= rows, s, -1e30)
+            if n == 4:
+                s = jnp.where(cols > rows, s, -1e30)
+            most = jnp.max(s, axis=1, keepdims=True) - penalty
+            top = most if top is None else jnp.maximum(top, most)
+            scores.append(s)
+        total = jnp.zeros((BLOCK, 1), F32)
+        o = jnp.zeros((BLOCK, HD), F32)
+        for s, (kv, penalty) in zip(scores, blocks):
+            p = jnp.exp2(s - (top + penalty))
+            total += jnp.sum(p, axis=1, keepdims=True)
+            o += dot(p.astype(BF), kv[:, 256 + h * HD : 256 + (h + 1) * HD])
+        o_ref[0, :, h * HD : (h + 1) * HD] = (o / total).astype(BF)
+
+
+def attention(place, dx, *args):
     return pl.pallas_call(
         attention_kernel,
-        grid=(n,),
         in_specs=[pl.BlockSpec(memory_space=pltpu.SMEM)] + in_vmem(5),
-        out_specs=pl.BlockSpec((1, BLOCK, 256), lambda i: (i, 0, 0)),
-        out_shape=jax.ShapeDtypeStruct((n, BLOCK, 256), BF),
-        compiler_params=params(20),
-        cost_estimate=pl.CostEstimate(
-            flops=n * 8 * BLOCK * 2048 * HD, bytes_accessed=5 << 20, transcendentals=n * 2 * BLOCK * 2048
-        ),
-    )(jnp.concatenate([place, jnp.array(offsets, jnp.int32)]), q, km, kt, vm, vt)
+        out_specs=pl.BlockSpec(memory_space=pltpu.VMEM),
+        out_shape=jax.ShapeDtypeStruct((1, BLOCK, 256), BF),
+        compiler_params=params(16),
+        cost_estimate=pl.CostEstimate(flops=8 * BLOCK * 2048 * HD, bytes_accessed=5 << 20, transcendentals=2 * BLOCK * 2048),
+    )(jnp.concatenate([place, jnp.array([dx], jnp.int32)]), *args)
 
 
 def collect_kernel(place_ref, a_ref, b_ref, c_ref, d_ref, o_ref):
@@ -371,24 +390,25 @@
     halo = lax.ppermute(audio[-8:], CTX, [(i, i + 1) for i in range(127)])
     embed = stream_embed[0]
     *chunks, mine = split(at, qkv_weight, embed)
-    w00 = jnp.stack([chunks[0]] + [shift(chunks[dx], dx) for dx in (1, 2, 3)])
+    arrived = [shift(chunks[dx], dx) for dx in (1, 2, 3)]
     rest = swap(mine, "tp")
+
+    latent = encoder(halo, audio, res_conv[0], res_out[0], down_conv[0])
+    other = swap(latent, "tp")
+    a = stack([latent, other])
+    al, ar = shift(a, 1), shift(a, 3)
+    b = stack([lax.ppermute(latent, ("yl", "z"), behind), lax.ppermute(other, ("yl", "z"), behind)])
+    bl, br = shift(b, 1), shift(b, 3)
+    af, bf = shift(al, 1), shift(br, 3)
+
+    w00 = stack([chunks[0]] + arrived, (latent, rest))
     w10 = swap(w00, "yl")
     w01 = swap(w00, "c")
     w11 = swap(w10, "c")
-
-    latent = encoder(halo, audio, res_conv[0], res_out[0], down_conv[0])
-    other = swap(latent, "tp")
-    prev = lax.ppermute(latent, ("yl", "z"), behind)
-    a = jnp.stack([latent, other])
-    al, ar = shift(a, 1), shift(a, 3)
-    b = jnp.stack([prev, lax.ppermute(other, ("yl", "z"), behind)])
-    bl, br = shift(b, 1), shift(b, 3)
-    pieces = (a, al, ar, shift(al, 1), b, bl, br, shift(br, 3))
-
-    packed = partial_weights(at, (w00, w01, w10, w11), mine, rest, norm_gain[None], speaker_table)
+    packed = partial_weights(at, (w00, w01, w10, w11), mine, rest, norm_gain[None], speaker_table, (a,))
     packed = lax.all_to_all(packed, "z", 0, 0, tiled=True)
-    m, lines = sum_weights(packed)
+    give = give_term(at, latent, embed, (b,))
+    m, lines = sum_weights(packed, (al, ar, give))
     m00 = lax.all_to_all(m, "z", 0, 0, tiled=True).reshape(256, 768)
     m10 = swap(m00, "yl")
     m01 = swap(m00, "c")
@@ -400,23 +420,24 @@
     turn = jnp.sum((bounds[:, :, None, None] <= frames[None, None]).astype(jnp.int32), axis=1)
     active = (turn % 2 == 1).astype(F32)
 
-    got = swap(give_term(at, latent, embed, (other, w11)), "tp")
+    got = swap(give, "tp")
     embedded, square = embed_rows(at, latent, embed, got, active, speaker_table)
     square = square + swap(square, "tp")
     scale = lax.rsqrt(square[0:1] * (1.0 / D) + 1e-05)
     scale = jnp.concatenate([lax.ppermute(scale, ("yl", "z"), behind), scale])
     scales = [scale] + [shift(scale, 4 - dx) for dx in (1, 2, 3)]
 
-    ms = (m00, m01, m10, m11)
-    km, q = project(True, at, pieces, ms, lines, active, scales)
-    kt = swap(km, "c")
-    (vm,) = project(False, at, pieces, ms, lines, active, scales)
-    vt = swap(vm, "c")
+    kv, half = (4, BLOCK, 512), (4, BLOCK, 256)
+    side = (active, *scales)
+    om, q, whole = project(project_own_kernel, (kv, half, (1024, 768)), at, a, al, ar, af, m00, m01, m10, m11, lines, *side)
+    ot = swap(om, "c")
+    (pm,) = project(project_prev_kernel, (kv,), at, b, bl, br, bf, whole, lines, *side)
+    pt = swap(pm, "c")
 
     place = jnp.stack([x_at, core, (row == 0).astype(jnp.int32)]).astype(jnp.int32)
     parts = [None] * 4
     for dx in (2, 1, 3, 0):
-        part = attention(place, (dx,), q, km, kt, vm, vt)
+        part = attention(place, dx, q, om, ot, pm, pt)
         parts[dx] = shift(part, dx) if dx else part
     return embedded, collect(place, parts)
 

time: 175 us -> 167 us (0.954)
  the two profiles are of different devices: /device:TPU:1 before, /device:TPU:8 now
where the time goes in v4:
time: 167 us; the launch traced here: 165 us
  waiting for transfers between devices  69.6 us (42%)
  starting transfers between devices  50.3 us (30%)
  Pallas kernels  32.3 us (19%)
  local copies, waits for them, and re-layouts  11.4 us (7%)
    ppermute x15, starting transfers between devices, shift(): return lax.ppermute(a, 'x', [(i, (i + by) % 4) for i in range(4)])  20.4 us
    ppermute x15, waiting for transfers between devices, shift(): return lax.ppermute(a, 'x', [(i, (i + by) % 4) for i in range(4)])  19.5 us
    ppermute x12, waiting for transfers between devices, swap(): return lax.ppermute(a, axis, SWAP)  15.8 us
    pallas_call x4, Pallas kernels, attention(): pl.pallas_call(attention_kernel, in_specs=[pl.BlockSpec(memory_space=pltp...  12.2 us
    all_to_all x1, waiting for transfers between devices, on_device(): m00 = lax.all_to_all(m, 'z', 0, 0, tiled=True).reshape(256, 768)  11.8 us
    unnamed x42, local copies, waits for them, and re-layouts  10.7 us
    ppermute x1, waiting for transfers between devices, on_device(): lax.ppermute(latent, ('yl', 'z'), behind)  10.3 us
    all_to_all x1, starting transfers between devices, on_device(): packed = lax.all_to_all(packed, 'z', 0, 0, tiled=True)  7.65 us
  transfers between devices with their start and end apart: 33, of which 16 were waited for; matrix products, arithmetic and copies ran while one was open for 1% of the time, Pallas kernels for 13%

profile of v4, /device:TPU:8, one launch (start us, length us, event | category | flops | bytes accessed | tf_op | source)
XLA Modules:
  0.0 165.5 jit_solution(5458437647655621933)
XLA Ops:
  0.6 0.6 stack.42.at_ref
  1.3 2.5 %shard_map.145 = (bf16[3,32,256]{2,1,0:T(8,128)(2,1)}, bf16[3,32,256]{2,1,0:T(8,128)(2,1)}, bf16[3,32,256]{2,1,0:T(8,128)(2,1)}, bf16[3,32,256]{2,1,0:T(8,128)(2,1)}, bf16[2,128,256]{2,1,0:T(8,128)(2,1)}) custom-call(s32[7]{0:T(128)} %stack.42.at_ref, bf16[3,32,1024]{2,1,0:T(8,128)(2,1)} %w_ref.1, bf16[512,4096]{1,0:T(8,128)(2,1)} %bitcast.17, ...), custom_call_target="tpu_custom_call" | custom-call | tf_op jit(solution)/shard_map/pallas_call | solution.py:92
  3.8 2.3 %collective-permute-start.11 = (bf16[2,128,256]{2,1,0:T(8,128)(2,1)}, bf16[2,128,256]{2,1,0:T(8,128)(2,1)S(1)}, u32[]{:S(2)}, u32[]{:S(2)}) collective-permute-start(bf16[2,128,256]{2,1,0:T(8,128)(2,1)} %get-tuple-element.19.mine_ref), channel_id=1, source_target_pairs={{0,1},{1,0},{2,3},{3,2},{4,5},{5,4},{6,7},{7,6},{8,9},{9,8},{10,11... | collective-permute-start | bytes 393224 | tf_op jit(solution)/shard_map/ppermute | solution.py:74
  6.1 1.9 %collective-permute-start = (bf16[8,512]{1,0:T(8,128)(2,1)S(1)}, bf16[8,512]{1,0:T(8,128)(2,1)S(1)}, u32[]{:S(2)}, u32[]{:S(2)}) collective-permute-start(bf16[8,512]{1,0:T(8,128)(2,1)S(1)} %slice_bitcast_fusion), channel_id=1, source_target_pairs={{0,2},{2,4},{4,6},{6,8},{8,10},{10,12},{12,14},{14,16},{16,18},{18... | collective-permute-start | bytes 24584 | tf_op jit(solution)/shard_map/ppermute | solution.py:390
  8.0 2.8 %collective-permute-start.10 = (bf16[3,32,256]{2,1,0:T(8,128)(2,1)}, bf16[3,32,256]{2,1,0:T(8,128)(2,1)S(1)}, u32[]{:S(2)}, u32[]{:S(2)}) collective-permute-start(bf16[3,32,256]{2,1,0:T(8,128)(2,1)} %get-tuple-element.18), channel_id=1, source_target_pairs={{0,12},{4,0},{8,4},{12,8},{1,13},{5,1},{9,5},{13,9},{2,14},{6,2},{... | collective-permute-start | bytes 147464 | tf_op jit(solution)/shard_map/ppermute | solution.py:78
  10.9 2.3 %collective-permute-start.9 = (bf16[3,32,256]{2,1,0:T(8,128)(2,1)}, bf16[3,32,256]{2,1,0:T(8,128)(2,1)S(1)}, u32[]{:S(2)}, u32[]{:S(2)}) collective-permute-start(bf16[3,32,256]{2,1,0:T(8,128)(2,1)} %get-tuple-element.17), channel_id=1, source_target_pairs={{0,8},{4,12},{8,0},{12,4},{1,9},{5,13},{9,1},{13,5},{2,10},{6,14},... | collective-permute-start | bytes 147464 | tf_op jit(solution)/shard_map/ppermute | solution.py:78
  13.1 4.4 %collective-permute-done.halo_ref = bf16[8,512]{1,0:T(8,128)(2,1)S(1)} collective-permute-done((bf16[8,512]{1,0:T(8,128)(2,1)S(1)}, bf16[8,512]{1,0:T(8,128)(2,1)S(1)}, u32[]{:S(2)}, u32[]{:S(2)}) %collective-permute-start) | collective-permute-done | bytes 8224 | tf_op jit(solution)/shard_map/ppermute | solution.py:390
  17.5 1.6 copy-done.17
  19.1 2.5 %shard_map.140.latent_ref.refs_0_.refs_4_ = bf16[256,512]{1,0:T(8,128)(2,1)S(1)} custom-call(bf16[8,512]{1,0:T(8,128)(2,1)S(1)} %collective-permute-done.halo_ref, bf16[512,512]{1,0:T(8,128)(2,1)S(1)} %bitcast.26, bf16[3,512,256]{2,1,0:T(8,128)(2,1)S(1)} %bitcast.28, bf16[256,512]{1,0:T(8,128)(2,1)S(1)} %bitcast.29, bf16[4,512,512]{2,1,0:T(8,128)(2,1)S(1)} %bitcast.27), custom_call_target="tpu_custom_call" | custom-call | flops 1100000000 | bytes 4194304 | tf_op jit(solution)/shard_map/pallas_call | solution.py:62
  22.0 5.7 %collective-permute-done.13.w10 = bf16[4,3,32,256]{3,2,1,0:T(8,128)(2,1)S(1)} collective-permute-done((bf16[4,3,32,256]{3,2,1,0:T(8,128)(2,1)S(1)}, bf16[4,3,32,256]{3,2,1,0:T(8,128)(2,1)S(1)}, u32[]{:S(2)}, u32[]{:S(2)}) %collective-permute-start.13) | collective-permute-done | bytes 196640 | tf_op jit(solution)/shard_map/ppermute | solution.py:74
  27.7 2.9 %collective-permute-done.2.refs_1_ = bf16[256,512]{1,0:T(8,128)(2,1)S(1)} collective-permute-done((bf16[256,512]{1,0:T(8,128)(2,1)S(1)}, bf16[256,512]{1,0:T(8,128)(2,1)S(1)}, u32[]{:S(2)}, u32[]{:S(2)}) %collective-permute-start.2) | collective-permute-done | bytes 262176 | tf_op jit(solution)/shard_map/ppermute | solution.py:74
  30.8 1.9 %shard_map.147 = bf16[8,32,896]{2,1,0:T(8,128)(2,1)} custom-call(s32[7]{0:T(128)S(1)} %copy-done.15, bf16[4,3,32,256]{3,2,1,0:T(8,128)(2,1)S(1)} %shard_map.146.w00, bf16[4,3,32,256]{3,2,1,0:T(8,128)(2,1)S(1)} %collective-permute-done.12.w01, bf16[4,3,32,256]{3,2,1,0:T(8,128)(2,1)S(1)} %collective-permute-done.13.w10, ...), custom_call_target="tpu_custom_call" | custom-call | flops 210000000 | bytes 2097152 | tf_op jit(solution)/shard_map/pallas_call | solution.py:161
  32.7 7.7 %all-to-all-start = ((bf16[8,32,896]{2,1,0:T(8,128)(2,1)}), bf16[8,32,896]{2,1,0:T(8,128)(2,1)S(1)}, u32[]{:S(2)}, u32[]{:S(2)}) async-start(bf16[8,32,896]{2,1,0:T(8,128)(2,1)} %shard_map.147), calls=%async_computation | async-start | bytes 917504 | tf_op jit(solution)/shard_map/all_to_all | solution.py:409
  40.4 1.5 collective-permute-start.5
  41.9 1.7 %collective-permute-start.6 = (bf16[2,256,512]{2,1,0:T(8,128)(2,1)S(1)}, bf16[2,256,512]{2,1,0:T(8,128)(2,1)S(1)}, u32[]{:S(2)}, u32[]{:S(2)}) collective-permute-start(bf16[2,256,512]{2,1,0:T(8,128)(2,1)S(1)} %shard_map.144.refs_0_.a), channel_id=1, source_target_pairs={{0,12},{4,0},{8,4},{12,8},{1,13},{5,1},{9,5},{13,9},{2,14},{6,2},{... | collective-permute-start | bytes 1572872 | tf_op jit(solution)/shard_map/ppermute | solution.py:78
  43.6 3.9 %collective-permute-start.1 = (bf16[256,512]{1,0:T(8,128)(2,1)S(1)}, bf16[256,512]{1,0:T(8,128)(2,1)S(1)}, u32[]{:S(2)}, u32[]{:S(2)}) collective-permute-start(bf16[256,512]{1,0:T(8,128)(2,1)S(1)} %shard_map.140.latent_ref.refs_0_.refs_4_), channel_id=1, source_target_pairs={{0,16},{16,32},{32,48},{48,64},{64,80},{80,96},{96,112},{112,128},... | collective-permute-start | bytes 786440 | tf_op jit(solution)/shard_map/ppermute | solution.py:400
  47.5 3.4 %collective-permute-start.3 = (bf16[256,512]{1,0:T(8,128)(2,1)S(1)}, bf16[256,512]{1,0:T(8,128)(2,1)S(1)}, u32[]{:S(2)}, u32[]{:S(2)}) collective-permute-start(bf16[256,512]{1,0:T(8,128)(2,1)S(1)} %collective-permute-done.2.refs_1_), channel_id=1, source_target_pairs={{0,16},{16,32},{32,48},{48,64},{64,80},{80,96},{96,112},{112,128},... | collective-permute-start | bytes 786440 | tf_op jit(solution)/shard_map/ppermute | solution.py:400
  50.9 10.3 %collective-permute-done.1.refs_0_ = bf16[256,512]{1,0:T(8,128)(2,1)S(1)} collective-permute-done((bf16[256,512]{1,0:T(8,128)(2,1)S(1)}, bf16[256,512]{1,0:T(8,128)(2,1)S(1)}, u32[]{:S(2)}, u32[]{:S(2)}) %collective-permute-start.1) | collective-permute-done | bytes 262176 | tf_op jit(solution)/shard_map/ppermute | solution.py:400
  61.2 4.6 %collective-permute-done.3.refs_1_ = bf16[256,512]{1,0:T(8,128)(2,1)S(1)} collective-permute-done((bf16[256,512]{1,0:T(8,128)(2,1)S(1)}, bf16[256,512]{1,0:T(8,128)(2,1)S(1)}, u32[]{:S(2)}, u32[]{:S(2)}) %collective-permute-start.3) | collective-permute-done | bytes 262176 | tf_op jit(solution)/shard_map/ppermute | solution.py:400
  65.8 2.2 %copy-done = bf16[1,512,4096]{2,1,0:T(8,128)(2,1)S(1)} copy-done((bf16[1,512,4096]{2,1,0:T(8,128)(2,1)S(1)}, bf16[1,512,4096]{2,1,0:T(8,128)(2,1)}, u32[]{:S(2)}) %copy-start) | copy-done | bytes 4194328
  68.0 1.7 %shard_map.142.refs_2_ = bf16[256,2048]{1,0:T(8,128)(2,1)S(1)} custom-call(s32[7]{0:T(128)S(1)} %copy-done.15, bf16[256,512]{1,0:T(8,128)(2,1)S(1)} %shard_map.140.latent_ref.refs_0_.refs_4_, bf16[512,4096]{1,0:T(8,128)(2,1)S(1)} %bitcast.19, bf16[2,256,512]{2,1,0:T(8,128)(2,1)S(1)} %shard_map.141.refs_0_.b), custom_call_target="tpu_custom_call" | custom-call | flops 540000000 | bytes 3145728 | tf_op jit(solution)/shard_map/pallas_call | solution.py:207
  69.6 1.2 collective-permute-start.4
  70.8 0.8 copy-done.5
  71.6 0.8 copy-done.8
  72.4 1.0 copy-done.6
  73.5 1.0 copy-done.9
  74.5 0.8 shard_map.148
  75.3 5.0 %all-to-all-start.1 = ((bf16[8,32,768]{2,1,0:T(8,128)(2,1)}), bf16[8,32,768]{2,1,0:T(8,128)(2,1)S(1)}, u32[]{:S(2)}, u32[]{:S(2)}) async-start(bf16[8,32,768]{2,1,0:T(8,128)(2,1)} %get-tuple-element.20), calls=%async_computation.1 | async-start | bytes 786432 | tf_op jit(solution)/shard_map/all_to_all | solution.py:412
  80.5 0.2 reduce_window_sum.11
  80.8 1.8 %collective-permute-start.25 = (bf16[2,256,512]{2,1,0:T(8,128)(2,1)S(1)}, bf16[2,256,512]{2,1,0:T(8,128)(2,1)}, u32[]{:S(2)}, u32[]{:S(2)}) collective-permute-start(bf16[2,256,512]{2,1,0:T(8,128)(2,1)S(1)} %shard_map.141.refs_0_.b), channel_id=1, source_target_pairs={{0,12},{4,0},{8,4},{12,8},{1,13},{5,1},{9,5},{13,9},{2,14},{6,2},{... | collective-permute-start | bytes 1572872 | tf_op jit(solution)/shard_map/ppermute | solution.py:78
  82.6 11.8 %all-to-all-done.1 = bf16[8,32,768]{2,1,0:T(8,128)(2,1)S(1)} async-done(((bf16[8,32,768]{2,1,0:T(8,128)(2,1)}), bf16[8,32,768]{2,1,0:T(8,128)(2,1)S(1)}, u32[]{:S(2)}, u32[]{:S(2)}) %all-to-all-start.1) | async-done | bytes 393248 | tf_op jit(solution)/shard_map/all_to_all | solution.py:412
  94.4 0.7 collective-permute-start.16
  95.2 1.2 collective-permute-done.4.got_ref
  96.4 2.2 %copy-done.1 = bf16[1,512,4096]{2,1,0:T(8,128)(2,1)S(1)} copy-done((bf16[1,512,4096]{2,1,0:T(8,128)(2,1)S(1)}, bf16[1,512,4096]{2,1,0:T(8,128)(2,1)}, u32[]{:S(2)}) %copy-start.1) | copy-done | bytes 4194328
  98.6 3.9 %shard_map.143 = (bf16[256,2048]{1,0:T(8,128)(2,1)}, f32[8,256]{1,0:T(8,128)S(1)}) custom-call(s32[7]{0:T(128)S(1)} %copy-done.15, bf16[256,512]{1,0:T(8,128)(2,1)S(1)} %shard_map.140.latent_ref.refs_0_.refs_4_, bf16[512,4096]{1,0:T(8,128)(2,1)S(1)} %bitcast.20, bf16[256,2048]{1,0:T(8,128)(2,1)} %collective-permute-done.4.got_ref, ...), custom_call_target="tpu_custom_call" | custom-call | flops 540000000 | bytes 5242880 | tf_op jit(solution)/shard_map/pallas_call | solution.py:246
  102.4 0.6 collective-permute-start.18
  103.0 1.7 %collective-permute-start.7 = (bf16[2,256,512]{2,1,0:T(8,128)(2,1)S(1)}, bf16[2,256,512]{2,1,0:T(8,128)(2,1)S(1)}, u32[]{:S(2)}, u32[]{:S(2)}) collective-permute-start(bf16[2,256,512]{2,1,0:T(8,128)(2,1)S(1)} %copy-done.7), channel_id=1, source_target_pairs={{0,4},{4,8},{8,12},{12,0},{1,5},{5,9},{9,13},{13,1},{2,6},{6,10},{... | collective-permute-start | bytes 1572872 | tf_op jit(solution)/shard_map/ppermute | solution.py:78
  104.7 0.5 collective-permute-start.17
  105.2 2.4 %collective-permute-done.18 = f32[8,256]{1,0:T(8,128)S(1)} collective-permute-done((f32[8,256]{1,0:T(8,128)S(1)}, f32[8,256]{1,0:T(8,128)S(1)}, u32[]{:S(2)}, u32[]{:S(2)}) %collective-permute-start.18) | collective-permute-done | bytes 8224 | tf_op jit(solution)/shard_map/ppermute | solution.py:74
  107.6 1.9 %collective-permute-start.19 = (f32[1,256]{1,0:T(1,128)S(1)}, f32[1,256]{1,0:T(1,128)S(1)}, u32[]{:S(2)}, u32[]{:S(2)}) collective-permute-start(f32[1,256]{1,0:T(1,128)S(1)} %add_rsqrt_fusion), channel_id=1, source_target_pairs={{0,16},{16,32},{32,48},{48,64},{64,80},{80,96},{96,112},{112,128},... | collective-permute-start | bytes 3080 | tf_op jit(solution)/shard_map/ppermute | solution.py:427
  109.5 2.3 %collective-permute-start.24 = (bf16[2,256,512]{2,1,0:T(8,128)(2,1)S(1)}, bf16[2,256,512]{2,1,0:T(8,128)(2,1)S(1)}, u32[]{:S(2)}, u32[]{:S(2)}) collective-permute-start(bf16[2,256,512]{2,1,0:T(8,128)(2,1)S(1)} %shard_map.141.refs_0_.b), channel_id=1, source_target_pairs={{0,4},{4,8},{8,12},{12,0},{1,5},{5,9},{9,13},{13,1},{2,6},{6,10},{... | collective-permute-start | bytes 1572872 | tf_op jit(solution)/shard_map/ppermute | solution.py:78
  111.8 3.4 %collective-permute-done.19 = f32[1,256]{1,0:T(1,128)S(1)} collective-permute-done((f32[1,256]{1,0:T(1,128)S(1)}, f32[1,256]{1,0:T(1,128)S(1)}, u32[]{:S(2)}, u32[]{:S(2)}) %collective-permute-start.19) | collective-permute-done | bytes 1056 | tf_op jit(solution)/shard_map/ppermute | solution.py:427
  115.2 1.8 %collective-permute-start.26 = (bf16[2,256,512]{2,1,0:T(8,128)(2,1)}, bf16[2,256,512]{2,1,0:T(8,128)(2,1)S(1)}, u32[]{:S(2)}, u32[]{:S(2)}) collective-permute-start(bf16[2,256,512]{2,1,0:T(8,128)(2,1)} %collective-permute-done.25.br), channel_id=1, source_target_pairs={{0,12},{4,0},{8,4},{12,8},{1,13},{5,1},{9,5},{13,9},{2,14},{6,2},{... | collective-permute-start | bytes 1572872 | tf_op jit(solution)/shard_map/ppermute | solution.py:78
  117.0 2.1 %collective-permute-done.7.af = bf16[2,256,512]{2,1,0:T(8,128)(2,1)S(1)} collective-permute-done((bf16[2,256,512]{2,1,0:T(8,128)(2,1)S(1)}, bf16[2,256,512]{2,1,0:T(8,128)(2,1)S(1)}, u32[]{:S(2)}, u32[]{:S(2)}) %collective-permute-start.7) | collective-permute-done | bytes 524320 | tf_op jit(solution)/shard_map/ppermute | solution.py:78
  119.3 6.8 %collective-permute-done.20.s1 = f32[2,256]{1,0:T(2,128)S(1)} collective-permute-done((f32[2,256]{1,0:T(2,128)S(1)}, f32[2,256]{1,0:T(2,128)S(1)}, u32[]{:S(2)}, u32[]{:S(2)}) %collective-permute-start.20) | collective-permute-done | bytes 2080 | tf_op jit(solution)/shard_map/ppermute | solution.py:78
  126.0 1.2 collective-permute-start.21
  127.2 3.9 %collective-permute-done.21.s2 = f32[2,256]{1,0:T(2,128)S(1)} collective-permute-done((f32[2,256]{1,0:T(2,128)S(1)}, f32[2,256]{1,0:T(2,128)S(1)}, u32[]{:S(2)}, u32[]{:S(2)}) %collective-permute-start.21) | collective-permute-done | bytes 2080 | tf_op jit(solution)/shard_map/ppermute | solution.py:78
  131.1 0.8 collective-permute-start.22
  131.9 4.0 %collective-permute-done.22.s3 = f32[2,256]{1,0:T(2,128)S(1)} collective-permute-done((f32[2,256]{1,0:T(2,128)S(1)}, f32[2,256]{1,0:T(2,128)S(1)}, u32[]{:S(2)}, u32[]{:S(2)}) %collective-permute-start.22) | collective-permute-done | bytes 2080 | tf_op jit(solution)/shard_map/ppermute | solution.py:78
  135.9 2.6 %shard_map.149 = (bf16[4,256,512]{2,1,0:T(8,128)(2,1)S(1)}, bf16[4,256,256]{2,1,0:T(8,128)(2,1)S(1)}, bf16[1024,768]{1,0:T(8,128)(2,1)S(1)}) custom-call(s32[7]{0:T(128)S(1)} %copy-done.15, bf16[2,256,512]{2,1,0:T(8,128)(2,1)S(1)} %shard_map.144.refs_0_.a, bf16[2,256,512]{2,1,0:T(8,128)(2,1)S(1)} %copy-done.7, bf16[2,256,512]{2,1,0:T(8,128)(2,1)S(1)} %copy-done.10, ...), custom_call_target="tpu_custom_call" | custom-call | flops 1600000000 | bytes 6291456 | tf_op jit(solution)/shard_map/pallas_call | solution.py:297
  138.6 2.7 %shard_map.150.pm_ref = bf16[4,256,512]{2,1,0:T(8,128)(2,1)S(1)} custom-call(s32[7]{0:T(128)S(1)} %copy-done.15, bf16[2,256,512]{2,1,0:T(8,128)(2,1)S(1)} %shard_map.141.refs_0_.b, bf16[2,256,512]{2,1,0:T(8,128)(2,1)S(1)} %collective-permute-done.24.bl, bf16[2,256,512]{2,1,0:T(8,128)(2,1)} %collective-permute-done.25.br, ...), custom_call_target="tpu_custom_call" | custom-call | flops 1600000000 | bytes 6291456 | tf_op jit(solution)/shard_map/pallas_call | solution.py:297
  141.4 0.5 collective-permute-start.23
  142.1 2.0 %collective-permute-done.27.pt_ref = bf16[4,256,512]{2,1,0:T(8,128)(2,1)S(1)} collective-permute-done((bf16[4,256,512]{2,1,0:T(8,128)(2,1)S(1)}, bf16[4,256,512]{2,1,0:T(8,128)(2,1)S(1)}, u32[]{:S(2)}, u32[]{:S(2)}) %collective-permute-start.27) | collective-permute-done | bytes 1048608 | tf_op jit(solution)/shard_map/ppermute | solution.py:74
  144.0 1.6 collective-permute-done.23.ot_ref
  145.7 1.0 copy-done.3
  146.7 3.0 %shard_map.154 = bf16[1,256,256]{2,1,0:T(8,128)(2,1)S(1)} custom-call(s32[4]{0:T(128)S(1)} %get-tuple-element.26.place_ref, bf16[4,256,256]{2,1,0:T(8,128)(2,1)S(1)} %copy-done.3, bf16[4,256,512]{2,1,0:T(8,128)(2,1)S(1)} %get-tuple-element.24.om_ref, bf16[4,256,512]{2,1,0:T(8,128)(2,1)} %collective-permute-done.23.ot_ref, ...), custom_call_target="tpu_custom_call" | custom-call | flops 536870912 | bytes 5242880 | tf_op jit(solution)/shard_map/pallas_call | solution.py:343
  149.8 1.4 collective-permute-start.30
  151.1 3.0 %shard_map.153 = bf16[1,256,256]{2,1,0:T(8,128)(2,1)S(1)} custom-call(s32[4]{0:T(128)S(1)} %get-tuple-element.28.place_ref, bf16[4,256,256]{2,1,0:T(8,128)(2,1)S(1)} %copy-done.3, bf16[4,256,512]{2,1,0:T(8,128)(2,1)S(1)} %get-tuple-element.24.om_ref, bf16[4,256,512]{2,1,0:T(8,128)(2,1)} %collective-permute-done.23.ot_ref, ...), custom_call_target="tpu_custom_call" | custom-call | flops 536870912 | bytes 5242880 | tf_op jit(solution)/shard_map/pallas_call | solution.py:343
  154.1 0.4 collective-permute-start.29
  154.6 3.1 %shard_map.152 = bf16[1,256,256]{2,1,0:T(8,128)(2,1)S(1)} custom-call(s32[4]{0:T(128)S(1)} %get-tuple-element.29.place_ref, bf16[4,256,256]{2,1,0:T(8,128)(2,1)S(1)} %copy-done.3, bf16[4,256,512]{2,1,0:T(8,128)(2,1)S(1)} %get-tuple-element.24.om_ref, bf16[4,256,512]{2,1,0:T(8,128)(2,1)} %collective-permute-done.23.ot_ref, ...), custom_call_target="tpu_custom_call" | custom-call | flops 536870912 | bytes 5242880 | tf_op jit(solution)/shard_map/pallas_call | solution.py:343
  157.6 0.6 collective-permute-start.28
  158.4 3.0 %shard_map.151.a_ref = bf16[1,256,256]{2,1,0:T(8,128)(2,1)S(1)} custom-call(s32[4]{0:T(128)S(1)} %get-tuple-element.30.place_ref, bf16[4,256,256]{2,1,0:T(8,128)(2,1)S(1)} %copy-done.4, bf16[4,256,512]{2,1,0:T(8,128)(2,1)S(1)} %get-tuple-element.24.om_ref, bf16[4,256,512]{2,1,0:T(8,128)(2,1)} %collective-permute-done.23.ot_ref, ...), custom_call_target="tpu_custom_call" | custom-call | flops 536870912 | bytes 5242880 | tf_op jit(solution)/shard_map/pallas_call | solution.py:343
  161.4 2.6 %collective-permute-done.28.b_ref = bf16[1,256,256]{2,1,0:T(8,128)(2,1)S(1)} collective-permute-done((bf16[1,256,256]{2,1,0:T(8,128)(2,1)S(1)}, bf16[1,256,256]{2,1,0:T(8,128)(2,1)S(1)}, u32[]{:S(2)}, u32[]{:S(2)}) %collective-permute-start.28) | collective-permute-done | bytes 131104 | tf_op jit(solution)/shard_map/ppermute | solution.py:78
  164.0 1.4 shard_map.155
  (75 shorter events, 1.4 us)
Async XLA Ops:
  1.3 4.8 %copy-start.16 = (bf16[1,512,512]{2,1,0:T(8,128)(2,1)S(1)}, bf16[1,512,512]{2,1,0:T(8,128)(2,1)}, u32[]{:S(2)}) copy-start(bf16[1,512,512]{2,1,0:T(8,128)(2,1)} %param.13) | copy-start | bytes 1572868
  1.3 16.2 %copy-start.18 = (bf16[1,3,512,256]{3,2,1,0:T(8,128)(2,1)S(1)}, bf16[1,3,512,256]{3,2,1,0:T(8,128)(2,1)}, u32[]{:S(2)}) copy-start(bf16[1,3,512,256]{3,2,1,0:T(8,128)(2,1)} %param.14) | copy-start | bytes 2359300
  1.3 16.2 %copy-start.19 = (bf16[1,256,512]{2,1,0:T(8,128)(2,1)S(1)}, bf16[1,256,512]{2,1,0:T(8,128)(2,1)}, u32[]{:S(2)}) copy-start(bf16[1,256,512]{2,1,0:T(8,128)(2,1)} %param.15) | copy-start | bytes 786436
  3.8 17.9 %copy-start.14 = (bf16[3,32,256]{2,1,0:T(8,128)(2,1)S(1)}, bf16[3,32,256]{2,1,0:T(8,128)(2,1)}, u32[]{:S(2)}) copy-start(bf16[3,32,256]{2,1,0:T(8,128)(2,1)} %get-tuple-element.15.refs_0_) | copy-start | bytes 147460
  3.8 17.9 %collective-permute-start.11 = (bf16[2,128,256]{2,1,0:T(8,128)(2,1)}, bf16[2,128,256]{2,1,0:T(8,128)(2,1)S(1)}, u32[]{:S(2)}, u32[]{:S(2)}) collective-permute-start(bf16[2,128,256]{2,1,0:T(8,128)(2,1)} %get-tuple-element.19.mine_ref), channel_id=1, source_target_pairs={{0,1},{1,0},{2,3},{3,2},{4,5},{5,4},{6,7},{7,6},{8,9},{9,8},{10,11... | collective-permute-start | bytes 393224 | tf_op jit(solution)/shard_map/ppermute | solution.py:74
  6.1 11.4 %collective-permute-start = (bf16[8,512]{1,0:T(8,128)(2,1)S(1)}, bf16[8,512]{1,0:T(8,128)(2,1)S(1)}, u32[]{:S(2)}, u32[]{:S(2)}) collective-permute-start(bf16[8,512]{1,0:T(8,128)(2,1)S(1)} %slice_bitcast_fusion), channel_id=1, source_target_pairs={{0,2},{2,4},{4,6},{6,8},{8,10},{10,12},{12,14},{14,16},{16,18},{18... | collective-permute-start | bytes 24584 | tf_op jit(solution)/shard_map/ppermute | solution.py:390
  8.0 13.7 %collective-permute-start.10 = (bf16[3,32,256]{2,1,0:T(8,128)(2,1)}, bf16[3,32,256]{2,1,0:T(8,128)(2,1)S(1)}, u32[]{:S(2)}, u32[]{:S(2)}) collective-permute-start(bf16[3,32,256]{2,1,0:T(8,128)(2,1)} %get-tuple-element.18), channel_id=1, source_target_pairs={{0,12},{4,0},{8,4},{12,8},{1,13},{5,1},{9,5},{13,9},{2,14},{6,2},{... | collective-permute-start | bytes 147464 | tf_op jit(solution)/shard_map/ppermute | solution.py:78
  10.8 10.8 %collective-permute-start.8 = (bf16[3,32,256]{2,1,0:T(8,128)(2,1)}, bf16[3,32,256]{2,1,0:T(8,128)(2,1)S(1)}, u32[]{:S(2)}, u32[]{:S(2)}) collective-permute-start(bf16[3,32,256]{2,1,0:T(8,128)(2,1)} %get-tuple-element.16), channel_id=1, source_target_pairs={{0,4},{4,8},{8,12},{12,0},{1,5},{5,9},{9,13},{13,1},{2,6},{6,10},{... | collective-permute-start | bytes 147464 | tf_op jit(solution)/shard_map/ppermute | solution.py:78
  10.9 10.8 %collective-permute-start.9 = (bf16[3,32,256]{2,1,0:T(8,128)(2,1)}, bf16[3,32,256]{2,1,0:T(8,128)(2,1)S(1)}, u32[]{:S(2)}, u32[]{:S(2)}) collective-permute-start(bf16[3,32,256]{2,1,0:T(8,128)(2,1)} %get-tuple-element.17), channel_id=1, source_target_pairs={{0,8},{4,12},{8,0},{12,4},{1,9},{5,13},{9,1},{13,5},{2,10},{6,14},... | collective-permute-start | bytes 147464 | tf_op jit(solution)/shard_map/ppermute | solution.py:78
  17.5 1.6 copy-start.17
  19.1 11.6 %copy-start.11 = (f32[2,4096]{1,0:T(2,128)S(1)}, f32[2,4096]{1,0:T(2,128)}, u32[]{:S(2)}) copy-start(f32[2,4096]{1,0:T(2,128)} %t1.1) | copy-start | bytes 98308
  19.1 11.6 %copy-start.12 = (bf16[2,128,256]{2,1,0:T(8,128)(2,1)S(1)}, bf16[2,128,256]{2,1,0:T(8,128)(2,1)}, u32[]{:S(2)}) copy-start(bf16[2,128,256]{2,1,0:T(8,128)(2,1)} %get-tuple-element.19.mine_ref) | copy-start | bytes 393220
  19.1 11.6 %copy-start.13 = (f32[4096]{0:T(1024)S(1)}, f32[4096]{0:T(1024)}, u32[]{:S(2)}) copy-start(f32[4096]{0:T(1024)} %param.20) | copy-start | bytes 49156
  19.1 11.6 %copy-start.15 = (s32[7]{0:T(128)S(1)}, s32[7]{0:T(128)}, u32[]{:S(2)}) copy-start(s32[7]{0:T(128)} %stack.42.at_ref) | copy-start | bytes 88
  21.7 6.0 %collective-permute-start.13 = (bf16[4,3,32,256]{3,2,1,0:T(8,128)(2,1)S(1)}, bf16[4,3,32,256]{3,2,1,0:T(8,128)(2,1)S(1)}, u32[]{:S(2)}, u32[]{:S(2)}) collective-permute-start(bf16[4,3,32,256]{3,2,1,0:T(8,128)(2,1)S(1)} %shard_map.146.w00), channel_id=1, source_target_pairs={{0,128},{128,0},{1,129},{129,1},{2,130},{130,2},{3,131},{131,3},{4... | collective-permute-start | bytes 589832 | tf_op jit(solution)/shard_map/ppermute | solution.py:74
  21.8 8.8 %collective-permute-start.2 = (bf16[256,512]{1,0:T(8,128)(2,1)S(1)}, bf16[256,512]{1,0:T(8,128)(2,1)S(1)}, u32[]{:S(2)}, u32[]{:S(2)}) collective-permute-start(bf16[256,512]{1,0:T(8,128)(2,1)S(1)} %shard_map.140.latent_ref.refs_0_.refs_4_), channel_id=1, source_target_pairs={{0,1},{1,0},{2,3},{3,2},{4,5},{5,4},{6,7},{7,6},{8,9},{9,8},{10,11... | collective-permute-start | bytes 786440 | tf_op jit(solution)/shard_map/ppermute | solution.py:74
  21.9 8.8 %collective-permute-start.12 = (bf16[4,3,32,256]{3,2,1,0:T(8,128)(2,1)S(1)}, bf16[4,3,32,256]{3,2,1,0:T(8,128)(2,1)S(1)}, u32[]{:S(2)}, u32[]{:S(2)}) collective-permute-start(bf16[4,3,32,256]{3,2,1,0:T(8,128)(2,1)S(1)} %shard_map.146.w00), channel_id=1, source_target_pairs={{0,2},{2,0},{1,3},{3,1},{4,6},{6,4},{5,7},{7,5},{8,10},{10,8},{9,1... | collective-permute-start | bytes 589832 | tf_op jit(solution)/shard_map/ppermute | solution.py:74
  27.7 3.0 %collective-permute-start.14 = (bf16[4,3,32,256]{3,2,1,0:T(8,128)(2,1)S(1)}, bf16[4,3,32,256]{3,2,1,0:T(8,128)(2,1)S(1)}, u32[]{:S(2)}, u32[]{:S(2)}) collective-permute-start(bf16[4,3,32,256]{3,2,1,0:T(8,128)(2,1)S(1)} %collective-permute-done.13.w10), channel_id=1, source_target_pairs={{0,2},{2,0},{1,3},{3,1},{4,6},{6,4},{5,7},{7,5},{8,10},{10,8},{9,1... | collective-permute-start | bytes 589832 | tf_op jit(solution)/shard_map/ppermute | solution.py:74
  32.7 39.7 %all-to-all-start = ((bf16[8,32,896]{2,1,0:T(8,128)(2,1)}), bf16[8,32,896]{2,1,0:T(8,128)(2,1)S(1)}, u32[]{:S(2)}, u32[]{:S(2)}) async-start(bf16[8,32,896]{2,1,0:T(8,128)(2,1)} %shard_map.147), calls=%async_computation | async-start | bytes 917504 | tf_op jit(solution)/shard_map/all_to_all | solution.py:409
  40.4 30.5 %collective-permute-start.5 = (bf16[2,256,512]{2,1,0:T(8,128)(2,1)S(1)}, bf16[2,256,512]{2,1,0:T(8,128)(2,1)S(1)}, u32[]{:S(2)}, u32[]{:S(2)}) collective-permute-start(bf16[2,256,512]{2,1,0:T(8,128)(2,1)S(1)} %shard_map.144.refs_0_.a), channel_id=1, source_target_pairs={{0,4},{4,8},{8,12},{12,0},{1,5},{5,9},{9,13},{13,1},{2,6},{6,10},{... | collective-permute-start | bytes 1572872 | tf_op jit(solution)/shard_map/ppermute | solution.py:78
  41.9 29.7 %collective-permute-start.6 = (bf16[2,256,512]{2,1,0:T(8,128)(2,1)S(1)}, bf16[2,256,512]{2,1,0:T(8,128)(2,1)S(1)}, u32[]{:S(2)}, u32[]{:S(2)}) collective-permute-start(bf16[2,256,512]{2,1,0:T(8,128)(2,1)S(1)} %shard_map.144.refs_0_.a), channel_id=1, source_target_pairs={{0,12},{4,0},{8,4},{12,8},{1,13},{5,1},{9,5},{13,9},{2,14},{6,2},{... | collective-permute-start | bytes 1572872 | tf_op jit(solution)/shard_map/ppermute | solution.py:78
  43.6 17.6 %collective-permute-start.1 = (bf16[256,512]{1,0:T(8,128)(2,1)S(1)}, bf16[256,512]{1,0:T(8,128)(2,1)S(1)}, u32[]{:S(2)}, u32[]{:S(2)}) collective-permute-start(bf16[256,512]{1,0:T(8,128)(2,1)S(1)} %shard_map.140.latent_ref.refs_0_.refs_4_), channel_id=1, source_target_pairs={{0,16},{16,32},{32,48},{48,64},{64,80},{80,96},{96,112},{112,128},... | collective-permute-start | bytes 786440 | tf_op jit(solution)/shard_map/ppermute | solution.py:400
  47.5 18.2 %collective-permute-start.3 = (bf16[256,512]{1,0:T(8,128)(2,1)S(1)}, bf16[256,512]{1,0:T(8,128)(2,1)S(1)}, u32[]{:S(2)}, u32[]{:S(2)}) collective-permute-start(bf16[256,512]{1,0:T(8,128)(2,1)S(1)} %collective-permute-done.2.refs_1_), channel_id=1, source_target_pairs={{0,16},{16,32},{32,48},{48,64},{64,80},{80,96},{96,112},{112,128},... | collective-permute-start | bytes 786440 | tf_op jit(solution)/shard_map/ppermute | solution.py:400
  65.8 2.2 %copy-start = (bf16[1,512,4096]{2,1,0:T(8,128)(2,1)S(1)}, bf16[1,512,4096]{2,1,0:T(8,128)(2,1)}, u32[]{:S(2)}) copy-start(bf16[1,512,4096]{2,1,0:T(8,128)(2,1)} %param.17) | copy-start | bytes 12582916
  68.0 12.6 %copy-start.20 = (s32[2,32]{1,0:T(2,128)S(1)}, s32[2,32]{1,0:T(2,128)}, u32[]{:S(2)}) copy-start(s32[2,32]{1,0:T(2,128)} %param.18) | copy-start | bytes 772
  69.6 26.7 %collective-permute-start.4 = (bf16[256,2048]{1,0:T(8,128)(2,1)S(1)}, bf16[256,2048]{1,0:T(8,128)(2,1)}, u32[]{:S(2)}, u32[]{:S(2)}) collective-permute-start(bf16[256,2048]{1,0:T(8,128)(2,1)S(1)} %shard_map.142.refs_2_), channel_id=1, source_target_pairs={{0,1},{1,0},{2,3},{3,2},{4,5},{5,4},{6,7},{7,6},{8,9},{9,8},{10,11... | collective-permute-start | bytes 3145736 | tf_op jit(solution)/shard_map/ppermute | solution.py:74
  70.8 0.8 copy-start.5
  71.6 0.8 copy-start.8
  72.4 1.0 copy-start.6
  73.5 1.0 copy-start.9
  75.3 19.1 %all-to-all-start.1 = ((bf16[8,32,768]{2,1,0:T(8,128)(2,1)}), bf16[8,32,768]{2,1,0:T(8,128)(2,1)S(1)}, u32[]{:S(2)}, u32[]{:S(2)}) async-start(bf16[8,32,768]{2,1,0:T(8,128)(2,1)} %get-tuple-element.20), calls=%async_computation.1 | async-start | bytes 786432 | tf_op jit(solution)/shard_map/all_to_all | solution.py:412
  80.8 28.7 %collective-permute-start.25 = (bf16[2,256,512]{2,1,0:T(8,128)(2,1)S(1)}, bf16[2,256,512]{2,1,0:T(8,128)(2,1)}, u32[]{:S(2)}, u32[]{:S(2)}) collective-permute-start(bf16[2,256,512]{2,1,0:T(8,128)(2,1)S(1)} %shard_map.141.refs_0_.b), channel_id=1, source_target_pairs={{0,12},{4,0},{8,4},{12,8},{1,13},{5,1},{9,5},{13,9},{2,14},{6,2},{... | collective-permute-start | bytes 1572872 | tf_op jit(solution)/shard_map/ppermute | solution.py:78
  94.4 10.3 %collective-permute-start.16 = (bf16[256,768]{1,0:T(8,128)(2,1)S(1)}, bf16[256,768]{1,0:T(8,128)(2,1)S(1)}, u32[]{:S(2)}, u32[]{:S(2)}) collective-permute-start(bf16[256,768]{1,0:T(8,128)(2,1)S(1)} %bitcast.21), channel_id=1, source_target_pairs={{0,128},{128,0},{1,129},{129,1},{2,130},{130,2},{3,131},{131,3},{4... | collective-permute-start | bytes 1179656 | tf_op jit(solution)/shard_map/ppermute | solution.py:74
  96.4 2.2 %copy-start.1 = (bf16[1,512,4096]{2,1,0:T(8,128)(2,1)S(1)}, bf16[1,512,4096]{2,1,0:T(8,128)(2,1)}, u32[]{:S(2)}) copy-start(bf16[1,512,4096]{2,1,0:T(8,128)(2,1)} %param.17) | copy-start | bytes 12582916
  98.6 4.4 %copy-start.7 = (bf16[2,256,512]{2,1,0:T(8,128)(2,1)S(1)}, bf16[2,256,512]{2,1,0:T(8,128)(2,1)}, u32[]{:S(2)}) copy-start(bf16[2,256,512]{2,1,0:T(8,128)(2,1)} %copy-done.5) | copy-start | bytes 1572868
  98.6 37.3 %copy-start.10 = (bf16[2,256,512]{2,1,0:T(8,128)(2,1)S(1)}, bf16[2,256,512]{2,1,0:T(8,128)(2,1)}, u32[]{:S(2)}) copy-start(bf16[2,256,512]{2,1,0:T(8,128)(2,1)} %copy-done.8) | copy-start | bytes 1572868
  102.4 5.2 %collective-permute-start.18 = (f32[8,256]{1,0:T(8,128)S(1)}, f32[8,256]{1,0:T(8,128)S(1)}, u32[]{:S(2)}, u32[]{:S(2)}) collective-permute-start(f32[8,256]{1,0:T(8,128)S(1)} %get-tuple-element.22), channel_id=1, source_target_pairs={{0,1},{1,0},{2,3},{3,2},{4,5},{5,4},{6,7},{7,6},{8,9},{9,8},{10,11... | collective-permute-start | bytes 24584 | tf_op jit(solution)/shard_map/ppermute | solution.py:74
  103.0 16.1 %collective-permute-start.7 = (bf16[2,256,512]{2,1,0:T(8,128)(2,1)S(1)}, bf16[2,256,512]{2,1,0:T(8,128)(2,1)S(1)}, u32[]{:S(2)}, u32[]{:S(2)}) collective-permute-start(bf16[2,256,512]{2,1,0:T(8,128)(2,1)S(1)} %copy-done.7), channel_id=1, source_target_pairs={{0,4},{4,8},{8,12},{12,0},{1,5},{5,9},{9,13},{13,1},{2,6},{6,10},{... | collective-permute-start | bytes 1572872 | tf_op jit(solution)/shard_map/ppermute | solution.py:78
  104.7 31.2 %collective-permute-start.15 = (bf16[256,768]{1,0:T(8,128)(2,1)S(1)}, bf16[256,768]{1,0:T(8,128)(2,1)S(1)}, u32[]{:S(2)}, u32[]{:S(2)}) collective-permute-start(bf16[256,768]{1,0:T(8,128)(2,1)S(1)} %bitcast.22), channel_id=1, source_target_pairs={{0,2},{2,0},{1,3},{3,1},{4,6},{6,4},{5,7},{7,5},{8,10},{10,8},{9,1... | collective-permute-start | bytes 1179656 | tf_op jit(solution)/shard_map/ppermute | solution.py:74
  104.7 31.2 %collective-permute-start.17 = (bf16[256,768]{1,0:T(8,128)(2,1)S(1)}, bf16[256,768]{1,0:T(8,128)(2,1)S(1)}, u32[]{:S(2)}, u32[]{:S(2)}) collective-permute-start(bf16[256,768]{1,0:T(8,128)(2,1)S(1)} %collective-permute-done.16.m10), channel_id=1, source_target_pairs={{0,2},{2,0},{1,3},{3,1},{4,6},{6,4},{5,7},{7,5},{8,10},{10,8},{9,1... | collective-permute-start | bytes 1179656 | tf_op jit(solution)/shard_map/ppermute | solution.py:74
  107.6 7.6 %collective-permute-start.19 = (f32[1,256]{1,0:T(1,128)S(1)}, f32[1,256]{1,0:T(1,128)S(1)}, u32[]{:S(2)}, u32[]{:S(2)}) collective-permute-start(f32[1,256]{1,0:T(1,128)S(1)} %add_rsqrt_fusion), channel_id=1, source_target_pairs={{0,16},{16,32},{32,48},{48,64},{64,80},{80,96},{96,112},{112,128},... | collective-permute-start | bytes 3080 | tf_op jit(solution)/shard_map/ppermute | solution.py:427
  109.5 29.1 %collective-permute-start.24 = (bf16[2,256,512]{2,1,0:T(8,128)(2,1)S(1)}, bf16[2,256,512]{2,1,0:T(8,128)(2,1)S(1)}, u32[]{:S(2)}, u32[]{:S(2)}) collective-permute-start(bf16[2,256,512]{2,1,0:T(8,128)(2,1)S(1)} %shard_map.141.refs_0_.b), channel_id=1, source_target_pairs={{0,4},{4,8},{8,12},{12,0},{1,5},{5,9},{9,13},{13,1},{2,6},{6,10},{... | collective-permute-start | bytes 1572872 | tf_op jit(solution)/shard_map/ppermute | solution.py:78
  115.2 23.4 %collective-permute-start.26 = (bf16[2,256,512]{2,1,0:T(8,128)(2,1)}, bf16[2,256,512]{2,1,0:T(8,128)(2,1)S(1)}, u32[]{:S(2)}, u32[]{:S(2)}) collective-permute-start(bf16[2,256,512]{2,1,0:T(8,128)(2,1)} %collective-permute-done.25.br), channel_id=1, source_target_pairs={{0,12},{4,0},{8,4},{12,8},{1,13},{5,1},{9,5},{13,9},{2,14},{6,2},{... | collective-permute-start | bytes 1572872 | tf_op jit(solution)/shard_map/ppermute | solution.py:78
  119.1 6.9 %collective-permute-start.20 = (f32[2,256]{1,0:T(2,128)S(1)}, f32[2,256]{1,0:T(2,128)S(1)}, u32[]{:S(2)}, u32[]{:S(2)}) collective-permute-start(f32[2,256]{1,0:T(2,128)S(1)} %pad_maximum_fusion.s0), channel_id=1, source_target_pairs={{0,12},{4,0},{8,4},{12,8},{1,13},{5,1},{9,5},{13,9},{2,14},{6,2},{... | collective-permute-start | bytes 6152 | tf_op jit(solution)/shard_map/ppermute | solution.py:78
  126.0 5.1 %collective-permute-start.21 = (f32[2,256]{1,0:T(2,128)S(1)}, f32[2,256]{1,0:T(2,128)S(1)}, u32[]{:S(2)}, u32[]{:S(2)}) collective-permute-start(f32[2,256]{1,0:T(2,128)S(1)} %pad_maximum_fusion.s0), channel_id=1, source_target_pairs={{0,8},{4,12},{8,0},{12,4},{1,9},{5,13},{9,1},{13,5},{2,10},{6,14},... | collective-permute-start | bytes 6152 | tf_op jit(solution)/shard_map/ppermute | solution.py:78
  131.1 4.8 %collective-permute-start.22 = (f32[2,256]{1,0:T(2,128)S(1)}, f32[2,256]{1,0:T(2,128)S(1)}, u32[]{:S(2)}, u32[]{:S(2)}) collective-permute-start(f32[2,256]{1,0:T(2,128)S(1)} %pad_maximum_fusion.s0), channel_id=1, source_target_pairs={{0,4},{4,8},{8,12},{12,0},{1,5},{5,9},{9,13},{13,1},{2,6},{6,10},{... | collective-permute-start | bytes 6152 | tf_op jit(solution)/shard_map/ppermute | solution.py:78
  138.6 2.7 %copy-start.2 = (bf16[4,256,256]{2,1,0:T(8,128)(2,1)}, bf16[4,256,256]{2,1,0:T(8,128)(2,1)S(1)}, u32[]{:S(2)}) copy-start(bf16[4,256,256]{2,1,0:T(8,128)(2,1)S(1)} %get-tuple-element.23.q_ref) | copy-start | bytes 1572868
  141.3 2.7 %collective-permute-start.27 = (bf16[4,256,512]{2,1,0:T(8,128)(2,1)S(1)}, bf16[4,256,512]{2,1,0:T(8,128)(2,1)S(1)}, u32[]{:S(2)}, u32[]{:S(2)}) collective-permute-start(bf16[4,256,512]{2,1,0:T(8,128)(2,1)S(1)} %shard_map.150.pm_ref), channel_id=1, source_target_pairs={{0,2},{2,0},{1,3},{3,1},{4,6},{6,4},{5,7},{7,5},{8,10},{10,8},{9,1... | collective-permute-start | bytes 3145736 | tf_op jit(solution)/shard_map/ppermute | solution.py:74
  141.4 4.3 %collective-permute-start.23 = (bf16[4,256,512]{2,1,0:T(8,128)(2,1)S(1)}, bf16[4,256,512]{2,1,0:T(8,128)(2,1)}, u32[]{:S(2)}, u32[]{:S(2)}) collective-permute-start(bf16[4,256,512]{2,1,0:T(8,128)(2,1)S(1)} %get-tuple-element.24.om_ref), channel_id=1, source_target_pairs={{0,2},{2,0},{1,3},{3,1},{4,6},{6,4},{5,7},{7,5},{8,10},{10,8},{9,1... | collective-permute-start | bytes 3145736 | tf_op jit(solution)/shard_map/ppermute | solution.py:74
  145.7 1.0 copy-start.3
  149.8 11.7 %collective-permute-start.30 = (bf16[1,256,256]{2,1,0:T(8,128)(2,1)S(1)}, bf16[1,256,256]{2,1,0:T(8,128)(2,1)S(1)}, u32[]{:S(2)}, u32[]{:S(2)}) collective-permute-start(bf16[1,256,256]{2,1,0:T(8,128)(2,1)S(1)} %shard_map.154), channel_id=1, source_target_pairs={{0,12},{4,0},{8,4},{12,8},{1,13},{5,1},{9,5},{13,9},{2,14},{6,2},{... | collective-permute-start | bytes 393224 | tf_op jit(solution)/shard_map/ppermute | solution.py:78
  154.1 7.3 %collective-permute-start.29 = (bf16[1,256,256]{2,1,0:T(8,128)(2,1)S(1)}, bf16[1,256,256]{2,1,0:T(8,128)(2,1)S(1)}, u32[]{:S(2)}, u32[]{:S(2)}) collective-permute-start(bf16[1,256,256]{2,1,0:T(8,128)(2,1)S(1)} %shard_map.153), channel_id=1, source_target_pairs={{0,8},{4,12},{8,0},{12,4},{1,9},{5,13},{9,1},{13,5},{2,10},{6,14},... | collective-permute-start | bytes 393224 | tf_op jit(solution)/shard_map/ppermute | solution.py:78
  154.6 3.8 %copy-start.4 = (bf16[4,256,256]{2,1,0:T(8,128)(2,1)S(1)}, bf16[4,256,256]{2,1,0:T(8,128)(2,1)}, u32[]{:S(2)}) copy-start(bf16[4,256,256]{2,1,0:T(8,128)(2,1)} %copy-done.2) | copy-start | bytes 1572868
  157.6 6.4 %collective-permute-start.28 = (bf16[1,256,256]{2,1,0:T(8,128)(2,1)S(1)}, bf16[1,256,256]{2,1,0:T(8,128)(2,1)S(1)}, u32[]{:S(2)}, u32[]{:S(2)}) collective-permute-start(bf16[1,256,256]{2,1,0:T(8,128)(2,1)S(1)} %shard_map.152), channel_id=1, source_target_pairs={{0,4},{4,8},{8,12},{12,0},{1,5},{5,9},{9,13},{13,1},{2,6},{6,10},{... | collective-permute-start | bytes 393224 | tf_op jit(solution)/shard_map/ppermute | solution.py:78

commit v5 on v4

--- a/solution.py
+++ b/solution.py
@@ -12,10 +12,12 @@
 D = 4096
 CH = 512
 CTX = ("yl", "z", "x", "c")
+ROW = ("x", "c")
 SWAP = [(0, 1), (1, 0)]
 BF = jnp.bfloat16
 F32 = jnp.float32
 LOG2E = 1.4426950408889634
+NO_COST = pl.CostEstimate(flops=0, bytes_accessed=0, transcendentals=0)
 
 
 def elu(v):
@@ -66,7 +68,7 @@
         out_shape=jax.ShapeDtypeStruct((BLOCK, CH), BF),
         scratch_shapes=[pltpu.VMEM((528, CH), F32), pltpu.VMEM((CH // 128, 520, 128), F32)],
         compiler_params=params(20),
-        cost_estimate=pl.CostEstimate(flops=1100000000, bytes_accessed=4 << 20, transcendentals=600000),
+        cost_estimate=NO_COST,
     )(halo, audio, taps, back, down)
 
 
@@ -106,7 +108,7 @@
 
 
 def unused(after):
-    return [pl.BlockSpec(memory_space=pl.ANY)] * len(after)
+    return in_vmem(len(after))
 
 
 def stack_kernel(n, *refs):
@@ -121,6 +123,7 @@
         out_specs=pl.BlockSpec(memory_space=pltpu.VMEM),
         out_shape=jax.ShapeDtypeStruct((len(parts),) + parts[0].shape, parts[0].dtype),
         compiler_params=params(4),
+        cost_estimate=NO_COST,
     )(*parts, *after)
 
 
@@ -172,7 +175,7 @@
         ),
         out_shape=jax.ShapeDtypeStruct((8, 32, 896), BF),
         compiler_params=params(16),
-        cost_estimate=pl.CostEstimate(flops=210000000, bytes_accessed=2 << 20, transcendentals=0),
+        cost_estimate=NO_COST,
     )(at, *ws, mine, rest, gain, gain, table, table, *after)
 
 
@@ -196,36 +199,50 @@
         out_specs=in_vmem(2),
         out_shape=[jax.ShapeDtypeStruct((8, 32, 768), BF), jax.ShapeDtypeStruct((8, 768), F32)],
         compiler_params=params(8),
+        cost_estimate=NO_COST,
     )(packed, *after)
 
 
-def give_kernel(at_ref, latent_ref, embed_ref, *refs):
-    refs[-1][...] = dot(latent_ref[...], embed_ref[...]).astype(BF)
-
-
-def give_term(at, latent, embed, after):
-    return pl.pallas_call(
-        give_kernel,
+def term_kernel(at_ref, latent_ref, embed_ref, *refs):
+    give_ref, own_ref = refs[-2:]
+    term = dot(latent_ref[...], embed_ref[...])
+    mine = at_ref[5] == pl.program_id(0) // 2
+
+    @pl.when(mine)
+    def _():
+        own_ref[...] = term
+
+    @pl.when(jnp.logical_not(mine))
+    def _():
+        give_ref[...] = term.astype(BF)
+
+
+def terms(at, latent, embed, after):
+    def give_at(i, at):
+        return (0, jnp.where(at[5] == 0, jnp.maximum(i - 2, 0), jnp.minimum(i, 1)))
+
+    def own_at(i, at):
+        return (0, jnp.where(at[5] == 1, jnp.maximum(i - 2, 0), jnp.minimum(i, 1)))
+
+    return pl.pallas_call(
+        term_kernel,
         grid_spec=pltpu.PrefetchScalarGridSpec(
             num_scalar_prefetch=1,
-            grid=(2,),
-            in_specs=[
-                pl.BlockSpec((BLOCK, CH), lambda i, at: (0, 0)),
-                pl.BlockSpec((CH, 1024), lambda i, at: (0, (1 - at[5]) * 2 + i)),
-            ]
+            grid=(4,),
+            in_specs=[pl.BlockSpec((BLOCK, CH), lambda i, at: (0, 0)), pl.BlockSpec((CH, 1024), lambda i, at: (0, i))]
             + unused(after),
-            out_specs=pl.BlockSpec((BLOCK, 1024), lambda i, at: (0, i)),
+            out_specs=[pl.BlockSpec((BLOCK, 1024), give_at), pl.BlockSpec((BLOCK, 1024), own_at)],
         ),
-        out_shape=jax.ShapeDtypeStruct((BLOCK, D // 2), BF),
+        out_shape=[jax.ShapeDtypeStruct((BLOCK, D // 2), BF), jax.ShapeDtypeStruct((BLOCK, D // 2), F32)],
         compiler_params=params(16),
-        cost_estimate=pl.CostEstimate(flops=540000000, bytes_accessed=3 << 20, transcendentals=0),
+        cost_estimate=NO_COST,
     )(at, latent, embed, *after)
 
 
-def embed_kernel(at_ref, latent_ref, embed_ref, got_ref, active_ref, table_ref, out_ref, square_ref):
+def embed_kernel(at_ref, own_ref, got_ref, active_ref, table_ref, out_ref, square_ref):
     act = active_ref[:, pl.ds(at_ref[3] + 4, 1), :].reshape(2, BLOCK)
     cols = jnp.concatenate([act, jnp.zeros((6, BLOCK), F32)], axis=0).T
-    x = dot(latent_ref[...], embed_ref[...]) + got_ref[...].astype(F32)
+    x = own_ref[...] + got_ref[...].astype(F32)
     x = x + cols[:, 0:1] * table_ref[0:1] + cols[:, 1:2] * table_ref[1:2]
     out_ref[...] = x.astype(BF)
     square = jnp.sum(x * x, axis=1, keepdims=True)
@@ -240,8 +257,7 @@
         square_ref[...] += square
 
 
-def embed_rows(at, latent, embed, got, active, table):
-    mine = lambda rows: pl.BlockSpec((rows, 1024), lambda i, at: (0, at[5] * 2 + i))
+def embed_rows(at, own, got, active, table):
     tile = pl.BlockSpec((BLOCK, 1024), lambda i, at: (0, i))
     return pl.pallas_call(
         embed_kernel,
@@ -249,21 +265,20 @@
             num_scalar_prefetch=1,
             grid=(2,),
             in_specs=[
-                pl.BlockSpec((BLOCK, CH), lambda i, at: (0, 0)),
-                mine(CH),
+                tile,
                 tile,
                 pl.BlockSpec((2, 8, BLOCK), lambda i, at: (0, 0, 0)),
-                mine(2),
+                pl.BlockSpec((2, 1024), lambda i, at: (0, at[5] * 2 + i)),
             ],
             out_specs=[tile, pl.BlockSpec((8, BLOCK), lambda i, at: (0, 0))],
         ),
         out_shape=[jax.ShapeDtypeStruct((BLOCK, D // 2), BF), jax.ShapeDtypeStruct((8, BLOCK), F32)],
-        compiler_params=params(20),
-        cost_estimate=pl.CostEstimate(flops=540000000, bytes_accessed=5 << 20, transcendentals=0),
-    )(at, latent, embed, got, active, table)
-
-
-def project_rows(row, blocks, m_ref, line_ref, active_ref, scales, at_ref, kv_ref, q_ref):
+        compiler_params=params(16),
+        cost_estimate=NO_COST,
+    )(at, own, got, active, table)
+
+
+def project_rows(row, blocks, m_ref, line_ref, active_ref, at_ref, kv_ref, q_ref):
     x = at_ref[3]
     cols = slice(0, 768) if q_ref is not None else slice(256, 768)
     w0, w1 = m_ref[0:512, cols], m_ref[512:1024, cols]
@@ -271,26 +286,26 @@
     for dx in range(4):
         at = lax.rem(x + dx, 4)
         act = active_ref[:, pl.ds(4 * row + at, 1), :].reshape(2, BLOCK)
-        side = jnp.concatenate([act, scales[dx][row : row + 1, :], jnp.zeros((5, BLOCK), F32)], axis=0).T
+        side = jnp.concatenate([act, jnp.zeros((6, BLOCK), F32)], axis=0).T
         acc = dot(blocks[dx][0], w0) + dot(blocks[dx][1], w1)
-        acc = (acc + side[:, 0:1] * line[0:1] + side[:, 1:2] * line[1:2]) * side[:, 2:3]
+        acc = acc + side[:, 0:1] * line[0:1] + side[:, 1:2] * line[1:2]
         kv_ref[at] = acc[:, -512:].astype(BF)
         if q_ref is not None:
-            q_ref[at] = (acc[:, :256] * (HD**-0.5 * LOG2E)).astype(BF)
-
-
-def project_own_kernel(at_ref, a, al, ar, af, m00, m01, m10, m11, line_ref, active_ref, s0, s1, s2, s3, kv_ref, q_ref, m_ref):
+            q_ref[at] = acc[:, :256]
+
+
+def project_own_kernel(at_ref, a, al, ar, af, m00, m01, m10, m11, line_ref, active_ref, kv_ref, q_ref, m_ref):
     core, yl = at_ref[4], at_ref[6]
     for y, pair in enumerate(((m00, m01), (m10, m11))):
         for c, ref in enumerate(pair):
             row = ((yl ^ y) * 2 + (core ^ c)) * 128
             for s in range(2):
                 m_ref[pl.ds(pl.multiple_of(s * 512 + row, 128), 128), :] = ref[s * 128 : (s + 1) * 128, :]
-    project_rows(1, (a, ar, af, al), m_ref, line_ref, active_ref, (s0, s1, s2, s3), at_ref, kv_ref, q_ref)
-
-
-def project_prev_kernel(at_ref, b, bl, br, bf, m_ref, line_ref, active_ref, s0, s1, s2, s3, kv_ref):
-    project_rows(0, (b, br, bf, bl), m_ref, line_ref, active_ref, (s0, s1, s2, s3), at_ref, kv_ref, None)
+    project_rows(1, (a, ar, af, al), m_ref, line_ref, active_ref, at_ref, kv_ref, q_ref)
+
+
+def project_prev_kernel(at_ref, b, bl, br, bf, m_ref, line_ref, active_ref, after_ref, kv_ref):
+    project_rows(0, (b, br, bf, bl), m_ref, line_ref, active_ref, at_ref, kv_ref, None)
 
 
 def project(kernel, outs, *args):
@@ -298,31 +313,34 @@
         kernel,
         in_specs=[pl.BlockSpec(memory_space=pltpu.SMEM)] + in_vmem(len(args) - 1),
         out_specs=in_vmem(len(outs)),
-        out_shape=[jax.ShapeDtypeStruct(o, BF) for o in outs],
-        compiler_params=params(16),
-        cost_estimate=pl.CostEstimate(flops=1600000000, bytes_accessed=6 << 20, transcendentals=0),
+        out_shape=outs,
+        compiler_params=params(10),
+        cost_estimate=NO_COST,
     )(*args)
 
 
-def attention_kernel(place_ref, q_ref, om_ref, ot_ref, pm_ref, pt_ref, o_ref):
+def attention_kernel(place_ref, q_ref, om_ref, ot_ref, pm_ref, pt_ref, own_ref, prev_ref, o_ref):
     at = lax.rem(place_ref[0] + place_ref[3], 4)
     core = place_ref[1]
     first = place_ref[2]
     rows = lax.broadcasted_iota(jnp.int32, (BLOCK, BLOCK), 0)
     cols = lax.broadcasted_iota(jnp.int32, (BLOCK, BLOCK), 1)
     blocks = []
-    for own_ref, prev_ref, begin in ((om_ref, pm_ref, at + 1), (ot_ref, pt_ref, at + core)):
+    for kv_own, kv_prev, begin, parity in ((om_ref, pm_ref, at + 1, core), (ot_ref, pt_ref, at + core, 1 - core)):
         for j in range(4):
             m = begin + j
             i = lax.rem(m, 4)
-            blocks.append((jnp.where(m >= 4, own_ref[i], prev_ref[i]), jnp.where((m < 4) & (first == 1), 1e30, 0.0)))
+            kv = jnp.where(m >= 4, kv_own[i], kv_prev[i])
+            factor = jnp.where(m >= 4, own_ref[pl.ds(2 * i + parity, 1), :], prev_ref[pl.ds(2 * i + parity, 1), :])
+            blocks.append((kv, factor, jnp.where((m < 4) & (first == 1), 1e30, 0.0)))
+    mine = jnp.broadcast_to(own_ref[pl.ds(2 * at + core, 1), :] * (HD**-0.5 * LOG2E), (8, BLOCK)).T[:, 0:1]
     contract = (((1,), (1,)), ((), ()))
     for h in range(2):
-        q = q_ref[at, :, h * HD : (h + 1) * HD]
+        q = (q_ref[at, :, h * HD : (h + 1) * HD] * mine).astype(BF)
         scores = []
         top = None
-        for n, (kv, penalty) in enumerate(blocks):
-            s = lax.dot_general(q, kv[:, h * HD : (h + 1) * HD], contract, preferred_element_type=F32)
+        for n, (kv, factor, penalty) in enumerate(blocks):
+            s = lax.dot_general(q, kv[:, h * HD : (h + 1) * HD], contract, preferred_element_type=F32) * factor
             if n == 3:
                 s = jnp.where(cols <= rows, s, -1e30)
             if n == 4:
@@ -332,21 +350,21 @@
             scores.append(s)
         total = jnp.zeros((BLOCK, 1), F32)
         o = jnp.zeros((BLOCK, HD), F32)
-        for s, (kv, penalty) in zip(scores, blocks):
+        for s, (kv, factor, penalty) in zip(scores, blocks):
             p = jnp.exp2(s - (top + penalty))
             total += jnp.sum(p, axis=1, keepdims=True)
-            o += dot(p.astype(BF), kv[:, 256 + h * HD : 256 + (h + 1) * HD])
+            o += dot((p * factor).astype(BF), kv[:, 256 + h * HD : 256 + (h + 1) * HD])
         o_ref[0, :, h * HD : (h + 1) * HD] = (o / total).astype(BF)
 
 
 def attention(place, dx, *args):
     return pl.pallas_call(
         attention_kernel,
-        in_specs=[pl.BlockSpec(memory_space=pltpu.SMEM)] + in_vmem(5),
+        in_specs=[pl.BlockSpec(memory_space=pltpu.SMEM)] + in_vmem(7),
         out_specs=pl.BlockSpec(memory_space=pltpu.VMEM),
         out_shape=jax.ShapeDtypeStruct((1, BLOCK, 256), BF),
-        compiler_params=params(16),
-        cost_estimate=pl.CostEstimate(flops=8 * BLOCK * 2048 * HD, bytes_accessed=5 << 20, transcendentals=2 * BLOCK * 2048),
+        compiler_params=params(8),
+        cost_estimate=NO_COST,
     )(jnp.concatenate([place, jnp.array([dx], jnp.int32)]), *args)
 
 
@@ -394,10 +412,12 @@
     rest = swap(mine, "tp")
 
     latent = encoder(halo, audio, res_conv[0], res_out[0], down_conv[0])
+    give, own = terms(at, latent, embed, ())
     other = swap(latent, "tp")
     a = stack([latent, other])
+    prev = lax.ppermute(latent, ("yl", "z"), behind)
+    b = stack([prev, lax.ppermute(other, ("yl", "z"), behind)])
     al, ar = shift(a, 1), shift(a, 3)
-    b = stack([lax.ppermute(latent, ("yl", "z"), behind), lax.ppermute(other, ("yl", "z"), behind)])
     bl, br = shift(b, 1), shift(b, 3)
     af, bf = shift(al, 1), shift(br, 3)
 
@@ -405,15 +425,9 @@
     w10 = swap(w00, "yl")
     w01 = swap(w00, "c")
     w11 = swap(w10, "c")
-    packed = partial_weights(at, (w00, w01, w10, w11), mine, rest, norm_gain[None], speaker_table, (a,))
+    packed = partial_weights(at, (w00, w01, w10, w11), mine, rest, norm_gain[None], speaker_table, (give, a, prev))
     packed = lax.all_to_all(packed, "z", 0, 0, tiled=True)
-    give = give_term(at, latent, embed, (b,))
-    m, lines = sum_weights(packed, (al, ar, give))
-    m00 = lax.all_to_all(m, "z", 0, 0, tiled=True).reshape(256, 768)
-    m10 = swap(m00, "yl")
-    m01 = swap(m00, "c")
-    m11 = swap(m10, "c")
-
+    m, lines = sum_weights(packed, (al, ar, b))
     bounds = jnp.cumsum(turn_lengths, axis=1)
     start = ((row - 1 + jnp.arange(2)[:, None]) * 8 + 2 * jnp.arange(4)[None, :] + core) * BLOCK
     frames = start.reshape(8, 1) + jnp.arange(BLOCK)
@@ -421,23 +435,32 @@
     active = (turn % 2 == 1).astype(F32)
 
     got = swap(give, "tp")
-    embedded, square = embed_rows(at, latent, embed, got, active, speaker_table)
+    embedded, square = embed_rows(at, own, got, active, speaker_table)
     square = square + swap(square, "tp")
     scale = lax.rsqrt(square[0:1] * (1.0 / D) + 1e-05)
-    scale = jnp.concatenate([lax.ppermute(scale, ("yl", "z"), behind), scale])
-    scales = [scale] + [shift(scale, 4 - dx) for dx in (1, 2, 3)]
-
-    kv, half = (4, BLOCK, 512), (4, BLOCK, 256)
-    side = (active, *scales)
-    om, q, whole = project(project_own_kernel, (kv, half, (1024, 768)), at, a, al, ar, af, m00, m01, m10, m11, lines, *side)
+    m00 = lax.all_to_all(m, "z", 0, 0, tiled=True).reshape(256, 768)
+    (m00,) = stack([m00], (scale, bl, br))
+    m10 = swap(m00, "yl")
+    m01 = swap(m00, "c")
+    scales = lax.all_to_all(jnp.broadcast_to(scale, (8, BLOCK)), ROW, 0, 0, tiled=True)
+    (m10,) = stack([m10], (scales,))
+    m11 = swap(m10, "c")
+    scales_prev = lax.ppermute(scales, ("yl", "z"), behind)
+
+    kv = jax.ShapeDtypeStruct((4, BLOCK, 512), BF)
+    half = jax.ShapeDtypeStruct((4, BLOCK, 256), F32)
+    full = jax.ShapeDtypeStruct((1024, 768), BF)
+    om, q, whole = project(
+        project_own_kernel, (kv, half, full), at, a, al, ar, af, m00, m01, m10, m11, lines, active
+    )
     ot = swap(om, "c")
-    (pm,) = project(project_prev_kernel, (kv,), at, b, bl, br, bf, whole, lines, *side)
+    (pm,) = project(project_prev_kernel, (kv,), at, b, bl, br, bf, whole, lines, active, scales_prev)
     pt = swap(pm, "c")
 
     place = jnp.stack([x_at, core, (row == 0).astype(jnp.int32)]).astype(jnp.int32)
     parts = [None] * 4
     for dx in (2, 1, 3, 0):
-        part = attention(place, dx, q, om, ot, pm, pt)
+        part = attention(place, dx, q, om, ot, pm, pt, scales, scales_prev)
         parts[dx] = shift(part, dx) if dx else part
     return embedded, collect(place, parts)
 

time: 167 us -> 145 us (0.87)
  waiting for transfers between devices: 69.6 us -> 35 us
  blocking collectives: 0 us -> 8.24 us
  Pallas kernels: 32.3 us -> 37.5 us
  local copies, waits for them, and re-layouts: 11.4 us -> 8.03 us
  starting transfers between devices: 50.3 us -> 53.6 us
    ppermute x15 -> x12, waiting for transfers between devices: 19.5 us -> 2.36 us  [shift(): return lax.ppermute(a, 'x', [(i, (i + by) % 4) for i in range(4)])]
    all_to_all x1, waiting for transfers between devices: 11.8 us -> 0.01 us  [on_device(): m00 = lax.all_to_all(m, 'z', 0, 0, tiled=True).reshape(256, 768)]
    ppermute x12, starting transfers between devices: 6.11 us -> 16.8 us  [swap(): return lax.ppermute(a, axis, SWAP)]
    all_to_all x0 -> x1, blocking collectives: none -> 8.24 us  [on_device(): lax.all_to_all(jnp.broadcast_to(scale, (8, BLOCK)), ROW, 0, 0, tiled=True)]
    ppermute x3, waiting for transfers between devices: 18.2 us -> 11.3 us  [the longest x1 9.86 us: on_device(): b = stack([prev, lax.ppermute(other, ('yl', 'z'), behind)])]
    unnamed x42 -> x45, local copies, waits for them, and re-layouts: 10.7 us -> 7.33 us
    ppermute x1, waiting for transfers between devices: 4.37 us -> 7.26 us  [on_device(): halo = lax.ppermute(audio[-8:], CTX, [(i, i + 1) for i in range(127)])]
    all_to_all x1, starting transfers between devices: 7.65 us -> 4.76 us  [on_device(): packed = lax.all_to_all(packed, 'z', 0, 0, tiled=True)]
  transfers between devices with their start and end apart: 33 -> 30, of which waited for: 16 -> 11; matrix products, arithmetic and copies ran while one was open for 1% -> 1% of each run, Pallas kernels for 13% -> 17%
where the time goes in v5:
time: 145 us; the launch traced here: 144 us
  starting transfers between devices  53.6 us (37%)
  Pallas kernels  37.5 us (26%)
  waiting for transfers between devices  35 us (24%)
  blocking collectives  8.24 us (6%)
  local copies, waits for them, and re-layouts  8.03 us (6%)
    ppermute x12, starting transfers between devices, shift(): return lax.ppermute(a, 'x', [(i, (i + by) % 4) for i in range(4)])  18.7 us
    ppermute x12, starting transfers between devices, swap(): return lax.ppermute(a, axis, SWAP)  16.8 us
    pallas_call x4, Pallas kernels, attention(): pl.pallas_call(attention_kernel, in_specs=[pl.BlockSpec(memory_space=pltp...  14.7 us
    ppermute x12, waiting for transfers between devices, swap(): return lax.ppermute(a, axis, SWAP)  14.1 us
    ppermute x1, waiting for transfers between devices, on_device(): b = stack([prev, lax.ppermute(other, ('yl', 'z'), behind)])  9.86 us
    all_to_all x1, blocking collectives, on_device(): lax.all_to_all(jnp.broadcast_to(scale, (8, BLOCK)), ROW, 0, 0, tiled=True)  8.24 us
    unnamed x45, local copies, waits for them, and re-layouts  7.33 us
    ppermute x1, waiting for transfers between devices, on_device(): halo = lax.ppermute(audio[-8:], CTX, [(i, i + 1) for i in range(127)])  7.26 us
  transfers between devices with their start and end apart: 30, of which 11 were waited for; matrix products, arithmetic and copies ran while one was open for 1% of the time, Pallas kernels for 17%

profile of v5, /device:TPU:8, one launch (start us, length us, event | category | flops | bytes accessed | tf_op | source)
XLA Modules:
  0.0 144.2 jit_solution(669394732990103217)
XLA Ops:
  0.6 0.6 stack.42.at_ref
  1.3 2.7 %shard_map.144 = (bf16[3,32,256]{2,1,0:T(8,128)(2,1)}, bf16[3,32,256]{2,1,0:T(8,128)(2,1)}, bf16[3,32,256]{2,1,0:T(8,128)(2,1)}, bf16[3,32,256]{2,1,0:T(8,128)(2,1)}, bf16[2,128,256]{2,1,0:T(8,128)(2,1)}) custom-call(s32[7]{0:T(128)} %stack.42.at_ref, bf16[3,32,1024]{2,1,0:T(8,128)(2,1)} %w_ref.1, bf16[512,4096]{1,0:T(8,128)(2,1)} %bitcast.23, ...), custom_call_target="tpu_custom_call" | custom-call | tf_op jit(solution)/shard_map/pallas_call | solution.py:94
  4.0 2.3 %collective-permute-start.9 = (bf16[2,128,256]{2,1,0:T(8,128)(2,1)}, bf16[2,128,256]{2,1,0:T(8,128)(2,1)S(1)}, u32[]{:S(2)}, u32[]{:S(2)}) collective-permute-start(bf16[2,128,256]{2,1,0:T(8,128)(2,1)} %get-tuple-element.23.mine_ref), channel_id=1, source_target_pairs={{0,1},{1,0},{2,3},{3,2},{4,5},{5,4},{6,7},{7,6},{8,9},{9,8},{10,11... | collective-permute-start | bytes 393224 | tf_op jit(solution)/shard_map/ppermute | solution.py:76
  6.3 1.5 %collective-permute-start.6 = (bf16[3,32,256]{2,1,0:T(8,128)(2,1)}, bf16[3,32,256]{2,1,0:T(8,128)(2,1)S(1)}, u32[]{:S(2)}, u32[]{:S(2)}) collective-permute-start(bf16[3,32,256]{2,1,0:T(8,128)(2,1)} %get-tuple-element.20), channel_id=1, source_target_pairs={{0,4},{4,8},{8,12},{12,0},{1,5},{5,9},{9,13},{13,1},{2,6},{6,10},{... | collective-permute-start | bytes 147464 | tf_op jit(solution)/shard_map/ppermute | solution.py:80
  7.8 2.7 %collective-permute-start.7 = (bf16[3,32,256]{2,1,0:T(8,128)(2,1)}, bf16[3,32,256]{2,1,0:T(8,128)(2,1)S(1)}, u32[]{:S(2)}, u32[]{:S(2)}) collective-permute-start(bf16[3,32,256]{2,1,0:T(8,128)(2,1)} %get-tuple-element.21), channel_id=1, source_target_pairs={{0,8},{4,12},{8,0},{12,4},{1,9},{5,13},{9,1},{13,5},{2,10},{6,14},... | collective-permute-start | bytes 147464 | tf_op jit(solution)/shard_map/ppermute | solution.py:80
  10.5 1.4 collective-permute-start.8
  11.9 1.9 %collective-permute-start = (bf16[8,512]{1,0:T(8,128)(2,1)S(1)}, bf16[8,512]{1,0:T(8,128)(2,1)S(1)}, u32[]{:S(2)}, u32[]{:S(2)}) collective-permute-start(bf16[8,512]{1,0:T(8,128)(2,1)S(1)} %slice_bitcast_fusion), channel_id=1, source_target_pairs={{0,2},{2,4},{4,6},{6,8},{8,10},{10,12},{12,14},{14,16},{16,18},{18... | collective-permute-start | bytes 24584 | tf_op jit(solution)/shard_map/ppermute | solution.py:408
  13.9 7.3 %collective-permute-done.halo_ref = bf16[8,512]{1,0:T(8,128)(2,1)S(1)} collective-permute-done((bf16[8,512]{1,0:T(8,128)(2,1)S(1)}, bf16[8,512]{1,0:T(8,128)(2,1)S(1)}, u32[]{:S(2)}, u32[]{:S(2)}) %collective-permute-start) | collective-permute-done | bytes 8224 | tf_op jit(solution)/shard_map/ppermute | solution.py:408
  21.1 0.9 copy-done.16
  22.1 2.5 %shard_map.140.latent_ref.refs_0_.refs_4_ = bf16[256,512]{1,0:T(8,128)(2,1)S(1)} custom-call(bf16[8,512]{1,0:T(8,128)(2,1)S(1)} %collective-permute-done.halo_ref, bf16[512,512]{1,0:T(8,128)(2,1)S(1)} %bitcast.34, bf16[3,512,256]{2,1,0:T(8,128)(2,1)S(1)} %bitcast.33, bf16[256,512]{1,0:T(8,128)(2,1)S(1)} %bitcast.41, bf16[4,512,512]{2,1,0:T(8,128)(2,1)S(1)} %bitcast.26), custom_call_target="tpu_custom_call" | custom-call | tf_op jit(solution)/shard_map/pallas_call | solution.py:64
  24.7 0.8 copy-done.19
  25.5 0.1 collective-permute-start.11
  25.6 1.3 collective-permute-start.2
  26.9 1.9 %collective-permute-start.13 = (bf16[256,512]{1,0:T(8,128)(2,1)S(1)}, bf16[256,512]{1,0:T(8,128)(2,1)S(1)}, u32[]{:S(2)}, u32[]{:S(2)}) collective-permute-start(bf16[256,512]{1,0:T(8,128)(2,1)S(1)} %shard_map.140.latent_ref.refs_0_.refs_4_), channel_id=1, source_target_pairs={{0,16},{16,32},{32,48},{48,64},{64,80},{80,96},{96,112},{112,128},... | collective-permute-start | bytes 786440 | tf_op jit(solution)/shard_map/ppermute | solution.py:418
  28.9 0.1 collective-permute-start.10
  29.0 5.1 %collective-permute-done.11.w10 = bf16[4,3,32,256]{3,2,1,0:T(8,128)(2,1)S(1)} collective-permute-done((bf16[4,3,32,256]{3,2,1,0:T(8,128)(2,1)S(1)}, bf16[4,3,32,256]{3,2,1,0:T(8,128)(2,1)S(1)}, u32[]{:S(2)}, u32[]{:S(2)}) %collective-permute-start.11) | collective-permute-done | bytes 196640 | tf_op jit(solution)/shard_map/ppermute | solution.py:76
  34.1 3.1 %shard_map.141 = (bf16[256,2048]{1,0:T(8,128)(2,1)S(1)}, f32[256,2048]{1,0:T(8,128)S(1)}) custom-call(s32[7]{0:T(128)S(1)} %copy-done.20, bf16[256,512]{1,0:T(8,128)(2,1)S(1)} %shard_map.140.latent_ref.refs_0_.refs_4_, bf16[512,4096]{1,0:T(8,128)(2,1)S(1)} %bitcast.25), custom_call_target="tpu_custom_call" | custom-call | tf_op jit(solution)/shard_map/pallas_call | solution.py:227
  37.2 1.3 copy-done.5
  38.6 0.4 collective-permute-done.13.refs_2_.refs_0_
  39.0 0.5 copy-done.12
  39.5 2.0 %shard_map.146 = bf16[8,32,896]{2,1,0:T(8,128)(2,1)} custom-call(s32[7]{0:T(128)S(1)} %copy-done.20, bf16[4,3,32,256]{3,2,1,0:T(8,128)(2,1)S(1)} %shard_map.145.w00, bf16[4,3,32,256]{3,2,1,0:T(8,128)(2,1)S(1)} %collective-permute-done.10.w01, bf16[4,3,32,256]{3,2,1,0:T(8,128)(2,1)S(1)} %collective-permute-done.11.w10, ...), custom_call_target="tpu_custom_call" | custom-call | tf_op jit(solution)/shard_map/pallas_call | solution.py:164
  41.5 4.8 %all-to-all-start = ((bf16[8,32,896]{2,1,0:T(8,128)(2,1)}), bf16[8,32,896]{2,1,0:T(8,128)(2,1)S(1)}, u32[]{:S(2)}, u32[]{:S(2)}) async-start(bf16[8,32,896]{2,1,0:T(8,128)(2,1)} %shard_map.146), calls=%async_computation | async-start | bytes 917504 | tf_op jit(solution)/shard_map/all_to_all | solution.py:429
  46.3 0.1 collective-permute-start.3
  46.3 3.2 %collective-permute-start.4 = (bf16[2,256,512]{2,1,0:T(8,128)(2,1)S(1)}, bf16[2,256,512]{2,1,0:T(8,128)(2,1)S(1)}, u32[]{:S(2)}, u32[]{:S(2)}) collective-permute-start(bf16[2,256,512]{2,1,0:T(8,128)(2,1)S(1)} %shard_map.143.refs_1_.a), channel_id=1, source_target_pairs={{0,12},{4,0},{8,4},{12,8},{1,13},{5,1},{9,5},{13,9},{2,14},{6,2},{... | collective-permute-start | bytes 1572872 | tf_op jit(solution)/shard_map/ppermute | solution.py:80
  49.6 3.3 %collective-permute-start.1 = (bf16[256,2048]{1,0:T(8,128)(2,1)}, bf16[256,2048]{1,0:T(8,128)(2,1)}, u32[]{:S(2)}, u32[]{:S(2)}) collective-permute-start(bf16[256,2048]{1,0:T(8,128)(2,1)} %copy-done.12), channel_id=1, source_target_pairs={{0,1},{1,0},{2,3},{3,2},{4,5},{5,4},{6,7},{7,6},{8,9},{9,8},{10,11... | collective-permute-start | bytes 3145736 | tf_op jit(solution)/shard_map/ppermute | solution.py:76
  52.8 3.8 %collective-permute-start.14 = (bf16[256,512]{1,0:T(8,128)(2,1)S(1)}, bf16[256,512]{1,0:T(8,128)(2,1)S(1)}, u32[]{:S(2)}, u32[]{:S(2)}) collective-permute-start(bf16[256,512]{1,0:T(8,128)(2,1)S(1)} %collective-permute-done.2.refs_1_), channel_id=1, source_target_pairs={{0,16},{16,32},{32,48},{48,64},{64,80},{80,96},{96,112},{112,128},... | collective-permute-start | bytes 786440 | tf_op jit(solution)/shard_map/ppermute | solution.py:419
  56.8 0.1 mul.48
  56.9 9.9 %collective-permute-done.14.refs_1_ = bf16[256,512]{1,0:T(8,128)(2,1)S(1)} collective-permute-done((bf16[256,512]{1,0:T(8,128)(2,1)S(1)}, bf16[256,512]{1,0:T(8,128)(2,1)S(1)}, u32[]{:S(2)}, u32[]{:S(2)}) %collective-permute-start.14) | collective-permute-done | bytes 262176 | tf_op jit(solution)/shard_map/ppermute | solution.py:419
  66.8 0.9 shard_map.148
  67.8 3.8 %all-to-all-start.1 = ((bf16[8,32,768]{2,1,0:T(8,128)(2,1)}), bf16[8,32,768]{2,1,0:T(8,128)(2,1)S(1)}, u32[]{:S(2)}, u32[]{:S(2)}) async-start(bf16[8,32,768]{2,1,0:T(8,128)(2,1)} %get-tuple-element.24), calls=%async_computation.1 | async-start | bytes 786432 | tf_op jit(solution)/shard_map/all_to_all | solution.py:441
  71.6 0.2 reduce_window_sum.11
  71.8 0.8 collective-permute-start.17
  72.6 1.3 collective-permute-start.16
  73.9 0.1 convert_reduce_fusion
  74.0 2.1 %collective-permute-done.1.got_ref = bf16[256,2048]{1,0:T(8,128)(2,1)} collective-permute-done((bf16[256,2048]{1,0:T(8,128)(2,1)}, bf16[256,2048]{1,0:T(8,128)(2,1)}, u32[]{:S(2)}, u32[]{:S(2)}) %collective-permute-start.1) | collective-permute-done | bytes 1048608 | tf_op jit(solution)/shard_map/ppermute | solution.py:76
  76.1 1.6 %copy-done.6 = f32[256,2048]{1,0:T(8,128)S(1)} copy-done((f32[256,2048]{1,0:T(8,128)S(1)}, f32[256,2048]{1,0:T(8,128)}, u32[]{:S(2)}) %copy-start.6) | copy-done | bytes 2097176
  77.7 3.6 %shard_map.142 = (bf16[256,2048]{1,0:T(8,128)(2,1)}, f32[8,256]{1,0:T(8,128)S(1)}) custom-call(s32[7]{0:T(128)S(1)} %copy-done.20, f32[256,2048]{1,0:T(8,128)S(1)} %copy-done.6, bf16[256,2048]{1,0:T(8,128)(2,1)} %collective-permute-done.1.got_ref, f32[2,8,256]{2,1,0:T(8,128)S(1)} %fusion.2.active_ref, f32[2,4096]{1,0:T(2,128)S(1)} %copy-done.15), custom_call_target="tpu_custom_call" | custom-call | tf_op jit(solution)/shard_map/pallas_call | solution.py:262
  81.3 1.9 %collective-permute-start.15 = (f32[8,256]{1,0:T(8,128)S(1)}, f32[8,256]{1,0:T(8,128)S(1)}, u32[]{:S(2)}, u32[]{:S(2)}) collective-permute-start(f32[8,256]{1,0:T(8,128)S(1)} %get-tuple-element.25), channel_id=1, source_target_pairs={{0,1},{1,0},{2,3},{3,2},{4,5},{5,4},{6,7},{7,6},{8,9},{9,8},{10,11... | collective-permute-start | bytes 24584 | tf_op jit(solution)/shard_map/ppermute | solution.py:76
  83.2 3.3 %collective-permute-done.15 = f32[8,256]{1,0:T(8,128)S(1)} collective-permute-done((f32[8,256]{1,0:T(8,128)S(1)}, f32[8,256]{1,0:T(8,128)S(1)}, u32[]{:S(2)}, u32[]{:S(2)}) %collective-permute-start.15) | collective-permute-done | bytes 8224 | tf_op jit(solution)/shard_map/ppermute | solution.py:76
  86.5 0.5 collective-permute-done.16.refs_2_.bl
  87.0 1.3 shard_map.149
  88.3 6.6 %collective-permute-start.19 = (bf16[256,768]{1,0:T(8,128)(2,1)S(1)}, bf16[256,768]{1,0:T(8,128)(2,1)S(1)}, u32[]{:S(2)}, u32[]{:S(2)}) collective-permute-start(bf16[256,768]{1,0:T(8,128)(2,1)S(1)} %bitcast.30), channel_id=1, source_target_pairs={{0,128},{128,0},{1,129},{129,1},{2,130},{130,2},{3,131},{131,3},{4... | collective-permute-start | bytes 1179656 | tf_op jit(solution)/shard_map/ppermute | solution.py:76
  94.9 3.2 %collective-permute-start.22 = (bf16[2,256,512]{2,1,0:T(8,128)(2,1)}, bf16[2,256,512]{2,1,0:T(8,128)(2,1)S(1)}, u32[]{:S(2)}, u32[]{:S(2)}) collective-permute-start(bf16[2,256,512]{2,1,0:T(8,128)(2,1)} %collective-permute-done.17.refs_3_.br), channel_id=1, source_target_pairs={{0,12},{4,0},{8,4},{12,8},{1,13},{5,1},{9,5},{13,9},{2,14},{6,2},{... | collective-permute-start | bytes 1572872 | tf_op jit(solution)/shard_map/ppermute | solution.py:80
  98.2 8.2 %all_to_all.18 = f32[8,1,256]{2,1,0:T(1,128)S(1)} all-to-all(f32[8,1,256]{2,1,0:T(1,128)S(1)} %broadcast_in_dim.5), channel_id=1, replica_groups=mesh['yl'=2,'z'=8,'x'=4,'c'=2,'tp'=2] {'x','c'}, dimensions={0} | all-to-all | bytes 16384 | tf_op jit(solution)/shard_map/all_to_all | solution.py:445
  106.5 0.5 collective-permute-start.20
  107.0 1.9 %collective-permute-start.23 = (f32[8,256]{1,0:T(8,128)S(1)}, f32[8,256]{1,0:T(8,128)S(1)}, u32[]{:S(2)}, u32[]{:S(2)}) collective-permute-start(f32[8,256]{1,0:T(8,128)S(1)} %bitcast.36), channel_id=1, source_target_pairs={{0,16},{16,32},{32,48},{48,64},{64,80},{80,96},{96,112},{112,128},... | collective-permute-start | bytes 24584 | tf_op jit(solution)/shard_map/ppermute | solution.py:448
  109.0 1.0 copy-done.9
  110.1 1.0 copy-done.11
  111.1 2.6 %shard_map.151 = (bf16[4,256,512]{2,1,0:T(8,128)(2,1)S(1)}, f32[4,256,256]{2,1,0:T(8,128)S(1)}, bf16[1024,768]{1,0:T(8,128)(2,1)S(1)}) custom-call(s32[7]{0:T(128)S(1)} %copy-done.20, bf16[2,256,512]{2,1,0:T(8,128)(2,1)S(1)} %shard_map.143.refs_1_.a, bf16[2,256,512]{2,1,0:T(8,128)(2,1)S(1)} %copy-done.9, bf16[2,256,512]{2,1,0:T(8,128)(2,1)S(1)} %copy-done.11, ...), custom_call_target="tpu_custom_call" | custom-call | tf_op jit(solution)/shard_map/pallas_call | solution.py:312
  113.7 1.0 collective-permute-done.23.after_ref.prev_ref
  114.7 2.5 %shard_map.152.pm_ref = bf16[4,256,512]{2,1,0:T(8,128)(2,1)S(1)} custom-call(s32[7]{0:T(128)S(1)} %copy-done.20, bf16[2,256,512]{2,1,0:T(8,128)(2,1)S(1)} %copy-done.2, bf16[2,256,512]{2,1,0:T(8,128)(2,1)S(1)} %copy-done.4, bf16[2,256,512]{2,1,0:T(8,128)(2,1)} %collective-permute-done.17.refs_3_.br, bf16[2,256,512]{2,1,0:T(8,128)(2,1)S(1)} %collective-permute-done.22.bf, ...), custom_call_target="tpu_custom_call" | custom-call | tf_op jit(solution)/shard_map/pallas_call | solution.py:312
  117.2 0.1 collective-permute-start.24
  117.3 0.5 collective-permute-start.21
  118.0 2.1 %collective-permute-done.24.pt_ref = bf16[4,256,512]{2,1,0:T(8,128)(2,1)} collective-permute-done((bf16[4,256,512]{2,1,0:T(8,128)(2,1)S(1)}, bf16[4,256,512]{2,1,0:T(8,128)(2,1)}, u32[]{:S(2)}, u32[]{:S(2)}) %collective-permute-start.24) | collective-permute-done | bytes 1048608 | tf_op jit(solution)/shard_map/ppermute | solution.py:76
  120.1 1.5 %collective-permute-done.21.ot_ref = bf16[4,256,512]{2,1,0:T(8,128)(2,1)} collective-permute-done((bf16[4,256,512]{2,1,0:T(8,128)(2,1)S(1)}, bf16[4,256,512]{2,1,0:T(8,128)(2,1)}, u32[]{:S(2)}, u32[]{:S(2)}) %collective-permute-start.21) | collective-permute-done | bytes 1048608 | tf_op jit(solution)/shard_map/ppermute | solution.py:76
  121.6 3.7 %shard_map.156 = bf16[1,256,256]{2,1,0:T(8,128)(2,1)S(1)} custom-call(s32[4]{0:T(128)S(1)} %get-tuple-element.30.place_ref, f32[4,256,256]{2,1,0:T(8,128)S(1)} %get-tuple-element.27.q_ref, bf16[4,256,512]{2,1,0:T(8,128)(2,1)S(1)} %get-tuple-element.28.om_ref, bf16[4,256,512]{2,1,0:T(8,128)(2,1)} %collective-permute-done.21.ot_ref, ...), custom_call_target="tpu_custom_call" | custom-call | tf_op jit(solution)/shard_map/pallas_call | solution.py:361
  125.3 3.5 %collective-permute-start.27 = (bf16[1,256,256]{2,1,0:T(8,128)(2,1)S(1)}, bf16[1,256,256]{2,1,0:T(8,128)(2,1)S(1)}, u32[]{:S(2)}, u32[]{:S(2)}) collective-permute-start(bf16[1,256,256]{2,1,0:T(8,128)(2,1)S(1)} %shard_map.156), channel_id=1, source_target_pairs={{0,12},{4,0},{8,4},{12,8},{1,13},{5,1},{9,5},{13,9},{2,14},{6,2},{... | collective-permute-start | bytes 393224 | tf_op jit(solution)/shard_map/ppermute | solution.py:80
  128.7 3.7 %shard_map.155 = bf16[1,256,256]{2,1,0:T(8,128)(2,1)S(1)} custom-call(s32[4]{0:T(128)S(1)} %get-tuple-element.32.place_ref, f32[4,256,256]{2,1,0:T(8,128)S(1)} %get-tuple-element.27.q_ref, bf16[4,256,512]{2,1,0:T(8,128)(2,1)S(1)} %get-tuple-element.28.om_ref, bf16[4,256,512]{2,1,0:T(8,128)(2,1)} %collective-permute-done.21.ot_ref, ...), custom_call_target="tpu_custom_call" | custom-call | tf_op jit(solution)/shard_map/pallas_call | solution.py:361
  132.4 0.1 collective-permute-start.26
  132.5 3.7 %shard_map.154 = bf16[1,256,256]{2,1,0:T(8,128)(2,1)S(1)} custom-call(s32[4]{0:T(128)S(1)} %get-tuple-element.33.place_ref, f32[4,256,256]{2,1,0:T(8,128)S(1)} %get-tuple-element.27.q_ref, bf16[4,256,512]{2,1,0:T(8,128)(2,1)S(1)} %get-tuple-element.28.om_ref, bf16[4,256,512]{2,1,0:T(8,128)(2,1)} %collective-permute-done.21.ot_ref, ...), custom_call_target="tpu_custom_call" | custom-call | tf_op jit(solution)/shard_map/pallas_call | solution.py:361
  136.2 0.9 collective-permute-start.25
  137.2 3.7 %shard_map.153.a_ref = bf16[1,256,256]{2,1,0:T(8,128)(2,1)S(1)} custom-call(s32[4]{0:T(128)S(1)} %get-tuple-element.34.place_ref, f32[4,256,256]{2,1,0:T(8,128)S(1)} %get-tuple-element.27.q_ref, bf16[4,256,512]{2,1,0:T(8,128)(2,1)S(1)} %get-tuple-element.28.om_ref, bf16[4,256,512]{2,1,0:T(8,128)(2,1)} %collective-permute-done.21.ot_ref, ...), custom_call_target="tpu_custom_call" | custom-call | tf_op jit(solution)/shard_map/pallas_call | solution.py:361
  140.9 1.8 %collective-permute-done.25.b_ref = bf16[1,256,256]{2,1,0:T(8,128)(2,1)S(1)} collective-permute-done((bf16[1,256,256]{2,1,0:T(8,128)(2,1)S(1)}, bf16[1,256,256]{2,1,0:T(8,128)(2,1)S(1)}, u32[]{:S(2)}, u32[]{:S(2)}) %collective-permute-start.25) | collective-permute-done | bytes 131104 | tf_op jit(solution)/shard_map/ppermute | solution.py:80
  142.8 1.4 shard_map.157
  (75 shorter events, 0.7 us)
Async XLA Ops:
  1.2 10.7 %copy-start.14 = (bf16[1,512,512]{2,1,0:T(8,128)(2,1)S(1)}, bf16[1,512,512]{2,1,0:T(8,128)(2,1)}, u32[]{:S(2)}) copy-start(bf16[1,512,512]{2,1,0:T(8,128)(2,1)} %param.13) | copy-start | bytes 1572868
  1.2 19.9 %copy-start.7 = (bf16[1,4,512,512]{3,2,1,0:T(8,128)(2,1)S(1)}, bf16[1,4,512,512]{3,2,1,0:T(8,128)(2,1)}, u32[]{:S(2)}) copy-start(bf16[1,4,512,512]{3,2,1,0:T(8,128)(2,1)} %param.16) | copy-start | bytes 6291460
  1.2 19.9 %copy-start.13 = (bf16[1,3,512,256]{3,2,1,0:T(8,128)(2,1)S(1)}, bf16[1,3,512,256]{3,2,1,0:T(8,128)(2,1)}, u32[]{:S(2)}) copy-start(bf16[1,3,512,256]{3,2,1,0:T(8,128)(2,1)} %param.14) | copy-start | bytes 2359300
  1.2 32.8 %copy-start.20 = (s32[7]{0:T(128)S(1)}, s32[7]{0:T(128)}, u32[]{:S(2)}) copy-start(s32[7]{0:T(128)} %stack.42.at_ref) | copy-start | bytes 88
  4.0 20.7 %collective-permute-start.9 = (bf16[2,128,256]{2,1,0:T(8,128)(2,1)}, bf16[2,128,256]{2,1,0:T(8,128)(2,1)S(1)}, u32[]{:S(2)}, u32[]{:S(2)}) collective-permute-start(bf16[2,128,256]{2,1,0:T(8,128)(2,1)} %get-tuple-element.23.mine_ref), channel_id=1, source_target_pairs={{0,1},{1,0},{2,3},{3,2},{4,5},{5,4},{6,7},{7,6},{8,9},{9,8},{10,11... | collective-permute-start | bytes 393224 | tf_op jit(solution)/shard_map/ppermute | solution.py:76
  6.3 18.3 %collective-permute-start.6 = (bf16[3,32,256]{2,1,0:T(8,128)(2,1)}, bf16[3,32,256]{2,1,0:T(8,128)(2,1)S(1)}, u32[]{:S(2)}, u32[]{:S(2)}) collective-permute-start(bf16[3,32,256]{2,1,0:T(8,128)(2,1)} %get-tuple-element.20), channel_id=1, source_target_pairs={{0,4},{4,8},{8,12},{12,0},{1,5},{5,9},{9,13},{13,1},{2,6},{6,10},{... | collective-permute-start | bytes 147464 | tf_op jit(solution)/shard_map/ppermute | solution.py:80
  7.8 16.9 %collective-permute-start.7 = (bf16[3,32,256]{2,1,0:T(8,128)(2,1)}, bf16[3,32,256]{2,1,0:T(8,128)(2,1)S(1)}, u32[]{:S(2)}, u32[]{:S(2)}) collective-permute-start(bf16[3,32,256]{2,1,0:T(8,128)(2,1)} %get-tuple-element.21), channel_id=1, source_target_pairs={{0,8},{4,12},{8,0},{12,4},{1,9},{5,13},{9,1},{13,5},{2,10},{6,14},... | collective-permute-start | bytes 147464 | tf_op jit(solution)/shard_map/ppermute | solution.py:80
  10.5 14.1 %collective-permute-start.8 = (bf16[3,32,256]{2,1,0:T(8,128)(2,1)}, bf16[3,32,256]{2,1,0:T(8,128)(2,1)S(1)}, u32[]{:S(2)}, u32[]{:S(2)}) collective-permute-start(bf16[3,32,256]{2,1,0:T(8,128)(2,1)} %get-tuple-element.22), channel_id=1, source_target_pairs={{0,12},{4,0},{8,4},{12,8},{1,13},{5,1},{9,5},{13,9},{2,14},{6,2},{... | collective-permute-start | bytes 147464 | tf_op jit(solution)/shard_map/ppermute | solution.py:80
  11.9 9.2 %collective-permute-start = (bf16[8,512]{1,0:T(8,128)(2,1)S(1)}, bf16[8,512]{1,0:T(8,128)(2,1)S(1)}, u32[]{:S(2)}, u32[]{:S(2)}) collective-permute-start(bf16[8,512]{1,0:T(8,128)(2,1)S(1)} %slice_bitcast_fusion), channel_id=1, source_target_pairs={{0,2},{2,4},{4,6},{6,8},{8,10},{10,12},{12,14},{14,16},{16,18},{18... | collective-permute-start | bytes 24584 | tf_op jit(solution)/shard_map/ppermute | solution.py:408
  21.1 1.0 copy-start.16
  22.1 12.0 %copy-start = (bf16[1,512,4096]{2,1,0:T(8,128)(2,1)S(1)}, bf16[1,512,4096]{2,1,0:T(8,128)(2,1)}, u32[]{:S(2)}) copy-start(bf16[1,512,4096]{2,1,0:T(8,128)(2,1)} %param.17) | copy-start | bytes 12582916
  24.7 0.8 copy-start.19
  25.5 14.0 %copy-start.15 = (f32[2,4096]{1,0:T(2,128)S(1)}, f32[2,4096]{1,0:T(2,128)}, u32[]{:S(2)}) copy-start(f32[2,4096]{1,0:T(2,128)} %t1.1) | copy-start | bytes 98308
  25.5 14.0 %copy-start.17 = (bf16[2,128,256]{2,1,0:T(8,128)(2,1)S(1)}, bf16[2,128,256]{2,1,0:T(8,128)(2,1)}, u32[]{:S(2)}) copy-start(bf16[2,128,256]{2,1,0:T(8,128)(2,1)} %get-tuple-element.23.mine_ref) | copy-start | bytes 393220
  25.5 14.0 %copy-start.18 = (f32[4096]{0:T(1024)S(1)}, f32[4096]{0:T(1024)}, u32[]{:S(2)}) copy-start(f32[4096]{0:T(1024)} %param.20) | copy-start | bytes 49156
  25.5 8.6 %collective-permute-start.11 = (bf16[4,3,32,256]{3,2,1,0:T(8,128)(2,1)S(1)}, bf16[4,3,32,256]{3,2,1,0:T(8,128)(2,1)S(1)}, u32[]{:S(2)}, u32[]{:S(2)}) collective-permute-start(bf16[4,3,32,256]{3,2,1,0:T(8,128)(2,1)S(1)} %shard_map.145.w00), channel_id=1, source_target_pairs={{0,128},{128,0},{1,129},{129,1},{2,130},{130,2},{3,131},{131,3},{4... | collective-permute-start | bytes 589832 | tf_op jit(solution)/shard_map/ppermute | solution.py:76
  25.6 12.9 %collective-permute-start.2 = (bf16[256,512]{1,0:T(8,128)(2,1)S(1)}, bf16[256,512]{1,0:T(8,128)(2,1)S(1)}, u32[]{:S(2)}, u32[]{:S(2)}) collective-permute-start(bf16[256,512]{1,0:T(8,128)(2,1)S(1)} %shard_map.140.latent_ref.refs_0_.refs_4_), channel_id=1, source_target_pairs={{0,1},{1,0},{2,3},{3,2},{4,5},{5,4},{6,7},{7,6},{8,9},{9,8},{10,11... | collective-permute-start | bytes 786440 | tf_op jit(solution)/shard_map/ppermute | solution.py:76
  26.9 12.1 %collective-permute-start.13 = (bf16[256,512]{1,0:T(8,128)(2,1)S(1)}, bf16[256,512]{1,0:T(8,128)(2,1)S(1)}, u32[]{:S(2)}, u32[]{:S(2)}) collective-permute-start(bf16[256,512]{1,0:T(8,128)(2,1)S(1)} %shard_map.140.latent_ref.refs_0_.refs_4_), channel_id=1, source_target_pairs={{0,16},{16,32},{32,48},{48,64},{64,80},{80,96},{96,112},{112,128},... | collective-permute-start | bytes 786440 | tf_op jit(solution)/shard_map/ppermute | solution.py:418
  28.9 10.1 %collective-permute-start.10 = (bf16[4,3,32,256]{3,2,1,0:T(8,128)(2,1)S(1)}, bf16[4,3,32,256]{3,2,1,0:T(8,128)(2,1)S(1)}, u32[]{:S(2)}, u32[]{:S(2)}) collective-permute-start(bf16[4,3,32,256]{3,2,1,0:T(8,128)(2,1)S(1)} %shard_map.145.w00), channel_id=1, source_target_pairs={{0,2},{2,0},{1,3},{3,1},{4,6},{6,4},{5,7},{7,5},{8,10},{10,8},{9,1... | collective-permute-start | bytes 589832 | tf_op jit(solution)/shard_map/ppermute | solution.py:76
  34.1 4.9 %collective-permute-start.12 = (bf16[4,3,32,256]{3,2,1,0:T(8,128)(2,1)S(1)}, bf16[4,3,32,256]{3,2,1,0:T(8,128)(2,1)S(1)}, u32[]{:S(2)}, u32[]{:S(2)}) collective-permute-start(bf16[4,3,32,256]{3,2,1,0:T(8,128)(2,1)S(1)} %collective-permute-done.11.w10), channel_id=1, source_target_pairs={{0,2},{2,0},{1,3},{3,1},{4,6},{6,4},{5,7},{7,5},{8,10},{10,8},{9,1... | collective-permute-start | bytes 589832 | tf_op jit(solution)/shard_map/ppermute | solution.py:76
  37.2 1.3 copy-start.5
  38.6 1.0 copy-start.12
  41.5 25.3 %all-to-all-start = ((bf16[8,32,896]{2,1,0:T(8,128)(2,1)}), bf16[8,32,896]{2,1,0:T(8,128)(2,1)S(1)}, u32[]{:S(2)}, u32[]{:S(2)}) async-start(bf16[8,32,896]{2,1,0:T(8,128)(2,1)} %shard_map.146), calls=%async_computation | async-start | bytes 917504 | tf_op jit(solution)/shard_map/all_to_all | solution.py:429
  46.2 25.4 %copy-start.21 = (s32[2,32]{1,0:T(2,128)S(1)}, s32[2,32]{1,0:T(2,128)}, u32[]{:S(2)}) copy-start(s32[2,32]{1,0:T(2,128)} %param.18) | copy-start | bytes 772
  46.3 20.5 %collective-permute-start.3 = (bf16[2,256,512]{2,1,0:T(8,128)(2,1)S(1)}, bf16[2,256,512]{2,1,0:T(8,128)(2,1)S(1)}, u32[]{:S(2)}, u32[]{:S(2)}) collective-permute-start(bf16[2,256,512]{2,1,0:T(8,128)(2,1)S(1)} %shard_map.143.refs_1_.a), channel_id=1, source_target_pairs={{0,4},{4,8},{8,12},{12,0},{1,5},{5,9},{9,13},{13,1},{2,6},{6,10},{... | collective-permute-start | bytes 1572872 | tf_op jit(solution)/shard_map/ppermute | solution.py:80
  46.3 20.4 %collective-permute-start.4 = (bf16[2,256,512]{2,1,0:T(8,128)(2,1)S(1)}, bf16[2,256,512]{2,1,0:T(8,128)(2,1)S(1)}, u32[]{:S(2)}, u32[]{:S(2)}) collective-permute-start(bf16[2,256,512]{2,1,0:T(8,128)(2,1)S(1)} %shard_map.143.refs_1_.a), channel_id=1, source_target_pairs={{0,12},{4,0},{8,4},{12,8},{1,13},{5,1},{9,5},{13,9},{2,14},{6,2},{... | collective-permute-start | bytes 1572872 | tf_op jit(solution)/shard_map/ppermute | solution.py:80
  49.6 26.5 %collective-permute-start.1 = (bf16[256,2048]{1,0:T(8,128)(2,1)}, bf16[256,2048]{1,0:T(8,128)(2,1)}, u32[]{:S(2)}, u32[]{:S(2)}) collective-permute-start(bf16[256,2048]{1,0:T(8,128)(2,1)} %copy-done.12), channel_id=1, source_target_pairs={{0,1},{1,0},{2,3},{3,2},{4,5},{5,4},{6,7},{7,6},{8,9},{9,8},{10,11... | collective-permute-start | bytes 3145736 | tf_op jit(solution)/shard_map/ppermute | solution.py:76
  52.8 13.9 %collective-permute-start.14 = (bf16[256,512]{1,0:T(8,128)(2,1)S(1)}, bf16[256,512]{1,0:T(8,128)(2,1)S(1)}, u32[]{:S(2)}, u32[]{:S(2)}) collective-permute-start(bf16[256,512]{1,0:T(8,128)(2,1)S(1)} %collective-permute-done.2.refs_1_), channel_id=1, source_target_pairs={{0,16},{16,32},{32,48},{48,64},{64,80},{80,96},{96,112},{112,128},... | collective-permute-start | bytes 786440 | tf_op jit(solution)/shard_map/ppermute | solution.py:419
  66.8 14.6 %copy-start.1 = (bf16[2,256,512]{2,1,0:T(8,128)(2,1)}, bf16[2,256,512]{2,1,0:T(8,128)(2,1)S(1)}, u32[]{:S(2)}) copy-start(bf16[2,256,512]{2,1,0:T(8,128)(2,1)S(1)} %shard_map.147.refs_2_.b) | copy-start | bytes 1572868
  66.8 28.1 %copy-start.8 = (bf16[2,256,512]{2,1,0:T(8,128)(2,1)}, bf16[2,256,512]{2,1,0:T(8,128)(2,1)S(1)}, u32[]{:S(2)}) copy-start(bf16[2,256,512]{2,1,0:T(8,128)(2,1)S(1)} %collective-permute-done.3.refs_0_.al) | copy-start | bytes 1572868
  66.8 5.0 %copy-start.10 = (bf16[2,256,512]{2,1,0:T(8,128)(2,1)}, bf16[2,256,512]{2,1,0:T(8,128)(2,1)S(1)}, u32[]{:S(2)}) copy-start(bf16[2,256,512]{2,1,0:T(8,128)(2,1)S(1)} %collective-permute-done.4.refs_1_.ar) | copy-start | bytes 1572868
  67.8 19.3 %all-to-all-start.1 = ((bf16[8,32,768]{2,1,0:T(8,128)(2,1)}), bf16[8,32,768]{2,1,0:T(8,128)(2,1)S(1)}, u32[]{:S(2)}, u32[]{:S(2)}) async-start(bf16[8,32,768]{2,1,0:T(8,128)(2,1)} %get-tuple-element.24), calls=%async_computation.1 | async-start | bytes 786432 | tf_op jit(solution)/shard_map/all_to_all | solution.py:441
  71.8 14.7 %collective-permute-start.17 = (bf16[2,256,512]{2,1,0:T(8,128)(2,1)S(1)}, bf16[2,256,512]{2,1,0:T(8,128)(2,1)}, u32[]{:S(2)}, u32[]{:S(2)}) collective-permute-start(bf16[2,256,512]{2,1,0:T(8,128)(2,1)S(1)} %shard_map.147.refs_2_.b), channel_id=1, source_target_pairs={{0,12},{4,0},{8,4},{12,8},{1,13},{5,1},{9,5},{13,9},{2,14},{6,2},{... | collective-permute-start | bytes 1572872 | tf_op jit(solution)/shard_map/ppermute | solution.py:80
  72.6 14.4 %collective-permute-start.16 = (bf16[2,256,512]{2,1,0:T(8,128)(2,1)S(1)}, bf16[2,256,512]{2,1,0:T(8,128)(2,1)S(1)}, u32[]{:S(2)}, u32[]{:S(2)}) collective-permute-start(bf16[2,256,512]{2,1,0:T(8,128)(2,1)S(1)} %shard_map.147.refs_2_.b), channel_id=1, source_target_pairs={{0,4},{4,8},{8,12},{12,0},{1,5},{5,9},{9,13},{13,1},{2,6},{6,10},{... | collective-permute-start | bytes 1572872 | tf_op jit(solution)/shard_map/ppermute | solution.py:80
  76.1 1.6 %copy-start.6 = (f32[256,2048]{1,0:T(8,128)S(1)}, f32[256,2048]{1,0:T(8,128)}, u32[]{:S(2)}) copy-start(f32[256,2048]{1,0:T(8,128)} %copy-done.5) | copy-start | bytes 6291460
  81.3 5.2 %collective-permute-start.15 = (f32[8,256]{1,0:T(8,128)S(1)}, f32[8,256]{1,0:T(8,128)S(1)}, u32[]{:S(2)}, u32[]{:S(2)}) collective-permute-start(f32[8,256]{1,0:T(8,128)S(1)} %get-tuple-element.25), channel_id=1, source_target_pairs={{0,1},{1,0},{2,3},{3,2},{4,5},{5,4},{6,7},{7,6},{8,9},{9,8},{10,11... | collective-permute-start | bytes 24584 | tf_op jit(solution)/shard_map/ppermute | solution.py:76
  87.0 22.0 %copy-start.3 = (bf16[2,256,512]{2,1,0:T(8,128)(2,1)}, bf16[2,256,512]{2,1,0:T(8,128)(2,1)S(1)}, u32[]{:S(2)}) copy-start(bf16[2,256,512]{2,1,0:T(8,128)(2,1)S(1)} %collective-permute-done.16.refs_2_.bl) | copy-start | bytes 1572868
  88.3 18.2 %collective-permute-start.19 = (bf16[256,768]{1,0:T(8,128)(2,1)S(1)}, bf16[256,768]{1,0:T(8,128)(2,1)S(1)}, u32[]{:S(2)}, u32[]{:S(2)}) collective-permute-start(bf16[256,768]{1,0:T(8,128)(2,1)S(1)} %bitcast.30), channel_id=1, source_target_pairs={{0,128},{128,0},{1,129},{129,1},{2,130},{130,2},{3,131},{131,3},{4... | collective-permute-start | bytes 1179656 | tf_op jit(solution)/shard_map/ppermute | solution.py:76
  94.9 14.0 %collective-permute-start.5 = (bf16[2,256,512]{2,1,0:T(8,128)(2,1)S(1)}, bf16[2,256,512]{2,1,0:T(8,128)(2,1)S(1)}, u32[]{:S(2)}, u32[]{:S(2)}) collective-permute-start(bf16[2,256,512]{2,1,0:T(8,128)(2,1)S(1)} %collective-permute-done.3.refs_0_.al), channel_id=1, source_target_pairs={{0,4},{4,8},{8,12},{12,0},{1,5},{5,9},{9,13},{13,1},{2,6},{6,10},{... | collective-permute-start | bytes 1572872 | tf_op jit(solution)/shard_map/ppermute | solution.py:80
  94.9 19.8 %collective-permute-start.22 = (bf16[2,256,512]{2,1,0:T(8,128)(2,1)}, bf16[2,256,512]{2,1,0:T(8,128)(2,1)S(1)}, u32[]{:S(2)}, u32[]{:S(2)}) collective-permute-start(bf16[2,256,512]{2,1,0:T(8,128)(2,1)} %collective-permute-done.17.refs_3_.br), channel_id=1, source_target_pairs={{0,12},{4,0},{8,4},{12,8},{1,13},{5,1},{9,5},{13,9},{2,14},{6,2},{... | collective-permute-start | bytes 1572872 | tf_op jit(solution)/shard_map/ppermute | solution.py:80
  106.4 2.6 %collective-permute-start.18 = (bf16[256,768]{1,0:T(8,128)(2,1)S(1)}, bf16[256,768]{1,0:T(8,128)(2,1)S(1)}, u32[]{:S(2)}, u32[]{:S(2)}) collective-permute-start(bf16[256,768]{1,0:T(8,128)(2,1)S(1)} %bitcast.31), channel_id=1, source_target_pairs={{0,2},{2,0},{1,3},{3,1},{4,6},{6,4},{5,7},{7,5},{8,10},{10,8},{9,1... | collective-permute-start | bytes 1179656 | tf_op jit(solution)/shard_map/ppermute | solution.py:76
  106.5 8.2 %copy-start.2 = (bf16[2,256,512]{2,1,0:T(8,128)(2,1)S(1)}, bf16[2,256,512]{2,1,0:T(8,128)(2,1)}, u32[]{:S(2)}) copy-start(bf16[2,256,512]{2,1,0:T(8,128)(2,1)} %copy-done.1) | copy-start | bytes 1572868
  106.5 2.5 %collective-permute-start.20 = (bf16[256,768]{1,0:T(8,128)(2,1)S(1)}, bf16[256,768]{1,0:T(8,128)(2,1)S(1)}, u32[]{:S(2)}, u32[]{:S(2)}) collective-permute-start(bf16[256,768]{1,0:T(8,128)(2,1)S(1)} %bitcast.28), channel_id=1, source_target_pairs={{0,2},{2,0},{1,3},{3,1},{4,6},{6,4},{5,7},{7,5},{8,10},{10,8},{9,1... | collective-permute-start | bytes 1179656 | tf_op jit(solution)/shard_map/ppermute | solution.py:76
  107.0 7.6 %collective-permute-start.23 = (f32[8,256]{1,0:T(8,128)S(1)}, f32[8,256]{1,0:T(8,128)S(1)}, u32[]{:S(2)}, u32[]{:S(2)}) collective-permute-start(f32[8,256]{1,0:T(8,128)S(1)} %bitcast.36), channel_id=1, source_target_pairs={{0,16},{16,32},{32,48},{48,64},{64,80},{80,96},{96,112},{112,128},... | collective-permute-start | bytes 24584 | tf_op jit(solution)/shard_map/ppermute | solution.py:448
  109.0 1.0 copy-start.9
  110.1 1.0 copy-start.11
  111.1 3.6 %copy-start.4 = (bf16[2,256,512]{2,1,0:T(8,128)(2,1)S(1)}, bf16[2,256,512]{2,1,0:T(8,128)(2,1)}, u32[]{:S(2)}) copy-start(bf16[2,256,512]{2,1,0:T(8,128)(2,1)} %copy-done.3) | copy-start | bytes 1572868
  117.2 2.9 %collective-permute-start.24 = (bf16[4,256,512]{2,1,0:T(8,128)(2,1)S(1)}, bf16[4,256,512]{2,1,0:T(8,128)(2,1)}, u32[]{:S(2)}, u32[]{:S(2)}) collective-permute-start(bf16[4,256,512]{2,1,0:T(8,128)(2,1)S(1)} %shard_map.152.pm_ref), channel_id=1, source_target_pairs={{0,2},{2,0},{1,3},{3,1},{4,6},{6,4},{5,7},{7,5},{8,10},{10,8},{9,1... | collective-permute-start | bytes 3145736 | tf_op jit(solution)/shard_map/ppermute | solution.py:76
  117.3 4.3 %collective-permute-start.21 = (bf16[4,256,512]{2,1,0:T(8,128)(2,1)S(1)}, bf16[4,256,512]{2,1,0:T(8,128)(2,1)}, u32[]{:S(2)}, u32[]{:S(2)}) collective-permute-start(bf16[4,256,512]{2,1,0:T(8,128)(2,1)S(1)} %get-tuple-element.28.om_ref), channel_id=1, source_target_pairs={{0,2},{2,0},{1,3},{3,1},{4,6},{6,4},{5,7},{7,5},{8,10},{10,8},{9,1... | collective-permute-start | bytes 3145736 | tf_op jit(solution)/shard_map/ppermute | solution.py:76
  125.3 15.6 %collective-permute-start.27 = (bf16[1,256,256]{2,1,0:T(8,128)(2,1)S(1)}, bf16[1,256,256]{2,1,0:T(8,128)(2,1)S(1)}, u32[]{:S(2)}, u32[]{:S(2)}) collective-permute-start(bf16[1,256,256]{2,1,0:T(8,128)(2,1)S(1)} %shard_map.156), channel_id=1, source_target_pairs={{0,12},{4,0},{8,4},{12,8},{1,13},{5,1},{9,5},{13,9},{2,14},{6,2},{... | collective-permute-start | bytes 393224 | tf_op jit(solution)/shard_map/ppermute | solution.py:80
  132.4 8.5 %collective-permute-start.26 = (bf16[1,256,256]{2,1,0:T(8,128)(2,1)S(1)}, bf16[1,256,256]{2,1,0:T(8,128)(2,1)S(1)}, u32[]{:S(2)}, u32[]{:S(2)}) collective-permute-start(bf16[1,256,256]{2,1,0:T(8,128)(2,1)S(1)} %shard_map.155), channel_id=1, source_target_pairs={{0,8},{4,12},{8,0},{12,4},{1,9},{5,13},{9,1},{13,5},{2,10},{6,14},... | collective-permute-start | bytes 393224 | tf_op jit(solution)/shard_map/ppermute | solution.py:80
  136.2 6.6 %collective-permute-start.25 = (bf16[1,256,256]{2,1,0:T(8,128)(2,1)S(1)}, bf16[1,256,256]{2,1,0:T(8,128)(2,1)S(1)}, u32[]{:S(2)}, u32[]{:S(2)}) collective-permute-start(bf16[1,256,256]{2,1,0:T(8,128)(2,1)S(1)} %shard_map.154), channel_id=1, source_target_pairs={{0,4},{4,8},{8,12},{12,0},{1,5},{5,9},{9,13},{13,1},{2,6},{6,10},{... | collective-permute-start | bytes 393224 | tf_op jit(solution)/shard_map/ppermute | solution.py:80

commit v6 on v5

--- a/solution.py
+++ b/solution.py
@@ -12,7 +12,6 @@
 D = 4096
 CH = 512
 CTX = ("yl", "z", "x", "c")
-ROW = ("x", "c")
 SWAP = [(0, 1), (1, 0)]
 BF = jnp.bfloat16
 F32 = jnp.float32
@@ -210,7 +209,7 @@
 
     @pl.when(mine)
     def _():
-        own_ref[...] = term
+        own_ref[...] = term.astype(BF)
 
     @pl.when(jnp.logical_not(mine))
     def _():
@@ -233,16 +232,17 @@
             + unused(after),
             out_specs=[pl.BlockSpec((BLOCK, 1024), give_at), pl.BlockSpec((BLOCK, 1024), own_at)],
         ),
-        out_shape=[jax.ShapeDtypeStruct((BLOCK, D // 2), BF), jax.ShapeDtypeStruct((BLOCK, D // 2), F32)],
+        out_shape=[jax.ShapeDtypeStruct((BLOCK, D // 2), BF)] * 2,
         compiler_params=params(16),
         cost_estimate=NO_COST,
     )(at, latent, embed, *after)
 
 
-def embed_kernel(at_ref, own_ref, got_ref, active_ref, table_ref, out_ref, square_ref):
+def embed_kernel(at_ref, own_ref, got_ref, active_ref, table_ref, *refs):
+    out_ref, square_ref = refs[-2:]
     act = active_ref[:, pl.ds(at_ref[3] + 4, 1), :].reshape(2, BLOCK)
     cols = jnp.concatenate([act, jnp.zeros((6, BLOCK), F32)], axis=0).T
-    x = own_ref[...] + got_ref[...].astype(F32)
+    x = own_ref[...].astype(F32) + got_ref[...].astype(F32)
     x = x + cols[:, 0:1] * table_ref[0:1] + cols[:, 1:2] * table_ref[1:2]
     out_ref[...] = x.astype(BF)
     square = jnp.sum(x * x, axis=1, keepdims=True)
@@ -257,7 +257,7 @@
         square_ref[...] += square
 
 
-def embed_rows(at, own, got, active, table):
+def embed_rows(at, own, got, active, table, after):
     tile = pl.BlockSpec((BLOCK, 1024), lambda i, at: (0, i))
     return pl.pallas_call(
         embed_kernel,
@@ -269,16 +269,17 @@
                 tile,
                 pl.BlockSpec((2, 8, BLOCK), lambda i, at: (0, 0, 0)),
                 pl.BlockSpec((2, 1024), lambda i, at: (0, at[5] * 2 + i)),
-            ],
+            ]
+            + unused(after),
             out_specs=[tile, pl.BlockSpec((8, BLOCK), lambda i, at: (0, 0))],
         ),
         out_shape=[jax.ShapeDtypeStruct((BLOCK, D // 2), BF), jax.ShapeDtypeStruct((8, BLOCK), F32)],
         compiler_params=params(16),
-        cost_estimate=NO_COST,
-    )(at, own, got, active, table)
-
-
-def project_rows(row, blocks, m_ref, line_ref, active_ref, at_ref, kv_ref, q_ref):
+        cost_estimate=pl.CostEstimate(flops=20000000000, bytes_accessed=0, transcendentals=0),
+    )(at, own, got, active, table, *after)
+
+
+def project_rows(row, blocks, m_ref, line_ref, active_ref, scale_ref, at_ref, kv_ref, q_ref):
     x = at_ref[3]
     cols = slice(0, 768) if q_ref is not None else slice(256, 768)
     w0, w1 = m_ref[0:512, cols], m_ref[512:1024, cols]
@@ -286,26 +287,26 @@
     for dx in range(4):
         at = lax.rem(x + dx, 4)
         act = active_ref[:, pl.ds(4 * row + at, 1), :].reshape(2, BLOCK)
-        side = jnp.concatenate([act, jnp.zeros((6, BLOCK), F32)], axis=0).T
+        side = jnp.concatenate([act, scale_ref[pl.ds(at, 1), :], jnp.zeros((5, BLOCK), F32)], axis=0).T
         acc = dot(blocks[dx][0], w0) + dot(blocks[dx][1], w1)
-        acc = acc + side[:, 0:1] * line[0:1] + side[:, 1:2] * line[1:2]
+        acc = (acc + side[:, 0:1] * line[0:1] + side[:, 1:2] * line[1:2]) * side[:, 2:3]
         kv_ref[at] = acc[:, -512:].astype(BF)
         if q_ref is not None:
-            q_ref[at] = acc[:, :256]
-
-
-def project_own_kernel(at_ref, a, al, ar, af, m00, m01, m10, m11, line_ref, active_ref, kv_ref, q_ref, m_ref):
+            q_ref[at] = (acc[:, :256] * (HD**-0.5 * LOG2E)).astype(BF)
+
+
+def project_own_kernel(at_ref, a, al, ar, af, m00, m01, m10, m11, line_ref, active_ref, scale_ref, kv_ref, q_ref, m_ref):
     core, yl = at_ref[4], at_ref[6]
     for y, pair in enumerate(((m00, m01), (m10, m11))):
         for c, ref in enumerate(pair):
             row = ((yl ^ y) * 2 + (core ^ c)) * 128
             for s in range(2):
                 m_ref[pl.ds(pl.multiple_of(s * 512 + row, 128), 128), :] = ref[s * 128 : (s + 1) * 128, :]
-    project_rows(1, (a, ar, af, al), m_ref, line_ref, active_ref, at_ref, kv_ref, q_ref)
-
-
-def project_prev_kernel(at_ref, b, bl, br, bf, m_ref, line_ref, active_ref, after_ref, kv_ref):
-    project_rows(0, (b, br, bf, bl), m_ref, line_ref, active_ref, at_ref, kv_ref, None)
+    project_rows(1, (a, ar, af, al), m_ref, line_ref, active_ref, scale_ref, at_ref, kv_ref, q_ref)
+
+
+def project_prev_kernel(at_ref, b, bl, br, bf, m_ref, line_ref, active_ref, scale_ref, kv_ref):
+    project_rows(0, (b, br, bf, bl), m_ref, line_ref, active_ref, scale_ref, at_ref, kv_ref, None)
 
 
 def project(kernel, outs, *args):
@@ -319,59 +320,55 @@
     )(*args)
 
 
-def attention_kernel(place_ref, q_ref, om_ref, ot_ref, pm_ref, pt_ref, own_ref, prev_ref, o_ref):
-    at = lax.rem(place_ref[0] + place_ref[3], 4)
-    core = place_ref[1]
-    first = place_ref[2]
-    rows = lax.broadcasted_iota(jnp.int32, (BLOCK, BLOCK), 0)
-    cols = lax.broadcasted_iota(jnp.int32, (BLOCK, BLOCK), 1)
-    blocks = []
-    for kv_own, kv_prev, begin, parity in ((om_ref, pm_ref, at + 1, core), (ot_ref, pt_ref, at + core, 1 - core)):
-        for j in range(4):
-            m = begin + j
-            i = lax.rem(m, 4)
-            kv = jnp.where(m >= 4, kv_own[i], kv_prev[i])
-            factor = jnp.where(m >= 4, own_ref[pl.ds(2 * i + parity, 1), :], prev_ref[pl.ds(2 * i + parity, 1), :])
-            blocks.append((kv, factor, jnp.where((m < 4) & (first == 1), 1e30, 0.0)))
-    mine = jnp.broadcast_to(own_ref[pl.ds(2 * at + core, 1), :] * (HD**-0.5 * LOG2E), (8, BLOCK)).T[:, 0:1]
+def attention_kernel(n, place_ref, q_ref, om_ref, ot_ref, pm_ref, pt_ref, *o_refs):
+    x, core, first = place_ref[0], place_ref[1], place_ref[2]
+    half = BLOCK // 2
+    cols = lax.broadcasted_iota(jnp.int32, (half, BLOCK), 1)
+    ones = jnp.ones((8 * BLOCK, HD), BF)
     contract = (((1,), (1,)), ((), ()))
-    for h in range(2):
-        q = (q_ref[at, :, h * HD : (h + 1) * HD] * mine).astype(BF)
-        scores = []
-        top = None
-        for n, (kv, factor, penalty) in enumerate(blocks):
-            s = lax.dot_general(q, kv[:, h * HD : (h + 1) * HD], contract, preferred_element_type=F32) * factor
-            if n == 3:
-                s = jnp.where(cols <= rows, s, -1e30)
-            if n == 4:
-                s = jnp.where(cols > rows, s, -1e30)
-            most = jnp.max(s, axis=1, keepdims=True) - penalty
-            top = most if top is None else jnp.maximum(top, most)
-            scores.append(s)
-        total = jnp.zeros((BLOCK, 1), F32)
-        o = jnp.zeros((BLOCK, HD), F32)
-        for s, (kv, factor, penalty) in zip(scores, blocks):
-            p = jnp.exp2(s - (top + penalty))
-            total += jnp.sum(p, axis=1, keepdims=True)
-            o += dot((p * factor).astype(BF), kv[:, 256 + h * HD : 256 + (h + 1) * HD])
-        o_ref[0, :, h * HD : (h + 1) * HD] = (o / total).astype(BF)
-
-
-def attention(place, dx, *args):
-    return pl.pallas_call(
-        attention_kernel,
-        in_specs=[pl.BlockSpec(memory_space=pltpu.SMEM)] + in_vmem(7),
-        out_specs=pl.BlockSpec(memory_space=pltpu.VMEM),
-        out_shape=jax.ShapeDtypeStruct((1, BLOCK, 256), BF),
-        compiler_params=params(8),
-        cost_estimate=NO_COST,
-    )(jnp.concatenate([place, jnp.array([dx], jnp.int32)]), *args)
+    for step in range(n):
+        at = lax.rem(x + place_ref[3 + step], 4)
+        blocks, penalties = [], []
+        for own_ref, prev_ref, begin in ((om_ref, pm_ref, at + 1), (ot_ref, pt_ref, at + core)):
+            for j in range(4):
+                m = begin + j
+                i = lax.rem(m, 4)
+                blocks.append(jnp.where(m >= 4, own_ref[i], prev_ref[i]))
+                penalties.append(jnp.where((m < 4) & (first == 1), 1e30, 0.0))
+        kv = jnp.concatenate(blocks, axis=0)
+        for h in range(2):
+            q = q_ref[at, :, h * HD : (h + 1) * HD]
+            k = kv[:, h * HD : (h + 1) * HD]
+            v = jnp.concatenate([kv[:, 256 + h * HD : 256 + (h + 1) * HD], ones], axis=1)
+            for begin in (0, half):
+                rows = lax.broadcasted_iota(jnp.int32, (half, BLOCK), 0) + begin
+                s = lax.dot_general(q[begin : begin + half], k, contract, preferred_element_type=F32)
+                s = [s[:, j * BLOCK : (j + 1) * BLOCK] for j in range(8)]
+                s[3] = jnp.where(cols <= rows, s[3], -1e30)
+                s[4] = jnp.where(cols > rows, s[4], -1e30)
+                tops = [jnp.max(v, axis=1, keepdims=True) - penalty for v, penalty in zip(s, penalties)]
+                top = functools.reduce(jnp.maximum, tops)
+                p = [jnp.exp2(v - (top + penalty)).astype(BF) for v, penalty in zip(s, penalties)]
+                o = dot(jnp.concatenate(p, axis=1), v)
+                o_refs[step][begin : begin + half, h * HD : (h + 1) * HD] = (o[:, :HD] / o[:, HD:]).astype(BF)
+
+
+def attention(place, offsets, *args):
+    n = len(offsets)
+    return pl.pallas_call(
+        functools.partial(attention_kernel, n),
+        in_specs=[pl.BlockSpec(memory_space=pltpu.SMEM)] + in_vmem(5),
+        out_specs=in_vmem(n),
+        out_shape=[jax.ShapeDtypeStruct((BLOCK, 256), BF)] * n,
+        compiler_params=params(16),
+        cost_estimate=NO_COST,
+    )(jnp.concatenate([place, jnp.array(offsets, jnp.int32)]), *args)
 
 
 def collect_kernel(place_ref, a_ref, b_ref, c_ref, d_ref, o_ref):
     for dx, ref in enumerate((a_ref, b_ref, c_ref, d_ref)):
         at = lax.rem(place_ref[0] + 4 - dx, 4)
-        o_ref[:, pl.ds(pl.multiple_of(at * 256, 256), 256)] = ref[0]
+        o_ref[:, pl.ds(pl.multiple_of(at * 256, 256), 256)] = ref[...]
 
 
 def collect(place, parts):
@@ -427,7 +424,7 @@
     w11 = swap(w10, "c")
     packed = partial_weights(at, (w00, w01, w10, w11), mine, rest, norm_gain[None], speaker_table, (give, a, prev))
     packed = lax.all_to_all(packed, "z", 0, 0, tiled=True)
-    m, lines = sum_weights(packed, (al, ar, b))
+    m, lines = sum_weights(packed, (al, ar))
     bounds = jnp.cumsum(turn_lengths, axis=1)
     start = ((row - 1 + jnp.arange(2)[:, None]) * 8 + 2 * jnp.arange(4)[None, :] + core) * BLOCK
     frames = start.reshape(8, 1) + jnp.arange(BLOCK)
@@ -435,34 +432,35 @@
     active = (turn % 2 == 1).astype(F32)
 
     got = swap(give, "tp")
-    embedded, square = embed_rows(at, own, got, active, speaker_table)
+    embedded, square = embed_rows(at, own, got, active, speaker_table, ())
     square = square + swap(square, "tp")
     scale = lax.rsqrt(square[0:1] * (1.0 / D) + 1e-05)
     m00 = lax.all_to_all(m, "z", 0, 0, tiled=True).reshape(256, 768)
     (m00,) = stack([m00], (scale, bl, br))
     m10 = swap(m00, "yl")
     m01 = swap(m00, "c")
-    scales = lax.all_to_all(jnp.broadcast_to(scale, (8, BLOCK)), ROW, 0, 0, tiled=True)
+    scales = lax.all_to_all(jnp.broadcast_to(scale, (4, BLOCK)), "x", 0, 0, tiled=True)
     (m10,) = stack([m10], (scales,))
     m11 = swap(m10, "c")
     scales_prev = lax.ppermute(scales, ("yl", "z"), behind)
 
     kv = jax.ShapeDtypeStruct((4, BLOCK, 512), BF)
-    half = jax.ShapeDtypeStruct((4, BLOCK, 256), F32)
+    half = jax.ShapeDtypeStruct((4, BLOCK, 256), BF)
     full = jax.ShapeDtypeStruct((1024, 768), BF)
     om, q, whole = project(
-        project_own_kernel, (kv, half, full), at, a, al, ar, af, m00, m01, m10, m11, lines, active
+        project_own_kernel, (kv, half, full), at, a, al, ar, af, m00, m01, m10, m11, lines, active, scales
     )
     ot = swap(om, "c")
     (pm,) = project(project_prev_kernel, (kv,), at, b, bl, br, bf, whole, lines, active, scales_prev)
     pt = swap(pm, "c")
 
     place = jnp.stack([x_at, core, (row == 0).astype(jnp.int32)]).astype(jnp.int32)
-    parts = [None] * 4
-    for dx in (2, 1, 3, 0):
-        part = attention(place, dx, q, om, ot, pm, pt, scales, scales_prev)
-        parts[dx] = shift(part, dx) if dx else part
-    return embedded, collect(place, parts)
+    blocks = (q, om, ot, pm, pt)
+    sent = (2, 1, 3)
+    parts = dict(zip(sent, attention(place, sent, *blocks)))
+    parts = {dx: shift(part, dx) for dx, part in parts.items()}
+    (parts[0],) = attention(place, (0,), *blocks)
+    return embedded, collect(place, [parts[dx] for dx in range(4)])
 
 
 def solution(mesh):

time: 145 us -> 141 us (0.972)
  starting transfers between devices: 53.6 us -> 47.2 us
  Pallas kernels: 37.5 us -> 31.5 us
  local copies, waits for them, and re-layouts: 8.03 us -> 11.6 us
  waiting for transfers between devices: 35 us -> 36.8 us
  blocking collectives: 8.24 us -> 9.93 us
    ppermute x12, starting transfers between devices: 16.8 us -> 8.63 us  [swap(): return lax.ppermute(a, axis, SWAP)]
    pallas_call x4 -> x2, Pallas kernels: 14.7 us -> 8.51 us  [attention(): pl.pallas_call(functools.partial(attention_kernel, n), in_specs=[pl.Block...]
    unnamed x45 -> x57, local copies, waits for them, and re-layouts: 7.33 us -> 10.9 us
    all_to_all x1, waiting for transfers between devices: 0.01 us -> 2.19 us  [on_device(): m00 = lax.all_to_all(m, 'z', 0, 0, tiled=True).reshape(256, 768)]
    all_to_all x1, blocking collectives: 8.24 us -> 9.93 us  [on_device(): lax.all_to_all(jnp.broadcast_to(scale, (4, BLOCK)), 'x', 0, 0, tiled=True)]
    ppermute x12, waiting for transfers between devices: 14.1 us -> 12.5 us  [swap(): return lax.ppermute(a, axis, SWAP)]
    ppermute x1, waiting for transfers between devices: 9.86 us -> 11.3 us  [on_device(): b = stack([prev, lax.ppermute(other, ('yl', 'z'), behind)])]
  transfers between devices with their start and end apart: 30 -> 30, of which waited for: 11 -> 9; matrix products, arithmetic and copies ran while one was open for 1% -> 1% of each run, Pallas kernels for 17% -> 14%
where the time goes in v6:
time: 141 us; the launch traced here: 139 us
  starting transfers between devices  47.2 us (33%)
  waiting for transfers between devices  36.8 us (26%)
  Pallas kernels  31.5 us (22%)
  local copies, waits for them, and re-layouts  11.6 us (8%)
  blocking collectives  9.93 us (7%)
    ppermute x12, starting transfers between devices, shift(): return lax.ppermute(a, 'x', [(i, (i + by) % 4) for i in range(4)])  18.7 us
    ppermute x12, waiting for transfers between devices, swap(): return lax.ppermute(a, axis, SWAP)  12.5 us
    ppermute x1, waiting for transfers between devices, on_device(): b = stack([prev, lax.ppermute(other, ('yl', 'z'), behind)])  11.3 us
    unnamed x57, local copies, waits for them, and re-layouts  10.9 us
    all_to_all x1, blocking collectives, on_device(): lax.all_to_all(jnp.broadcast_to(scale, (4, BLOCK)), 'x', 0, 0, tiled=True)  9.93 us
    ppermute x12, starting transfers between devices, swap(): return lax.ppermute(a, axis, SWAP)  8.63 us
    pallas_call x2, Pallas kernels, attention(): pl.pallas_call(functools.partial(attention_kernel, n), in_specs=[pl.Block...  8.51 us
    ppermute x1, waiting for transfers between devices, on_device(): halo = lax.ppermute(audio[-8:], CTX, [(i, i + 1) for i in range(127)])  7.26 us
  transfers between devices with their start and end apart: 30, of which 9 were waited for; matrix products, arithmetic and copies ran while one was open for 1% of the time, Pallas kernels for 14%

profile of v6, /device:TPU:8, one launch (start us, length us, event | category | flops | bytes accessed | tf_op | source)
XLA Modules:
  0.0 139.3 jit_solution(7340541154448605081)
XLA Ops:
  0.6 0.7 stack.42.at_ref
  1.3 2.6 %shard_map.126 = (bf16[3,32,256]{2,1,0:T(8,128)(2,1)}, bf16[3,32,256]{2,1,0:T(8,128)(2,1)}, bf16[3,32,256]{2,1,0:T(8,128)(2,1)}, bf16[3,32,256]{2,1,0:T(8,128)(2,1)}, bf16[2,128,256]{2,1,0:T(8,128)(2,1)}) custom-call(s32[7]{0:T(128)} %stack.42.at_ref, bf16[3,32,1024]{2,1,0:T(8,128)(2,1)} %w_ref.1, bf16[512,4096]{1,0:T(8,128)(2,1)} %bitcast.23, ...), custom_call_target="tpu_custom_call" | custom-call | tf_op jit(solution)/shard_map/pallas_call | solution.py:93
  3.9 2.3 %collective-permute-start.9 = (bf16[2,128,256]{2,1,0:T(8,128)(2,1)}, bf16[2,128,256]{2,1,0:T(8,128)(2,1)S(1)}, u32[]{:S(2)}, u32[]{:S(2)}) collective-permute-start(bf16[2,128,256]{2,1,0:T(8,128)(2,1)} %get-tuple-element.26.mine_ref), channel_id=1, source_target_pairs={{0,1},{1,0},{2,3},{3,2},{4,5},{5,4},{6,7},{7,6},{8,9},{9,8},{10,11... | collective-permute-start | bytes 393224 | tf_op jit(solution)/shard_map/ppermute | solution.py:75
  6.2 1.5 %collective-permute-start.6 = (bf16[3,32,256]{2,1,0:T(8,128)(2,1)}, bf16[3,32,256]{2,1,0:T(8,128)(2,1)S(1)}, u32[]{:S(2)}, u32[]{:S(2)}) collective-permute-start(bf16[3,32,256]{2,1,0:T(8,128)(2,1)} %get-tuple-element.23), channel_id=1, source_target_pairs={{0,4},{4,8},{8,12},{12,0},{1,5},{5,9},{9,13},{13,1},{2,6},{6,10},{... | collective-permute-start | bytes 147464 | tf_op jit(solution)/shard_map/ppermute | solution.py:79
  7.7 2.7 %collective-permute-start.7 = (bf16[3,32,256]{2,1,0:T(8,128)(2,1)}, bf16[3,32,256]{2,1,0:T(8,128)(2,1)S(1)}, u32[]{:S(2)}, u32[]{:S(2)}) collective-permute-start(bf16[3,32,256]{2,1,0:T(8,128)(2,1)} %get-tuple-element.24), channel_id=1, source_target_pairs={{0,8},{4,12},{8,0},{12,4},{1,9},{5,13},{9,1},{13,5},{2,10},{6,14},... | collective-permute-start | bytes 147464 | tf_op jit(solution)/shard_map/ppermute | solution.py:79
  10.4 1.4 %collective-permute-start.8 = (bf16[3,32,256]{2,1,0:T(8,128)(2,1)}, bf16[3,32,256]{2,1,0:T(8,128)(2,1)S(1)}, u32[]{:S(2)}, u32[]{:S(2)}) collective-permute-start(bf16[3,32,256]{2,1,0:T(8,128)(2,1)} %get-tuple-element.25), channel_id=1, source_target_pairs={{0,12},{4,0},{8,4},{12,8},{1,13},{5,1},{9,5},{13,9},{2,14},{6,2},{... | collective-permute-start | bytes 147464 | tf_op jit(solution)/shard_map/ppermute | solution.py:79
  11.8 1.9 %collective-permute-start = (bf16[8,512]{1,0:T(8,128)(2,1)S(1)}, bf16[8,512]{1,0:T(8,128)(2,1)S(1)}, u32[]{:S(2)}, u32[]{:S(2)}) collective-permute-start(bf16[8,512]{1,0:T(8,128)(2,1)S(1)} %slice_bitcast_fusion), channel_id=1, source_target_pairs={{0,2},{2,4},{4,6},{6,8},{8,10},{10,12},{12,14},{14,16},{16,18},{18... | collective-permute-start | bytes 24584 | tf_op jit(solution)/shard_map/ppermute | solution.py:405
  13.8 7.3 %collective-permute-done.halo_ref = bf16[8,512]{1,0:T(8,128)(2,1)S(1)} collective-permute-done((bf16[8,512]{1,0:T(8,128)(2,1)S(1)}, bf16[8,512]{1,0:T(8,128)(2,1)S(1)}, u32[]{:S(2)}, u32[]{:S(2)}) %collective-permute-start) | collective-permute-done | bytes 8224 | tf_op jit(solution)/shard_map/ppermute | solution.py:405
  21.0 1.1 copy-done.9
  22.2 2.5 %shard_map.122.latent_ref.refs_0_.refs_4_ = bf16[256,512]{1,0:T(8,128)(2,1)S(1)} custom-call(bf16[8,512]{1,0:T(8,128)(2,1)S(1)} %collective-permute-done.halo_ref, bf16[512,512]{1,0:T(8,128)(2,1)S(1)} %bitcast.34, bf16[3,512,256]{2,1,0:T(8,128)(2,1)S(1)} %bitcast.33, bf16[256,512]{1,0:T(8,128)(2,1)S(1)} %bitcast.35, bf16[4,512,512]{2,1,0:T(8,128)(2,1)S(1)} %bitcast.26), custom_call_target="tpu_custom_call" | custom-call | tf_op jit(solution)/shard_map/pallas_call | solution.py:63
  24.8 0.8 copy-done.19
  25.6 0.1 collective-permute-start.11
  25.7 1.3 collective-permute-start.2
  27.0 1.9 %collective-permute-start.13 = (bf16[256,512]{1,0:T(8,128)(2,1)S(1)}, bf16[256,512]{1,0:T(8,128)(2,1)S(1)}, u32[]{:S(2)}, u32[]{:S(2)}) collective-permute-start(bf16[256,512]{1,0:T(8,128)(2,1)S(1)} %shard_map.122.latent_ref.refs_0_.refs_4_), channel_id=1, source_target_pairs={{0,16},{16,32},{32,48},{48,64},{64,80},{80,96},{96,112},{112,128},... | collective-permute-start | bytes 786440 | tf_op jit(solution)/shard_map/ppermute | solution.py:415
  28.9 0.1 collective-permute-start.10
  29.0 5.1 %collective-permute-done.11.w10 = bf16[4,3,32,256]{3,2,1,0:T(8,128)(2,1)S(1)} collective-permute-done((bf16[4,3,32,256]{3,2,1,0:T(8,128)(2,1)S(1)}, bf16[4,3,32,256]{3,2,1,0:T(8,128)(2,1)S(1)}, u32[]{:S(2)}, u32[]{:S(2)}) %collective-permute-start.11) | collective-permute-done | bytes 196640 | tf_op jit(solution)/shard_map/ppermute | solution.py:75
  34.2 3.8 %shard_map.123 = (bf16[256,2048]{1,0:T(8,128)(2,1)}, bf16[256,2048]{1,0:T(8,128)(2,1)S(1)}) custom-call(s32[7]{0:T(128)S(1)} %copy-done.20, bf16[256,512]{1,0:T(8,128)(2,1)S(1)} %shard_map.122.latent_ref.refs_0_.refs_4_, bf16[512,4096]{1,0:T(8,128)(2,1)S(1)} %bitcast.25), custom_call_target="tpu_custom_call" | custom-call | tf_op jit(solution)/shard_map/pallas_call | solution.py:226
  37.9 1.0 copy-done.24
  39.0 1.4 %collective-permute-start.1 = (bf16[256,2048]{1,0:T(8,128)(2,1)}, bf16[256,2048]{1,0:T(8,128)(2,1)}, u32[]{:S(2)}, u32[]{:S(2)}) collective-permute-start(bf16[256,2048]{1,0:T(8,128)(2,1)} %get-tuple-element.20.refs_0_), channel_id=1, source_target_pairs={{0,1},{1,0},{2,3},{3,2},{4,5},{5,4},{6,7},{7,6},{8,9},{9,8},{10,11... | collective-permute-start | bytes 3145736 | tf_op jit(solution)/shard_map/ppermute | solution.py:75
  40.5 3.2 %shard_map.128 = bf16[8,32,896]{2,1,0:T(8,128)(2,1)} custom-call(s32[7]{0:T(128)S(1)} %copy-done.20, bf16[4,3,32,256]{3,2,1,0:T(8,128)(2,1)S(1)} %shard_map.127.w00, bf16[4,3,32,256]{3,2,1,0:T(8,128)(2,1)S(1)} %collective-permute-done.10.w01, bf16[4,3,32,256]{3,2,1,0:T(8,128)(2,1)S(1)} %collective-permute-done.11.w10, ...), custom_call_target="tpu_custom_call" | custom-call | tf_op jit(solution)/shard_map/pallas_call | solution.py:163
  43.6 5.8 %all-to-all-start = ((bf16[8,32,896]{2,1,0:T(8,128)(2,1)}), bf16[8,32,896]{2,1,0:T(8,128)(2,1)}, u32[]{:S(2)}, u32[]{:S(2)}) async-start(bf16[8,32,896]{2,1,0:T(8,128)(2,1)} %shard_map.128), calls=%async_computation | async-start | bytes 917504 | tf_op jit(solution)/shard_map/all_to_all | solution.py:426
  49.6 0.2 reduce_window_sum.11
  49.8 3.2 %collective-permute-start.4 = (bf16[2,256,512]{2,1,0:T(8,128)(2,1)S(1)}, bf16[2,256,512]{2,1,0:T(8,128)(2,1)S(1)}, u32[]{:S(2)}, u32[]{:S(2)}) collective-permute-start(bf16[2,256,512]{2,1,0:T(8,128)(2,1)S(1)} %shard_map.125.refs_1_.a), channel_id=1, source_target_pairs={{0,12},{4,0},{8,4},{12,8},{1,13},{5,1},{9,5},{13,9},{2,14},{6,2},{... | collective-permute-start | bytes 1572872 | tf_op jit(solution)/shard_map/ppermute | solution.py:79
  53.1 3.9 %collective-permute-start.15 = (bf16[256,512]{1,0:T(8,128)(2,1)S(1)}, bf16[256,512]{1,0:T(8,128)(2,1)S(1)}, u32[]{:S(2)}, u32[]{:S(2)}) collective-permute-start(bf16[256,512]{1,0:T(8,128)(2,1)S(1)} %collective-permute-done.2.refs_1_), channel_id=1, source_target_pairs={{0,16},{16,32},{32,48},{48,64},{64,80},{80,96},{96,112},{112,128},... | collective-permute-start | bytes 786440 | tf_op jit(solution)/shard_map/ppermute | solution.py:416
  57.0 0.1 convert_reduce_fusion
  57.2 11.3 %collective-permute-done.15.refs_1_ = bf16[256,512]{1,0:T(8,128)(2,1)S(1)} collective-permute-done((bf16[256,512]{1,0:T(8,128)(2,1)S(1)}, bf16[256,512]{1,0:T(8,128)(2,1)S(1)}, u32[]{:S(2)}, u32[]{:S(2)}) %collective-permute-start.15) | collective-permute-done | bytes 262176 | tf_op jit(solution)/shard_map/ppermute | solution.py:416
  68.7 2.0 %collective-permute-start.16 = (bf16[2,256,512]{2,1,0:T(8,128)(2,1)S(1)}, bf16[2,256,512]{2,1,0:T(8,128)(2,1)S(1)}, u32[]{:S(2)}, u32[]{:S(2)}) collective-permute-start(bf16[2,256,512]{2,1,0:T(8,128)(2,1)S(1)} %shard_map.130.b), channel_id=1, source_target_pairs={{0,4},{4,8},{8,12},{12,0},{1,5},{5,9},{9,13},{13,1},{2,6},{6,10},{... | collective-permute-start | bytes 1572872 | tf_op jit(solution)/shard_map/ppermute | solution.py:79
  70.7 1.1 shard_map.129
  71.8 0.7 copy-done.11
  72.6 0.6 copy-done.16
  73.2 4.4 %all-to-all-start.1 = ((bf16[8,32,768]{2,1,0:T(8,128)(2,1)}), bf16[8,32,768]{2,1,0:T(8,128)(2,1)S(1)}, u32[]{:S(2)}, u32[]{:S(2)}) async-start(bf16[8,32,768]{2,1,0:T(8,128)(2,1)} %copy-done.11), calls=%async_computation.1 | async-start | bytes 786432 | tf_op jit(solution)/shard_map/all_to_all | solution.py:438
  77.6 0.7 copy-done.14
  78.4 0.7 copy-done.21
  79.0 1.2 copy-done.25
  80.2 3.6 %shard_map.124 = (bf16[256,2048]{1,0:T(8,128)(2,1)}, f32[8,256]{1,0:T(8,128)S(1)}) custom-call(s32[7]{0:T(128)S(1)} %copy-done.21, bf16[256,2048]{1,0:T(8,128)(2,1)S(1)} %copy-done.25, bf16[256,2048]{1,0:T(8,128)(2,1)} %collective-permute-done.1.got_ref, f32[2,8,256]{2,1,0:T(8,128)S(1)} %fusion.2.active_ref, f32[2,4096]{1,0:T(2,128)S(1)} %copy-done.14), custom_call_target="tpu_custom_call" | custom-call | flops 20000000000 | tf_op jit(solution)/shard_map/pallas_call | solution.py:262
  83.9 1.5 %collective-permute-start.14 = (f32[8,256]{1,0:T(8,128)S(1)}, f32[8,256]{1,0:T(8,128)S(1)}, u32[]{:S(2)}, u32[]{:S(2)}) collective-permute-start(f32[8,256]{1,0:T(8,128)S(1)} %get-tuple-element.28), channel_id=1, source_target_pairs={{0,1},{1,0},{2,3},{3,2},{4,5},{5,4},{6,7},{7,6},{8,9},{9,8},{10,11... | collective-permute-start | bytes 24584 | tf_op jit(solution)/shard_map/ppermute | solution.py:75
  85.3 3.7 %collective-permute-done.14 = f32[8,256]{1,0:T(8,128)S(1)} collective-permute-done((f32[8,256]{1,0:T(8,128)S(1)}, f32[8,256]{1,0:T(8,128)S(1)}, u32[]{:S(2)}, u32[]{:S(2)}) %collective-permute-start.14) | collective-permute-done | bytes 8224 | tf_op jit(solution)/shard_map/ppermute | solution.py:75
  89.0 0.6 add_rsqrt_fusion.refs_1_
  89.6 2.2 %all-to-all-done.1 = bf16[8,32,768]{2,1,0:T(8,128)(2,1)S(1)} async-done(((bf16[8,32,768]{2,1,0:T(8,128)(2,1)}), bf16[8,32,768]{2,1,0:T(8,128)(2,1)S(1)}, u32[]{:S(2)}, u32[]{:S(2)}) %all-to-all-start.1) | async-done | bytes 393248 | tf_op jit(solution)/shard_map/all_to_all | solution.py:438
  91.8 0.7 copy-done.23
  92.5 0.8 collective-permute-start.19
  93.2 0.3 collective-permute-start.5
  93.5 2.9 %collective-permute-start.22 = (bf16[2,256,512]{2,1,0:T(8,128)(2,1)S(1)}, bf16[2,256,512]{2,1,0:T(8,128)(2,1)S(1)}, u32[]{:S(2)}, u32[]{:S(2)}) collective-permute-start(bf16[2,256,512]{2,1,0:T(8,128)(2,1)S(1)} %collective-permute-done.17.refs_3_.br), channel_id=1, source_target_pairs={{0,12},{4,0},{8,4},{12,8},{1,13},{5,1},{9,5},{13,9},{2,14},{6,2},{... | collective-permute-start | bytes 1572872 | tf_op jit(solution)/shard_map/ppermute | solution.py:79
  96.5 9.9 %all_to_all.18 = f32[4,1,256]{2,1,0:T(1,128)S(1)} all-to-all(f32[4,1,256]{2,1,0:T(1,128)S(1)} %broadcast_in_dim.5), channel_id=1, replica_groups=mesh['yl'=2,'z'=8,'x'=4,'c'=2,'tp'=2] {'x'}, dimensions={0} | all-to-all | bytes 8192 | tf_op jit(solution)/shard_map/all_to_all | solution.py:442
  106.5 0.6 collective-permute-start.20
  107.0 1.9 %collective-permute-start.23 = (f32[4,256]{1,0:T(4,128)S(1)}, f32[4,256]{1,0:T(4,128)S(1)}, u32[]{:S(2)}, u32[]{:S(2)}) collective-permute-start(f32[4,256]{1,0:T(4,128)S(1)} %bitcast.39), channel_id=1, source_target_pairs={{0,16},{16,32},{32,48},{48,64},{64,80},{80,96},{96,112},{112,128},... | collective-permute-start | bytes 12296 | tf_op jit(solution)/shard_map/ppermute | solution.py:445
  109.0 0.7 copy-done.17
  109.7 0.7 copy-done.22
  110.4 2.6 %shard_map.133 = (bf16[4,256,512]{2,1,0:T(8,128)(2,1)S(1)}, bf16[4,256,256]{2,1,0:T(8,128)(2,1)S(1)}, bf16[1024,768]{1,0:T(8,128)(2,1)S(1)}) custom-call(s32[7]{0:T(128)S(1)} %copy-done.22, bf16[2,256,512]{2,1,0:T(8,128)(2,1)S(1)} %shard_map.125.refs_1_.a, bf16[2,256,512]{2,1,0:T(8,128)(2,1)S(1)} %collective-permute-done.3.refs_0_.al, ...), custom_call_target="tpu_custom_call" | custom-call | tf_op jit(solution)/shard_map/pallas_call | solution.py:313
  113.0 0.8 copy-done.1
  113.8 0.8 collective-permute-done.23.scale_ref
  114.7 2.0 %shard_map.134.pm_ref = bf16[4,256,512]{2,1,0:T(8,128)(2,1)S(1)} custom-call(s32[7]{0:T(128)S(1)} %copy-done.22, bf16[2,256,512]{2,1,0:T(8,128)(2,1)S(1)} %copy-done.8, bf16[2,256,512]{2,1,0:T(8,128)(2,1)S(1)} %copy-done.6, bf16[2,256,512]{2,1,0:T(8,128)(2,1)S(1)} %collective-permute-done.17.refs_3_.br, bf16[2,256,512]{2,1,0:T(8,128)(2,1)S(1)} %collective-permute-done.22.bf, ...), custom_call_target="tpu_custom_call" | custom-call | tf_op jit(solution)/shard_map/pallas_call | solution.py:313
  116.7 0.1 collective-permute-start.24
  116.8 0.5 collective-permute-start.21
  117.4 2.1 %collective-permute-done.24.pt_ref = bf16[4,256,512]{2,1,0:T(8,128)(2,1)S(1)} collective-permute-done((bf16[4,256,512]{2,1,0:T(8,128)(2,1)S(1)}, bf16[4,256,512]{2,1,0:T(8,128)(2,1)S(1)}, u32[]{:S(2)}, u32[]{:S(2)}) %collective-permute-start.24) | collective-permute-done | bytes 1048608 | tf_op jit(solution)/shard_map/ppermute | solution.py:75
  119.5 1.6 %collective-permute-done.21.ot_ref = bf16[4,256,512]{2,1,0:T(8,128)(2,1)} collective-permute-done((bf16[4,256,512]{2,1,0:T(8,128)(2,1)S(1)}, bf16[4,256,512]{2,1,0:T(8,128)(2,1)}, u32[]{:S(2)}, u32[]{:S(2)}) %collective-permute-start.21) | collective-permute-done | bytes 1048608 | tf_op jit(solution)/shard_map/ppermute | solution.py:75
  121.1 1.0 copy-done.2
  122.2 5.5 %shard_map.136 = (bf16[256,256]{1,0:T(8,128)(2,1)S(1)}, bf16[256,256]{1,0:T(8,128)(2,1)S(1)}, bf16[256,256]{1,0:T(8,128)(2,1)S(1)}) custom-call(s32[6]{0:T(128)S(1)} %pad_add_fusion.2.place_ref, bf16[4,256,256]{2,1,0:T(8,128)(2,1)S(1)} %copy-done.2, bf16[4,256,512]{2,1,0:T(8,128)(2,1)S(1)} %get-tuple-element.31.om_ref, ...), custom_call_target="tpu_custom_call" | custom-call | tf_op jit(solution)/shard_map/pallas_call | solution.py:358
  127.7 1.2 collective-permute-start.25
  128.9 2.7 %collective-permute-start.26 = (bf16[256,256]{1,0:T(8,128)(2,1)S(1)}, bf16[256,256]{1,0:T(8,128)(2,1)S(1)}, u32[]{:S(2)}, u32[]{:S(2)}) collective-permute-start(bf16[256,256]{1,0:T(8,128)(2,1)S(1)} %get-tuple-element.34), channel_id=1, source_target_pairs={{0,8},{4,12},{8,0},{12,4},{1,9},{5,13},{9,1},{13,5},{2,10},{6,14},... | collective-permute-start | bytes 393224 | tf_op jit(solution)/shard_map/ppermute | solution.py:79
  131.6 0.5 collective-permute-start.27
  132.3 3.0 %shard_map.135.a_ref = bf16[256,256]{1,0:T(8,128)(2,1)S(1)} custom-call(s32[4]{0:T(128)S(1)} %pad_add_fusion.1.place_ref, bf16[4,256,256]{2,1,0:T(8,128)(2,1)S(1)} %copy-done.3, bf16[4,256,512]{2,1,0:T(8,128)(2,1)S(1)} %get-tuple-element.31.om_ref, bf16[4,256,512]{2,1,0:T(8,128)(2,1)} %collective-permute-done.21.ot_ref, ...), custom_call_target="tpu_custom_call" | custom-call | tf_op jit(solution)/shard_map/pallas_call | solution.py:358
  135.3 2.6 %collective-permute-done.26.c_ref = bf16[256,256]{1,0:T(8,128)(2,1)S(1)} collective-permute-done((bf16[256,256]{1,0:T(8,128)(2,1)S(1)}, bf16[256,256]{1,0:T(8,128)(2,1)S(1)}, u32[]{:S(2)}, u32[]{:S(2)}) %collective-permute-start.26) | collective-permute-done | bytes 131104 | tf_op jit(solution)/shard_map/ppermute | solution.py:79
  137.9 1.4 %shard_map.137 = bf16[256,1024]{1,0:T(8,128)(2,1)} custom-call(s32[3]{0:T(128)S(1)} %pad_add_fusion.place_ref, bf16[256,256]{1,0:T(8,128)(2,1)S(1)} %shard_map.135.a_ref, bf16[256,256]{1,0:T(8,128)(2,1)S(1)} %collective-permute-done.25.b_ref, bf16[256,256]{1,0:T(8,128)(2,1)S(1)} %collective-permute-done.26.c_ref, ...), custom_call_target="tpu_custom_call" | custom-call | tf_op jit(solution)/shard_map/pallas_call | solution.py:375
  (85 shorter events, 0.9 us)
Async XLA Ops:
  1.3 10.5 %copy-start.10 = (bf16[1,512,512]{2,1,0:T(8,128)(2,1)S(1)}, bf16[1,512,512]{2,1,0:T(8,128)(2,1)}, u32[]{:S(2)}) copy-start(bf16[1,512,512]{2,1,0:T(8,128)(2,1)} %param.11) | copy-start | bytes 1572868
  1.3 19.7 %copy-start.4 = (bf16[1,4,512,512]{3,2,1,0:T(8,128)(2,1)S(1)}, bf16[1,4,512,512]{3,2,1,0:T(8,128)(2,1)}, u32[]{:S(2)}) copy-start(bf16[1,4,512,512]{3,2,1,0:T(8,128)(2,1)} %param.14) | copy-start | bytes 6291460
  1.3 19.7 %copy-start.12 = (bf16[1,256,512]{2,1,0:T(8,128)(2,1)S(1)}, bf16[1,256,512]{2,1,0:T(8,128)(2,1)}, u32[]{:S(2)}) copy-start(bf16[1,256,512]{2,1,0:T(8,128)(2,1)} %param.13) | copy-start | bytes 786436
  1.3 32.9 %copy-start.20 = (s32[7]{0:T(128)S(1)}, s32[7]{0:T(128)}, u32[]{:S(2)}) copy-start(s32[7]{0:T(128)} %stack.42.at_ref) | copy-start | bytes 88
  3.9 20.9 %collective-permute-start.9 = (bf16[2,128,256]{2,1,0:T(8,128)(2,1)}, bf16[2,128,256]{2,1,0:T(8,128)(2,1)S(1)}, u32[]{:S(2)}, u32[]{:S(2)}) collective-permute-start(bf16[2,128,256]{2,1,0:T(8,128)(2,1)} %get-tuple-element.26.mine_ref), channel_id=1, source_target_pairs={{0,1},{1,0},{2,3},{3,2},{4,5},{5,4},{6,7},{7,6},{8,9},{9,8},{10,11... | collective-permute-start | bytes 393224 | tf_op jit(solution)/shard_map/ppermute | solution.py:75
  6.2 18.5 %collective-permute-start.6 = (bf16[3,32,256]{2,1,0:T(8,128)(2,1)}, bf16[3,32,256]{2,1,0:T(8,128)(2,1)S(1)}, u32[]{:S(2)}, u32[]{:S(2)}) collective-permute-start(bf16[3,32,256]{2,1,0:T(8,128)(2,1)} %get-tuple-element.23), channel_id=1, source_target_pairs={{0,4},{4,8},{8,12},{12,0},{1,5},{5,9},{9,13},{13,1},{2,6},{6,10},{... | collective-permute-start | bytes 147464 | tf_op jit(solution)/shard_map/ppermute | solution.py:79
  7.7 17.0 %collective-permute-start.7 = (bf16[3,32,256]{2,1,0:T(8,128)(2,1)}, bf16[3,32,256]{2,1,0:T(8,128)(2,1)S(1)}, u32[]{:S(2)}, u32[]{:S(2)}) collective-permute-start(bf16[3,32,256]{2,1,0:T(8,128)(2,1)} %get-tuple-element.24), channel_id=1, source_target_pairs={{0,8},{4,12},{8,0},{12,4},{1,9},{5,13},{9,1},{13,5},{2,10},{6,14},... | collective-permute-start | bytes 147464 | tf_op jit(solution)/shard_map/ppermute | solution.py:79
  10.4 14.3 %collective-permute-start.8 = (bf16[3,32,256]{2,1,0:T(8,128)(2,1)}, bf16[3,32,256]{2,1,0:T(8,128)(2,1)S(1)}, u32[]{:S(2)}, u32[]{:S(2)}) collective-permute-start(bf16[3,32,256]{2,1,0:T(8,128)(2,1)} %get-tuple-element.25), channel_id=1, source_target_pairs={{0,12},{4,0},{8,4},{12,8},{1,13},{5,1},{9,5},{13,9},{2,14},{6,2},{... | collective-permute-start | bytes 147464 | tf_op jit(solution)/shard_map/ppermute | solution.py:79
  11.8 9.2 %collective-permute-start = (bf16[8,512]{1,0:T(8,128)(2,1)S(1)}, bf16[8,512]{1,0:T(8,128)(2,1)S(1)}, u32[]{:S(2)}, u32[]{:S(2)}) collective-permute-start(bf16[8,512]{1,0:T(8,128)(2,1)S(1)} %slice_bitcast_fusion), channel_id=1, source_target_pairs={{0,2},{2,4},{4,6},{6,8},{8,10},{10,12},{12,14},{14,16},{16,18},{18... | collective-permute-start | bytes 24584 | tf_op jit(solution)/shard_map/ppermute | solution.py:405
  21.0 1.1 copy-start.9
  22.2 12.0 %copy-start = (bf16[1,512,4096]{2,1,0:T(8,128)(2,1)S(1)}, bf16[1,512,4096]{2,1,0:T(8,128)(2,1)}, u32[]{:S(2)}) copy-start(bf16[1,512,4096]{2,1,0:T(8,128)(2,1)} %param.15) | copy-start | bytes 12582916
  24.7 0.8 copy-start.19
  25.6 14.9 %copy-start.13 = (f32[2,4096]{1,0:T(2,128)S(1)}, f32[2,4096]{1,0:T(2,128)}, u32[]{:S(2)}) copy-start(f32[2,4096]{1,0:T(2,128)} %t1.1) | copy-start | bytes 98308
  25.6 14.9 %copy-start.15 = (bf16[2,128,256]{2,1,0:T(8,128)(2,1)S(1)}, bf16[2,128,256]{2,1,0:T(8,128)(2,1)}, u32[]{:S(2)}) copy-start(bf16[2,128,256]{2,1,0:T(8,128)(2,1)} %get-tuple-element.26.mine_ref) | copy-start | bytes 393220
  25.6 14.9 %copy-start.18 = (f32[4096]{0:T(1024)S(1)}, f32[4096]{0:T(1024)}, u32[]{:S(2)}) copy-start(f32[4096]{0:T(1024)} %param.18) | copy-start | bytes 49156
  25.6 8.6 %collective-permute-start.11 = (bf16[4,3,32,256]{3,2,1,0:T(8,128)(2,1)S(1)}, bf16[4,3,32,256]{3,2,1,0:T(8,128)(2,1)S(1)}, u32[]{:S(2)}, u32[]{:S(2)}) collective-permute-start(bf16[4,3,32,256]{3,2,1,0:T(8,128)(2,1)S(1)} %shard_map.127.w00), channel_id=1, source_target_pairs={{0,128},{128,0},{1,129},{129,1},{2,130},{130,2},{3,131},{131,3},{4... | collective-permute-start | bytes 589832 | tf_op jit(solution)/shard_map/ppermute | solution.py:75
  25.7 14.7 %collective-permute-start.2 = (bf16[256,512]{1,0:T(8,128)(2,1)S(1)}, bf16[256,512]{1,0:T(8,128)(2,1)S(1)}, u32[]{:S(2)}, u32[]{:S(2)}) collective-permute-start(bf16[256,512]{1,0:T(8,128)(2,1)S(1)} %shard_map.122.latent_ref.refs_0_.refs_4_), channel_id=1, source_target_pairs={{0,1},{1,0},{2,3},{3,2},{4,5},{5,4},{6,7},{7,6},{8,9},{9,8},{10,11... | collective-permute-start | bytes 786440 | tf_op jit(solution)/shard_map/ppermute | solution.py:75
  27.0 13.4 %collective-permute-start.13 = (bf16[256,512]{1,0:T(8,128)(2,1)S(1)}, bf16[256,512]{1,0:T(8,128)(2,1)S(1)}, u32[]{:S(2)}, u32[]{:S(2)}) collective-permute-start(bf16[256,512]{1,0:T(8,128)(2,1)S(1)} %shard_map.122.latent_ref.refs_0_.refs_4_), channel_id=1, source_target_pairs={{0,16},{16,32},{32,48},{48,64},{64,80},{80,96},{96,112},{112,128},... | collective-permute-start | bytes 786440 | tf_op jit(solution)/shard_map/ppermute | solution.py:415
  28.9 11.5 %collective-permute-start.10 = (bf16[4,3,32,256]{3,2,1,0:T(8,128)(2,1)S(1)}, bf16[4,3,32,256]{3,2,1,0:T(8,128)(2,1)S(1)}, u32[]{:S(2)}, u32[]{:S(2)}) collective-permute-start(bf16[4,3,32,256]{3,2,1,0:T(8,128)(2,1)S(1)} %shard_map.127.w00), channel_id=1, source_target_pairs={{0,2},{2,0},{1,3},{3,1},{4,6},{6,4},{5,7},{7,5},{8,10},{10,8},{9,1... | collective-permute-start | bytes 589832 | tf_op jit(solution)/shard_map/ppermute | solution.py:75
  34.2 6.3 %collective-permute-start.12 = (bf16[4,3,32,256]{3,2,1,0:T(8,128)(2,1)S(1)}, bf16[4,3,32,256]{3,2,1,0:T(8,128)(2,1)S(1)}, u32[]{:S(2)}, u32[]{:S(2)}) collective-permute-start(bf16[4,3,32,256]{3,2,1,0:T(8,128)(2,1)S(1)} %collective-permute-done.11.w10), channel_id=1, source_target_pairs={{0,2},{2,0},{1,3},{3,1},{4,6},{6,4},{5,7},{7,5},{8,10},{10,8},{9,1... | collective-permute-start | bytes 589832 | tf_op jit(solution)/shard_map/ppermute | solution.py:75
  37.9 1.0 copy-start.24
  39.0 38.6 %collective-permute-start.1 = (bf16[256,2048]{1,0:T(8,128)(2,1)}, bf16[256,2048]{1,0:T(8,128)(2,1)}, u32[]{:S(2)}, u32[]{:S(2)}) collective-permute-start(bf16[256,2048]{1,0:T(8,128)(2,1)} %get-tuple-element.20.refs_0_), channel_id=1, source_target_pairs={{0,1},{1,0},{2,3},{3,2},{4,5},{5,4},{6,7},{7,6},{8,9},{9,8},{10,11... | collective-permute-start | bytes 3145736 | tf_op jit(solution)/shard_map/ppermute | solution.py:75
  40.5 9.1 %copy-start.26 = (s32[2,32]{1,0:T(2,128)S(1)}, s32[2,32]{1,0:T(2,128)}, u32[]{:S(2)}) copy-start(s32[2,32]{1,0:T(2,128)} %param.16) | copy-start | bytes 772
  43.6 27.1 %all-to-all-start = ((bf16[8,32,896]{2,1,0:T(8,128)(2,1)}), bf16[8,32,896]{2,1,0:T(8,128)(2,1)}, u32[]{:S(2)}, u32[]{:S(2)}) async-start(bf16[8,32,896]{2,1,0:T(8,128)(2,1)} %shard_map.128), calls=%async_computation | async-start | bytes 917504 | tf_op jit(solution)/shard_map/all_to_all | solution.py:426
  49.8 20.9 %collective-permute-start.3 = (bf16[2,256,512]{2,1,0:T(8,128)(2,1)S(1)}, bf16[2,256,512]{2,1,0:T(8,128)(2,1)S(1)}, u32[]{:S(2)}, u32[]{:S(2)}) collective-permute-start(bf16[2,256,512]{2,1,0:T(8,128)(2,1)S(1)} %shard_map.125.refs_1_.a), channel_id=1, source_target_pairs={{0,4},{4,8},{8,12},{12,0},{1,5},{5,9},{9,13},{13,1},{2,6},{6,10},{... | collective-permute-start | bytes 1572872 | tf_op jit(solution)/shard_map/ppermute | solution.py:79
  49.8 20.9 %collective-permute-start.4 = (bf16[2,256,512]{2,1,0:T(8,128)(2,1)S(1)}, bf16[2,256,512]{2,1,0:T(8,128)(2,1)S(1)}, u32[]{:S(2)}, u32[]{:S(2)}) collective-permute-start(bf16[2,256,512]{2,1,0:T(8,128)(2,1)S(1)} %shard_map.125.refs_1_.a), channel_id=1, source_target_pairs={{0,12},{4,0},{8,4},{12,8},{1,13},{5,1},{9,5},{13,9},{2,14},{6,2},{... | collective-permute-start | bytes 1572872 | tf_op jit(solution)/shard_map/ppermute | solution.py:79
  53.1 15.4 %collective-permute-start.15 = (bf16[256,512]{1,0:T(8,128)(2,1)S(1)}, bf16[256,512]{1,0:T(8,128)(2,1)S(1)}, u32[]{:S(2)}, u32[]{:S(2)}) collective-permute-start(bf16[256,512]{1,0:T(8,128)(2,1)S(1)} %collective-permute-done.2.refs_1_), channel_id=1, source_target_pairs={{0,16},{16,32},{32,48},{48,64},{64,80},{80,96},{96,112},{112,128},... | collective-permute-start | bytes 786440 | tf_op jit(solution)/shard_map/ppermute | solution.py:416
  68.6 15.3 %copy-start.7 = (bf16[2,256,512]{2,1,0:T(8,128)(2,1)}, bf16[2,256,512]{2,1,0:T(8,128)(2,1)S(1)}, u32[]{:S(2)}) copy-start(bf16[2,256,512]{2,1,0:T(8,128)(2,1)S(1)} %shard_map.130.b) | copy-start | bytes 1572868
  68.6 21.0 %collective-permute-start.17 = (bf16[2,256,512]{2,1,0:T(8,128)(2,1)S(1)}, bf16[2,256,512]{2,1,0:T(8,128)(2,1)S(1)}, u32[]{:S(2)}, u32[]{:S(2)}) collective-permute-start(bf16[2,256,512]{2,1,0:T(8,128)(2,1)S(1)} %shard_map.130.b), channel_id=1, source_target_pairs={{0,12},{4,0},{8,4},{12,8},{1,13},{5,1},{9,5},{13,9},{2,14},{6,2},{... | collective-permute-start | bytes 1572872 | tf_op jit(solution)/shard_map/ppermute | solution.py:79
  68.7 20.9 %collective-permute-start.16 = (bf16[2,256,512]{2,1,0:T(8,128)(2,1)S(1)}, bf16[2,256,512]{2,1,0:T(8,128)(2,1)S(1)}, u32[]{:S(2)}, u32[]{:S(2)}) collective-permute-start(bf16[2,256,512]{2,1,0:T(8,128)(2,1)S(1)} %shard_map.130.b), channel_id=1, source_target_pairs={{0,4},{4,8},{8,12},{12,0},{1,5},{5,9},{9,13},{13,1},{2,6},{6,10},{... | collective-permute-start | bytes 1572872 | tf_op jit(solution)/shard_map/ppermute | solution.py:79
  71.8 0.7 copy-start.11
  72.6 0.6 copy-start.16
  73.2 18.6 %all-to-all-start.1 = ((bf16[8,32,768]{2,1,0:T(8,128)(2,1)}), bf16[8,32,768]{2,1,0:T(8,128)(2,1)S(1)}, u32[]{:S(2)}, u32[]{:S(2)}) async-start(bf16[8,32,768]{2,1,0:T(8,128)(2,1)} %copy-done.11), calls=%async_computation.1 | async-start | bytes 786432 | tf_op jit(solution)/shard_map/all_to_all | solution.py:438
  77.6 0.8 copy-start.14
  78.4 0.7 copy-start.21
  79.0 1.2 copy-start.25
  83.9 5.2 %collective-permute-start.14 = (f32[8,256]{1,0:T(8,128)S(1)}, f32[8,256]{1,0:T(8,128)S(1)}, u32[]{:S(2)}, u32[]{:S(2)}) collective-permute-start(f32[8,256]{1,0:T(8,128)S(1)} %get-tuple-element.28), channel_id=1, source_target_pairs={{0,1},{1,0},{2,3},{3,2},{4,5},{5,4},{6,7},{7,6},{8,9},{9,8},{10,11... | collective-permute-start | bytes 24584 | tf_op jit(solution)/shard_map/ppermute | solution.py:75
  89.6 19.4 %copy-start.5 = (bf16[2,256,512]{2,1,0:T(8,128)(2,1)}, bf16[2,256,512]{2,1,0:T(8,128)(2,1)S(1)}, u32[]{:S(2)}) copy-start(bf16[2,256,512]{2,1,0:T(8,128)(2,1)S(1)} %collective-permute-done.16.refs_2_.bl) | copy-start | bytes 1572868
  91.8 0.7 copy-start.23
  92.5 13.9 %collective-permute-start.19 = (bf16[256,768]{1,0:T(8,128)(2,1)S(1)}, bf16[256,768]{1,0:T(8,128)(2,1)S(1)}, u32[]{:S(2)}, u32[]{:S(2)}) collective-permute-start(bf16[256,768]{1,0:T(8,128)(2,1)S(1)} %bitcast.27), channel_id=1, source_target_pairs={{0,128},{128,0},{1,129},{129,1},{2,130},{130,2},{3,131},{131,3},{4... | collective-permute-start | bytes 1179656 | tf_op jit(solution)/shard_map/ppermute | solution.py:75
  93.2 15.7 %collective-permute-start.5 = (bf16[2,256,512]{2,1,0:T(8,128)(2,1)S(1)}, bf16[2,256,512]{2,1,0:T(8,128)(2,1)S(1)}, u32[]{:S(2)}, u32[]{:S(2)}) collective-permute-start(bf16[2,256,512]{2,1,0:T(8,128)(2,1)S(1)} %collective-permute-done.3.refs_0_.al), channel_id=1, source_target_pairs={{0,4},{4,8},{8,12},{12,0},{1,5},{5,9},{9,13},{13,1},{2,6},{6,10},{... | collective-permute-start | bytes 1572872 | tf_op jit(solution)/shard_map/ppermute | solution.py:79
  93.5 21.1 %collective-permute-start.22 = (bf16[2,256,512]{2,1,0:T(8,128)(2,1)S(1)}, bf16[2,256,512]{2,1,0:T(8,128)(2,1)S(1)}, u32[]{:S(2)}, u32[]{:S(2)}) collective-permute-start(bf16[2,256,512]{2,1,0:T(8,128)(2,1)S(1)} %collective-permute-done.17.refs_3_.br), channel_id=1, source_target_pairs={{0,12},{4,0},{8,4},{12,8},{1,13},{5,1},{9,5},{13,9},{2,14},{6,2},{... | collective-permute-start | bytes 1572872 | tf_op jit(solution)/shard_map/ppermute | solution.py:79
  106.4 2.6 %collective-permute-start.18 = (bf16[256,768]{1,0:T(8,128)(2,1)S(1)}, bf16[256,768]{1,0:T(8,128)(2,1)S(1)}, u32[]{:S(2)}, u32[]{:S(2)}) collective-permute-start(bf16[256,768]{1,0:T(8,128)(2,1)S(1)} %bitcast.28), channel_id=1, source_target_pairs={{0,2},{2,0},{1,3},{3,1},{4,6},{6,4},{5,7},{7,5},{8,10},{10,8},{9,1... | collective-permute-start | bytes 1179656 | tf_op jit(solution)/shard_map/ppermute | solution.py:75
  106.4 8.2 %copy-start.8 = (bf16[2,256,512]{2,1,0:T(8,128)(2,1)S(1)}, bf16[2,256,512]{2,1,0:T(8,128)(2,1)}, u32[]{:S(2)}) copy-start(bf16[2,256,512]{2,1,0:T(8,128)(2,1)} %copy-done.7) | copy-start | bytes 1572868
  106.5 2.5 %collective-permute-start.20 = (bf16[256,768]{1,0:T(8,128)(2,1)S(1)}, bf16[256,768]{1,0:T(8,128)(2,1)S(1)}, u32[]{:S(2)}, u32[]{:S(2)}) collective-permute-start(bf16[256,768]{1,0:T(8,128)(2,1)S(1)} %bitcast.30), channel_id=1, source_target_pairs={{0,2},{2,0},{1,3},{3,1},{4,6},{6,4},{5,7},{7,5},{8,10},{10,8},{9,1... | collective-permute-start | bytes 1179656 | tf_op jit(solution)/shard_map/ppermute | solution.py:75
  107.0 7.6 %collective-permute-start.23 = (f32[4,256]{1,0:T(4,128)S(1)}, f32[4,256]{1,0:T(4,128)S(1)}, u32[]{:S(2)}, u32[]{:S(2)}) collective-permute-start(f32[4,256]{1,0:T(4,128)S(1)} %bitcast.39), channel_id=1, source_target_pairs={{0,16},{16,32},{32,48},{48,64},{64,80},{80,96},{96,112},{112,128},... | collective-permute-start | bytes 12296 | tf_op jit(solution)/shard_map/ppermute | solution.py:445
  109.0 0.7 copy-start.17
  109.7 0.7 copy-start.22
  110.4 4.3 %copy-start.6 = (bf16[2,256,512]{2,1,0:T(8,128)(2,1)S(1)}, bf16[2,256,512]{2,1,0:T(8,128)(2,1)}, u32[]{:S(2)}) copy-start(bf16[2,256,512]{2,1,0:T(8,128)(2,1)} %copy-done.5) | copy-start | bytes 1572868
  113.0 0.8 copy-start.1
  114.7 2.7 %copy-start.27 = (s32[3]{0:T(128)S(1)}, s32[3]{0:T(128)}, u32[]{:S(2)}) copy-start(s32[3]{0:T(128)} %constant.57.clone) | copy-start | bytes 40
  116.7 2.7 %collective-permute-start.24 = (bf16[4,256,512]{2,1,0:T(8,128)(2,1)S(1)}, bf16[4,256,512]{2,1,0:T(8,128)(2,1)S(1)}, u32[]{:S(2)}, u32[]{:S(2)}) collective-permute-start(bf16[4,256,512]{2,1,0:T(8,128)(2,1)S(1)} %shard_map.134.pm_ref), channel_id=1, source_target_pairs={{0,2},{2,0},{1,3},{3,1},{4,6},{6,4},{5,7},{7,5},{8,10},{10,8},{9,1... | collective-permute-start | bytes 3145736 | tf_op jit(solution)/shard_map/ppermute | solution.py:75
  116.8 4.3 %collective-permute-start.21 = (bf16[4,256,512]{2,1,0:T(8,128)(2,1)S(1)}, bf16[4,256,512]{2,1,0:T(8,128)(2,1)}, u32[]{:S(2)}, u32[]{:S(2)}) collective-permute-start(bf16[4,256,512]{2,1,0:T(8,128)(2,1)S(1)} %get-tuple-element.31.om_ref), channel_id=1, source_target_pairs={{0,2},{2,0},{1,3},{3,1},{4,6},{6,4},{5,7},{7,5},{8,10},{10,8},{9,1... | collective-permute-start | bytes 3145736 | tf_op jit(solution)/shard_map/ppermute | solution.py:75
  121.1 1.0 copy-start.2
  122.2 10.2 %copy-start.3 = (bf16[4,256,256]{2,1,0:T(8,128)(2,1)S(1)}, bf16[4,256,256]{2,1,0:T(8,128)(2,1)}, u32[]{:S(2)}) copy-start(bf16[4,256,256]{2,1,0:T(8,128)(2,1)} %copy-done.1) | copy-start | bytes 1572868
  127.7 7.7 %collective-permute-start.25 = (bf16[256,256]{1,0:T(8,128)(2,1)S(1)}, bf16[256,256]{1,0:T(8,128)(2,1)S(1)}, u32[]{:S(2)}, u32[]{:S(2)}) collective-permute-start(bf16[256,256]{1,0:T(8,128)(2,1)S(1)} %get-tuple-element.33), channel_id=1, source_target_pairs={{0,4},{4,8},{8,12},{12,0},{1,5},{5,9},{9,13},{13,1},{2,6},{6,10},{... | collective-permute-start | bytes 393224 | tf_op jit(solution)/shard_map/ppermute | solution.py:79
  128.9 9.0 %collective-permute-start.26 = (bf16[256,256]{1,0:T(8,128)(2,1)S(1)}, bf16[256,256]{1,0:T(8,128)(2,1)S(1)}, u32[]{:S(2)}, u32[]{:S(2)}) collective-permute-start(bf16[256,256]{1,0:T(8,128)(2,1)S(1)} %get-tuple-element.34), channel_id=1, source_target_pairs={{0,8},{4,12},{8,0},{12,4},{1,9},{5,13},{9,1},{13,5},{2,10},{6,14},... | collective-permute-start | bytes 393224 | tf_op jit(solution)/shard_map/ppermute | solution.py:79
  131.6 6.3 %collective-permute-start.27 = (bf16[256,256]{1,0:T(8,128)(2,1)S(1)}, bf16[256,256]{1,0:T(8,128)(2,1)S(1)}, u32[]{:S(2)}, u32[]{:S(2)}) collective-permute-start(bf16[256,256]{1,0:T(8,128)(2,1)S(1)} %get-tuple-element.35), channel_id=1, source_target_pairs={{0,12},{4,0},{8,4},{12,8},{1,13},{5,1},{9,5},{13,9},{2,14},{6,2},{... | collective-permute-start | bytes 393224 | tf_op jit(solution)/shard_map/ppermute | solution.py:79

commit v7 on v6

--- a/solution.py
+++ b/solution.py
@@ -287,7 +287,7 @@
     for dx in range(4):
         at = lax.rem(x + dx, 4)
         act = active_ref[:, pl.ds(4 * row + at, 1), :].reshape(2, BLOCK)
-        side = jnp.concatenate([act, scale_ref[pl.ds(at, 1), :], jnp.zeros((5, BLOCK), F32)], axis=0).T
+        side = jnp.concatenate([act, scale_ref[pl.ds(at ^ x, 1), :], jnp.zeros((5, BLOCK), F32)], axis=0).T
         acc = dot(blocks[dx][0], w0) + dot(blocks[dx][1], w1)
         acc = (acc + side[:, 0:1] * line[0:1] + side[:, 1:2] * line[1:2]) * side[:, 2:3]
         kv_ref[at] = acc[:, -512:].astype(BF)
@@ -424,7 +424,7 @@
     w11 = swap(w10, "c")
     packed = partial_weights(at, (w00, w01, w10, w11), mine, rest, norm_gain[None], speaker_table, (give, a, prev))
     packed = lax.all_to_all(packed, "z", 0, 0, tiled=True)
-    m, lines = sum_weights(packed, (al, ar))
+    m, lines = sum_weights(packed, ())
     bounds = jnp.cumsum(turn_lengths, axis=1)
     start = ((row - 1 + jnp.arange(2)[:, None]) * 8 + 2 * jnp.arange(4)[None, :] + core) * BLOCK
     frames = start.reshape(8, 1) + jnp.arange(BLOCK)
@@ -432,15 +432,17 @@
     active = (turn % 2 == 1).astype(F32)
 
     got = swap(give, "tp")
-    embedded, square = embed_rows(at, own, got, active, speaker_table, ())
-    square = square + swap(square, "tp")
-    scale = lax.rsqrt(square[0:1] * (1.0 / D) + 1e-05)
+    embedded, square = embed_rows(at, own, got, active, speaker_table, (al, ar, b))
+    square = square[0:1]
+    beside = lax.ppermute(square, "x", [(i, i ^ 1) for i in range(4)])
+    across = lax.ppermute(square, ("x", "tp"), [(i, i ^ 3) for i in range(8)])
+    square = jnp.concatenate([square + swap(square, "tp"), beside + across])
+    scale = lax.rsqrt(square * (1.0 / D) + 1e-05)
+    scales = jnp.concatenate([scale, lax.ppermute(scale, "x", [(i, i ^ 2) for i in range(4)])])
     m00 = lax.all_to_all(m, "z", 0, 0, tiled=True).reshape(256, 768)
-    (m00,) = stack([m00], (scale, bl, br))
+    (m00,) = stack([m00], (scales, bl, br))
     m10 = swap(m00, "yl")
     m01 = swap(m00, "c")
-    scales = lax.all_to_all(jnp.broadcast_to(scale, (4, BLOCK)), "x", 0, 0, tiled=True)
-    (m10,) = stack([m10], (scales,))
     m11 = swap(m10, "c")
     scales_prev = lax.ppermute(scales, ("yl", "z"), behind)
 

time: 141 us -> 137 us (0.972)
  blocking collectives: 9.93 us -> 0 us
  starting transfers between devices: 47.2 us -> 52.9 us
  waiting for transfers between devices: 36.8 us -> 42.3 us
  local copies, waits for them, and re-layouts: 11.6 us -> 6.79 us
    all_to_all x1 -> x0, blocking collectives: 9.93 us -> none  [on_device(): lax.all_to_all(jnp.broadcast_to(scale, (4, BLOCK)), 'x', 0, 0, tiled=True)]
    ppermute x0 -> x3, waiting for transfers between devices: none -> 5.15 us  [the longest x1 4.08 us: on_device(): lax.ppermute(scale, 'x', [(i, i ^ 2) for i in range(4)])]
    unnamed x57 -> x38, local copies, waits for them, and re-layouts: 10.9 us -> 6.03 us
    ppermute x0 -> x3, starting transfers between devices: none -> 4.31 us  [the longest x1 3.2 us: on_device(): across = lax.ppermute(square, ('x', 'tp'), [(i, i ^ 3) for i in range(8)])]
    ppermute x12, waiting for transfers between devices: 2.63 us -> 5.02 us  [shift(): return lax.ppermute(a, 'x', [(i, (i + by) % 4) for i in range(4)])]
    all_to_all x1, waiting for transfers between devices: 2.19 us -> 0.01 us  [on_device(): m00 = lax.all_to_all(m, 'z', 0, 0, tiled=True).reshape(256, 768)]
    ppermute x1, starting transfers between devices: 1.91 us -> 3.91 us  [on_device(): scales_prev = lax.ppermute(scales, ('yl', 'z'), behind)]
    ppermute x12, starting transfers between devices: 18.7 us -> 16.9 us  [shift(): return lax.ppermute(a, 'x', [(i, (i + by) % 4) for i in range(4)])]
  transfers between devices with their start and end apart: 30 -> 33, of which waited for: 9 -> 13; matrix products, arithmetic and copies ran while one was open for 1% -> 1% of each run, Pallas kernels for 14% -> 15%
where the time goes in v7:
time: 137 us; the launch traced here: 136 us
  starting transfers between devices  52.9 us (39%)
  waiting for transfers between devices  42.3 us (31%)
  Pallas kernels  32 us (23%)
  local copies, waits for them, and re-layouts  6.79 us (5%)
    ppermute x12, starting transfers between devices, shift(): return lax.ppermute(a, 'x', [(i, (i + by) % 4) for i in range(4)])  16.9 us
    ppermute x1, waiting for transfers between devices, on_device(): b = stack([prev, lax.ppermute(other, ('yl', 'z'), behind)])  12.2 us
    ppermute x12, waiting for transfers between devices, swap(): return lax.ppermute(a, axis, SWAP)  11.4 us
    ppermute x12, starting transfers between devices, swap(): return lax.ppermute(a, axis, SWAP)  9.3 us
    pallas_call x2, Pallas kernels, attention(): pl.pallas_call(functools.partial(attention_kernel, n), in_specs=[pl.Block...  8.51 us
    ppermute x1, waiting for transfers between devices, on_device(): halo = lax.ppermute(audio[-8:], CTX, [(i, i + 1) for i in range(127)])  7.26 us
    all_to_all x1, starting transfers between devices, on_device(): packed = lax.all_to_all(packed, 'z', 0, 0, tiled=True)  7.13 us
    unnamed x38, local copies, waits for them, and re-layouts  6.03 us
  transfers between devices with their start and end apart: 33, of which 13 were waited for; matrix products, arithmetic and copies ran while one was open for 1% of the time, Pallas kernels for 15%

profile of v7, /device:TPU:8, one launch (start us, length us, event | category | flops | bytes accessed | tf_op | source)
XLA Modules:
  0.0 135.8 jit_solution(17061325905941819051)
XLA Ops:
  0.6 0.7 stack.42.at_ref
  1.3 2.6 %shard_map.127 = (bf16[3,32,256]{2,1,0:T(8,128)(2,1)}, bf16[3,32,256]{2,1,0:T(8,128)(2,1)}, bf16[3,32,256]{2,1,0:T(8,128)(2,1)}, bf16[3,32,256]{2,1,0:T(8,128)(2,1)}, bf16[2,128,256]{2,1,0:T(8,128)(2,1)}) custom-call(s32[7]{0:T(128)} %stack.42.at_ref, bf16[3,32,1024]{2,1,0:T(8,128)(2,1)} %w_ref.1, bf16[512,4096]{1,0:T(8,128)(2,1)} %bitcast.18, ...), custom_call_target="tpu_custom_call" | custom-call | tf_op jit(solution)/shard_map/pallas_call | solution.py:93
  3.9 2.3 %collective-permute-start.11 = (bf16[2,128,256]{2,1,0:T(8,128)(2,1)}, bf16[2,128,256]{2,1,0:T(8,128)(2,1)S(1)}, u32[]{:S(2)}, u32[]{:S(2)}) collective-permute-start(bf16[2,128,256]{2,1,0:T(8,128)(2,1)} %get-tuple-element.26.mine_ref), channel_id=1, source_target_pairs={{0,1},{1,0},{2,3},{3,2},{4,5},{5,4},{6,7},{7,6},{8,9},{9,8},{10,11... | collective-permute-start | bytes 393224 | tf_op jit(solution)/shard_map/ppermute | solution.py:75
  6.2 2.8 %collective-permute-start.10 = (bf16[3,32,256]{2,1,0:T(8,128)(2,1)}, bf16[3,32,256]{2,1,0:T(8,128)(2,1)S(1)}, u32[]{:S(2)}, u32[]{:S(2)}) collective-permute-start(bf16[3,32,256]{2,1,0:T(8,128)(2,1)} %get-tuple-element.25), channel_id=1, source_target_pairs={{0,12},{4,0},{8,4},{12,8},{1,13},{5,1},{9,5},{13,9},{2,14},{6,2},{... | collective-permute-start | bytes 147464 | tf_op jit(solution)/shard_map/ppermute | solution.py:79
  9.0 2.3 %collective-permute-start.9 = (bf16[3,32,256]{2,1,0:T(8,128)(2,1)}, bf16[3,32,256]{2,1,0:T(8,128)(2,1)S(1)}, u32[]{:S(2)}, u32[]{:S(2)}) collective-permute-start(bf16[3,32,256]{2,1,0:T(8,128)(2,1)} %get-tuple-element.24), channel_id=1, source_target_pairs={{0,8},{4,12},{8,0},{12,4},{1,9},{5,13},{9,1},{13,5},{2,10},{6,14},... | collective-permute-start | bytes 147464 | tf_op jit(solution)/shard_map/ppermute | solution.py:79
  11.3 1.9 %collective-permute-start = (bf16[8,512]{1,0:T(8,128)(2,1)S(1)}, bf16[8,512]{1,0:T(8,128)(2,1)S(1)}, u32[]{:S(2)}, u32[]{:S(2)}) collective-permute-start(bf16[8,512]{1,0:T(8,128)(2,1)S(1)} %slice_bitcast_fusion), channel_id=1, source_target_pairs={{0,2},{2,4},{4,6},{6,8},{8,10},{10,12},{12,14},{14,16},{16,18},{18... | collective-permute-start | bytes 24584 | tf_op jit(solution)/shard_map/ppermute | solution.py:405
  13.2 7.3 %collective-permute-done.halo_ref = bf16[8,512]{1,0:T(8,128)(2,1)S(1)} collective-permute-done((bf16[8,512]{1,0:T(8,128)(2,1)S(1)}, bf16[8,512]{1,0:T(8,128)(2,1)S(1)}, u32[]{:S(2)}, u32[]{:S(2)}) %collective-permute-start) | collective-permute-done | bytes 8224 | tf_op jit(solution)/shard_map/ppermute | solution.py:405
  20.4 1.1 copy-done.7
  21.6 2.5 %shard_map.122.latent_ref.refs_0_.refs_4_ = bf16[256,512]{1,0:T(8,128)(2,1)S(1)} custom-call(bf16[8,512]{1,0:T(8,128)(2,1)S(1)} %collective-permute-done.halo_ref, bf16[512,512]{1,0:T(8,128)(2,1)S(1)} %bitcast.27, bf16[3,512,256]{2,1,0:T(8,128)(2,1)S(1)} %bitcast.26, bf16[256,512]{1,0:T(8,128)(2,1)S(1)} %bitcast.28, bf16[4,512,512]{2,1,0:T(8,128)(2,1)S(1)} %bitcast.21), custom_call_target="tpu_custom_call" | custom-call | tf_op jit(solution)/shard_map/pallas_call | solution.py:63
  24.2 0.8 copy-done.13
  25.0 0.1 collective-permute-start.13
  25.1 1.3 collective-permute-start.2
  26.4 1.9 %collective-permute-start.5 = (bf16[256,512]{1,0:T(8,128)(2,1)S(1)}, bf16[256,512]{1,0:T(8,128)(2,1)S(1)}, u32[]{:S(2)}, u32[]{:S(2)}) collective-permute-start(bf16[256,512]{1,0:T(8,128)(2,1)S(1)} %shard_map.122.latent_ref.refs_0_.refs_4_), channel_id=1, source_target_pairs={{0,16},{16,32},{32,48},{48,64},{64,80},{80,96},{96,112},{112,128},... | collective-permute-start | bytes 786440 | tf_op jit(solution)/shard_map/ppermute | solution.py:415
  28.4 0.1 collective-permute-start.12
  28.5 2.3 %collective-permute-done.13.w10 = bf16[4,3,32,256]{3,2,1,0:T(8,128)(2,1)S(1)} collective-permute-done((bf16[4,3,32,256]{3,2,1,0:T(8,128)(2,1)S(1)}, bf16[4,3,32,256]{3,2,1,0:T(8,128)(2,1)S(1)}, u32[]{:S(2)}, u32[]{:S(2)}) %collective-permute-start.13) | collective-permute-done | bytes 196640 | tf_op jit(solution)/shard_map/ppermute | solution.py:75
  30.8 3.8 %shard_map.123 = (bf16[256,2048]{1,0:T(8,128)(2,1)}, bf16[256,2048]{1,0:T(8,128)(2,1)S(1)}) custom-call(s32[7]{0:T(128)S(1)} %copy-done.14, bf16[256,512]{1,0:T(8,128)(2,1)S(1)} %shard_map.122.latent_ref.refs_0_.refs_4_, bf16[512,4096]{1,0:T(8,128)(2,1)S(1)} %bitcast.20), custom_call_target="tpu_custom_call" | custom-call | tf_op jit(solution)/shard_map/pallas_call | solution.py:226
  34.6 1.0 copy-done.15
  35.5 1.7 %collective-permute-start.1 = (bf16[256,2048]{1,0:T(8,128)(2,1)}, bf16[256,2048]{1,0:T(8,128)(2,1)}, u32[]{:S(2)}, u32[]{:S(2)}) collective-permute-start(bf16[256,2048]{1,0:T(8,128)(2,1)} %get-tuple-element.20.refs_0_), channel_id=1, source_target_pairs={{0,1},{1,0},{2,3},{3,2},{4,5},{5,4},{6,7},{7,6},{8,9},{9,8},{10,11... | collective-permute-start | bytes 3145736 | tf_op jit(solution)/shard_map/ppermute | solution.py:75
  37.3 1.2 collective-permute-done.5.refs_0_.refs_2_
  38.5 3.2 %shard_map.129 = bf16[8,32,896]{2,1,0:T(8,128)(2,1)} custom-call(s32[7]{0:T(128)S(1)} %copy-done.14, bf16[4,3,32,256]{3,2,1,0:T(8,128)(2,1)S(1)} %shard_map.128.w00, bf16[4,3,32,256]{3,2,1,0:T(8,128)(2,1)S(1)} %collective-permute-done.12.w01, bf16[4,3,32,256]{3,2,1,0:T(8,128)(2,1)S(1)} %collective-permute-done.13.w10, ...), custom_call_target="tpu_custom_call" | custom-call | tf_op jit(solution)/shard_map/pallas_call | solution.py:163
  41.7 7.1 %all-to-all-start = ((bf16[8,32,896]{2,1,0:T(8,128)(2,1)}), bf16[8,32,896]{2,1,0:T(8,128)(2,1)S(1)}, u32[]{:S(2)}, u32[]{:S(2)}) async-start(bf16[8,32,896]{2,1,0:T(8,128)(2,1)} %shard_map.129), calls=%async_computation | async-start | bytes 917504 | tf_op jit(solution)/shard_map/all_to_all | solution.py:426
  48.9 0.1 mul.48
  49.0 0.2 reduce_window_sum.11
  49.2 3.2 %collective-permute-start.4 = (bf16[2,256,512]{2,1,0:T(8,128)(2,1)S(1)}, bf16[2,256,512]{2,1,0:T(8,128)(2,1)}, u32[]{:S(2)}, u32[]{:S(2)}) collective-permute-start(bf16[2,256,512]{2,1,0:T(8,128)(2,1)S(1)} %shard_map.124.refs_1_.a), channel_id=1, source_target_pairs={{0,12},{4,0},{8,4},{12,8},{1,13},{5,1},{9,5},{13,9},{2,14},{6,2},{... | collective-permute-start | bytes 1572872 | tf_op jit(solution)/shard_map/ppermute | solution.py:79
  52.5 3.9 %collective-permute-start.6 = (bf16[256,512]{1,0:T(8,128)(2,1)S(1)}, bf16[256,512]{1,0:T(8,128)(2,1)S(1)}, u32[]{:S(2)}, u32[]{:S(2)}) collective-permute-start(bf16[256,512]{1,0:T(8,128)(2,1)S(1)} %collective-permute-done.2.refs_1_), channel_id=1, source_target_pairs={{0,16},{16,32},{32,48},{48,64},{64,80},{80,96},{96,112},{112,128},... | collective-permute-start | bytes 786440 | tf_op jit(solution)/shard_map/ppermute | solution.py:416
  56.5 0.1 convert_reduce_fusion
  56.6 12.2 %collective-permute-done.6.refs_1_ = bf16[256,512]{1,0:T(8,128)(2,1)S(1)} collective-permute-done((bf16[256,512]{1,0:T(8,128)(2,1)S(1)}, bf16[256,512]{1,0:T(8,128)(2,1)S(1)}, u32[]{:S(2)}, u32[]{:S(2)}) %collective-permute-start.6) | collective-permute-done | bytes 262176 | tf_op jit(solution)/shard_map/ppermute | solution.py:416
  68.8 0.3 collective-permute-start.20
  69.1 1.8 %collective-permute-start.19 = (bf16[2,256,512]{2,1,0:T(8,128)(2,1)S(1)}, bf16[2,256,512]{2,1,0:T(8,128)(2,1)S(1)}, u32[]{:S(2)}, u32[]{:S(2)}) collective-permute-start(bf16[2,256,512]{2,1,0:T(8,128)(2,1)S(1)} %shard_map.125.refs_2_.b), channel_id=1, source_target_pairs={{0,4},{4,8},{8,12},{12,0},{1,5},{5,9},{9,13},{13,1},{2,6},{6,10},{... | collective-permute-start | bytes 1572872 | tf_op jit(solution)/shard_map/ppermute | solution.py:79
  70.9 0.8 shard_map.130
  71.7 3.6 %all-to-all-start.1 = ((bf16[8,32,768]{2,1,0:T(8,128)(2,1)}), bf16[8,32,768]{2,1,0:T(8,128)(2,1)S(1)}, u32[]{:S(2)}, u32[]{:S(2)}) async-start(bf16[8,32,768]{2,1,0:T(8,128)(2,1)} %get-tuple-element.27), calls=%async_computation.1 | async-start | bytes 786432 | tf_op jit(solution)/shard_map/all_to_all | solution.py:442
  75.4 1.2 copy-done.16
  76.6 4.0 %shard_map.126 = (bf16[256,2048]{1,0:T(8,128)(2,1)}, f32[8,256]{1,0:T(8,128)S(1)}) custom-call(s32[7]{0:T(128)S(1)} %copy-done.14, bf16[256,2048]{1,0:T(8,128)(2,1)S(1)} %copy-done.16, bf16[256,2048]{1,0:T(8,128)(2,1)} %collective-permute-done.1.got_ref, f32[2,8,256]{2,1,0:T(8,128)S(1)} %fusion.2.active_ref, f32[2,4096]{1,0:T(2,128)S(1)} %copy-done.10, ...), custom_call_target="tpu_custom_call" | custom-call | flops 20000000000 | tf_op jit(solution)/shard_map/pallas_call | solution.py:262
  80.6 3.2 %collective-permute-start.17 = (f32[1,256]{1,0:T(1,128)S(1)}, f32[1,256]{1,0:T(1,128)S(1)}, u32[]{:S(2)}, u32[]{:S(2)}) collective-permute-start(f32[1,256]{1,0:T(1,128)S(1)} %slice.11), channel_id=1, source_target_pairs={{0,5},{1,4},{4,1},{5,0},{8,13},{9,12},{12,9},{13,8},{2,7},{3,6},{6... | collective-permute-start | bytes 3080 | tf_op jit(solution)/shard_map/ppermute | solution.py:438
  83.8 1.8 %collective-permute-start.15 = (f32[1,256]{1,0:T(1,128)S(1)}, f32[1,256]{1,0:T(1,128)S(1)}, u32[]{:S(2)}, u32[]{:S(2)}) collective-permute-start(f32[1,256]{1,0:T(1,128)S(1)} %slice.11), channel_id=1, source_target_pairs={{0,1},{1,0},{2,3},{3,2},{4,5},{5,4},{6,7},{7,6},{8,9},{9,8},{10,11... | collective-permute-start | bytes 3080 | tf_op jit(solution)/shard_map/ppermute | solution.py:75
  85.6 1.1 collective-permute-done.17
  86.6 2.2 %collective-permute-done.15 = f32[1,256]{1,0:T(1,128)S(1)} collective-permute-done((f32[1,256]{1,0:T(1,128)S(1)}, f32[1,256]{1,0:T(1,128)S(1)}, u32[]{:S(2)}, u32[]{:S(2)}) %collective-permute-start.15) | collective-permute-done | bytes 1056 | tf_op jit(solution)/shard_map/ppermute | solution.py:75
  88.9 1.1 collective-permute-start.18
  90.0 4.1 %collective-permute-done.18 = f32[2,256]{1,0:T(2,128)S(1)} collective-permute-done((f32[2,256]{1,0:T(2,128)S(1)}, f32[2,256]{1,0:T(2,128)S(1)}, u32[]{:S(2)}, u32[]{:S(2)}) %collective-permute-start.18) | collective-permute-done | bytes 2080 | tf_op jit(solution)/shard_map/ppermute | solution.py:441
  94.1 1.4 %collective-permute-start.22 = (bf16[256,768]{1,0:T(8,128)(2,1)S(1)}, bf16[256,768]{1,0:T(8,128)(2,1)S(1)}, u32[]{:S(2)}, u32[]{:S(2)}) collective-permute-start(bf16[256,768]{1,0:T(8,128)(2,1)S(1)} %bitcast.22), channel_id=1, source_target_pairs={{0,128},{128,0},{1,129},{129,1},{2,130},{130,2},{3,131},{131,3},{4... | collective-permute-start | bytes 1179656 | tf_op jit(solution)/shard_map/ppermute | solution.py:75
  95.6 0.3 collective-permute-start.7
  95.8 3.0 %collective-permute-start.25 = (bf16[2,256,512]{2,1,0:T(8,128)(2,1)S(1)}, bf16[2,256,512]{2,1,0:T(8,128)(2,1)S(1)}, u32[]{:S(2)}, u32[]{:S(2)}) collective-permute-start(bf16[2,256,512]{2,1,0:T(8,128)(2,1)S(1)} %collective-permute-done.20.refs_3_.br), channel_id=1, source_target_pairs={{0,12},{4,0},{8,4},{12,8},{1,13},{5,1},{9,5},{13,9},{2,14},{6,2},{... | collective-permute-start | bytes 1572872 | tf_op jit(solution)/shard_map/ppermute | solution.py:79
  98.8 3.2 %collective-permute-done.22.m10 = bf16[256,768]{1,0:T(8,128)(2,1)S(1)} collective-permute-done((bf16[256,768]{1,0:T(8,128)(2,1)S(1)}, bf16[256,768]{1,0:T(8,128)(2,1)S(1)}, u32[]{:S(2)}, u32[]{:S(2)}) %collective-permute-start.22) | collective-permute-done | bytes 393248 | tf_op jit(solution)/shard_map/ppermute | solution.py:75
  102.0 3.9 %collective-permute-start.26 = (f32[4,256]{1,0:T(4,128)S(1)}, f32[4,256]{1,0:T(4,128)S(1)}, u32[]{:S(2)}, u32[]{:S(2)}) collective-permute-start(f32[4,256]{1,0:T(4,128)S(1)} %pad_maximum_fusion.refs_1_.scale_ref), channel_id=1, source_target_pairs={{0,16},{16,32},{32,48},{48,64},{64,80},{80,96},{96,112},{112,128},... | collective-permute-start | bytes 12296 | tf_op jit(solution)/shard_map/ppermute | solution.py:447
  105.9 1.2 collective-permute-done.7.af
  107.1 3.2 %shard_map.132 = (bf16[4,256,512]{2,1,0:T(8,128)(2,1)S(1)}, bf16[4,256,256]{2,1,0:T(8,128)(2,1)S(1)}, bf16[1024,768]{1,0:T(8,128)(2,1)S(1)}) custom-call(s32[7]{0:T(128)S(1)} %copy-done.14, bf16[2,256,512]{2,1,0:T(8,128)(2,1)S(1)} %shard_map.124.refs_1_.a, bf16[2,256,512]{2,1,0:T(8,128)(2,1)} %collective-permute-done.3.refs_0_.al, ...), custom_call_target="tpu_custom_call" | custom-call | tf_op jit(solution)/shard_map/pallas_call | solution.py:313
  110.4 0.8 copy-done.1
  111.2 2.0 %shard_map.133.pm_ref = bf16[4,256,512]{2,1,0:T(8,128)(2,1)S(1)} custom-call(s32[7]{0:T(128)S(1)} %copy-done.14, bf16[2,256,512]{2,1,0:T(8,128)(2,1)S(1)} %copy-done.6, bf16[2,256,512]{2,1,0:T(8,128)(2,1)S(1)} %collective-permute-done.19.refs_2_.bl, bf16[2,256,512]{2,1,0:T(8,128)(2,1)S(1)} %collective-permute-done.20.refs_3_.br, ...), custom_call_target="tpu_custom_call" | custom-call | tf_op jit(solution)/shard_map/pallas_call | solution.py:313
  113.2 0.1 collective-permute-start.27
  113.3 0.5 collective-permute-start.24
  113.8 0.1 pad_add_fusion.2.place_ref
  113.9 2.1 %collective-permute-done.27.pt_ref = bf16[4,256,512]{2,1,0:T(8,128)(2,1)S(1)} collective-permute-done((bf16[4,256,512]{2,1,0:T(8,128)(2,1)S(1)}, bf16[4,256,512]{2,1,0:T(8,128)(2,1)S(1)}, u32[]{:S(2)}, u32[]{:S(2)}) %collective-permute-start.27) | collective-permute-done | bytes 1048608 | tf_op jit(solution)/shard_map/ppermute | solution.py:75
  115.9 1.6 %collective-permute-done.24.ot_ref = bf16[4,256,512]{2,1,0:T(8,128)(2,1)} collective-permute-done((bf16[4,256,512]{2,1,0:T(8,128)(2,1)S(1)}, bf16[4,256,512]{2,1,0:T(8,128)(2,1)}, u32[]{:S(2)}, u32[]{:S(2)}) %collective-permute-start.24) | collective-permute-done | bytes 1048608 | tf_op jit(solution)/shard_map/ppermute | solution.py:75
  117.6 1.0 copy-done.2
  118.6 5.5 %shard_map.135 = (bf16[256,256]{1,0:T(8,128)(2,1)S(1)}, bf16[256,256]{1,0:T(8,128)(2,1)S(1)}, bf16[256,256]{1,0:T(8,128)(2,1)S(1)}) custom-call(s32[6]{0:T(128)S(1)} %pad_add_fusion.2.place_ref, bf16[4,256,256]{2,1,0:T(8,128)(2,1)S(1)} %copy-done.2, bf16[4,256,512]{2,1,0:T(8,128)(2,1)S(1)} %get-tuple-element.31.om_ref, ...), custom_call_target="tpu_custom_call" | custom-call | tf_op jit(solution)/shard_map/pallas_call | solution.py:358
  124.1 0.1 collective-permute-start.28
  124.2 2.0 %collective-permute-start.29 = (bf16[256,256]{1,0:T(8,128)(2,1)S(1)}, bf16[256,256]{1,0:T(8,128)(2,1)S(1)}, u32[]{:S(2)}, u32[]{:S(2)}) collective-permute-start(bf16[256,256]{1,0:T(8,128)(2,1)S(1)} %get-tuple-element.34), channel_id=1, source_target_pairs={{0,8},{4,12},{8,0},{12,4},{1,9},{5,13},{9,1},{13,5},{2,10},{6,14},... | collective-permute-start | bytes 393224 | tf_op jit(solution)/shard_map/ppermute | solution.py:79
  126.2 1.2 collective-permute-start.30
  127.4 0.1 pad_add_fusion.place_ref
  127.5 0.1 pad_add_fusion.1.place_ref
  127.6 3.0 %shard_map.134.a_ref = bf16[256,256]{1,0:T(8,128)(2,1)S(1)} custom-call(s32[4]{0:T(128)S(1)} %pad_add_fusion.1.place_ref, bf16[4,256,256]{2,1,0:T(8,128)(2,1)S(1)} %copy-done.3, bf16[4,256,512]{2,1,0:T(8,128)(2,1)S(1)} %get-tuple-element.31.om_ref, bf16[4,256,512]{2,1,0:T(8,128)(2,1)} %collective-permute-done.24.ot_ref, ...), custom_call_target="tpu_custom_call" | custom-call | tf_op jit(solution)/shard_map/pallas_call | solution.py:358
  130.6 3.1 %collective-permute-done.28.b_ref = bf16[256,256]{1,0:T(8,128)(2,1)S(1)} collective-permute-done((bf16[256,256]{1,0:T(8,128)(2,1)S(1)}, bf16[256,256]{1,0:T(8,128)(2,1)S(1)}, u32[]{:S(2)}, u32[]{:S(2)}) %collective-permute-start.28) | collective-permute-done | bytes 131104 | tf_op jit(solution)/shard_map/ppermute | solution.py:79
  133.8 0.6 collective-permute-done.30.d_ref
  134.4 1.4 %shard_map.136 = bf16[256,1024]{1,0:T(8,128)(2,1)} custom-call(s32[3]{0:T(128)S(1)} %pad_add_fusion.place_ref, bf16[256,256]{1,0:T(8,128)(2,1)S(1)} %shard_map.134.a_ref, bf16[256,256]{1,0:T(8,128)(2,1)S(1)} %collective-permute-done.28.b_ref, bf16[256,256]{1,0:T(8,128)(2,1)S(1)} %collective-permute-done.29.c_ref, ...), custom_call_target="tpu_custom_call" | custom-call | tf_op jit(solution)/shard_map/pallas_call | solution.py:375
  (73 shorter events, 0.5 us)
Async XLA Ops:
  1.3 9.9 %copy-start.8 = (bf16[1,512,512]{2,1,0:T(8,128)(2,1)S(1)}, bf16[1,512,512]{2,1,0:T(8,128)(2,1)}, u32[]{:S(2)}) copy-start(bf16[1,512,512]{2,1,0:T(8,128)(2,1)} %param.11) | copy-start | bytes 1572868
  1.3 19.1 %copy-start.4 = (bf16[1,4,512,512]{3,2,1,0:T(8,128)(2,1)S(1)}, bf16[1,4,512,512]{3,2,1,0:T(8,128)(2,1)}, u32[]{:S(2)}) copy-start(bf16[1,4,512,512]{3,2,1,0:T(8,128)(2,1)} %param.14) | copy-start | bytes 6291460
  1.3 19.1 %copy-start.9 = (bf16[1,256,512]{2,1,0:T(8,128)(2,1)S(1)}, bf16[1,256,512]{2,1,0:T(8,128)(2,1)}, u32[]{:S(2)}) copy-start(bf16[1,256,512]{2,1,0:T(8,128)(2,1)} %param.13) | copy-start | bytes 786436
  1.3 29.5 %copy-start.14 = (s32[7]{0:T(128)S(1)}, s32[7]{0:T(128)}, u32[]{:S(2)}) copy-start(s32[7]{0:T(128)} %stack.42.at_ref) | copy-start | bytes 88
  3.9 20.3 %collective-permute-start.11 = (bf16[2,128,256]{2,1,0:T(8,128)(2,1)}, bf16[2,128,256]{2,1,0:T(8,128)(2,1)S(1)}, u32[]{:S(2)}, u32[]{:S(2)}) collective-permute-start(bf16[2,128,256]{2,1,0:T(8,128)(2,1)} %get-tuple-element.26.mine_ref), channel_id=1, source_target_pairs={{0,1},{1,0},{2,3},{3,2},{4,5},{5,4},{6,7},{7,6},{8,9},{9,8},{10,11... | collective-permute-start | bytes 393224 | tf_op jit(solution)/shard_map/ppermute | solution.py:75
  6.2 17.9 %collective-permute-start.10 = (bf16[3,32,256]{2,1,0:T(8,128)(2,1)}, bf16[3,32,256]{2,1,0:T(8,128)(2,1)S(1)}, u32[]{:S(2)}, u32[]{:S(2)}) collective-permute-start(bf16[3,32,256]{2,1,0:T(8,128)(2,1)} %get-tuple-element.25), channel_id=1, source_target_pairs={{0,12},{4,0},{8,4},{12,8},{1,13},{5,1},{9,5},{13,9},{2,14},{6,2},{... | collective-permute-start | bytes 147464 | tf_op jit(solution)/shard_map/ppermute | solution.py:79
  9.0 15.2 %collective-permute-start.8 = (bf16[3,32,256]{2,1,0:T(8,128)(2,1)}, bf16[3,32,256]{2,1,0:T(8,128)(2,1)S(1)}, u32[]{:S(2)}, u32[]{:S(2)}) collective-permute-start(bf16[3,32,256]{2,1,0:T(8,128)(2,1)} %get-tuple-element.23), channel_id=1, source_target_pairs={{0,4},{4,8},{8,12},{12,0},{1,5},{5,9},{9,13},{13,1},{2,6},{6,10},{... | collective-permute-start | bytes 147464 | tf_op jit(solution)/shard_map/ppermute | solution.py:79
  9.0 15.2 %collective-permute-start.9 = (bf16[3,32,256]{2,1,0:T(8,128)(2,1)}, bf16[3,32,256]{2,1,0:T(8,128)(2,1)S(1)}, u32[]{:S(2)}, u32[]{:S(2)}) collective-permute-start(bf16[3,32,256]{2,1,0:T(8,128)(2,1)} %get-tuple-element.24), channel_id=1, source_target_pairs={{0,8},{4,12},{8,0},{12,4},{1,9},{5,13},{9,1},{13,5},{2,10},{6,14},... | collective-permute-start | bytes 147464 | tf_op jit(solution)/shard_map/ppermute | solution.py:79
  11.3 9.2 %collective-permute-start = (bf16[8,512]{1,0:T(8,128)(2,1)S(1)}, bf16[8,512]{1,0:T(8,128)(2,1)S(1)}, u32[]{:S(2)}, u32[]{:S(2)}) collective-permute-start(bf16[8,512]{1,0:T(8,128)(2,1)S(1)} %slice_bitcast_fusion), channel_id=1, source_target_pairs={{0,2},{2,4},{4,6},{6,8},{8,10},{10,12},{12,14},{14,16},{16,18},{18... | collective-permute-start | bytes 24584 | tf_op jit(solution)/shard_map/ppermute | solution.py:405
  20.4 1.1 copy-start.7
  21.6 9.2 %copy-start = (bf16[1,512,4096]{2,1,0:T(8,128)(2,1)S(1)}, bf16[1,512,4096]{2,1,0:T(8,128)(2,1)}, u32[]{:S(2)}) copy-start(bf16[1,512,4096]{2,1,0:T(8,128)(2,1)} %param.15) | copy-start | bytes 12582916
  24.2 0.8 copy-start.13
  25.0 13.5 %copy-start.10 = (f32[2,4096]{1,0:T(2,128)S(1)}, f32[2,4096]{1,0:T(2,128)}, u32[]{:S(2)}) copy-start(f32[2,4096]{1,0:T(2,128)} %t1.1) | copy-start | bytes 98308
  25.0 13.5 %copy-start.11 = (bf16[2,128,256]{2,1,0:T(8,128)(2,1)S(1)}, bf16[2,128,256]{2,1,0:T(8,128)(2,1)}, u32[]{:S(2)}) copy-start(bf16[2,128,256]{2,1,0:T(8,128)(2,1)} %get-tuple-element.26.mine_ref) | copy-start | bytes 393220
  25.0 13.5 %copy-start.12 = (f32[4096]{0:T(1024)S(1)}, f32[4096]{0:T(1024)}, u32[]{:S(2)}) copy-start(f32[4096]{0:T(1024)} %param.18) | copy-start | bytes 49156
  25.0 5.8 %collective-permute-start.13 = (bf16[4,3,32,256]{3,2,1,0:T(8,128)(2,1)S(1)}, bf16[4,3,32,256]{3,2,1,0:T(8,128)(2,1)S(1)}, u32[]{:S(2)}, u32[]{:S(2)}) collective-permute-start(bf16[4,3,32,256]{3,2,1,0:T(8,128)(2,1)S(1)} %shard_map.128.w00), channel_id=1, source_target_pairs={{0,128},{128,0},{1,129},{129,1},{2,130},{130,2},{3,131},{131,3},{4... | collective-permute-start | bytes 589832 | tf_op jit(solution)/shard_map/ppermute | solution.py:75
  25.1 12.1 %collective-permute-start.2 = (bf16[256,512]{1,0:T(8,128)(2,1)S(1)}, bf16[256,512]{1,0:T(8,128)(2,1)S(1)}, u32[]{:S(2)}, u32[]{:S(2)}) collective-permute-start(bf16[256,512]{1,0:T(8,128)(2,1)S(1)} %shard_map.122.latent_ref.refs_0_.refs_4_), channel_id=1, source_target_pairs={{0,1},{1,0},{2,3},{3,2},{4,5},{5,4},{6,7},{7,6},{8,9},{9,8},{10,11... | collective-permute-start | bytes 786440 | tf_op jit(solution)/shard_map/ppermute | solution.py:75
  26.4 12.1 %collective-permute-start.5 = (bf16[256,512]{1,0:T(8,128)(2,1)S(1)}, bf16[256,512]{1,0:T(8,128)(2,1)S(1)}, u32[]{:S(2)}, u32[]{:S(2)}) collective-permute-start(bf16[256,512]{1,0:T(8,128)(2,1)S(1)} %shard_map.122.latent_ref.refs_0_.refs_4_), channel_id=1, source_target_pairs={{0,16},{16,32},{32,48},{48,64},{64,80},{80,96},{96,112},{112,128},... | collective-permute-start | bytes 786440 | tf_op jit(solution)/shard_map/ppermute | solution.py:415
  28.4 10.1 %collective-permute-start.12 = (bf16[4,3,32,256]{3,2,1,0:T(8,128)(2,1)S(1)}, bf16[4,3,32,256]{3,2,1,0:T(8,128)(2,1)S(1)}, u32[]{:S(2)}, u32[]{:S(2)}) collective-permute-start(bf16[4,3,32,256]{3,2,1,0:T(8,128)(2,1)S(1)} %shard_map.128.w00), channel_id=1, source_target_pairs={{0,2},{2,0},{1,3},{3,1},{4,6},{6,4},{5,7},{7,5},{8,10},{10,8},{9,1... | collective-permute-start | bytes 589832 | tf_op jit(solution)/shard_map/ppermute | solution.py:75
  30.8 7.7 %collective-permute-start.14 = (bf16[4,3,32,256]{3,2,1,0:T(8,128)(2,1)S(1)}, bf16[4,3,32,256]{3,2,1,0:T(8,128)(2,1)S(1)}, u32[]{:S(2)}, u32[]{:S(2)}) collective-permute-start(bf16[4,3,32,256]{3,2,1,0:T(8,128)(2,1)S(1)} %collective-permute-done.13.w10), channel_id=1, source_target_pairs={{0,2},{2,0},{1,3},{3,1},{4,6},{6,4},{5,7},{7,5},{8,10},{10,8},{9,1... | collective-permute-start | bytes 589832 | tf_op jit(solution)/shard_map/ppermute | solution.py:75
  34.6 1.0 copy-start.15
  35.5 39.8 %collective-permute-start.1 = (bf16[256,2048]{1,0:T(8,128)(2,1)}, bf16[256,2048]{1,0:T(8,128)(2,1)}, u32[]{:S(2)}, u32[]{:S(2)}) collective-permute-start(bf16[256,2048]{1,0:T(8,128)(2,1)} %get-tuple-element.20.refs_0_), channel_id=1, source_target_pairs={{0,1},{1,0},{2,3},{3,2},{4,5},{5,4},{6,7},{7,6},{8,9},{9,8},{10,11... | collective-permute-start | bytes 3145736 | tf_op jit(solution)/shard_map/ppermute | solution.py:75
  38.5 10.5 %copy-start.17 = (s32[2,32]{1,0:T(2,128)S(1)}, s32[2,32]{1,0:T(2,128)}, u32[]{:S(2)}) copy-start(s32[2,32]{1,0:T(2,128)} %param.16) | copy-start | bytes 772
  41.7 29.2 %all-to-all-start = ((bf16[8,32,896]{2,1,0:T(8,128)(2,1)}), bf16[8,32,896]{2,1,0:T(8,128)(2,1)S(1)}, u32[]{:S(2)}, u32[]{:S(2)}) async-start(bf16[8,32,896]{2,1,0:T(8,128)(2,1)} %shard_map.129), calls=%async_computation | async-start | bytes 917504 | tf_op jit(solution)/shard_map/all_to_all | solution.py:426
  49.2 26.1 %collective-permute-start.3 = (bf16[2,256,512]{2,1,0:T(8,128)(2,1)S(1)}, bf16[2,256,512]{2,1,0:T(8,128)(2,1)}, u32[]{:S(2)}, u32[]{:S(2)}) collective-permute-start(bf16[2,256,512]{2,1,0:T(8,128)(2,1)S(1)} %shard_map.124.refs_1_.a), channel_id=1, source_target_pairs={{0,4},{4,8},{8,12},{12,0},{1,5},{5,9},{9,13},{13,1},{2,6},{6,10},{... | collective-permute-start | bytes 1572872 | tf_op jit(solution)/shard_map/ppermute | solution.py:79
  49.2 26.1 %collective-permute-start.4 = (bf16[2,256,512]{2,1,0:T(8,128)(2,1)S(1)}, bf16[2,256,512]{2,1,0:T(8,128)(2,1)}, u32[]{:S(2)}, u32[]{:S(2)}) collective-permute-start(bf16[2,256,512]{2,1,0:T(8,128)(2,1)S(1)} %shard_map.124.refs_1_.a), channel_id=1, source_target_pairs={{0,12},{4,0},{8,4},{12,8},{1,13},{5,1},{9,5},{13,9},{2,14},{6,2},{... | collective-permute-start | bytes 1572872 | tf_op jit(solution)/shard_map/ppermute | solution.py:79
  52.5 16.2 %collective-permute-start.6 = (bf16[256,512]{1,0:T(8,128)(2,1)S(1)}, bf16[256,512]{1,0:T(8,128)(2,1)S(1)}, u32[]{:S(2)}, u32[]{:S(2)}) collective-permute-start(bf16[256,512]{1,0:T(8,128)(2,1)S(1)} %collective-permute-done.2.refs_1_), channel_id=1, source_target_pairs={{0,16},{16,32},{32,48},{48,64},{64,80},{80,96},{96,112},{112,128},... | collective-permute-start | bytes 786440 | tf_op jit(solution)/shard_map/ppermute | solution.py:416
  68.8 11.8 %copy-start.5 = (bf16[2,256,512]{2,1,0:T(8,128)(2,1)}, bf16[2,256,512]{2,1,0:T(8,128)(2,1)S(1)}, u32[]{:S(2)}) copy-start(bf16[2,256,512]{2,1,0:T(8,128)(2,1)S(1)} %shard_map.125.refs_2_.b) | copy-start | bytes 1572868
  68.8 25.2 %collective-permute-start.20 = (bf16[2,256,512]{2,1,0:T(8,128)(2,1)S(1)}, bf16[2,256,512]{2,1,0:T(8,128)(2,1)S(1)}, u32[]{:S(2)}, u32[]{:S(2)}) collective-permute-start(bf16[2,256,512]{2,1,0:T(8,128)(2,1)S(1)} %shard_map.125.refs_2_.b), channel_id=1, source_target_pairs={{0,12},{4,0},{8,4},{12,8},{1,13},{5,1},{9,5},{13,9},{2,14},{6,2},{... | collective-permute-start | bytes 1572872 | tf_op jit(solution)/shard_map/ppermute | solution.py:79
  69.1 24.9 %collective-permute-start.19 = (bf16[2,256,512]{2,1,0:T(8,128)(2,1)S(1)}, bf16[2,256,512]{2,1,0:T(8,128)(2,1)S(1)}, u32[]{:S(2)}, u32[]{:S(2)}) collective-permute-start(bf16[2,256,512]{2,1,0:T(8,128)(2,1)S(1)} %shard_map.125.refs_2_.b), channel_id=1, source_target_pairs={{0,4},{4,8},{8,12},{12,0},{1,5},{5,9},{9,13},{13,1},{2,6},{6,10},{... | collective-permute-start | bytes 1572872 | tf_op jit(solution)/shard_map/ppermute | solution.py:79
  71.7 22.3 %all-to-all-start.1 = ((bf16[8,32,768]{2,1,0:T(8,128)(2,1)}), bf16[8,32,768]{2,1,0:T(8,128)(2,1)S(1)}, u32[]{:S(2)}, u32[]{:S(2)}) async-start(bf16[8,32,768]{2,1,0:T(8,128)(2,1)} %get-tuple-element.27), calls=%async_computation.1 | async-start | bytes 786432 | tf_op jit(solution)/shard_map/all_to_all | solution.py:442
  75.4 1.2 copy-start.16
  80.6 5.0 %collective-permute-start.16 = (f32[1,256]{1,0:T(1,128)S(1)}, f32[1,256]{1,0:T(1,128)S(1)}, u32[]{:S(2)}, u32[]{:S(2)}) collective-permute-start(f32[1,256]{1,0:T(1,128)S(1)} %slice.11), channel_id=1, source_target_pairs={{0,4},{4,0},{8,12},{12,8},{1,5},{5,1},{9,13},{13,9},{2,6},{6,2},{1... | collective-permute-start | bytes 3080 | tf_op jit(solution)/shard_map/ppermute | solution.py:437
  80.6 6.1 %collective-permute-start.17 = (f32[1,256]{1,0:T(1,128)S(1)}, f32[1,256]{1,0:T(1,128)S(1)}, u32[]{:S(2)}, u32[]{:S(2)}) collective-permute-start(f32[1,256]{1,0:T(1,128)S(1)} %slice.11), channel_id=1, source_target_pairs={{0,5},{1,4},{4,1},{5,0},{8,13},{9,12},{12,9},{13,8},{2,7},{3,6},{6... | collective-permute-start | bytes 3080 | tf_op jit(solution)/shard_map/ppermute | solution.py:438
  83.8 5.1 %collective-permute-start.15 = (f32[1,256]{1,0:T(1,128)S(1)}, f32[1,256]{1,0:T(1,128)S(1)}, u32[]{:S(2)}, u32[]{:S(2)}) collective-permute-start(f32[1,256]{1,0:T(1,128)S(1)} %slice.11), channel_id=1, source_target_pairs={{0,1},{1,0},{2,3},{3,2},{4,5},{5,4},{6,7},{7,6},{8,9},{9,8},{10,11... | collective-permute-start | bytes 3080 | tf_op jit(solution)/shard_map/ppermute | solution.py:75
  88.9 5.2 %collective-permute-start.18 = (f32[2,256]{1,0:T(2,128)S(1)}, f32[2,256]{1,0:T(2,128)S(1)}, u32[]{:S(2)}, u32[]{:S(2)}) collective-permute-start(f32[2,256]{1,0:T(2,128)S(1)} %fusion.4), channel_id=1, source_target_pairs={{0,8},{4,12},{8,0},{12,4},{1,9},{5,13},{9,1},{13,5},{2,10},{6,14},... | collective-permute-start | bytes 6152 | tf_op jit(solution)/shard_map/ppermute | solution.py:441
  94.1 17.1 %copy-start.6 = (bf16[2,256,512]{2,1,0:T(8,128)(2,1)S(1)}, bf16[2,256,512]{2,1,0:T(8,128)(2,1)}, u32[]{:S(2)}) copy-start(bf16[2,256,512]{2,1,0:T(8,128)(2,1)} %copy-done.5) | copy-start | bytes 1572868
  94.1 7.9 %collective-permute-start.22 = (bf16[256,768]{1,0:T(8,128)(2,1)S(1)}, bf16[256,768]{1,0:T(8,128)(2,1)S(1)}, u32[]{:S(2)}, u32[]{:S(2)}) collective-permute-start(bf16[256,768]{1,0:T(8,128)(2,1)S(1)} %bitcast.22), channel_id=1, source_target_pairs={{0,128},{128,0},{1,129},{129,1},{2,130},{130,2},{3,131},{131,3},{4... | collective-permute-start | bytes 1179656 | tf_op jit(solution)/shard_map/ppermute | solution.py:75
  95.6 11.6 %collective-permute-start.7 = (bf16[2,256,512]{2,1,0:T(8,128)(2,1)}, bf16[2,256,512]{2,1,0:T(8,128)(2,1)S(1)}, u32[]{:S(2)}, u32[]{:S(2)}) collective-permute-start(bf16[2,256,512]{2,1,0:T(8,128)(2,1)} %collective-permute-done.3.refs_0_.al), channel_id=1, source_target_pairs={{0,4},{4,8},{8,12},{12,0},{1,5},{5,9},{9,13},{13,1},{2,6},{6,10},{... | collective-permute-start | bytes 1572872 | tf_op jit(solution)/shard_map/ppermute | solution.py:79
  95.8 15.4 %collective-permute-start.25 = (bf16[2,256,512]{2,1,0:T(8,128)(2,1)S(1)}, bf16[2,256,512]{2,1,0:T(8,128)(2,1)S(1)}, u32[]{:S(2)}, u32[]{:S(2)}) collective-permute-start(bf16[2,256,512]{2,1,0:T(8,128)(2,1)S(1)} %collective-permute-done.20.refs_3_.br), channel_id=1, source_target_pairs={{0,12},{4,0},{8,4},{12,8},{1,13},{5,1},{9,5},{13,9},{2,14},{6,2},{... | collective-permute-start | bytes 1572872 | tf_op jit(solution)/shard_map/ppermute | solution.py:79
  98.8 8.3 %collective-permute-start.21 = (bf16[256,768]{1,0:T(8,128)(2,1)S(1)}, bf16[256,768]{1,0:T(8,128)(2,1)S(1)}, u32[]{:S(2)}, u32[]{:S(2)}) collective-permute-start(bf16[256,768]{1,0:T(8,128)(2,1)S(1)} %bitcast.23), channel_id=1, source_target_pairs={{0,2},{2,0},{1,3},{3,1},{4,6},{6,4},{5,7},{7,5},{8,10},{10,8},{9,1... | collective-permute-start | bytes 1179656 | tf_op jit(solution)/shard_map/ppermute | solution.py:75
  102.0 5.2 %collective-permute-start.23 = (bf16[256,768]{1,0:T(8,128)(2,1)S(1)}, bf16[256,768]{1,0:T(8,128)(2,1)S(1)}, u32[]{:S(2)}, u32[]{:S(2)}) collective-permute-start(bf16[256,768]{1,0:T(8,128)(2,1)S(1)} %collective-permute-done.22.m10), channel_id=1, source_target_pairs={{0,2},{2,0},{1,3},{3,1},{4,6},{6,4},{5,7},{7,5},{8,10},{10,8},{9,1... | collective-permute-start | bytes 1179656 | tf_op jit(solution)/shard_map/ppermute | solution.py:75
  102.0 9.2 %collective-permute-start.26 = (f32[4,256]{1,0:T(4,128)S(1)}, f32[4,256]{1,0:T(4,128)S(1)}, u32[]{:S(2)}, u32[]{:S(2)}) collective-permute-start(f32[4,256]{1,0:T(4,128)S(1)} %pad_maximum_fusion.refs_1_.scale_ref), channel_id=1, source_target_pairs={{0,16},{16,32},{32,48},{48,64},{64,80},{80,96},{96,112},{112,128},... | collective-permute-start | bytes 12296 | tf_op jit(solution)/shard_map/ppermute | solution.py:447
  110.4 0.8 copy-start.1
  111.2 2.6 %copy-start.18 = (s32[3]{0:T(128)S(1)}, s32[3]{0:T(128)}, u32[]{:S(2)}) copy-start(s32[3]{0:T(128)} %constant.57.clone) | copy-start | bytes 40
  113.2 2.7 %collective-permute-start.27 = (bf16[4,256,512]{2,1,0:T(8,128)(2,1)S(1)}, bf16[4,256,512]{2,1,0:T(8,128)(2,1)S(1)}, u32[]{:S(2)}, u32[]{:S(2)}) collective-permute-start(bf16[4,256,512]{2,1,0:T(8,128)(2,1)S(1)} %shard_map.133.pm_ref), channel_id=1, source_target_pairs={{0,2},{2,0},{1,3},{3,1},{4,6},{6,4},{5,7},{7,5},{8,10},{10,8},{9,1... | collective-permute-start | bytes 3145736 | tf_op jit(solution)/shard_map/ppermute | solution.py:75
  113.3 4.3 %collective-permute-start.24 = (bf16[4,256,512]{2,1,0:T(8,128)(2,1)S(1)}, bf16[4,256,512]{2,1,0:T(8,128)(2,1)}, u32[]{:S(2)}, u32[]{:S(2)}) collective-permute-start(bf16[4,256,512]{2,1,0:T(8,128)(2,1)S(1)} %get-tuple-element.31.om_ref), channel_id=1, source_target_pairs={{0,2},{2,0},{1,3},{3,1},{4,6},{6,4},{5,7},{7,5},{8,10},{10,8},{9,1... | collective-permute-start | bytes 3145736 | tf_op jit(solution)/shard_map/ppermute | solution.py:75
  117.6 1.0 copy-start.2
  118.6 9.0 %copy-start.3 = (bf16[4,256,256]{2,1,0:T(8,128)(2,1)S(1)}, bf16[4,256,256]{2,1,0:T(8,128)(2,1)}, u32[]{:S(2)}) copy-start(bf16[4,256,256]{2,1,0:T(8,128)(2,1)} %copy-done.1) | copy-start | bytes 1572868
  124.1 9.6 %collective-permute-start.28 = (bf16[256,256]{1,0:T(8,128)(2,1)S(1)}, bf16[256,256]{1,0:T(8,128)(2,1)S(1)}, u32[]{:S(2)}, u32[]{:S(2)}) collective-permute-start(bf16[256,256]{1,0:T(8,128)(2,1)S(1)} %get-tuple-element.33), channel_id=1, source_target_pairs={{0,4},{4,8},{8,12},{12,0},{1,5},{5,9},{9,13},{13,1},{2,6},{6,10},{... | collective-permute-start | bytes 393224 | tf_op jit(solution)/shard_map/ppermute | solution.py:79
  124.2 9.5 %collective-permute-start.29 = (bf16[256,256]{1,0:T(8,128)(2,1)S(1)}, bf16[256,256]{1,0:T(8,128)(2,1)S(1)}, u32[]{:S(2)}, u32[]{:S(2)}) collective-permute-start(bf16[256,256]{1,0:T(8,128)(2,1)S(1)} %get-tuple-element.34), channel_id=1, source_target_pairs={{0,8},{4,12},{8,0},{12,4},{1,9},{5,13},{9,1},{13,5},{2,10},{6,14},... | collective-permute-start | bytes 393224 | tf_op jit(solution)/shard_map/ppermute | solution.py:79
  126.2 8.2 %collective-permute-start.30 = (bf16[256,256]{1,0:T(8,128)(2,1)S(1)}, bf16[256,256]{1,0:T(8,128)(2,1)S(1)}, u32[]{:S(2)}, u32[]{:S(2)}) collective-permute-start(bf16[256,256]{1,0:T(8,128)(2,1)S(1)} %get-tuple-element.35), channel_id=1, source_target_pairs={{0,12},{4,0},{8,4},{12,8},{1,13},{5,1},{9,5},{13,9},{2,14},{6,2},{... | collective-permute-start | bytes 393224 | tf_op jit(solution)/shard_map/ppermute | solution.py:79

commit v8 on v7

--- a/solution.py
+++ b/solution.py
@@ -422,7 +422,7 @@
     w10 = swap(w00, "yl")
     w01 = swap(w00, "c")
     w11 = swap(w10, "c")
-    packed = partial_weights(at, (w00, w01, w10, w11), mine, rest, norm_gain[None], speaker_table, (give, a, prev))
+    packed = partial_weights(at, (w00, w01, w10, w11), mine, rest, norm_gain[None], speaker_table, (give, other, prev))
     packed = lax.all_to_all(packed, "z", 0, 0, tiled=True)
     m, lines = sum_weights(packed, ())
     bounds = jnp.cumsum(turn_lengths, axis=1)

time: 137 us -> 136 us (level)
    unnamed x38, local copies, waits for them, and re-layouts: 6.03 us -> 4.16 us
  transfers between devices with their start and end apart: 33 -> 33, of which waited for: 13 -> 14; matrix products, arithmetic and copies ran while one was open for 1% -> 1% of each run, Pallas kernels for 15% -> 15%
where the time goes in v8:
time: 136 us; the launch traced here: 135 us
  starting transfers between devices  53.1 us (39%)
  waiting for transfers between devices  41.9 us (31%)
  Pallas kernels  32.1 us (24%)
  local copies, waits for them, and re-layouts  5.62 us (4%)
    ppermute x12, starting transfers between devices, shift(): return lax.ppermute(a, 'x', [(i, (i + by) % 4) for i in range(4)])  17.7 us
    ppermute x1, waiting for transfers between devices, on_device(): b = stack([prev, lax.ppermute(other, ('yl', 'z'), behind)])  12 us
    ppermute x12, waiting for transfers between devices, swap(): return lax.ppermute(a, axis, SWAP)  11.4 us
    ppermute x12, starting transfers between devices, swap(): return lax.ppermute(a, axis, SWAP)  9.3 us
    pallas_call x2, Pallas kernels, attention(): pl.pallas_call(functools.partial(attention_kernel, n), in_specs=[pl.Block...  8.51 us
    ppermute x1, waiting for transfers between devices, on_device(): halo = lax.ppermute(audio[-8:], CTX, [(i, i + 1) for i in range(127)])  7.26 us
    all_to_all x1, starting transfers between devices, on_device(): packed = lax.all_to_all(packed, 'z', 0, 0, tiled=True)  6.1 us
    pallas_call x2, Pallas kernels, project(): pl.pallas_call(kernel, in_specs=[pl.BlockSpec(memory_space=pltpu.SMEM)] +...  5.19 us
  transfers between devices with their start and end apart: 33, of which 14 were waited for; matrix products, arithmetic and copies ran while one was open for 1% of the time, Pallas kernels for 15%

profile of v8, /device:TPU:8, one launch (start us, length us, event | category | flops | bytes accessed | tf_op | source)
XLA Modules:
  0.0 134.5 jit_solution(1013263872647079816)
XLA Ops:
  0.6 0.7 stack.42.at_ref
  1.3 2.7 %shard_map.127 = (bf16[3,32,256]{2,1,0:T(8,128)(2,1)}, bf16[3,32,256]{2,1,0:T(8,128)(2,1)}, bf16[3,32,256]{2,1,0:T(8,128)(2,1)}, bf16[3,32,256]{2,1,0:T(8,128)(2,1)}, bf16[2,128,256]{2,1,0:T(8,128)(2,1)}) custom-call(s32[7]{0:T(128)} %stack.42.at_ref, bf16[3,32,1024]{2,1,0:T(8,128)(2,1)} %w_ref.1, bf16[512,4096]{1,0:T(8,128)(2,1)} %bitcast.18, ...), custom_call_target="tpu_custom_call" | custom-call | tf_op jit(solution)/shard_map/pallas_call | solution.py:93
  4.0 2.3 %collective-permute-start.11 = (bf16[2,128,256]{2,1,0:T(8,128)(2,1)}, bf16[2,128,256]{2,1,0:T(8,128)(2,1)S(1)}, u32[]{:S(2)}, u32[]{:S(2)}) collective-permute-start(bf16[2,128,256]{2,1,0:T(8,128)(2,1)} %get-tuple-element.26.mine_ref), channel_id=1, source_target_pairs={{0,1},{1,0},{2,3},{3,2},{4,5},{5,4},{6,7},{7,6},{8,9},{9,8},{10,11... | collective-permute-start | bytes 393224 | tf_op jit(solution)/shard_map/ppermute | solution.py:75
  6.3 2.8 %collective-permute-start.10 = (bf16[3,32,256]{2,1,0:T(8,128)(2,1)}, bf16[3,32,256]{2,1,0:T(8,128)(2,1)S(1)}, u32[]{:S(2)}, u32[]{:S(2)}) collective-permute-start(bf16[3,32,256]{2,1,0:T(8,128)(2,1)} %get-tuple-element.25), channel_id=1, source_target_pairs={{0,12},{4,0},{8,4},{12,8},{1,13},{5,1},{9,5},{13,9},{2,14},{6,2},{... | collective-permute-start | bytes 147464 | tf_op jit(solution)/shard_map/ppermute | solution.py:79
  9.0 2.3 %collective-permute-start.9 = (bf16[3,32,256]{2,1,0:T(8,128)(2,1)}, bf16[3,32,256]{2,1,0:T(8,128)(2,1)S(1)}, u32[]{:S(2)}, u32[]{:S(2)}) collective-permute-start(bf16[3,32,256]{2,1,0:T(8,128)(2,1)} %get-tuple-element.24), channel_id=1, source_target_pairs={{0,8},{4,12},{8,0},{12,4},{1,9},{5,13},{9,1},{13,5},{2,10},{6,14},... | collective-permute-start | bytes 147464 | tf_op jit(solution)/shard_map/ppermute | solution.py:79
  11.3 0.7 slice_bitcast_fusion
  12.0 1.9 %collective-permute-start = (bf16[8,512]{1,0:T(8,128)(2,1)S(1)}, bf16[8,512]{1,0:T(8,128)(2,1)S(1)}, u32[]{:S(2)}, u32[]{:S(2)}) collective-permute-start(bf16[8,512]{1,0:T(8,128)(2,1)S(1)} %slice_bitcast_fusion), channel_id=1, source_target_pairs={{0,2},{2,4},{4,6},{6,8},{8,10},{10,12},{12,14},{14,16},{16,18},{18... | collective-permute-start | bytes 24584 | tf_op jit(solution)/shard_map/ppermute | solution.py:405
  13.9 7.3 %collective-permute-done.halo_ref = bf16[8,512]{1,0:T(8,128)(2,1)S(1)} collective-permute-done((bf16[8,512]{1,0:T(8,128)(2,1)S(1)}, bf16[8,512]{1,0:T(8,128)(2,1)S(1)}, u32[]{:S(2)}, u32[]{:S(2)}) %collective-permute-start) | collective-permute-done | bytes 8224 | tf_op jit(solution)/shard_map/ppermute | solution.py:405
  21.2 1.0 copy-done.8
  22.3 2.5 %shard_map.122.latent_ref.refs_0_.refs_4_ = bf16[256,512]{1,0:T(8,128)(2,1)S(1)} custom-call(bf16[8,512]{1,0:T(8,128)(2,1)S(1)} %collective-permute-done.halo_ref, bf16[512,512]{1,0:T(8,128)(2,1)S(1)} %bitcast.27, bf16[3,512,256]{2,1,0:T(8,128)(2,1)S(1)} %bitcast.26, bf16[256,512]{1,0:T(8,128)(2,1)S(1)} %bitcast.28, bf16[4,512,512]{2,1,0:T(8,128)(2,1)S(1)} %bitcast.21), custom_call_target="tpu_custom_call" | custom-call | tf_op jit(solution)/shard_map/pallas_call | solution.py:63
  24.9 0.8 copy-done.13
  25.7 0.1 collective-permute-start.13
  25.8 1.3 collective-permute-start.2
  27.1 1.9 %collective-permute-start.5 = (bf16[256,512]{1,0:T(8,128)(2,1)S(1)}, bf16[256,512]{1,0:T(8,128)(2,1)S(1)}, u32[]{:S(2)}, u32[]{:S(2)}) collective-permute-start(bf16[256,512]{1,0:T(8,128)(2,1)S(1)} %shard_map.122.latent_ref.refs_0_.refs_4_), channel_id=1, source_target_pairs={{0,16},{16,32},{32,48},{48,64},{64,80},{80,96},{96,112},{112,128},... | collective-permute-start | bytes 786440 | tf_op jit(solution)/shard_map/ppermute | solution.py:415
  29.1 0.1 collective-permute-start.12
  29.2 2.3 %collective-permute-done.13.w10 = bf16[4,3,32,256]{3,2,1,0:T(8,128)(2,1)S(1)} collective-permute-done((bf16[4,3,32,256]{3,2,1,0:T(8,128)(2,1)S(1)}, bf16[4,3,32,256]{3,2,1,0:T(8,128)(2,1)S(1)}, u32[]{:S(2)}, u32[]{:S(2)}) %collective-permute-start.13) | collective-permute-done | bytes 196640 | tf_op jit(solution)/shard_map/ppermute | solution.py:75
  31.5 3.8 %shard_map.123 = (bf16[256,2048]{1,0:T(8,128)(2,1)}, bf16[256,2048]{1,0:T(8,128)(2,1)S(1)}) custom-call(s32[7]{0:T(128)S(1)} %copy-done.14, bf16[256,512]{1,0:T(8,128)(2,1)S(1)} %shard_map.122.latent_ref.refs_0_.refs_4_, bf16[512,4096]{1,0:T(8,128)(2,1)S(1)} %bitcast.20), custom_call_target="tpu_custom_call" | custom-call | tf_op jit(solution)/shard_map/pallas_call | solution.py:226
  35.3 1.7 %collective-permute-start.1 = (bf16[256,2048]{1,0:T(8,128)(2,1)}, bf16[256,2048]{1,0:T(8,128)(2,1)}, u32[]{:S(2)}, u32[]{:S(2)}) collective-permute-start(bf16[256,2048]{1,0:T(8,128)(2,1)} %get-tuple-element.20.refs_0_), channel_id=1, source_target_pairs={{0,1},{1,0},{2,3},{3,2},{4,5},{5,4},{6,7},{7,6},{8,9},{9,8},{10,11... | collective-permute-start | bytes 3145736 | tf_op jit(solution)/shard_map/ppermute | solution.py:75
  36.9 2.3 %collective-permute-done.5.refs_0_.refs_2_ = bf16[256,512]{1,0:T(8,128)(2,1)S(1)} collective-permute-done((bf16[256,512]{1,0:T(8,128)(2,1)S(1)}, bf16[256,512]{1,0:T(8,128)(2,1)S(1)}, u32[]{:S(2)}, u32[]{:S(2)}) %collective-permute-start.5) | collective-permute-done | bytes 262176 | tf_op jit(solution)/shard_map/ppermute | solution.py:415
  39.2 3.2 %shard_map.129 = bf16[8,32,896]{2,1,0:T(8,128)(2,1)} custom-call(s32[7]{0:T(128)S(1)} %copy-done.14, bf16[4,3,32,256]{3,2,1,0:T(8,128)(2,1)S(1)} %shard_map.128.w00, bf16[4,3,32,256]{3,2,1,0:T(8,128)(2,1)S(1)} %collective-permute-done.12.w01, bf16[4,3,32,256]{3,2,1,0:T(8,128)(2,1)S(1)} %collective-permute-done.13.w10, ...), custom_call_target="tpu_custom_call" | custom-call | tf_op jit(solution)/shard_map/pallas_call | solution.py:163
  42.4 6.1 %all-to-all-start = ((bf16[8,32,896]{2,1,0:T(8,128)(2,1)}), bf16[8,32,896]{2,1,0:T(8,128)(2,1)S(1)}, u32[]{:S(2)}, u32[]{:S(2)}) async-start(bf16[8,32,896]{2,1,0:T(8,128)(2,1)} %shard_map.129), calls=%async_computation | async-start | bytes 917504 | tf_op jit(solution)/shard_map/all_to_all | solution.py:426
  48.6 0.1 mul.48
  48.7 0.2 reduce_window_sum.11
  48.9 0.1 collective-permute-start.3
  49.0 3.2 %collective-permute-start.4 = (bf16[2,256,512]{2,1,0:T(8,128)(2,1)S(1)}, bf16[2,256,512]{2,1,0:T(8,128)(2,1)}, u32[]{:S(2)}, u32[]{:S(2)}) collective-permute-start(bf16[2,256,512]{2,1,0:T(8,128)(2,1)S(1)} %shard_map.124.a), channel_id=1, source_target_pairs={{0,12},{4,0},{8,4},{12,8},{1,13},{5,1},{9,5},{13,9},{2,14},{6,2},{... | collective-permute-start | bytes 1572872 | tf_op jit(solution)/shard_map/ppermute | solution.py:79
  52.3 3.9 %collective-permute-start.6 = (bf16[256,512]{1,0:T(8,128)(2,1)S(1)}, bf16[256,512]{1,0:T(8,128)(2,1)S(1)}, u32[]{:S(2)}, u32[]{:S(2)}) collective-permute-start(bf16[256,512]{1,0:T(8,128)(2,1)S(1)} %collective-permute-done.2.refs_1_), channel_id=1, source_target_pairs={{0,16},{16,32},{32,48},{48,64},{64,80},{80,96},{96,112},{112,128},... | collective-permute-start | bytes 786440 | tf_op jit(solution)/shard_map/ppermute | solution.py:416
  56.2 0.1 convert_reduce_fusion
  56.4 12.0 %collective-permute-done.6.refs_1_ = bf16[256,512]{1,0:T(8,128)(2,1)S(1)} collective-permute-done((bf16[256,512]{1,0:T(8,128)(2,1)S(1)}, bf16[256,512]{1,0:T(8,128)(2,1)S(1)}, u32[]{:S(2)}, u32[]{:S(2)}) %collective-permute-start.6) | collective-permute-done | bytes 262176 | tf_op jit(solution)/shard_map/ppermute | solution.py:416
  68.5 1.3 collective-permute-start.20
  69.8 0.8 collective-permute-start.19
  70.6 0.8 shard_map.130
  71.4 3.6 %all-to-all-start.1 = ((bf16[8,32,768]{2,1,0:T(8,128)(2,1)}), bf16[8,32,768]{2,1,0:T(8,128)(2,1)S(1)}, u32[]{:S(2)}, u32[]{:S(2)}) async-start(bf16[8,32,768]{2,1,0:T(8,128)(2,1)} %get-tuple-element.27), calls=%async_computation.1 | async-start | bytes 786432 | tf_op jit(solution)/shard_map/all_to_all | solution.py:442
  75.0 1.2 copy-done.16
  76.2 4.0 %shard_map.126 = (bf16[256,2048]{1,0:T(8,128)(2,1)}, f32[8,256]{1,0:T(8,128)S(1)}) custom-call(s32[7]{0:T(128)S(1)} %copy-done.14, bf16[256,2048]{1,0:T(8,128)(2,1)S(1)} %copy-done.16, bf16[256,2048]{1,0:T(8,128)(2,1)} %collective-permute-done.1.got_ref, f32[2,8,256]{2,1,0:T(8,128)S(1)} %fusion.2.active_ref, f32[2,4096]{1,0:T(2,128)S(1)} %copy-done.10, ...), custom_call_target="tpu_custom_call" | custom-call | flops 20000000000 | tf_op jit(solution)/shard_map/pallas_call | solution.py:262
  80.2 3.2 %collective-permute-start.17 = (f32[1,256]{1,0:T(1,128)S(1)}, f32[1,256]{1,0:T(1,128)S(1)}, u32[]{:S(2)}, u32[]{:S(2)}) collective-permute-start(f32[1,256]{1,0:T(1,128)S(1)} %slice.11), channel_id=1, source_target_pairs={{0,5},{1,4},{4,1},{5,0},{8,13},{9,12},{12,9},{13,8},{2,7},{3,6},{6... | collective-permute-start | bytes 3080 | tf_op jit(solution)/shard_map/ppermute | solution.py:438
  83.4 1.8 %collective-permute-start.15 = (f32[1,256]{1,0:T(1,128)S(1)}, f32[1,256]{1,0:T(1,128)S(1)}, u32[]{:S(2)}, u32[]{:S(2)}) collective-permute-start(f32[1,256]{1,0:T(1,128)S(1)} %slice.11), channel_id=1, source_target_pairs={{0,1},{1,0},{2,3},{3,2},{4,5},{5,4},{6,7},{7,6},{8,9},{9,8},{10,11... | collective-permute-start | bytes 3080 | tf_op jit(solution)/shard_map/ppermute | solution.py:75
  85.2 1.1 collective-permute-done.17
  86.3 2.2 %collective-permute-done.15 = f32[1,256]{1,0:T(1,128)S(1)} collective-permute-done((f32[1,256]{1,0:T(1,128)S(1)}, f32[1,256]{1,0:T(1,128)S(1)}, u32[]{:S(2)}, u32[]{:S(2)}) %collective-permute-start.15) | collective-permute-done | bytes 1056 | tf_op jit(solution)/shard_map/ppermute | solution.py:75
  88.5 1.5 %collective-permute-start.18 = (f32[2,256]{1,0:T(2,128)S(1)}, f32[2,256]{1,0:T(2,128)S(1)}, u32[]{:S(2)}, u32[]{:S(2)}) collective-permute-start(f32[2,256]{1,0:T(2,128)S(1)} %fusion.4), channel_id=1, source_target_pairs={{0,8},{4,12},{8,0},{12,4},{1,9},{5,13},{9,1},{13,5},{2,10},{6,14},... | collective-permute-start | bytes 6152 | tf_op jit(solution)/shard_map/ppermute | solution.py:441
  90.0 3.6 %collective-permute-done.18 = f32[2,256]{1,0:T(2,128)S(1)} collective-permute-done((f32[2,256]{1,0:T(2,128)S(1)}, f32[2,256]{1,0:T(2,128)S(1)}, u32[]{:S(2)}, u32[]{:S(2)}) %collective-permute-start.18) | collective-permute-done | bytes 2080 | tf_op jit(solution)/shard_map/ppermute | solution.py:441
  93.8 1.4 %collective-permute-start.22 = (bf16[256,768]{1,0:T(8,128)(2,1)S(1)}, bf16[256,768]{1,0:T(8,128)(2,1)S(1)}, u32[]{:S(2)}, u32[]{:S(2)}) collective-permute-start(bf16[256,768]{1,0:T(8,128)(2,1)S(1)} %bitcast.22), channel_id=1, source_target_pairs={{0,128},{128,0},{1,129},{129,1},{2,130},{130,2},{3,131},{131,3},{4... | collective-permute-start | bytes 1179656 | tf_op jit(solution)/shard_map/ppermute | solution.py:75
  95.2 0.3 collective-permute-start.7
  95.5 3.0 %collective-permute-start.25 = (bf16[2,256,512]{2,1,0:T(8,128)(2,1)S(1)}, bf16[2,256,512]{2,1,0:T(8,128)(2,1)S(1)}, u32[]{:S(2)}, u32[]{:S(2)}) collective-permute-start(bf16[2,256,512]{2,1,0:T(8,128)(2,1)S(1)} %collective-permute-done.20.refs_3_.br), channel_id=1, source_target_pairs={{0,12},{4,0},{8,4},{12,8},{1,13},{5,1},{9,5},{13,9},{2,14},{6,2},{... | collective-permute-start | bytes 1572872 | tf_op jit(solution)/shard_map/ppermute | solution.py:79
  98.4 3.2 %collective-permute-done.22.m10 = bf16[256,768]{1,0:T(8,128)(2,1)S(1)} collective-permute-done((bf16[256,768]{1,0:T(8,128)(2,1)S(1)}, bf16[256,768]{1,0:T(8,128)(2,1)S(1)}, u32[]{:S(2)}, u32[]{:S(2)}) %collective-permute-start.22) | collective-permute-done | bytes 393248 | tf_op jit(solution)/shard_map/ppermute | solution.py:75
  101.6 3.9 %collective-permute-start.26 = (f32[4,256]{1,0:T(4,128)S(1)}, f32[4,256]{1,0:T(4,128)S(1)}, u32[]{:S(2)}, u32[]{:S(2)}) collective-permute-start(f32[4,256]{1,0:T(4,128)S(1)} %pad_maximum_fusion.refs_1_.scale_ref), channel_id=1, source_target_pairs={{0,16},{16,32},{32,48},{48,64},{64,80},{80,96},{96,112},{112,128},... | collective-permute-start | bytes 12296 | tf_op jit(solution)/shard_map/ppermute | solution.py:447
  105.6 1.1 collective-permute-done.7.af
  106.7 3.2 %shard_map.132 = (bf16[4,256,512]{2,1,0:T(8,128)(2,1)S(1)}, bf16[4,256,256]{2,1,0:T(8,128)(2,1)S(1)}, bf16[1024,768]{1,0:T(8,128)(2,1)S(1)}) custom-call(s32[7]{0:T(128)S(1)} %copy-done.14, bf16[2,256,512]{2,1,0:T(8,128)(2,1)S(1)} %shard_map.124.a, bf16[2,256,512]{2,1,0:T(8,128)(2,1)} %collective-permute-done.3.refs_0_.al, ...), custom_call_target="tpu_custom_call" | custom-call | tf_op jit(solution)/shard_map/pallas_call | solution.py:313
  110.0 2.0 %shard_map.133.pm_ref = bf16[4,256,512]{2,1,0:T(8,128)(2,1)S(1)} custom-call(s32[7]{0:T(128)S(1)} %copy-done.14, bf16[2,256,512]{2,1,0:T(8,128)(2,1)S(1)} %copy-done.6, bf16[2,256,512]{2,1,0:T(8,128)(2,1)S(1)} %collective-permute-done.19.refs_2_.bl, bf16[2,256,512]{2,1,0:T(8,128)(2,1)S(1)} %collective-permute-done.20.refs_3_.br, ...), custom_call_target="tpu_custom_call" | custom-call | tf_op jit(solution)/shard_map/pallas_call | solution.py:313
  112.0 0.1 collective-permute-start.27
  112.1 0.5 collective-permute-start.24
  112.6 0.1 pad_add_fusion.2.place_ref
  112.6 2.1 %collective-permute-done.27.pt_ref = bf16[4,256,512]{2,1,0:T(8,128)(2,1)S(1)} collective-permute-done((bf16[4,256,512]{2,1,0:T(8,128)(2,1)S(1)}, bf16[4,256,512]{2,1,0:T(8,128)(2,1)S(1)}, u32[]{:S(2)}, u32[]{:S(2)}) %collective-permute-start.27) | collective-permute-done | bytes 1048608 | tf_op jit(solution)/shard_map/ppermute | solution.py:75
  114.7 1.6 %collective-permute-done.24.ot_ref = bf16[4,256,512]{2,1,0:T(8,128)(2,1)} collective-permute-done((bf16[4,256,512]{2,1,0:T(8,128)(2,1)S(1)}, bf16[4,256,512]{2,1,0:T(8,128)(2,1)}, u32[]{:S(2)}, u32[]{:S(2)}) %collective-permute-start.24) | collective-permute-done | bytes 1048608 | tf_op jit(solution)/shard_map/ppermute | solution.py:75
  116.3 1.0 copy-done.2
  117.4 5.5 %shard_map.135 = (bf16[256,256]{1,0:T(8,128)(2,1)S(1)}, bf16[256,256]{1,0:T(8,128)(2,1)S(1)}, bf16[256,256]{1,0:T(8,128)(2,1)S(1)}) custom-call(s32[6]{0:T(128)S(1)} %pad_add_fusion.2.place_ref, bf16[4,256,256]{2,1,0:T(8,128)(2,1)S(1)} %copy-done.2, bf16[4,256,512]{2,1,0:T(8,128)(2,1)S(1)} %get-tuple-element.31.om_ref, ...), custom_call_target="tpu_custom_call" | custom-call | tf_op jit(solution)/shard_map/pallas_call | solution.py:358
  122.9 0.1 collective-permute-start.28
  123.0 3.1 %collective-permute-start.29 = (bf16[256,256]{1,0:T(8,128)(2,1)S(1)}, bf16[256,256]{1,0:T(8,128)(2,1)S(1)}, u32[]{:S(2)}, u32[]{:S(2)}) collective-permute-start(bf16[256,256]{1,0:T(8,128)(2,1)S(1)} %get-tuple-element.34), channel_id=1, source_target_pairs={{0,8},{4,12},{8,0},{12,4},{1,9},{5,13},{9,1},{13,5},{2,10},{6,14},... | collective-permute-start | bytes 393224 | tf_op jit(solution)/shard_map/ppermute | solution.py:79
  126.1 0.8 collective-permute-start.30
  127.0 0.1 pad_add_fusion.1.place_ref
  127.1 3.0 %shard_map.134.a_ref = bf16[256,256]{1,0:T(8,128)(2,1)S(1)} custom-call(s32[4]{0:T(128)S(1)} %pad_add_fusion.1.place_ref, bf16[4,256,256]{2,1,0:T(8,128)(2,1)S(1)} %copy-done.3, bf16[4,256,512]{2,1,0:T(8,128)(2,1)S(1)} %get-tuple-element.31.om_ref, bf16[4,256,512]{2,1,0:T(8,128)(2,1)} %collective-permute-done.24.ot_ref, ...), custom_call_target="tpu_custom_call" | custom-call | tf_op jit(solution)/shard_map/pallas_call | solution.py:358
  130.1 0.4 collective-permute-done.28.b_ref
  130.5 2.0 %collective-permute-done.29.c_ref = bf16[256,256]{1,0:T(8,128)(2,1)S(1)} collective-permute-done((bf16[256,256]{1,0:T(8,128)(2,1)S(1)}, bf16[256,256]{1,0:T(8,128)(2,1)S(1)}, u32[]{:S(2)}, u32[]{:S(2)}) %collective-permute-start.29) | collective-permute-done | bytes 131104 | tf_op jit(solution)/shard_map/ppermute | solution.py:79
  132.5 0.6 collective-permute-done.30.d_ref
  133.1 1.4 %shard_map.136 = bf16[256,1024]{1,0:T(8,128)(2,1)} custom-call(s32[3]{0:T(128)S(1)} %pad_add_fusion.place_ref, bf16[256,256]{1,0:T(8,128)(2,1)S(1)} %shard_map.134.a_ref, bf16[256,256]{1,0:T(8,128)(2,1)S(1)} %collective-permute-done.28.b_ref, bf16[256,256]{1,0:T(8,128)(2,1)S(1)} %collective-permute-done.29.c_ref, ...), custom_call_target="tpu_custom_call" | custom-call | tf_op jit(solution)/shard_map/pallas_call | solution.py:375
  (73 shorter events, 0.5 us)
Async XLA Ops:
  1.3 19.9 %copy-start.4 = (bf16[1,4,512,512]{3,2,1,0:T(8,128)(2,1)S(1)}, bf16[1,4,512,512]{3,2,1,0:T(8,128)(2,1)}, u32[]{:S(2)}) copy-start(bf16[1,4,512,512]{3,2,1,0:T(8,128)(2,1)} %param.14) | copy-start | bytes 6291460
  1.3 19.9 %copy-start.7 = (bf16[1,3,512,256]{3,2,1,0:T(8,128)(2,1)S(1)}, bf16[1,3,512,256]{3,2,1,0:T(8,128)(2,1)}, u32[]{:S(2)}) copy-start(bf16[1,3,512,256]{3,2,1,0:T(8,128)(2,1)} %param.12) | copy-start | bytes 2359300
  1.3 19.9 %copy-start.9 = (bf16[1,256,512]{2,1,0:T(8,128)(2,1)S(1)}, bf16[1,256,512]{2,1,0:T(8,128)(2,1)}, u32[]{:S(2)}) copy-start(bf16[1,256,512]{2,1,0:T(8,128)(2,1)} %param.13) | copy-start | bytes 786436
  1.3 30.2 %copy-start.14 = (s32[7]{0:T(128)S(1)}, s32[7]{0:T(128)}, u32[]{:S(2)}) copy-start(s32[7]{0:T(128)} %stack.42.at_ref) | copy-start | bytes 88
  4.0 20.9 %collective-permute-start.11 = (bf16[2,128,256]{2,1,0:T(8,128)(2,1)}, bf16[2,128,256]{2,1,0:T(8,128)(2,1)S(1)}, u32[]{:S(2)}, u32[]{:S(2)}) collective-permute-start(bf16[2,128,256]{2,1,0:T(8,128)(2,1)} %get-tuple-element.26.mine_ref), channel_id=1, source_target_pairs={{0,1},{1,0},{2,3},{3,2},{4,5},{5,4},{6,7},{7,6},{8,9},{9,8},{10,11... | collective-permute-start | bytes 393224 | tf_op jit(solution)/shard_map/ppermute | solution.py:75
  6.3 18.5 %collective-permute-start.10 = (bf16[3,32,256]{2,1,0:T(8,128)(2,1)}, bf16[3,32,256]{2,1,0:T(8,128)(2,1)S(1)}, u32[]{:S(2)}, u32[]{:S(2)}) collective-permute-start(bf16[3,32,256]{2,1,0:T(8,128)(2,1)} %get-tuple-element.25), channel_id=1, source_target_pairs={{0,12},{4,0},{8,4},{12,8},{1,13},{5,1},{9,5},{13,9},{2,14},{6,2},{... | collective-permute-start | bytes 147464 | tf_op jit(solution)/shard_map/ppermute | solution.py:79
  9.0 15.8 %collective-permute-start.8 = (bf16[3,32,256]{2,1,0:T(8,128)(2,1)}, bf16[3,32,256]{2,1,0:T(8,128)(2,1)S(1)}, u32[]{:S(2)}, u32[]{:S(2)}) collective-permute-start(bf16[3,32,256]{2,1,0:T(8,128)(2,1)} %get-tuple-element.23), channel_id=1, source_target_pairs={{0,4},{4,8},{8,12},{12,0},{1,5},{5,9},{9,13},{13,1},{2,6},{6,10},{... | collective-permute-start | bytes 147464 | tf_op jit(solution)/shard_map/ppermute | solution.py:79
  9.0 15.8 %collective-permute-start.9 = (bf16[3,32,256]{2,1,0:T(8,128)(2,1)}, bf16[3,32,256]{2,1,0:T(8,128)(2,1)S(1)}, u32[]{:S(2)}, u32[]{:S(2)}) collective-permute-start(bf16[3,32,256]{2,1,0:T(8,128)(2,1)} %get-tuple-element.24), channel_id=1, source_target_pairs={{0,8},{4,12},{8,0},{12,4},{1,9},{5,13},{9,1},{13,5},{2,10},{6,14},... | collective-permute-start | bytes 147464 | tf_op jit(solution)/shard_map/ppermute | solution.py:79
  12.0 9.2 %collective-permute-start = (bf16[8,512]{1,0:T(8,128)(2,1)S(1)}, bf16[8,512]{1,0:T(8,128)(2,1)S(1)}, u32[]{:S(2)}, u32[]{:S(2)}) collective-permute-start(bf16[8,512]{1,0:T(8,128)(2,1)S(1)} %slice_bitcast_fusion), channel_id=1, source_target_pairs={{0,2},{2,4},{4,6},{6,8},{8,10},{10,12},{12,14},{14,16},{16,18},{18... | collective-permute-start | bytes 24584 | tf_op jit(solution)/shard_map/ppermute | solution.py:405
  21.2 1.0 copy-start.8
  22.3 9.2 %copy-start = (bf16[1,512,4096]{2,1,0:T(8,128)(2,1)S(1)}, bf16[1,512,4096]{2,1,0:T(8,128)(2,1)}, u32[]{:S(2)}) copy-start(bf16[1,512,4096]{2,1,0:T(8,128)(2,1)} %param.15) | copy-start | bytes 12582916
  24.9 0.8 copy-start.13
  25.7 13.5 %copy-start.10 = (f32[2,4096]{1,0:T(2,128)S(1)}, f32[2,4096]{1,0:T(2,128)}, u32[]{:S(2)}) copy-start(f32[2,4096]{1,0:T(2,128)} %t1.1) | copy-start | bytes 98308
  25.7 13.5 %copy-start.11 = (bf16[2,128,256]{2,1,0:T(8,128)(2,1)S(1)}, bf16[2,128,256]{2,1,0:T(8,128)(2,1)}, u32[]{:S(2)}) copy-start(bf16[2,128,256]{2,1,0:T(8,128)(2,1)} %get-tuple-element.26.mine_ref) | copy-start | bytes 393220
  25.7 13.5 %copy-start.12 = (f32[4096]{0:T(1024)S(1)}, f32[4096]{0:T(1024)}, u32[]{:S(2)}) copy-start(f32[4096]{0:T(1024)} %param.18) | copy-start | bytes 49156
  25.7 5.8 %collective-permute-start.13 = (bf16[4,3,32,256]{3,2,1,0:T(8,128)(2,1)S(1)}, bf16[4,3,32,256]{3,2,1,0:T(8,128)(2,1)S(1)}, u32[]{:S(2)}, u32[]{:S(2)}) collective-permute-start(bf16[4,3,32,256]{3,2,1,0:T(8,128)(2,1)S(1)} %shard_map.128.w00), channel_id=1, source_target_pairs={{0,128},{128,0},{1,129},{129,1},{2,130},{130,2},{3,131},{131,3},{4... | collective-permute-start | bytes 589832 | tf_op jit(solution)/shard_map/ppermute | solution.py:75
  25.8 11.1 %collective-permute-start.2 = (bf16[256,512]{1,0:T(8,128)(2,1)S(1)}, bf16[256,512]{1,0:T(8,128)(2,1)S(1)}, u32[]{:S(2)}, u32[]{:S(2)}) collective-permute-start(bf16[256,512]{1,0:T(8,128)(2,1)S(1)} %shard_map.122.latent_ref.refs_0_.refs_4_), channel_id=1, source_target_pairs={{0,1},{1,0},{2,3},{3,2},{4,5},{5,4},{6,7},{7,6},{8,9},{9,8},{10,11... | collective-permute-start | bytes 786440 | tf_op jit(solution)/shard_map/ppermute | solution.py:75
  27.1 12.1 %collective-permute-start.5 = (bf16[256,512]{1,0:T(8,128)(2,1)S(1)}, bf16[256,512]{1,0:T(8,128)(2,1)S(1)}, u32[]{:S(2)}, u32[]{:S(2)}) collective-permute-start(bf16[256,512]{1,0:T(8,128)(2,1)S(1)} %shard_map.122.latent_ref.refs_0_.refs_4_), channel_id=1, source_target_pairs={{0,16},{16,32},{32,48},{48,64},{64,80},{80,96},{96,112},{112,128},... | collective-permute-start | bytes 786440 | tf_op jit(solution)/shard_map/ppermute | solution.py:415
  29.1 10.1 %collective-permute-start.12 = (bf16[4,3,32,256]{3,2,1,0:T(8,128)(2,1)S(1)}, bf16[4,3,32,256]{3,2,1,0:T(8,128)(2,1)S(1)}, u32[]{:S(2)}, u32[]{:S(2)}) collective-permute-start(bf16[4,3,32,256]{3,2,1,0:T(8,128)(2,1)S(1)} %shard_map.128.w00), channel_id=1, source_target_pairs={{0,2},{2,0},{1,3},{3,1},{4,6},{6,4},{5,7},{7,5},{8,10},{10,8},{9,1... | collective-permute-start | bytes 589832 | tf_op jit(solution)/shard_map/ppermute | solution.py:75
  31.5 7.7 %collective-permute-start.14 = (bf16[4,3,32,256]{3,2,1,0:T(8,128)(2,1)S(1)}, bf16[4,3,32,256]{3,2,1,0:T(8,128)(2,1)S(1)}, u32[]{:S(2)}, u32[]{:S(2)}) collective-permute-start(bf16[4,3,32,256]{3,2,1,0:T(8,128)(2,1)S(1)} %collective-permute-done.13.w10), channel_id=1, source_target_pairs={{0,2},{2,0},{1,3},{3,1},{4,6},{6,4},{5,7},{7,5},{8,10},{10,8},{9,1... | collective-permute-start | bytes 589832 | tf_op jit(solution)/shard_map/ppermute | solution.py:75
  35.2 13.7 %copy-start.15 = (bf16[256,2048]{1,0:T(8,128)(2,1)}, bf16[256,2048]{1,0:T(8,128)(2,1)S(1)}, u32[]{:S(2)}) copy-start(bf16[256,2048]{1,0:T(8,128)(2,1)S(1)} %get-tuple-element.19.own_ref) | copy-start | bytes 3145732
  35.3 13.4 %copy-start.17 = (s32[2,32]{1,0:T(2,128)S(1)}, s32[2,32]{1,0:T(2,128)}, u32[]{:S(2)}) copy-start(s32[2,32]{1,0:T(2,128)} %param.16) | copy-start | bytes 772
  35.3 39.8 %collective-permute-start.1 = (bf16[256,2048]{1,0:T(8,128)(2,1)}, bf16[256,2048]{1,0:T(8,128)(2,1)}, u32[]{:S(2)}, u32[]{:S(2)}) collective-permute-start(bf16[256,2048]{1,0:T(8,128)(2,1)} %get-tuple-element.20.refs_0_), channel_id=1, source_target_pairs={{0,1},{1,0},{2,3},{3,2},{4,5},{5,4},{6,7},{7,6},{8,9},{9,8},{10,11... | collective-permute-start | bytes 3145736 | tf_op jit(solution)/shard_map/ppermute | solution.py:75
  42.4 28.2 %all-to-all-start = ((bf16[8,32,896]{2,1,0:T(8,128)(2,1)}), bf16[8,32,896]{2,1,0:T(8,128)(2,1)S(1)}, u32[]{:S(2)}, u32[]{:S(2)}) async-start(bf16[8,32,896]{2,1,0:T(8,128)(2,1)} %shard_map.129), calls=%async_computation | async-start | bytes 917504 | tf_op jit(solution)/shard_map/all_to_all | solution.py:426
  48.9 26.1 %collective-permute-start.3 = (bf16[2,256,512]{2,1,0:T(8,128)(2,1)S(1)}, bf16[2,256,512]{2,1,0:T(8,128)(2,1)}, u32[]{:S(2)}, u32[]{:S(2)}) collective-permute-start(bf16[2,256,512]{2,1,0:T(8,128)(2,1)S(1)} %shard_map.124.a), channel_id=1, source_target_pairs={{0,4},{4,8},{8,12},{12,0},{1,5},{5,9},{9,13},{13,1},{2,6},{6,10},{... | collective-permute-start | bytes 1572872 | tf_op jit(solution)/shard_map/ppermute | solution.py:79
  49.0 26.0 %collective-permute-start.4 = (bf16[2,256,512]{2,1,0:T(8,128)(2,1)S(1)}, bf16[2,256,512]{2,1,0:T(8,128)(2,1)}, u32[]{:S(2)}, u32[]{:S(2)}) collective-permute-start(bf16[2,256,512]{2,1,0:T(8,128)(2,1)S(1)} %shard_map.124.a), channel_id=1, source_target_pairs={{0,12},{4,0},{8,4},{12,8},{1,13},{5,1},{9,5},{13,9},{2,14},{6,2},{... | collective-permute-start | bytes 1572872 | tf_op jit(solution)/shard_map/ppermute | solution.py:79
  52.3 16.1 %collective-permute-start.6 = (bf16[256,512]{1,0:T(8,128)(2,1)S(1)}, bf16[256,512]{1,0:T(8,128)(2,1)S(1)}, u32[]{:S(2)}, u32[]{:S(2)}) collective-permute-start(bf16[256,512]{1,0:T(8,128)(2,1)S(1)} %collective-permute-done.2.refs_1_), channel_id=1, source_target_pairs={{0,16},{16,32},{32,48},{48,64},{64,80},{80,96},{96,112},{112,128},... | collective-permute-start | bytes 786440 | tf_op jit(solution)/shard_map/ppermute | solution.py:416
  68.5 11.8 %copy-start.5 = (bf16[2,256,512]{2,1,0:T(8,128)(2,1)}, bf16[2,256,512]{2,1,0:T(8,128)(2,1)S(1)}, u32[]{:S(2)}) copy-start(bf16[2,256,512]{2,1,0:T(8,128)(2,1)S(1)} %shard_map.125.refs_2_.b) | copy-start | bytes 1572868
  68.5 25.2 %collective-permute-start.20 = (bf16[2,256,512]{2,1,0:T(8,128)(2,1)S(1)}, bf16[2,256,512]{2,1,0:T(8,128)(2,1)S(1)}, u32[]{:S(2)}, u32[]{:S(2)}) collective-permute-start(bf16[2,256,512]{2,1,0:T(8,128)(2,1)S(1)} %shard_map.125.refs_2_.b), channel_id=1, source_target_pairs={{0,12},{4,0},{8,4},{12,8},{1,13},{5,1},{9,5},{13,9},{2,14},{6,2},{... | collective-permute-start | bytes 1572872 | tf_op jit(solution)/shard_map/ppermute | solution.py:79
  69.8 23.9 %collective-permute-start.19 = (bf16[2,256,512]{2,1,0:T(8,128)(2,1)S(1)}, bf16[2,256,512]{2,1,0:T(8,128)(2,1)S(1)}, u32[]{:S(2)}, u32[]{:S(2)}) collective-permute-start(bf16[2,256,512]{2,1,0:T(8,128)(2,1)S(1)} %shard_map.125.refs_2_.b), channel_id=1, source_target_pairs={{0,4},{4,8},{8,12},{12,0},{1,5},{5,9},{9,13},{13,1},{2,6},{6,10},{... | collective-permute-start | bytes 1572872 | tf_op jit(solution)/shard_map/ppermute | solution.py:79
  71.4 22.3 %all-to-all-start.1 = ((bf16[8,32,768]{2,1,0:T(8,128)(2,1)}), bf16[8,32,768]{2,1,0:T(8,128)(2,1)S(1)}, u32[]{:S(2)}, u32[]{:S(2)}) async-start(bf16[8,32,768]{2,1,0:T(8,128)(2,1)} %get-tuple-element.27), calls=%async_computation.1 | async-start | bytes 786432 | tf_op jit(solution)/shard_map/all_to_all | solution.py:442
  75.0 1.2 copy-start.16
  80.2 5.0 %collective-permute-start.16 = (f32[1,256]{1,0:T(1,128)S(1)}, f32[1,256]{1,0:T(1,128)S(1)}, u32[]{:S(2)}, u32[]{:S(2)}) collective-permute-start(f32[1,256]{1,0:T(1,128)S(1)} %slice.11), channel_id=1, source_target_pairs={{0,4},{4,0},{8,12},{12,8},{1,5},{5,1},{9,13},{13,9},{2,6},{6,2},{1... | collective-permute-start | bytes 3080 | tf_op jit(solution)/shard_map/ppermute | solution.py:437
  80.2 6.1 %collective-permute-start.17 = (f32[1,256]{1,0:T(1,128)S(1)}, f32[1,256]{1,0:T(1,128)S(1)}, u32[]{:S(2)}, u32[]{:S(2)}) collective-permute-start(f32[1,256]{1,0:T(1,128)S(1)} %slice.11), channel_id=1, source_target_pairs={{0,5},{1,4},{4,1},{5,0},{8,13},{9,12},{12,9},{13,8},{2,7},{3,6},{6... | collective-permute-start | bytes 3080 | tf_op jit(solution)/shard_map/ppermute | solution.py:438
  83.4 5.1 %collective-permute-start.15 = (f32[1,256]{1,0:T(1,128)S(1)}, f32[1,256]{1,0:T(1,128)S(1)}, u32[]{:S(2)}, u32[]{:S(2)}) collective-permute-start(f32[1,256]{1,0:T(1,128)S(1)} %slice.11), channel_id=1, source_target_pairs={{0,1},{1,0},{2,3},{3,2},{4,5},{5,4},{6,7},{7,6},{8,9},{9,8},{10,11... | collective-permute-start | bytes 3080 | tf_op jit(solution)/shard_map/ppermute | solution.py:75
  88.5 5.2 %collective-permute-start.18 = (f32[2,256]{1,0:T(2,128)S(1)}, f32[2,256]{1,0:T(2,128)S(1)}, u32[]{:S(2)}, u32[]{:S(2)}) collective-permute-start(f32[2,256]{1,0:T(2,128)S(1)} %fusion.4), channel_id=1, source_target_pairs={{0,8},{4,12},{8,0},{12,4},{1,9},{5,13},{9,1},{13,5},{2,10},{6,14},... | collective-permute-start | bytes 6152 | tf_op jit(solution)/shard_map/ppermute | solution.py:441
  93.8 16.2 %copy-start.6 = (bf16[2,256,512]{2,1,0:T(8,128)(2,1)S(1)}, bf16[2,256,512]{2,1,0:T(8,128)(2,1)}, u32[]{:S(2)}) copy-start(bf16[2,256,512]{2,1,0:T(8,128)(2,1)} %copy-done.5) | copy-start | bytes 1572868
  93.8 7.9 %collective-permute-start.22 = (bf16[256,768]{1,0:T(8,128)(2,1)S(1)}, bf16[256,768]{1,0:T(8,128)(2,1)S(1)}, u32[]{:S(2)}, u32[]{:S(2)}) collective-permute-start(bf16[256,768]{1,0:T(8,128)(2,1)S(1)} %bitcast.22), channel_id=1, source_target_pairs={{0,128},{128,0},{1,129},{129,1},{2,130},{130,2},{3,131},{131,3},{4... | collective-permute-start | bytes 1179656 | tf_op jit(solution)/shard_map/ppermute | solution.py:75
  95.2 11.5 %collective-permute-start.7 = (bf16[2,256,512]{2,1,0:T(8,128)(2,1)}, bf16[2,256,512]{2,1,0:T(8,128)(2,1)S(1)}, u32[]{:S(2)}, u32[]{:S(2)}) collective-permute-start(bf16[2,256,512]{2,1,0:T(8,128)(2,1)} %collective-permute-done.3.refs_0_.al), channel_id=1, source_target_pairs={{0,4},{4,8},{8,12},{12,0},{1,5},{5,9},{9,13},{13,1},{2,6},{6,10},{... | collective-permute-start | bytes 1572872 | tf_op jit(solution)/shard_map/ppermute | solution.py:79
  95.5 14.5 %collective-permute-start.25 = (bf16[2,256,512]{2,1,0:T(8,128)(2,1)S(1)}, bf16[2,256,512]{2,1,0:T(8,128)(2,1)S(1)}, u32[]{:S(2)}, u32[]{:S(2)}) collective-permute-start(bf16[2,256,512]{2,1,0:T(8,128)(2,1)S(1)} %collective-permute-done.20.refs_3_.br), channel_id=1, source_target_pairs={{0,12},{4,0},{8,4},{12,8},{1,13},{5,1},{9,5},{13,9},{2,14},{6,2},{... | collective-permute-start | bytes 1572872 | tf_op jit(solution)/shard_map/ppermute | solution.py:79
  98.4 8.2 %collective-permute-start.21 = (bf16[256,768]{1,0:T(8,128)(2,1)S(1)}, bf16[256,768]{1,0:T(8,128)(2,1)S(1)}, u32[]{:S(2)}, u32[]{:S(2)}) collective-permute-start(bf16[256,768]{1,0:T(8,128)(2,1)S(1)} %bitcast.23), channel_id=1, source_target_pairs={{0,2},{2,0},{1,3},{3,1},{4,6},{6,4},{5,7},{7,5},{8,10},{10,8},{9,1... | collective-permute-start | bytes 1179656 | tf_op jit(solution)/shard_map/ppermute | solution.py:75
  101.6 5.0 %collective-permute-start.23 = (bf16[256,768]{1,0:T(8,128)(2,1)S(1)}, bf16[256,768]{1,0:T(8,128)(2,1)S(1)}, u32[]{:S(2)}, u32[]{:S(2)}) collective-permute-start(bf16[256,768]{1,0:T(8,128)(2,1)S(1)} %collective-permute-done.22.m10), channel_id=1, source_target_pairs={{0,2},{2,0},{1,3},{3,1},{4,6},{6,4},{5,7},{7,5},{8,10},{10,8},{9,1... | collective-permute-start | bytes 1179656 | tf_op jit(solution)/shard_map/ppermute | solution.py:75
  101.6 8.3 %collective-permute-start.26 = (f32[4,256]{1,0:T(4,128)S(1)}, f32[4,256]{1,0:T(4,128)S(1)}, u32[]{:S(2)}, u32[]{:S(2)}) collective-permute-start(f32[4,256]{1,0:T(4,128)S(1)} %pad_maximum_fusion.refs_1_.scale_ref), channel_id=1, source_target_pairs={{0,16},{16,32},{32,48},{48,64},{64,80},{80,96},{96,112},{112,128},... | collective-permute-start | bytes 12296 | tf_op jit(solution)/shard_map/ppermute | solution.py:447
  109.9 2.0 %copy-start.1 = (bf16[4,256,256]{2,1,0:T(8,128)(2,1)}, bf16[4,256,256]{2,1,0:T(8,128)(2,1)S(1)}, u32[]{:S(2)}) copy-start(bf16[4,256,256]{2,1,0:T(8,128)(2,1)S(1)} %get-tuple-element.30.q_ref) | copy-start | bytes 1572868
  110.0 2.6 %copy-start.18 = (s32[3]{0:T(128)S(1)}, s32[3]{0:T(128)}, u32[]{:S(2)}) copy-start(s32[3]{0:T(128)} %constant.57.clone) | copy-start | bytes 40
  112.0 2.7 %collective-permute-start.27 = (bf16[4,256,512]{2,1,0:T(8,128)(2,1)S(1)}, bf16[4,256,512]{2,1,0:T(8,128)(2,1)S(1)}, u32[]{:S(2)}, u32[]{:S(2)}) collective-permute-start(bf16[4,256,512]{2,1,0:T(8,128)(2,1)S(1)} %shard_map.133.pm_ref), channel_id=1, source_target_pairs={{0,2},{2,0},{1,3},{3,1},{4,6},{6,4},{5,7},{7,5},{8,10},{10,8},{9,1... | collective-permute-start | bytes 3145736 | tf_op jit(solution)/shard_map/ppermute | solution.py:75
  112.1 4.3 %collective-permute-start.24 = (bf16[4,256,512]{2,1,0:T(8,128)(2,1)S(1)}, bf16[4,256,512]{2,1,0:T(8,128)(2,1)}, u32[]{:S(2)}, u32[]{:S(2)}) collective-permute-start(bf16[4,256,512]{2,1,0:T(8,128)(2,1)S(1)} %get-tuple-element.31.om_ref), channel_id=1, source_target_pairs={{0,2},{2,0},{1,3},{3,1},{4,6},{6,4},{5,7},{7,5},{8,10},{10,8},{9,1... | collective-permute-start | bytes 3145736 | tf_op jit(solution)/shard_map/ppermute | solution.py:75
  116.3 1.0 copy-start.2
  117.4 9.7 %copy-start.3 = (bf16[4,256,256]{2,1,0:T(8,128)(2,1)S(1)}, bf16[4,256,256]{2,1,0:T(8,128)(2,1)}, u32[]{:S(2)}) copy-start(bf16[4,256,256]{2,1,0:T(8,128)(2,1)} %copy-done.1) | copy-start | bytes 1572868
  122.9 7.6 %collective-permute-start.28 = (bf16[256,256]{1,0:T(8,128)(2,1)S(1)}, bf16[256,256]{1,0:T(8,128)(2,1)S(1)}, u32[]{:S(2)}, u32[]{:S(2)}) collective-permute-start(bf16[256,256]{1,0:T(8,128)(2,1)S(1)} %get-tuple-element.33), channel_id=1, source_target_pairs={{0,4},{4,8},{8,12},{12,0},{1,5},{5,9},{9,13},{13,1},{2,6},{6,10},{... | collective-permute-start | bytes 393224 | tf_op jit(solution)/shard_map/ppermute | solution.py:79
  123.0 9.5 %collective-permute-start.29 = (bf16[256,256]{1,0:T(8,128)(2,1)S(1)}, bf16[256,256]{1,0:T(8,128)(2,1)S(1)}, u32[]{:S(2)}, u32[]{:S(2)}) collective-permute-start(bf16[256,256]{1,0:T(8,128)(2,1)S(1)} %get-tuple-element.34), channel_id=1, source_target_pairs={{0,8},{4,12},{8,0},{12,4},{1,9},{5,13},{9,1},{13,5},{2,10},{6,14},... | collective-permute-start | bytes 393224 | tf_op jit(solution)/shard_map/ppermute | solution.py:79
  126.1 7.0 %collective-permute-start.30 = (bf16[256,256]{1,0:T(8,128)(2,1)S(1)}, bf16[256,256]{1,0:T(8,128)(2,1)S(1)}, u32[]{:S(2)}, u32[]{:S(2)}) collective-permute-start(bf16[256,256]{1,0:T(8,128)(2,1)S(1)} %get-tuple-element.35), channel_id=1, source_target_pairs={{0,12},{4,0},{8,4},{12,8},{1,13},{5,1},{9,5},{13,9},{2,14},{6,2},{... | collective-permute-start | bytes 393224 | tf_op jit(solution)/shard_map/ppermute | solution.py:79

commit v9 on v8

--- a/solution.py
+++ b/solution.py
@@ -66,7 +66,7 @@
         out_specs=pl.BlockSpec(memory_space=pltpu.VMEM),
         out_shape=jax.ShapeDtypeStruct((BLOCK, CH), BF),
         scratch_shapes=[pltpu.VMEM((528, CH), F32), pltpu.VMEM((CH // 128, 520, 128), F32)],
-        compiler_params=params(20),
+        compiler_params=params(12),
         cost_estimate=NO_COST,
     )(halo, audio, taps, back, down)
 
@@ -173,7 +173,7 @@
             scratch_shapes=[pltpu.VMEM((2, 256, 768), BF)],
         ),
         out_shape=jax.ShapeDtypeStruct((8, 32, 896), BF),
-        compiler_params=params(16),
+        compiler_params=params(10),
         cost_estimate=NO_COST,
     )(at, *ws, mine, rest, gain, gain, table, table, *after)
 
@@ -233,7 +233,7 @@
             out_specs=[pl.BlockSpec((BLOCK, 1024), give_at), pl.BlockSpec((BLOCK, 1024), own_at)],
         ),
         out_shape=[jax.ShapeDtypeStruct((BLOCK, D // 2), BF)] * 2,
-        compiler_params=params(16),
+        compiler_params=params(10),
         cost_estimate=NO_COST,
     )(at, latent, embed, *after)
 
@@ -274,7 +274,7 @@
             out_specs=[tile, pl.BlockSpec((8, BLOCK), lambda i, at: (0, 0))],
         ),
         out_shape=[jax.ShapeDtypeStruct((BLOCK, D // 2), BF), jax.ShapeDtypeStruct((8, BLOCK), F32)],
-        compiler_params=params(16),
+        compiler_params=params(10),
         cost_estimate=pl.CostEstimate(flops=20000000000, bytes_accessed=0, transcendentals=0),
     )(at, own, got, active, table, *after)
 
@@ -360,7 +360,7 @@
         in_specs=[pl.BlockSpec(memory_space=pltpu.SMEM)] + in_vmem(5),
         out_specs=in_vmem(n),
         out_shape=[jax.ShapeDtypeStruct((BLOCK, 256), BF)] * n,
-        compiler_params=params(16),
+        compiler_params=params(10),
         cost_estimate=NO_COST,
     )(jnp.concatenate([place, jnp.array(offsets, jnp.int32)]), *args)
 
@@ -377,7 +377,7 @@
         in_specs=[pl.BlockSpec(memory_space=pltpu.SMEM)] + in_vmem(4),
         out_specs=pl.BlockSpec(memory_space=pltpu.VMEM),
         out_shape=jax.ShapeDtypeStruct((BLOCK, 1024), BF),
-        compiler_params=params(20),
+        compiler_params=params(12),
     )(place, *parts)
 
 

time: 136 us -> 137 us (level)
  transfers between devices with their start and end apart: 33 -> 33, of which waited for: 14 -> 13; matrix products, arithmetic and copies ran while one was open for 1% -> 1% of each run, Pallas kernels for 15% -> 15%
where the time goes in v9:
time: 137 us; the launch traced here: 136 us
  starting transfers between devices  53 us (39%)
  waiting for transfers between devices  42.2 us (31%)
  Pallas kernels  32.1 us (23%)
  local copies, waits for them, and re-layouts  6.61 us (5%)
    ppermute x12, starting transfers between devices, shift(): return lax.ppermute(a, 'x', [(i, (i + by) % 4) for i in range(4)])  17 us
    ppermute x1, waiting for transfers between devices, on_device(): b = stack([prev, lax.ppermute(other, ('yl', 'z'), behind)])  12 us
    ppermute x12, waiting for transfers between devices, swap(): return lax.ppermute(a, axis, SWAP)  11.4 us
    ppermute x12, starting transfers between devices, swap(): return lax.ppermute(a, axis, SWAP)  9.3 us
    pallas_call x2, Pallas kernels, attention(): pl.pallas_call(functools.partial(attention_kernel, n), in_specs=[pl.Block...  8.51 us
    ppermute x1, waiting for transfers between devices, on_device(): halo = lax.ppermute(audio[-8:], CTX, [(i, i + 1) for i in range(127)])  7.26 us
    all_to_all x1, starting transfers between devices, on_device(): packed = lax.all_to_all(packed, 'z', 0, 0, tiled=True)  7.08 us
    pallas_call x2, Pallas kernels, project(): pl.pallas_call(kernel, in_specs=[pl.BlockSpec(memory_space=pltpu.SMEM)] +...  5.21 us
  transfers between devices with their start and end apart: 33, of which 13 were waited for; matrix products, arithmetic and copies ran while one was open for 1% of the time, Pallas kernels for 15%

profile of v9, /device:TPU:8, one launch (start us, length us, event | category | flops | bytes accessed | tf_op | source)
XLA Modules:
  0.0 135.7 jit_solution(10555758844085443265)
XLA Ops:
  0.6 0.7 stack.42.at_ref
  1.3 2.7 %shard_map.127 = (bf16[3,32,256]{2,1,0:T(8,128)(2,1)}, bf16[3,32,256]{2,1,0:T(8,128)(2,1)}, bf16[3,32,256]{2,1,0:T(8,128)(2,1)}, bf16[3,32,256]{2,1,0:T(8,128)(2,1)}, bf16[2,128,256]{2,1,0:T(8,128)(2,1)}) custom-call(s32[7]{0:T(128)} %stack.42.at_ref, bf16[3,32,1024]{2,1,0:T(8,128)(2,1)} %w_ref.1, bf16[512,4096]{1,0:T(8,128)(2,1)} %bitcast.18, ...), custom_call_target="tpu_custom_call" | custom-call | tf_op jit(solution)/shard_map/pallas_call | solution.py:93
  4.0 2.3 %collective-permute-start.11 = (bf16[2,128,256]{2,1,0:T(8,128)(2,1)}, bf16[2,128,256]{2,1,0:T(8,128)(2,1)S(1)}, u32[]{:S(2)}, u32[]{:S(2)}) collective-permute-start(bf16[2,128,256]{2,1,0:T(8,128)(2,1)} %get-tuple-element.26.mine_ref), channel_id=1, source_target_pairs={{0,1},{1,0},{2,3},{3,2},{4,5},{5,4},{6,7},{7,6},{8,9},{9,8},{10,11... | collective-permute-start | bytes 393224 | tf_op jit(solution)/shard_map/ppermute | solution.py:75
  6.3 2.8 %collective-permute-start.10 = (bf16[3,32,256]{2,1,0:T(8,128)(2,1)}, bf16[3,32,256]{2,1,0:T(8,128)(2,1)S(1)}, u32[]{:S(2)}, u32[]{:S(2)}) collective-permute-start(bf16[3,32,256]{2,1,0:T(8,128)(2,1)} %get-tuple-element.25), channel_id=1, source_target_pairs={{0,12},{4,0},{8,4},{12,8},{1,13},{5,1},{9,5},{13,9},{2,14},{6,2},{... | collective-permute-start | bytes 147464 | tf_op jit(solution)/shard_map/ppermute | solution.py:79
  9.0 2.3 %collective-permute-start.9 = (bf16[3,32,256]{2,1,0:T(8,128)(2,1)}, bf16[3,32,256]{2,1,0:T(8,128)(2,1)S(1)}, u32[]{:S(2)}, u32[]{:S(2)}) collective-permute-start(bf16[3,32,256]{2,1,0:T(8,128)(2,1)} %get-tuple-element.24), channel_id=1, source_target_pairs={{0,8},{4,12},{8,0},{12,4},{1,9},{5,13},{9,1},{13,5},{2,10},{6,14},... | collective-permute-start | bytes 147464 | tf_op jit(solution)/shard_map/ppermute | solution.py:79
  11.3 0.7 slice_bitcast_fusion
  12.0 1.9 %collective-permute-start = (bf16[8,512]{1,0:T(8,128)(2,1)S(1)}, bf16[8,512]{1,0:T(8,128)(2,1)S(1)}, u32[]{:S(2)}, u32[]{:S(2)}) collective-permute-start(bf16[8,512]{1,0:T(8,128)(2,1)S(1)} %slice_bitcast_fusion), channel_id=1, source_target_pairs={{0,2},{2,4},{4,6},{6,8},{8,10},{10,12},{12,14},{14,16},{16,18},{18... | collective-permute-start | bytes 24584 | tf_op jit(solution)/shard_map/ppermute | solution.py:405
  13.9 7.3 %collective-permute-done.halo_ref = bf16[8,512]{1,0:T(8,128)(2,1)S(1)} collective-permute-done((bf16[8,512]{1,0:T(8,128)(2,1)S(1)}, bf16[8,512]{1,0:T(8,128)(2,1)S(1)}, u32[]{:S(2)}, u32[]{:S(2)}) %collective-permute-start) | collective-permute-done | bytes 8224 | tf_op jit(solution)/shard_map/ppermute | solution.py:405
  21.2 1.0 copy-done.8
  22.3 2.5 %shard_map.122.latent_ref.refs_0_.refs_4_ = bf16[256,512]{1,0:T(8,128)(2,1)S(1)} custom-call(bf16[8,512]{1,0:T(8,128)(2,1)S(1)} %collective-permute-done.halo_ref, bf16[512,512]{1,0:T(8,128)(2,1)S(1)} %bitcast.27, bf16[3,512,256]{2,1,0:T(8,128)(2,1)S(1)} %bitcast.26, bf16[256,512]{1,0:T(8,128)(2,1)S(1)} %bitcast.28, bf16[4,512,512]{2,1,0:T(8,128)(2,1)S(1)} %bitcast.21), custom_call_target="tpu_custom_call" | custom-call | tf_op jit(solution)/shard_map/pallas_call | solution.py:63
  24.9 0.8 copy-done.13
  25.7 0.1 collective-permute-start.13
  25.8 1.3 collective-permute-start.2
  27.1 1.9 %collective-permute-start.5 = (bf16[256,512]{1,0:T(8,128)(2,1)S(1)}, bf16[256,512]{1,0:T(8,128)(2,1)S(1)}, u32[]{:S(2)}, u32[]{:S(2)}) collective-permute-start(bf16[256,512]{1,0:T(8,128)(2,1)S(1)} %shard_map.122.latent_ref.refs_0_.refs_4_), channel_id=1, source_target_pairs={{0,16},{16,32},{32,48},{48,64},{64,80},{80,96},{96,112},{112,128},... | collective-permute-start | bytes 786440 | tf_op jit(solution)/shard_map/ppermute | solution.py:415
  29.1 0.1 collective-permute-start.12
  29.2 2.3 %collective-permute-done.13.w10 = bf16[4,3,32,256]{3,2,1,0:T(8,128)(2,1)S(1)} collective-permute-done((bf16[4,3,32,256]{3,2,1,0:T(8,128)(2,1)S(1)}, bf16[4,3,32,256]{3,2,1,0:T(8,128)(2,1)S(1)}, u32[]{:S(2)}, u32[]{:S(2)}) %collective-permute-start.13) | collective-permute-done | bytes 196640 | tf_op jit(solution)/shard_map/ppermute | solution.py:75
  31.5 3.8 %shard_map.123 = (bf16[256,2048]{1,0:T(8,128)(2,1)}, bf16[256,2048]{1,0:T(8,128)(2,1)S(1)}) custom-call(s32[7]{0:T(128)S(1)} %copy-done.14, bf16[256,512]{1,0:T(8,128)(2,1)S(1)} %shard_map.122.latent_ref.refs_0_.refs_4_, bf16[512,4096]{1,0:T(8,128)(2,1)S(1)} %bitcast.20), custom_call_target="tpu_custom_call" | custom-call | tf_op jit(solution)/shard_map/pallas_call | solution.py:226
  35.3 1.0 copy-done.15
  36.2 1.7 %collective-permute-start.1 = (bf16[256,2048]{1,0:T(8,128)(2,1)}, bf16[256,2048]{1,0:T(8,128)(2,1)}, u32[]{:S(2)}, u32[]{:S(2)}) collective-permute-start(bf16[256,2048]{1,0:T(8,128)(2,1)} %get-tuple-element.20.refs_0_), channel_id=1, source_target_pairs={{0,1},{1,0},{2,3},{3,2},{4,5},{5,4},{6,7},{7,6},{8,9},{9,8},{10,11... | collective-permute-start | bytes 3145736 | tf_op jit(solution)/shard_map/ppermute | solution.py:75
  37.9 1.3 collective-permute-done.5.refs_0_.refs_2_
  39.2 3.2 %shard_map.129 = bf16[8,32,896]{2,1,0:T(8,128)(2,1)} custom-call(s32[7]{0:T(128)S(1)} %copy-done.14, bf16[4,3,32,256]{3,2,1,0:T(8,128)(2,1)S(1)} %shard_map.128.w00, bf16[4,3,32,256]{3,2,1,0:T(8,128)(2,1)S(1)} %collective-permute-done.12.w01, bf16[4,3,32,256]{3,2,1,0:T(8,128)(2,1)S(1)} %collective-permute-done.13.w10, ...), custom_call_target="tpu_custom_call" | custom-call | tf_op jit(solution)/shard_map/pallas_call | solution.py:163
  42.4 7.1 %all-to-all-start = ((bf16[8,32,896]{2,1,0:T(8,128)(2,1)}), bf16[8,32,896]{2,1,0:T(8,128)(2,1)S(1)}, u32[]{:S(2)}, u32[]{:S(2)}) async-start(bf16[8,32,896]{2,1,0:T(8,128)(2,1)} %shard_map.129), calls=%async_computation | async-start | bytes 917504 | tf_op jit(solution)/shard_map/all_to_all | solution.py:426
  49.6 0.1 mul.48
  49.7 0.2 reduce_window_sum.11
  49.9 0.1 collective-permute-start.3
  50.0 3.2 %collective-permute-start.4 = (bf16[2,256,512]{2,1,0:T(8,128)(2,1)S(1)}, bf16[2,256,512]{2,1,0:T(8,128)(2,1)}, u32[]{:S(2)}, u32[]{:S(2)}) collective-permute-start(bf16[2,256,512]{2,1,0:T(8,128)(2,1)S(1)} %shard_map.124.a), channel_id=1, source_target_pairs={{0,12},{4,0},{8,4},{12,8},{1,13},{5,1},{9,5},{13,9},{2,14},{6,2},{... | collective-permute-start | bytes 1572872 | tf_op jit(solution)/shard_map/ppermute | solution.py:79
  53.3 3.9 %collective-permute-start.6 = (bf16[256,512]{1,0:T(8,128)(2,1)S(1)}, bf16[256,512]{1,0:T(8,128)(2,1)S(1)}, u32[]{:S(2)}, u32[]{:S(2)}) collective-permute-start(bf16[256,512]{1,0:T(8,128)(2,1)S(1)} %collective-permute-done.2.refs_1_), channel_id=1, source_target_pairs={{0,16},{16,32},{32,48},{48,64},{64,80},{80,96},{96,112},{112,128},... | collective-permute-start | bytes 786440 | tf_op jit(solution)/shard_map/ppermute | solution.py:416
  57.2 0.1 convert_reduce_fusion
  57.4 12.0 %collective-permute-done.6.refs_1_ = bf16[256,512]{1,0:T(8,128)(2,1)S(1)} collective-permute-done((bf16[256,512]{1,0:T(8,128)(2,1)S(1)}, bf16[256,512]{1,0:T(8,128)(2,1)S(1)}, u32[]{:S(2)}, u32[]{:S(2)}) %collective-permute-start.6) | collective-permute-done | bytes 262176 | tf_op jit(solution)/shard_map/ppermute | solution.py:416
  69.5 0.3 collective-permute-start.20
  69.8 1.8 %collective-permute-start.19 = (bf16[2,256,512]{2,1,0:T(8,128)(2,1)S(1)}, bf16[2,256,512]{2,1,0:T(8,128)(2,1)S(1)}, u32[]{:S(2)}, u32[]{:S(2)}) collective-permute-start(bf16[2,256,512]{2,1,0:T(8,128)(2,1)S(1)} %shard_map.125.refs_2_.b), channel_id=1, source_target_pairs={{0,4},{4,8},{8,12},{12,0},{1,5},{5,9},{9,13},{13,1},{2,6},{6,10},{... | collective-permute-start | bytes 1572872 | tf_op jit(solution)/shard_map/ppermute | solution.py:79
  71.6 0.8 shard_map.130
  72.4 3.6 %all-to-all-start.1 = ((bf16[8,32,768]{2,1,0:T(8,128)(2,1)}), bf16[8,32,768]{2,1,0:T(8,128)(2,1)S(1)}, u32[]{:S(2)}, u32[]{:S(2)}) async-start(bf16[8,32,768]{2,1,0:T(8,128)(2,1)} %get-tuple-element.27), calls=%async_computation.1 | async-start | bytes 786432 | tf_op jit(solution)/shard_map/all_to_all | solution.py:442
  76.0 1.2 copy-done.16
  77.2 4.0 %shard_map.126 = (bf16[256,2048]{1,0:T(8,128)(2,1)}, f32[8,256]{1,0:T(8,128)S(1)}) custom-call(s32[7]{0:T(128)S(1)} %copy-done.14, bf16[256,2048]{1,0:T(8,128)(2,1)S(1)} %copy-done.16, bf16[256,2048]{1,0:T(8,128)(2,1)} %collective-permute-done.1.got_ref, f32[2,8,256]{2,1,0:T(8,128)S(1)} %fusion.2.active_ref, f32[2,4096]{1,0:T(2,128)S(1)} %copy-done.10, ...), custom_call_target="tpu_custom_call" | custom-call | flops 20000000000 | tf_op jit(solution)/shard_map/pallas_call | solution.py:262
  81.2 3.2 %collective-permute-start.17 = (f32[1,256]{1,0:T(1,128)S(1)}, f32[1,256]{1,0:T(1,128)S(1)}, u32[]{:S(2)}, u32[]{:S(2)}) collective-permute-start(f32[1,256]{1,0:T(1,128)S(1)} %slice.11), channel_id=1, source_target_pairs={{0,5},{1,4},{4,1},{5,0},{8,13},{9,12},{12,9},{13,8},{2,7},{3,6},{6... | collective-permute-start | bytes 3080 | tf_op jit(solution)/shard_map/ppermute | solution.py:438
  84.4 1.8 %collective-permute-start.15 = (f32[1,256]{1,0:T(1,128)S(1)}, f32[1,256]{1,0:T(1,128)S(1)}, u32[]{:S(2)}, u32[]{:S(2)}) collective-permute-start(f32[1,256]{1,0:T(1,128)S(1)} %slice.11), channel_id=1, source_target_pairs={{0,1},{1,0},{2,3},{3,2},{4,5},{5,4},{6,7},{7,6},{8,9},{9,8},{10,11... | collective-permute-start | bytes 3080 | tf_op jit(solution)/shard_map/ppermute | solution.py:75
  86.2 1.1 collective-permute-done.17
  87.3 2.2 %collective-permute-done.15 = f32[1,256]{1,0:T(1,128)S(1)} collective-permute-done((f32[1,256]{1,0:T(1,128)S(1)}, f32[1,256]{1,0:T(1,128)S(1)}, u32[]{:S(2)}, u32[]{:S(2)}) %collective-permute-start.15) | collective-permute-done | bytes 1056 | tf_op jit(solution)/shard_map/ppermute | solution.py:75
  89.5 1.1 collective-permute-start.18
  90.6 4.1 %collective-permute-done.18 = f32[2,256]{1,0:T(2,128)S(1)} collective-permute-done((f32[2,256]{1,0:T(2,128)S(1)}, f32[2,256]{1,0:T(2,128)S(1)}, u32[]{:S(2)}, u32[]{:S(2)}) %collective-permute-start.18) | collective-permute-done | bytes 2080 | tf_op jit(solution)/shard_map/ppermute | solution.py:441
  94.8 1.4 %collective-permute-start.22 = (bf16[256,768]{1,0:T(8,128)(2,1)S(1)}, bf16[256,768]{1,0:T(8,128)(2,1)S(1)}, u32[]{:S(2)}, u32[]{:S(2)}) collective-permute-start(bf16[256,768]{1,0:T(8,128)(2,1)S(1)} %bitcast.22), channel_id=1, source_target_pairs={{0,128},{128,0},{1,129},{129,1},{2,130},{130,2},{3,131},{131,3},{4... | collective-permute-start | bytes 1179656 | tf_op jit(solution)/shard_map/ppermute | solution.py:75
  96.2 0.3 collective-permute-start.7
  96.5 3.0 %collective-permute-start.25 = (bf16[2,256,512]{2,1,0:T(8,128)(2,1)S(1)}, bf16[2,256,512]{2,1,0:T(8,128)(2,1)S(1)}, u32[]{:S(2)}, u32[]{:S(2)}) collective-permute-start(bf16[2,256,512]{2,1,0:T(8,128)(2,1)S(1)} %collective-permute-done.20.refs_3_.br), channel_id=1, source_target_pairs={{0,12},{4,0},{8,4},{12,8},{1,13},{5,1},{9,5},{13,9},{2,14},{6,2},{... | collective-permute-start | bytes 1572872 | tf_op jit(solution)/shard_map/ppermute | solution.py:79
  99.4 3.2 %collective-permute-done.22.m10 = bf16[256,768]{1,0:T(8,128)(2,1)S(1)} collective-permute-done((bf16[256,768]{1,0:T(8,128)(2,1)S(1)}, bf16[256,768]{1,0:T(8,128)(2,1)S(1)}, u32[]{:S(2)}, u32[]{:S(2)}) %collective-permute-start.22) | collective-permute-done | bytes 393248 | tf_op jit(solution)/shard_map/ppermute | solution.py:75
  102.6 3.9 %collective-permute-start.26 = (f32[4,256]{1,0:T(4,128)S(1)}, f32[4,256]{1,0:T(4,128)S(1)}, u32[]{:S(2)}, u32[]{:S(2)}) collective-permute-start(f32[4,256]{1,0:T(4,128)S(1)} %pad_maximum_fusion.refs_1_.scale_ref), channel_id=1, source_target_pairs={{0,16},{16,32},{32,48},{48,64},{64,80},{80,96},{96,112},{112,128},... | collective-permute-start | bytes 12296 | tf_op jit(solution)/shard_map/ppermute | solution.py:447
  106.5 1.2 collective-permute-done.7.af
  107.8 3.2 %shard_map.132 = (bf16[4,256,512]{2,1,0:T(8,128)(2,1)S(1)}, bf16[4,256,256]{2,1,0:T(8,128)(2,1)S(1)}, bf16[1024,768]{1,0:T(8,128)(2,1)S(1)}) custom-call(s32[7]{0:T(128)S(1)} %copy-done.14, bf16[2,256,512]{2,1,0:T(8,128)(2,1)S(1)} %shard_map.124.a, bf16[2,256,512]{2,1,0:T(8,128)(2,1)} %collective-permute-done.3.refs_0_.al, ...), custom_call_target="tpu_custom_call" | custom-call | tf_op jit(solution)/shard_map/pallas_call | solution.py:313
  111.1 2.0 %shard_map.133.pm_ref = bf16[4,256,512]{2,1,0:T(8,128)(2,1)S(1)} custom-call(s32[7]{0:T(128)S(1)} %copy-done.14, bf16[2,256,512]{2,1,0:T(8,128)(2,1)S(1)} %copy-done.6, bf16[2,256,512]{2,1,0:T(8,128)(2,1)S(1)} %collective-permute-done.19.refs_2_.bl, bf16[2,256,512]{2,1,0:T(8,128)(2,1)S(1)} %collective-permute-done.20.refs_3_.br, ...), custom_call_target="tpu_custom_call" | custom-call | tf_op jit(solution)/shard_map/pallas_call | solution.py:313
  113.1 0.1 collective-permute-start.27
  113.2 0.5 collective-permute-start.24
  113.7 0.1 pad_add_fusion.2.place_ref
  113.8 2.1 %collective-permute-done.27.pt_ref = bf16[4,256,512]{2,1,0:T(8,128)(2,1)S(1)} collective-permute-done((bf16[4,256,512]{2,1,0:T(8,128)(2,1)S(1)}, bf16[4,256,512]{2,1,0:T(8,128)(2,1)S(1)}, u32[]{:S(2)}, u32[]{:S(2)}) %collective-permute-start.27) | collective-permute-done | bytes 1048608 | tf_op jit(solution)/shard_map/ppermute | solution.py:75
  115.8 1.6 %collective-permute-done.24.ot_ref = bf16[4,256,512]{2,1,0:T(8,128)(2,1)} collective-permute-done((bf16[4,256,512]{2,1,0:T(8,128)(2,1)S(1)}, bf16[4,256,512]{2,1,0:T(8,128)(2,1)}, u32[]{:S(2)}, u32[]{:S(2)}) %collective-permute-start.24) | collective-permute-done | bytes 1048608 | tf_op jit(solution)/shard_map/ppermute | solution.py:75
  117.5 1.0 copy-done.2
  118.5 5.5 %shard_map.135 = (bf16[256,256]{1,0:T(8,128)(2,1)S(1)}, bf16[256,256]{1,0:T(8,128)(2,1)S(1)}, bf16[256,256]{1,0:T(8,128)(2,1)S(1)}) custom-call(s32[6]{0:T(128)S(1)} %pad_add_fusion.2.place_ref, bf16[4,256,256]{2,1,0:T(8,128)(2,1)S(1)} %copy-done.2, bf16[4,256,512]{2,1,0:T(8,128)(2,1)S(1)} %get-tuple-element.31.om_ref, ...), custom_call_target="tpu_custom_call" | custom-call | tf_op jit(solution)/shard_map/pallas_call | solution.py:358
  124.0 0.1 collective-permute-start.28
  124.1 2.1 %collective-permute-start.29 = (bf16[256,256]{1,0:T(8,128)(2,1)S(1)}, bf16[256,256]{1,0:T(8,128)(2,1)S(1)}, u32[]{:S(2)}, u32[]{:S(2)}) collective-permute-start(bf16[256,256]{1,0:T(8,128)(2,1)S(1)} %get-tuple-element.34), channel_id=1, source_target_pairs={{0,8},{4,12},{8,0},{12,4},{1,9},{5,13},{9,1},{13,5},{2,10},{6,14},... | collective-permute-start | bytes 393224 | tf_op jit(solution)/shard_map/ppermute | solution.py:79
  126.2 1.1 collective-permute-start.30
  127.4 0.1 pad_add_fusion.1.place_ref
  127.5 3.0 %shard_map.134.a_ref = bf16[256,256]{1,0:T(8,128)(2,1)S(1)} custom-call(s32[4]{0:T(128)S(1)} %pad_add_fusion.1.place_ref, bf16[4,256,256]{2,1,0:T(8,128)(2,1)S(1)} %copy-done.3, bf16[4,256,512]{2,1,0:T(8,128)(2,1)S(1)} %get-tuple-element.31.om_ref, bf16[4,256,512]{2,1,0:T(8,128)(2,1)} %collective-permute-done.24.ot_ref, ...), custom_call_target="tpu_custom_call" | custom-call | tf_op jit(solution)/shard_map/pallas_call | solution.py:358
  130.5 3.2 %collective-permute-done.28.b_ref = bf16[256,256]{1,0:T(8,128)(2,1)S(1)} collective-permute-done((bf16[256,256]{1,0:T(8,128)(2,1)S(1)}, bf16[256,256]{1,0:T(8,128)(2,1)S(1)}, u32[]{:S(2)}, u32[]{:S(2)}) %collective-permute-start.28) | collective-permute-done | bytes 131104 | tf_op jit(solution)/shard_map/ppermute | solution.py:79
  133.6 0.6 collective-permute-done.30.d_ref
  134.3 1.4 %shard_map.136 = bf16[256,1024]{1,0:T(8,128)(2,1)} custom-call(s32[3]{0:T(128)S(1)} %pad_add_fusion.place_ref, bf16[256,256]{1,0:T(8,128)(2,1)S(1)} %shard_map.134.a_ref, bf16[256,256]{1,0:T(8,128)(2,1)S(1)} %collective-permute-done.28.b_ref, bf16[256,256]{1,0:T(8,128)(2,1)S(1)} %collective-permute-done.29.c_ref, ...), custom_call_target="tpu_custom_call" | custom-call | tf_op jit(solution)/shard_map/pallas_call | solution.py:375
  (73 shorter events, 0.5 us)
Async XLA Ops:
  1.3 19.9 %copy-start.4 = (bf16[1,4,512,512]{3,2,1,0:T(8,128)(2,1)S(1)}, bf16[1,4,512,512]{3,2,1,0:T(8,128)(2,1)}, u32[]{:S(2)}) copy-start(bf16[1,4,512,512]{3,2,1,0:T(8,128)(2,1)} %param.14) | copy-start | bytes 6291460
  1.3 19.9 %copy-start.7 = (bf16[1,3,512,256]{3,2,1,0:T(8,128)(2,1)S(1)}, bf16[1,3,512,256]{3,2,1,0:T(8,128)(2,1)}, u32[]{:S(2)}) copy-start(bf16[1,3,512,256]{3,2,1,0:T(8,128)(2,1)} %param.12) | copy-start | bytes 2359300
  1.3 19.9 %copy-start.9 = (bf16[1,256,512]{2,1,0:T(8,128)(2,1)S(1)}, bf16[1,256,512]{2,1,0:T(8,128)(2,1)}, u32[]{:S(2)}) copy-start(bf16[1,256,512]{2,1,0:T(8,128)(2,1)} %param.13) | copy-start | bytes 786436
  1.3 30.2 %copy-start.14 = (s32[7]{0:T(128)S(1)}, s32[7]{0:T(128)}, u32[]{:S(2)}) copy-start(s32[7]{0:T(128)} %stack.42.at_ref) | copy-start | bytes 88
  4.0 20.9 %collective-permute-start.11 = (bf16[2,128,256]{2,1,0:T(8,128)(2,1)}, bf16[2,128,256]{2,1,0:T(8,128)(2,1)S(1)}, u32[]{:S(2)}, u32[]{:S(2)}) collective-permute-start(bf16[2,128,256]{2,1,0:T(8,128)(2,1)} %get-tuple-element.26.mine_ref), channel_id=1, source_target_pairs={{0,1},{1,0},{2,3},{3,2},{4,5},{5,4},{6,7},{7,6},{8,9},{9,8},{10,11... | collective-permute-start | bytes 393224 | tf_op jit(solution)/shard_map/ppermute | solution.py:75
  6.3 18.5 %collective-permute-start.10 = (bf16[3,32,256]{2,1,0:T(8,128)(2,1)}, bf16[3,32,256]{2,1,0:T(8,128)(2,1)S(1)}, u32[]{:S(2)}, u32[]{:S(2)}) collective-permute-start(bf16[3,32,256]{2,1,0:T(8,128)(2,1)} %get-tuple-element.25), channel_id=1, source_target_pairs={{0,12},{4,0},{8,4},{12,8},{1,13},{5,1},{9,5},{13,9},{2,14},{6,2},{... | collective-permute-start | bytes 147464 | tf_op jit(solution)/shard_map/ppermute | solution.py:79
  9.0 15.8 %collective-permute-start.8 = (bf16[3,32,256]{2,1,0:T(8,128)(2,1)}, bf16[3,32,256]{2,1,0:T(8,128)(2,1)S(1)}, u32[]{:S(2)}, u32[]{:S(2)}) collective-permute-start(bf16[3,32,256]{2,1,0:T(8,128)(2,1)} %get-tuple-element.23), channel_id=1, source_target_pairs={{0,4},{4,8},{8,12},{12,0},{1,5},{5,9},{9,13},{13,1},{2,6},{6,10},{... | collective-permute-start | bytes 147464 | tf_op jit(solution)/shard_map/ppermute | solution.py:79
  9.0 15.8 %collective-permute-start.9 = (bf16[3,32,256]{2,1,0:T(8,128)(2,1)}, bf16[3,32,256]{2,1,0:T(8,128)(2,1)S(1)}, u32[]{:S(2)}, u32[]{:S(2)}) collective-permute-start(bf16[3,32,256]{2,1,0:T(8,128)(2,1)} %get-tuple-element.24), channel_id=1, source_target_pairs={{0,8},{4,12},{8,0},{12,4},{1,9},{5,13},{9,1},{13,5},{2,10},{6,14},... | collective-permute-start | bytes 147464 | tf_op jit(solution)/shard_map/ppermute | solution.py:79
  12.0 9.2 %collective-permute-start = (bf16[8,512]{1,0:T(8,128)(2,1)S(1)}, bf16[8,512]{1,0:T(8,128)(2,1)S(1)}, u32[]{:S(2)}, u32[]{:S(2)}) collective-permute-start(bf16[8,512]{1,0:T(8,128)(2,1)S(1)} %slice_bitcast_fusion), channel_id=1, source_target_pairs={{0,2},{2,4},{4,6},{6,8},{8,10},{10,12},{12,14},{14,16},{16,18},{18... | collective-permute-start | bytes 24584 | tf_op jit(solution)/shard_map/ppermute | solution.py:405
  21.2 1.0 copy-start.8
  22.3 9.2 %copy-start = (bf16[1,512,4096]{2,1,0:T(8,128)(2,1)S(1)}, bf16[1,512,4096]{2,1,0:T(8,128)(2,1)}, u32[]{:S(2)}) copy-start(bf16[1,512,4096]{2,1,0:T(8,128)(2,1)} %param.15) | copy-start | bytes 12582916
  24.9 0.8 copy-start.13
  25.7 13.5 %copy-start.10 = (f32[2,4096]{1,0:T(2,128)S(1)}, f32[2,4096]{1,0:T(2,128)}, u32[]{:S(2)}) copy-start(f32[2,4096]{1,0:T(2,128)} %t1.1) | copy-start | bytes 98308
  25.7 13.5 %copy-start.11 = (bf16[2,128,256]{2,1,0:T(8,128)(2,1)S(1)}, bf16[2,128,256]{2,1,0:T(8,128)(2,1)}, u32[]{:S(2)}) copy-start(bf16[2,128,256]{2,1,0:T(8,128)(2,1)} %get-tuple-element.26.mine_ref) | copy-start | bytes 393220
  25.7 13.5 %copy-start.12 = (f32[4096]{0:T(1024)S(1)}, f32[4096]{0:T(1024)}, u32[]{:S(2)}) copy-start(f32[4096]{0:T(1024)} %param.18) | copy-start | bytes 49156
  25.7 5.8 %collective-permute-start.13 = (bf16[4,3,32,256]{3,2,1,0:T(8,128)(2,1)S(1)}, bf16[4,3,32,256]{3,2,1,0:T(8,128)(2,1)S(1)}, u32[]{:S(2)}, u32[]{:S(2)}) collective-permute-start(bf16[4,3,32,256]{3,2,1,0:T(8,128)(2,1)S(1)} %shard_map.128.w00), channel_id=1, source_target_pairs={{0,128},{128,0},{1,129},{129,1},{2,130},{130,2},{3,131},{131,3},{4... | collective-permute-start | bytes 589832 | tf_op jit(solution)/shard_map/ppermute | solution.py:75
  25.8 12.1 %collective-permute-start.2 = (bf16[256,512]{1,0:T(8,128)(2,1)S(1)}, bf16[256,512]{1,0:T(8,128)(2,1)S(1)}, u32[]{:S(2)}, u32[]{:S(2)}) collective-permute-start(bf16[256,512]{1,0:T(8,128)(2,1)S(1)} %shard_map.122.latent_ref.refs_0_.refs_4_), channel_id=1, source_target_pairs={{0,1},{1,0},{2,3},{3,2},{4,5},{5,4},{6,7},{7,6},{8,9},{9,8},{10,11... | collective-permute-start | bytes 786440 | tf_op jit(solution)/shard_map/ppermute | solution.py:75
  27.1 12.1 %collective-permute-start.5 = (bf16[256,512]{1,0:T(8,128)(2,1)S(1)}, bf16[256,512]{1,0:T(8,128)(2,1)S(1)}, u32[]{:S(2)}, u32[]{:S(2)}) collective-permute-start(bf16[256,512]{1,0:T(8,128)(2,1)S(1)} %shard_map.122.latent_ref.refs_0_.refs_4_), channel_id=1, source_target_pairs={{0,16},{16,32},{32,48},{48,64},{64,80},{80,96},{96,112},{112,128},... | collective-permute-start | bytes 786440 | tf_op jit(solution)/shard_map/ppermute | solution.py:415
  29.1 10.1 %collective-permute-start.12 = (bf16[4,3,32,256]{3,2,1,0:T(8,128)(2,1)S(1)}, bf16[4,3,32,256]{3,2,1,0:T(8,128)(2,1)S(1)}, u32[]{:S(2)}, u32[]{:S(2)}) collective-permute-start(bf16[4,3,32,256]{3,2,1,0:T(8,128)(2,1)S(1)} %shard_map.128.w00), channel_id=1, source_target_pairs={{0,2},{2,0},{1,3},{3,1},{4,6},{6,4},{5,7},{7,5},{8,10},{10,8},{9,1... | collective-permute-start | bytes 589832 | tf_op jit(solution)/shard_map/ppermute | solution.py:75
  31.5 7.7 %collective-permute-start.14 = (bf16[4,3,32,256]{3,2,1,0:T(8,128)(2,1)S(1)}, bf16[4,3,32,256]{3,2,1,0:T(8,128)(2,1)S(1)}, u32[]{:S(2)}, u32[]{:S(2)}) collective-permute-start(bf16[4,3,32,256]{3,2,1,0:T(8,128)(2,1)S(1)} %collective-permute-done.13.w10), channel_id=1, source_target_pairs={{0,2},{2,0},{1,3},{3,1},{4,6},{6,4},{5,7},{7,5},{8,10},{10,8},{9,1... | collective-permute-start | bytes 589832 | tf_op jit(solution)/shard_map/ppermute | solution.py:75
  35.2 1.0 copy-start.15
  36.2 13.4 %copy-start.17 = (s32[2,32]{1,0:T(2,128)S(1)}, s32[2,32]{1,0:T(2,128)}, u32[]{:S(2)}) copy-start(s32[2,32]{1,0:T(2,128)} %param.16) | copy-start | bytes 772
  36.2 39.8 %collective-permute-start.1 = (bf16[256,2048]{1,0:T(8,128)(2,1)}, bf16[256,2048]{1,0:T(8,128)(2,1)}, u32[]{:S(2)}, u32[]{:S(2)}) collective-permute-start(bf16[256,2048]{1,0:T(8,128)(2,1)} %get-tuple-element.20.refs_0_), channel_id=1, source_target_pairs={{0,1},{1,0},{2,3},{3,2},{4,5},{5,4},{6,7},{7,6},{8,9},{9,8},{10,11... | collective-permute-start | bytes 3145736 | tf_op jit(solution)/shard_map/ppermute | solution.py:75
  42.4 29.2 %all-to-all-start = ((bf16[8,32,896]{2,1,0:T(8,128)(2,1)}), bf16[8,32,896]{2,1,0:T(8,128)(2,1)S(1)}, u32[]{:S(2)}, u32[]{:S(2)}) async-start(bf16[8,32,896]{2,1,0:T(8,128)(2,1)} %shard_map.129), calls=%async_computation | async-start | bytes 917504 | tf_op jit(solution)/shard_map/all_to_all | solution.py:426
  49.9 26.1 %collective-permute-start.3 = (bf16[2,256,512]{2,1,0:T(8,128)(2,1)S(1)}, bf16[2,256,512]{2,1,0:T(8,128)(2,1)}, u32[]{:S(2)}, u32[]{:S(2)}) collective-permute-start(bf16[2,256,512]{2,1,0:T(8,128)(2,1)S(1)} %shard_map.124.a), channel_id=1, source_target_pairs={{0,4},{4,8},{8,12},{12,0},{1,5},{5,9},{9,13},{13,1},{2,6},{6,10},{... | collective-permute-start | bytes 1572872 | tf_op jit(solution)/shard_map/ppermute | solution.py:79
  50.0 26.0 %collective-permute-start.4 = (bf16[2,256,512]{2,1,0:T(8,128)(2,1)S(1)}, bf16[2,256,512]{2,1,0:T(8,128)(2,1)}, u32[]{:S(2)}, u32[]{:S(2)}) collective-permute-start(bf16[2,256,512]{2,1,0:T(8,128)(2,1)S(1)} %shard_map.124.a), channel_id=1, source_target_pairs={{0,12},{4,0},{8,4},{12,8},{1,13},{5,1},{9,5},{13,9},{2,14},{6,2},{... | collective-permute-start | bytes 1572872 | tf_op jit(solution)/shard_map/ppermute | solution.py:79
  53.3 16.1 %collective-permute-start.6 = (bf16[256,512]{1,0:T(8,128)(2,1)S(1)}, bf16[256,512]{1,0:T(8,128)(2,1)S(1)}, u32[]{:S(2)}, u32[]{:S(2)}) collective-permute-start(bf16[256,512]{1,0:T(8,128)(2,1)S(1)} %collective-permute-done.2.refs_1_), channel_id=1, source_target_pairs={{0,16},{16,32},{32,48},{48,64},{64,80},{80,96},{96,112},{112,128},... | collective-permute-start | bytes 786440 | tf_op jit(solution)/shard_map/ppermute | solution.py:416
  69.4 11.8 %copy-start.5 = (bf16[2,256,512]{2,1,0:T(8,128)(2,1)}, bf16[2,256,512]{2,1,0:T(8,128)(2,1)S(1)}, u32[]{:S(2)}) copy-start(bf16[2,256,512]{2,1,0:T(8,128)(2,1)S(1)} %shard_map.125.refs_2_.b) | copy-start | bytes 1572868
  69.5 25.2 %collective-permute-start.20 = (bf16[2,256,512]{2,1,0:T(8,128)(2,1)S(1)}, bf16[2,256,512]{2,1,0:T(8,128)(2,1)S(1)}, u32[]{:S(2)}, u32[]{:S(2)}) collective-permute-start(bf16[2,256,512]{2,1,0:T(8,128)(2,1)S(1)} %shard_map.125.refs_2_.b), channel_id=1, source_target_pairs={{0,12},{4,0},{8,4},{12,8},{1,13},{5,1},{9,5},{13,9},{2,14},{6,2},{... | collective-permute-start | bytes 1572872 | tf_op jit(solution)/shard_map/ppermute | solution.py:79
  69.8 24.9 %collective-permute-start.19 = (bf16[2,256,512]{2,1,0:T(8,128)(2,1)S(1)}, bf16[2,256,512]{2,1,0:T(8,128)(2,1)S(1)}, u32[]{:S(2)}, u32[]{:S(2)}) collective-permute-start(bf16[2,256,512]{2,1,0:T(8,128)(2,1)S(1)} %shard_map.125.refs_2_.b), channel_id=1, source_target_pairs={{0,4},{4,8},{8,12},{12,0},{1,5},{5,9},{9,13},{13,1},{2,6},{6,10},{... | collective-permute-start | bytes 1572872 | tf_op jit(solution)/shard_map/ppermute | solution.py:79
  72.4 22.3 %all-to-all-start.1 = ((bf16[8,32,768]{2,1,0:T(8,128)(2,1)}), bf16[8,32,768]{2,1,0:T(8,128)(2,1)S(1)}, u32[]{:S(2)}, u32[]{:S(2)}) async-start(bf16[8,32,768]{2,1,0:T(8,128)(2,1)} %get-tuple-element.27), calls=%async_computation.1 | async-start | bytes 786432 | tf_op jit(solution)/shard_map/all_to_all | solution.py:442
  76.0 1.2 copy-start.16
  81.2 5.0 %collective-permute-start.16 = (f32[1,256]{1,0:T(1,128)S(1)}, f32[1,256]{1,0:T(1,128)S(1)}, u32[]{:S(2)}, u32[]{:S(2)}) collective-permute-start(f32[1,256]{1,0:T(1,128)S(1)} %slice.11), channel_id=1, source_target_pairs={{0,4},{4,0},{8,12},{12,8},{1,5},{5,1},{9,13},{13,9},{2,6},{6,2},{1... | collective-permute-start | bytes 3080 | tf_op jit(solution)/shard_map/ppermute | solution.py:437
  81.2 6.1 %collective-permute-start.17 = (f32[1,256]{1,0:T(1,128)S(1)}, f32[1,256]{1,0:T(1,128)S(1)}, u32[]{:S(2)}, u32[]{:S(2)}) collective-permute-start(f32[1,256]{1,0:T(1,128)S(1)} %slice.11), channel_id=1, source_target_pairs={{0,5},{1,4},{4,1},{5,0},{8,13},{9,12},{12,9},{13,8},{2,7},{3,6},{6... | collective-permute-start | bytes 3080 | tf_op jit(solution)/shard_map/ppermute | solution.py:438
  84.4 5.1 %collective-permute-start.15 = (f32[1,256]{1,0:T(1,128)S(1)}, f32[1,256]{1,0:T(1,128)S(1)}, u32[]{:S(2)}, u32[]{:S(2)}) collective-permute-start(f32[1,256]{1,0:T(1,128)S(1)} %slice.11), channel_id=1, source_target_pairs={{0,1},{1,0},{2,3},{3,2},{4,5},{5,4},{6,7},{7,6},{8,9},{9,8},{10,11... | collective-permute-start | bytes 3080 | tf_op jit(solution)/shard_map/ppermute | solution.py:75
  89.5 5.2 %collective-permute-start.18 = (f32[2,256]{1,0:T(2,128)S(1)}, f32[2,256]{1,0:T(2,128)S(1)}, u32[]{:S(2)}, u32[]{:S(2)}) collective-permute-start(f32[2,256]{1,0:T(2,128)S(1)} %fusion.4), channel_id=1, source_target_pairs={{0,8},{4,12},{8,0},{12,4},{1,9},{5,13},{9,1},{13,5},{2,10},{6,14},... | collective-permute-start | bytes 6152 | tf_op jit(solution)/shard_map/ppermute | solution.py:441
  94.7 16.3 %copy-start.6 = (bf16[2,256,512]{2,1,0:T(8,128)(2,1)S(1)}, bf16[2,256,512]{2,1,0:T(8,128)(2,1)}, u32[]{:S(2)}) copy-start(bf16[2,256,512]{2,1,0:T(8,128)(2,1)} %copy-done.5) | copy-start | bytes 1572868
  94.8 7.9 %collective-permute-start.22 = (bf16[256,768]{1,0:T(8,128)(2,1)S(1)}, bf16[256,768]{1,0:T(8,128)(2,1)S(1)}, u32[]{:S(2)}, u32[]{:S(2)}) collective-permute-start(bf16[256,768]{1,0:T(8,128)(2,1)S(1)} %bitcast.22), channel_id=1, source_target_pairs={{0,128},{128,0},{1,129},{129,1},{2,130},{130,2},{3,131},{131,3},{4... | collective-permute-start | bytes 1179656 | tf_op jit(solution)/shard_map/ppermute | solution.py:75
  96.2 11.6 %collective-permute-start.7 = (bf16[2,256,512]{2,1,0:T(8,128)(2,1)}, bf16[2,256,512]{2,1,0:T(8,128)(2,1)S(1)}, u32[]{:S(2)}, u32[]{:S(2)}) collective-permute-start(bf16[2,256,512]{2,1,0:T(8,128)(2,1)} %collective-permute-done.3.refs_0_.al), channel_id=1, source_target_pairs={{0,4},{4,8},{8,12},{12,0},{1,5},{5,9},{9,13},{13,1},{2,6},{6,10},{... | collective-permute-start | bytes 1572872 | tf_op jit(solution)/shard_map/ppermute | solution.py:79
  96.5 14.6 %collective-permute-start.25 = (bf16[2,256,512]{2,1,0:T(8,128)(2,1)S(1)}, bf16[2,256,512]{2,1,0:T(8,128)(2,1)S(1)}, u32[]{:S(2)}, u32[]{:S(2)}) collective-permute-start(bf16[2,256,512]{2,1,0:T(8,128)(2,1)S(1)} %collective-permute-done.20.refs_3_.br), channel_id=1, source_target_pairs={{0,12},{4,0},{8,4},{12,8},{1,13},{5,1},{9,5},{13,9},{2,14},{6,2},{... | collective-permute-start | bytes 1572872 | tf_op jit(solution)/shard_map/ppermute | solution.py:79
  99.4 8.3 %collective-permute-start.21 = (bf16[256,768]{1,0:T(8,128)(2,1)S(1)}, bf16[256,768]{1,0:T(8,128)(2,1)S(1)}, u32[]{:S(2)}, u32[]{:S(2)}) collective-permute-start(bf16[256,768]{1,0:T(8,128)(2,1)S(1)} %bitcast.23), channel_id=1, source_target_pairs={{0,2},{2,0},{1,3},{3,1},{4,6},{6,4},{5,7},{7,5},{8,10},{10,8},{9,1... | collective-permute-start | bytes 1179656 | tf_op jit(solution)/shard_map/ppermute | solution.py:75
  102.6 5.2 %collective-permute-start.23 = (bf16[256,768]{1,0:T(8,128)(2,1)S(1)}, bf16[256,768]{1,0:T(8,128)(2,1)S(1)}, u32[]{:S(2)}, u32[]{:S(2)}) collective-permute-start(bf16[256,768]{1,0:T(8,128)(2,1)S(1)} %collective-permute-done.22.m10), channel_id=1, source_target_pairs={{0,2},{2,0},{1,3},{3,1},{4,6},{6,4},{5,7},{7,5},{8,10},{10,8},{9,1... | collective-permute-start | bytes 1179656 | tf_op jit(solution)/shard_map/ppermute | solution.py:75
  102.6 8.4 %collective-permute-start.26 = (f32[4,256]{1,0:T(4,128)S(1)}, f32[4,256]{1,0:T(4,128)S(1)}, u32[]{:S(2)}, u32[]{:S(2)}) collective-permute-start(f32[4,256]{1,0:T(4,128)S(1)} %pad_maximum_fusion.refs_1_.scale_ref), channel_id=1, source_target_pairs={{0,16},{16,32},{32,48},{48,64},{64,80},{80,96},{96,112},{112,128},... | collective-permute-start | bytes 12296 | tf_op jit(solution)/shard_map/ppermute | solution.py:447
  111.0 2.0 %copy-start.1 = (bf16[4,256,256]{2,1,0:T(8,128)(2,1)}, bf16[4,256,256]{2,1,0:T(8,128)(2,1)S(1)}, u32[]{:S(2)}) copy-start(bf16[4,256,256]{2,1,0:T(8,128)(2,1)S(1)} %get-tuple-element.30.q_ref) | copy-start | bytes 1572868
  111.1 2.6 %copy-start.18 = (s32[3]{0:T(128)S(1)}, s32[3]{0:T(128)}, u32[]{:S(2)}) copy-start(s32[3]{0:T(128)} %constant.57.clone) | copy-start | bytes 40
  113.1 2.7 %collective-permute-start.27 = (bf16[4,256,512]{2,1,0:T(8,128)(2,1)S(1)}, bf16[4,256,512]{2,1,0:T(8,128)(2,1)S(1)}, u32[]{:S(2)}, u32[]{:S(2)}) collective-permute-start(bf16[4,256,512]{2,1,0:T(8,128)(2,1)S(1)} %shard_map.133.pm_ref), channel_id=1, source_target_pairs={{0,2},{2,0},{1,3},{3,1},{4,6},{6,4},{5,7},{7,5},{8,10},{10,8},{9,1... | collective-permute-start | bytes 3145736 | tf_op jit(solution)/shard_map/ppermute | solution.py:75
  113.2 4.3 %collective-permute-start.24 = (bf16[4,256,512]{2,1,0:T(8,128)(2,1)S(1)}, bf16[4,256,512]{2,1,0:T(8,128)(2,1)}, u32[]{:S(2)}, u32[]{:S(2)}) collective-permute-start(bf16[4,256,512]{2,1,0:T(8,128)(2,1)S(1)} %get-tuple-element.31.om_ref), channel_id=1, source_target_pairs={{0,2},{2,0},{1,3},{3,1},{4,6},{6,4},{5,7},{7,5},{8,10},{10,8},{9,1... | collective-permute-start | bytes 3145736 | tf_op jit(solution)/shard_map/ppermute | solution.py:75
  117.5 1.0 copy-start.2
  118.5 9.0 %copy-start.3 = (bf16[4,256,256]{2,1,0:T(8,128)(2,1)S(1)}, bf16[4,256,256]{2,1,0:T(8,128)(2,1)}, u32[]{:S(2)}) copy-start(bf16[4,256,256]{2,1,0:T(8,128)(2,1)} %copy-done.1) | copy-start | bytes 1572868
  124.0 9.6 %collective-permute-start.28 = (bf16[256,256]{1,0:T(8,128)(2,1)S(1)}, bf16[256,256]{1,0:T(8,128)(2,1)S(1)}, u32[]{:S(2)}, u32[]{:S(2)}) collective-permute-start(bf16[256,256]{1,0:T(8,128)(2,1)S(1)} %get-tuple-element.33), channel_id=1, source_target_pairs={{0,4},{4,8},{8,12},{12,0},{1,5},{5,9},{9,13},{13,1},{2,6},{6,10},{... | collective-permute-start | bytes 393224 | tf_op jit(solution)/shard_map/ppermute | solution.py:79
  124.1 9.6 %collective-permute-start.29 = (bf16[256,256]{1,0:T(8,128)(2,1)S(1)}, bf16[256,256]{1,0:T(8,128)(2,1)S(1)}, u32[]{:S(2)}, u32[]{:S(2)}) collective-permute-start(bf16[256,256]{1,0:T(8,128)(2,1)S(1)} %get-tuple-element.34), channel_id=1, source_target_pairs={{0,8},{4,12},{8,0},{12,4},{1,9},{5,13},{9,1},{13,5},{2,10},{6,14},... | collective-permute-start | bytes 393224 | tf_op jit(solution)/shard_map/ppermute | solution.py:79
  126.2 8.1 %collective-permute-start.30 = (bf16[256,256]{1,0:T(8,128)(2,1)S(1)}, bf16[256,256]{1,0:T(8,128)(2,1)S(1)}, u32[]{:S(2)}, u32[]{:S(2)}) collective-permute-start(bf16[256,256]{1,0:T(8,128)(2,1)S(1)} %get-tuple-element.35), channel_id=1, source_target_pairs={{0,12},{4,0},{8,4},{12,8},{1,13},{5,1},{9,5},{13,9},{2,14},{6,2},{... | collective-permute-start | bytes 393224 | tf_op jit(solution)/shard_map/ppermute | solution.py:79
